TPU v7x, 32 devices: a whole 2x2x4 slice. The times are simulated.
32 devices in a mesh: ctx: 8 (over y, x, core), head: 4 (over z).
Axes of the slice: x: 2, y: 2, z: 4, core: 2. Of those that a mesh axis runs over, the one named last changes fastest.
Arguments:
- queries: float32 [4096, 8192], P('ctx', 'head'), as said below
- keys: float32 [4096, 8192], P('ctx', 'head')
- values: float32 [4096, 8192], P('ctx', 'head')
- head_gain: float32 [2, 64], P(None, 'head'), may hold values from 0.3 to 3
Outputs:
- mixed: float32 [4096, 8192], P('ctx', 'head')
Inputs may be any that keep to these rules, and one draw needn't show every extreme that they name: queries, keys and values are finite real numbers.
All inputs are finite; a program needn't handle non-finite values.
Results may differ from a plain program's by a relative error of at most 0.0003.
Values sent between devices are 32-bit elements; how exact they have to be, the bound alone decides.
No kernel may reach another device: no remote copies, remote signals or barrier semaphores. Data moves between devices by JAX's collectives and lax.ppermute only.
A program may use at most 128 MiB of HBM per device.

v0:
```python
import functools
import math

import jax
import jax.numpy as jnp
from jax import lax
from jax.experimental import pallas as pl
from jax.experimental.pallas import tpu as pltpu
from jax.sharding import PartitionSpec as P

HEADS = 64
HD = 128
WINDOW = 128
EPS = 1e-06
F32 = jnp.float32
BF16 = jnp.bfloat16
EXP2_SCALE = math.log2(math.e) / math.sqrt(HD)
VMEM_BYTES = 24 * 1024 * 1024


def halves(x):
    high = x.astype(BF16)
    low = (x - high.astype(F32)).astype(BF16)
    return high, low


def dot(a, b):
    return lax.dot_general(a, b, (((1,), (0,)), ((), ())), preferred_element_type=F32)


def dot_rows(a, b):
    return lax.dot_general(a, b, (((1,), (1,)), ((), ())), preferred_element_type=F32)


def dot_columns(a, b):
    return lax.dot_general(a, b, (((0,), (0,)), ((), ())), preferred_element_type=F32)


def side(a, b):
    return jnp.concatenate([a, b], axis=1)


def stack(a, b):
    return jnp.concatenate([a, b], axis=0)


def product(a_high, a_low, b_high, b_low):
    return dot(a_high, b_high) + dot(a_high, b_low) + dot(a_low, b_high)


def outer_state(k_high, k_low, v_high, v_low):
    grid = dot_columns(side(k_high, k_low), side(v_high, v_low))
    return grid[:HD, :HD] + (grid[:HD, HD:] + grid[HD:, :HD]) + grid[HD:, HD:]


def pair_scores(q_high, q_low, k_high, k_low):
    return dot_rows(side(q_high, q_low), side(k_high, k_high)) + dot_rows(q_high, k_low)


def lower_mask():
    rows = lax.broadcasted_iota(jnp.int32, (WINDOW, WINDOW), 0)
    columns = lax.broadcasted_iota(jnp.int32, (WINDOW, WINDOW), 1)
    return rows >= columns


def window_tile(scores, lower, values, gain):
    biggest = jnp.max(scores, axis=1, keepdims=True)
    weights = jnp.exp2((scores - biggest) * EXP2_SCALE)
    total = jnp.sum(weights, axis=1, keepdims=True)
    wide = side(jnp.where(lower, 0.0, weights), jnp.where(lower, weights, 0.0))
    out = product(*halves(wide), *values)
    return out * (gain / total)


def row_sums(square):
    ones = jnp.ones((8, HD), BF16)
    high, low = halves(square)
    return dot_rows(ones, high) + dot_rows(ones, low)


def totals_kernel(k_ref, v_ref, keep_ref, send_ref, tail_k_ref, tail_v_ref):
    core = lax.axis_index("ctx") % 2
    states = []
    for j in range(2):
        columns = slice(j * HD, (j + 1) * HD)
        states.append(outer_state(*halves(k_ref[:, columns]), *halves(v_ref[:, columns])))
    keep_ref[0] = jnp.where(core == 0, states[0], states[1])
    send_ref[0] = jnp.where(core == 0, states[1], states[0])
    rows = k_ref.shape[0]
    tail_k_ref[...] = k_ref[rows - WINDOW :, :]
    tail_v_ref[...] = v_ref[rows - WINDOW :, :]


def local_kernel(gain_ref, q_ref, k_ref, v_ref, a_ref, b_ref, sum_ref, square_ref):
    step = pl.program_id(0)
    lower = lower_mask()
    tiles = q_ref.shape[0] // WINDOW

    @pl.when(step == 0)
    def _():
        square_ref[...] = jnp.zeros_like(square_ref)

    for j in range(2):
        columns = slice(j * HD, (j + 1) * HD)
        gain_a = gain_ref[0, 2 * step + j]
        gain_b = gain_ref[1, 2 * step + j]
        state = None
        k_before = v_before = None
        for n in range(tiles):
            rows = slice(n * WINDOW, (n + 1) * WINDOW)
            q_high, q_low = halves(q_ref[rows, columns])
            k_now = halves(k_ref[rows, columns])
            v_now = halves(v_ref[rows, columns])
            if n == 0:
                now = pair_scores(q_high, q_low, *k_now)
                inner = jnp.where(lower, now, 0.0)
                b = product(*halves(inner), *v_now)
                a_ref[rows, columns] = jnp.zeros((WINDOW, HD), F32)
            else:
                both = pair_scores(
                    q_high, q_low, stack(k_before[0], k_now[0]), stack(k_before[1], k_now[1])
                )
                before, now = both[:, :WINDOW], both[:, WINDOW:]
                values = stack(v_before[0], v_now[0]), stack(v_before[1], v_now[1])
                a = window_tile(jnp.where(lower, now, before), lower, values, gain_a)
                a_ref[rows, columns] = a
                square_ref[rows, :] += a * a
                inner_high, inner_low = halves(jnp.where(lower, now, 0.0))
                state_high, state_low = halves(state)
                b = product(
                    side(inner_high, q_high),
                    side(inner_low, q_low),
                    stack(v_now[0], state_high),
                    stack(v_now[1], state_low),
                )
            b_ref[rows, columns] = b * gain_b
            if n < tiles - 1:
                added = outer_state(*k_now, *v_now)
                state = added if state is None else state + added
            k_before, v_before = k_now, v_now

    @pl.when(step == pl.num_programs(0) - 1)
    def _():
        sum_ref[...] = row_sums(square_ref[...])


def earlier_kernel(gain_ref, q_ref, b_ref, mine_ref, other_ref, sum_a_ref, out_ref, sums_ref, square_ref):
    step = pl.program_id(0)
    core = lax.axis_index("ctx") % 2

    @pl.when(step == 0)
    def _():
        square_ref[...] = jnp.zeros_like(square_ref)

    for j in range(2):
        columns = slice(j * HD, (j + 1) * HD)
        state = jnp.where(core == j, mine_ref[0], other_ref[0])
        gain_b = gain_ref[1, 2 * step + j]
        q_high, q_low = halves(q_ref[:, columns])
        b = b_ref[:, columns] + gain_b * product(q_high, q_low, *halves(state))
        out_ref[:, columns] = b
        square_ref[...] += b * b

    @pl.when(step == pl.num_programs(0) - 1)
    def _():
        row = lax.broadcasted_iota(jnp.int32, sums_ref.shape, 0)
        sums_ref[...] = jnp.where(row == 0, sum_a_ref[...], row_sums(square_ref[...]))


def first_tile_kernel(gain_ref, q_ref, k_ref, v_ref, tail_k_ref, tail_v_ref, a_ref, sum_ref, square_ref):
    step = pl.program_id(0)
    lower = lower_mask()
    reachable = jnp.logical_or(lower, lax.axis_index("ctx") > 0)

    @pl.when(step == 0)
    def _():
        square_ref[...] = jnp.zeros_like(square_ref)

    for j in range(2):
        columns = slice(j * HD, (j + 1) * HD)
        gain_a = gain_ref[0, 2 * step + j]
        q_high, q_low = halves(q_ref[:, columns])
        k_both = halves(stack(tail_k_ref[:, columns], k_ref[:, columns]))
        v_both = halves(stack(tail_v_ref[:, columns], v_ref[:, columns]))
        both = pair_scores(q_high, q_low, *k_both)
        scores = jnp.where(lower, both[:, WINDOW:], both[:, :WINDOW])
        scores = jnp.where(reachable, scores, -jnp.inf)
        a = window_tile(scores, lower, v_both, gain_a)
        a_ref[:, columns] = a
        square_ref[...] += a * a

    @pl.when(step == pl.num_programs(0) - 1)
    def _():
        sum_ref[...] = row_sums(square_ref[...])


def inverse_norm(total):
    return 1.0 / jnp.sqrt(total / (HEADS * HD) + EPS)


def scale_kernel(parts, *refs):
    sums, (a_ref, b_ref, out_ref) = refs[:parts], refs[-3:]
    total = sums[0][...]
    for part in sums[1:parts]:
        total = total + part[...]
    columns = inverse_norm(total).T
    out_ref[...] = a_ref[...] * columns[:, 0:1] + b_ref[...] * columns[:, 1:2]


def first_scale_kernel(parts, *refs):
    sums_b, sums_a = refs[:parts], refs[parts : 2 * parts]
    a_ref, b_ref, _, out_ref = refs[-4:]
    total_a, total_b = sums_a[0][...], sums_b[0][...]
    for part_a, part_b in zip(sums_a[1:], sums_b[1:]):
        total_a, total_b = total_a + part_a[...], total_b + part_b[...]
    inverse_a = inverse_norm(total_a).T[:, 0:1]
    inverse_b = inverse_norm(total_b).T[:, 1:2]
    out_ref[...] = a_ref[...] * inverse_a + b_ref[...] * inverse_b


def swap(block, axis, bit):
    return lax.ppermute(block, axis, [(i, i ^ bit) for i in range(lax.axis_size(axis))])


def everyone(block, axis):
    count = lax.axis_size(axis)
    return [block] + [
        lax.ppermute(block, axis, [(i, (i + s) % count) for i in range(count)]) for s in range(1, count)
    ]


def earlier_states(keep, send):
    count = lax.axis_size("ctx")
    index = lax.axis_index("ctx")
    devices = range(count)
    core = index % 2
    beside = swap(send, "ctx", 1)
    chip = keep + beside
    if count == 8:
        x = (index >> 1) % 2
        route = [(i, i ^ 2) for i in devices if i % 2 == 0]
        route += [(i, i + 4) for i in devices if i % 2 == 1 and i < 4]
        first = lax.ppermute(chip, "ctx", route)
        message = first + jnp.where((core == 0) | (x == 0), chip, 0.0)
        route = [(i, i + 4) for i in devices if i % 2 == 0 and i < 4]
        route += [(i, i ^ 2) for i in devices if i % 2 == 1 and i != 3]
        second = lax.ppermute(message, "ctx", route)
        earlier = jnp.where((core == 1) | (x == 1), first, 0.0) + second
    else:
        earlier = jnp.zeros_like(chip)
        running = chip
        bit = 2
        while bit < count:
            partner = swap(running, "ctx", bit)
            earlier = earlier + jnp.where((index & bit) != 0, partner, 0.0)
            running = running + partner
            bit *= 2
    mine = earlier + jnp.where(core == 1, beside, 0.0)
    other = swap(earlier + jnp.where(core == 0, keep, 0.0), "ctx", 1)
    return mine, other


def shards(queries, keys, values, head_gain):
    rows, width = queries.shape
    heads = head_gain.shape[1]
    steps = heads // 2
    parts = lax.axis_size("head")
    smem = pl.BlockSpec(memory_space=pltpu.SMEM)
    whole = pl.BlockSpec((rows, 2 * HD), lambda i: (0, i))
    top = pl.BlockSpec((WINDOW, 2 * HD), lambda i: (0, i))
    state = pl.BlockSpec((1, HD, HD), lambda i: (i, 0, 0))
    sums_block = pl.BlockSpec((8, rows), lambda i: (0, 0))
    first_sums_block = pl.BlockSpec((8, WINDOW), lambda i: (0, 0))

    def array(*shape):
        return jax.ShapeDtypeStruct(shape, F32)

    def call(kernel, name, flops, moved, **kwargs):
        return pl.pallas_call(
            kernel,
            name=name,
            compiler_params=pltpu.CompilerParams(vmem_limit_bytes=VMEM_BYTES),
            cost_estimate=pl.CostEstimate(flops=flops, bytes_accessed=moved, transcendentals=0),
            **kwargs,
        )

    size = rows * width * 4
    unit = 2 * rows * width * HD
    keep, send, tail_k, tail_v = call(
        totals_kernel,
        "totals",
        4 * unit,
        2 * size,
        grid=(steps,),
        in_specs=[whole, whole],
        out_specs=[state, state, top, top],
        out_shape=[
            array(steps, HD, HD),
            array(steps, HD, HD),
            array(WINDOW, width),
            array(WINDOW, width),
        ],
    )(keys, values)

    route = [(i, i + 1) for i in range(lax.axis_size("ctx") - 1)]
    mine, other = earlier_states(keep, send)
    before_k = lax.ppermute(tail_k, "ctx", route)
    before_v = lax.ppermute(tail_v, "ctx", route)

    window, linear, sum_a = call(
        local_kernel,
        "local",
        24 * unit,
        5 * size,
        grid=(steps,),
        in_specs=[smem, whole, whole, whole],
        out_specs=[whole, whole, sums_block],
        out_shape=[array(rows, width), array(rows, width), array(8, rows)],
        scratch_shapes=[pltpu.VMEM((rows, HD), F32)],
    )(head_gain, queries, keys, values)

    linear, sums = call(
        earlier_kernel,
        "earlier",
        3 * unit,
        3 * size,
        grid=(steps,),
        in_specs=[smem, whole, whole, state, state, sums_block],
        out_specs=[whole, sums_block],
        out_shape=[array(rows, width), array(8, rows)],
        scratch_shapes=[pltpu.VMEM((rows, HD), F32)],
    )(head_gain, queries, linear, mine, other, sum_a)
    all_sums = everyone(sums, "head")

    first_a, first_sum = call(
        first_tile_kernel,
        "first_tile",
        2 * unit,
        size,
        grid=(steps,),
        in_specs=[smem, top, top, top, top, top],
        out_specs=[top, first_sums_block],
        out_shape=[array(WINDOW, width), array(8, WINDOW)],
        scratch_shapes=[pltpu.VMEM((WINDOW, HD), F32)],
    )(head_gain, queries, keys, values, before_k, before_v)
    all_first = everyone(first_sum, "head")

    row_block = pl.BlockSpec((WINDOW, width), lambda i: (i + 1, 0))
    first_block = pl.BlockSpec((WINDOW, width), lambda i: (0, 0))
    out = call(
        functools.partial(scale_kernel, parts),
        "scale",
        unit // 64,
        2 * size,
        grid=(rows // WINDOW - 1,),
        in_specs=[pl.BlockSpec((8, WINDOW), lambda i: (0, i + 1))] * parts + [row_block, row_block],
        out_specs=row_block,
        out_shape=array(rows, width),
    )(*all_sums, window, linear)
    return call(
        functools.partial(first_scale_kernel, parts),
        "first_scale",
        unit // 256,
        size // 2,
        grid=(1,),
        in_specs=[first_sums_block] * (2 * parts)
        + [first_block, first_block, pl.BlockSpec(memory_space=pl.ANY)],
        out_specs=first_block,
        out_shape=array(rows, width),
        input_output_aliases={2 * parts + 2: 0},
    )(*all_sums, *all_first, first_a, linear, out)


def solution(mesh):
    in_specs = (P("ctx", "head"), P("ctx", "head"), P("ctx", "head"), P(None, "head"))
    out_specs = P("ctx", "head")
    return jax.shard_map(shards, mesh=mesh, in_specs=in_specs, out_specs=out_specs, check_vma=False)
```

profile of v0, /device:TPU:4, one launch (start us, length us, event | category | flops | bytes accessed | tf_op | source)
XLA Modules:
  0.0 119.8 jit_solution(8010770976530169842)
XLA Ops:
  0.0 2.2 %copy-done.1 = f32[512,2048]{1,0:T(8,128)S(1)} copy-done((f32[512,2048]{1,0:T(8,128)S(1)}, f32[512,2048]{1,0:T(8,128)}, u32[]{:S(2)}) %copy-start.1) | copy-done | bytes 4194328
  2.2 2.2 %copy-done.4 = f32[512,2048]{1,0:T(8,128)S(1)} copy-done((f32[512,2048]{1,0:T(8,128)S(1)}, f32[512,2048]{1,0:T(8,128)}, u32[]{:S(2)}) %copy-start.4) | copy-done | bytes 4194328
  4.4 4.5 %totals.1 = (f32[8,128,128]{2,1,0:T(8,128)S(1)}, f32[8,128,128]{2,1,0:T(8,128)S(1)}, f32[128,2048]{1,0:T(8,128)}, f32[128,2048]{1,0:T(8,128)S(1)}) custom-call(f32[512,2048]{1,0:T(8,128)S(1)} %copy-done.1, f32[512,2048]{1,0:T(8,128)S(1)} %copy-done.4), custom_call_target="tpu_custom_call" | custom-call | flops 1073741824 | bytes 8388608 | tf_op jit(solution)/shard_map/totals/pallas_call | solution.py:289
  8.8 1.0 copy-done.8
  9.9 1.9 %collective-permute-done = f32[8,128,128]{2,1,0:T(8,128)S(1)} collective-permute-done((f32[8,128,128]{2,1,0:T(8,128)S(1)}, f32[8,128,128]{2,1,0:T(8,128)S(1)}, u32[]{:S(2)}, u32[]{:S(2)}) %collective-permute-start) | collective-permute-done | bytes 524320 | tf_op jit(solution)/shard_map/ppermute | solution.py:222
  11.8 3.4 %collective-permute-start.1 = (f32[8,128,128]{2,1,0:T(8,128)S(1)}, f32[8,128,128]{2,1,0:T(8,128)S(1)}, u32[]{:S(2)}, u32[]{:S(2)}) collective-permute-start(f32[8,128,128]{2,1,0:T(8,128)S(1)} %add.24), channel_id=1, source_target_pairs={{0,8},{8,0},{16,24},{24,16},{4,20},{12,28},{1,9},{9,1},{17,25},{25... | collective-permute-start | bytes 1572872 | tf_op jit(solution)/shard_map/ppermute | solution.py:243
  15.3 7.7 %collective-permute-done.1 = f32[8,128,128]{2,1,0:T(8,128)S(1)} collective-permute-done((f32[8,128,128]{2,1,0:T(8,128)S(1)}, f32[8,128,128]{2,1,0:T(8,128)S(1)}, u32[]{:S(2)}, u32[]{:S(2)}) %collective-permute-start.1) | collective-permute-done | bytes 524320 | tf_op jit(solution)/shard_map/ppermute | solution.py:243
  23.8 1.3 %collective-permute-start.2 = (f32[8,128,128]{2,1,0:T(8,128)}, f32[8,128,128]{2,1,0:T(8,128)}, u32[]{:S(2)}, u32[]{:S(2)}) collective-permute-start(f32[8,128,128]{2,1,0:T(8,128)} %select_add_fusion.2), channel_id=1, source_target_pairs={{0,16},{8,24},{4,12},{20,28},{28,20},{1,17},{9,25},{5,13},{21,29},... | collective-permute-start | bytes 1572872 | tf_op jit(solution)/shard_map/ppermute | solution.py:247
  25.1 3.0 %collective-permute-start.7 = (f32[128,2048]{1,0:T(8,128)}, f32[128,2048]{1,0:T(8,128)S(1)}, u32[]{:S(2)}, u32[]{:S(2)}) collective-permute-start(f32[128,2048]{1,0:T(8,128)} %get-tuple-element.21), channel_id=1, source_target_pairs={{0,4},{4,8},{8,12},{12,16},{16,20},{20,24},{24,28},{1,5},{5,9},{9,... | collective-permute-start | bytes 3145736 | tf_op jit(solution)/shard_map/ppermute | solution.py:307
  28.2 2.4 %collective-permute-start.8 = (f32[128,2048]{1,0:T(8,128)}, f32[128,2048]{1,0:T(8,128)S(1)}, u32[]{:S(2)}, u32[]{:S(2)}) collective-permute-start(f32[128,2048]{1,0:T(8,128)} %copy-done.8), channel_id=1, source_target_pairs={{0,4},{4,8},{8,12},{12,16},{16,20},{20,24},{24,28},{1,5},{5,9},{9,... | collective-permute-start | bytes 3145736 | tf_op jit(solution)/shard_map/ppermute | solution.py:308
  30.6 27.1 %collective-permute-done.2 = f32[8,128,128]{2,1,0:T(8,128)} collective-permute-done((f32[8,128,128]{2,1,0:T(8,128)}, f32[8,128,128]{2,1,0:T(8,128)}, u32[]{:S(2)}, u32[]{:S(2)}) %collective-permute-start.2) | collective-permute-done | bytes 524320 | tf_op jit(solution)/shard_map/ppermute | solution.py:247
  57.7 1.3 %select_add_fusion = (f32[8,128,128]{2,1,0:T(8,128)S(1)}, f32[8,128,128]{2,1,0:T(8,128)S(1)}) fusion(f32[8,128,128]{2,1,0:T(8,128)S(1)} %get-tuple-element.17, pred[]{:T(512)S(6)} %eq.19, f32[8,128,128]{2,1,0:T(8,128)} %collective-permute-done.2, f32[8,128,128]{2,1,0:T(8,128)} %copy-done.9, pred[]{:T(512)S(6)} %or.6, ...), kind=kLoop, calls=%fused_computation | loop fusion | flops 786432 | bytes 3145731 | tf_op jit(solution)/shard_map/add | solution.py:259
  59.1 2.2 %copy-done = f32[512,2048]{1,0:T(8,128)S(1)} copy-done((f32[512,2048]{1,0:T(8,128)S(1)}, f32[512,2048]{1,0:T(8,128)}, u32[]{:S(2)}) %copy-start) | copy-done | bytes 4194328
  61.2 2.2 %copy-done.2 = f32[512,2048]{1,0:T(8,128)S(1)} copy-done((f32[512,2048]{1,0:T(8,128)S(1)}, f32[512,2048]{1,0:T(8,128)}, u32[]{:S(2)}) %copy-start.2) | copy-done | bytes 4194328
  63.4 2.2 %copy-done.5 = f32[512,2048]{1,0:T(8,128)S(1)} copy-done((f32[512,2048]{1,0:T(8,128)S(1)}, f32[512,2048]{1,0:T(8,128)}, u32[]{:S(2)}) %copy-start.5) | copy-done | bytes 4194328
  65.6 25.2 %local.1 = (f32[512,2048]{1,0:T(8,128)S(1)}, f32[512,2048]{1,0:T(8,128)S(1)}, f32[8,512]{1,0:T(8,128)S(1)}) custom-call(f32[2,16]{1,0:T(2,128)S(1)} %copy-done.7, f32[512,2048]{1,0:T(8,128)S(1)} %copy-done, f32[512,2048]{1,0:T(8,128)S(1)} %copy-done.2, f32[512,2048]{1,0:T(8,128)S(1)} %copy-done.5), custom_call_target="tpu_custom_call" | custom-call | flops 6442450944 | bytes 20971520 | tf_op jit(solution)/shard_map/local/pallas_call | solution.py:310
  90.9 4.9 %earlier.1 = (f32[512,2048]{1,0:T(8,128)S(1)}, f32[8,512]{1,0:T(8,128)S(1)}) custom-call(f32[2,16]{1,0:T(2,128)S(1)} %copy-done.7, f32[512,2048]{1,0:T(8,128)S(1)} %copy-done, f32[512,2048]{1,0:T(8,128)S(1)} %get-tuple-element.16.b_ref, f32[8,128,128]{2,1,0:T(8,128)S(1)} %get-tuple-element.28.mine_ref, f32[8,128,128]{2,1,0:T(8,128)S(1)} %collective-permute-done.3.other_ref, ...), custom_call_target="tpu_custom_call" | custom-call | flops 805306368 | bytes 12582912 | tf_op jit(solution)/shard_map/earlier/pallas_call | solution.py:322
  95.8 3.7 %collective-permute-start.6 = (f32[8,512]{1,0:T(8,128)S(1)}, f32[8,512]{1,0:T(8,128)S(1)}, u32[]{:S(2)}, u32[]{:S(2)}) collective-permute-start(f32[8,512]{1,0:T(8,128)S(1)} %get-tuple-element.20.refs_0_), channel_id=1, source_target_pairs={{0,3},{1,0},{2,1},{3,2},{4,7},{5,4},{6,5},{7,6},{8,11},{9,8},{10,9... | collective-permute-start | bytes 49160 | tf_op jit(solution)/shard_map/ppermute | solution.py:228
  100.5 8.6 %first_tile.1 = (f32[128,2048]{1,0:T(8,128)S(1)}, f32[8,128]{1,0:T(8,128)S(1)}) custom-call(f32[2,16]{1,0:T(2,128)S(1)} %copy-done.7, f32[512,2048]{1,0:T(8,128)S(1)} %copy-done, f32[512,2048]{1,0:T(8,128)S(1)} %copy-done.3, f32[512,2048]{1,0:T(8,128)S(1)} %copy-done.6, f32[128,2048]{1,0:T(8,128)S(1)} %collective-permute-done.7.tail_k_ref, ...), custom_call_target="tpu_custom_call" | custom-call | flops 536870912 | bytes 4194304 | tf_op jit(solution)/shard_map/first_tile/pallas_call | solution.py:335
  109.1 2.9 %collective-permute-start.11 = (f32[8,128]{1,0:T(8,128)S(1)}, f32[8,128]{1,0:T(8,128)S(1)}, u32[]{:S(2)}, u32[]{:S(2)}) collective-permute-start(f32[8,128]{1,0:T(8,128)S(1)} %get-tuple-element.23.refs_4_), channel_id=1, source_target_pairs={{0,3},{1,0},{2,1},{3,2},{4,7},{5,4},{6,5},{7,6},{8,11},{9,8},{10,9... | collective-permute-start | bytes 12296 | tf_op jit(solution)/shard_map/ppermute | solution.py:228
  112.0 1.1 collective-permute-start.10
  113.1 2.5 %scale.1.refs_10_ = f32[512,2048]{1,0:T(8,128)} custom-call(f32[8,512]{1,0:T(8,128)S(1)} %get-tuple-element.20.refs_0_, f32[8,512]{1,0:T(8,128)S(1)} %collective-permute-done.4.refs_1_, f32[8,512]{1,0:T(8,128)S(1)} %collective-permute-done.5.refs_2_, f32[8,512]{1,0:T(8,128)S(1)} %collective-permute-done.6.refs_3_, ...), custom_call_target="tpu_custom_call" | custom-call | flops 4194304 | bytes 8388608 | tf_op jit(solution)/shard_map/scale/pallas_call | solution.py:350
  116.5 2.0 %collective-permute-done.9.refs_5_ = f32[8,128]{1,0:T(8,128)S(1)} collective-permute-done((f32[8,128]{1,0:T(8,128)S(1)}, f32[8,128]{1,0:T(8,128)S(1)}, u32[]{:S(2)}, u32[]{:S(2)}) %collective-permute-start.9) | collective-permute-done | bytes 4128 | tf_op jit(solution)/shard_map/ppermute | solution.py:228
  118.5 1.3 %first_scale.1 = f32[512,2048]{1,0:T(8,128)} custom-call(f32[8,512]{1,0:T(8,128)S(1)} %get-tuple-element.20.refs_0_, f32[8,512]{1,0:T(8,128)S(1)} %collective-permute-done.4.refs_1_, f32[8,512]{1,0:T(8,128)S(1)} %collective-permute-done.5.refs_2_, f32[8,512]{1,0:T(8,128)S(1)} %collective-permute-done.6.refs_3_, ...), custom_call_target="tpu_custom_call", output_to_operand_aliasing={{}: (10, {})} | custom-call | flops 1048576 | bytes 2097152 | tf_op jit(solution)/shard_map/first_scale/pallas_call | solution.py:360
  (29 shorter events, 3.0 us)
Async XLA Ops:
  0.0 2.2 %copy-start.1 = (f32[512,2048]{1,0:T(8,128)S(1)}, f32[512,2048]{1,0:T(8,128)}, u32[]{:S(2)}) copy-start(f32[512,2048]{1,0:T(8,128)} %k_ref.5) | copy-start | bytes 12582916
  2.2 2.2 %copy-start.4 = (f32[512,2048]{1,0:T(8,128)S(1)}, f32[512,2048]{1,0:T(8,128)}, u32[]{:S(2)}) copy-start(f32[512,2048]{1,0:T(8,128)} %v_ref.5) | copy-start | bytes 12582916
  8.8 1.0 copy-start.8
  9.9 49.2 %copy-start.7 = (f32[2,16]{1,0:T(2,128)S(1)}, f32[2,16]{1,0:T(2,128)}, u32[]{:S(2)}) copy-start(f32[2,16]{1,0:T(2,128)} %gain_ref.5) | copy-start | bytes 388
  9.9 1.9 %collective-permute-start = (f32[8,128,128]{2,1,0:T(8,128)S(1)}, f32[8,128,128]{2,1,0:T(8,128)S(1)}, u32[]{:S(2)}, u32[]{:S(2)}) collective-permute-start(f32[8,128,128]{2,1,0:T(8,128)S(1)} %get-tuple-element.18), channel_id=1, source_target_pairs={{0,4},{4,0},{8,12},{12,8},{16,20},{20,16},{24,28},{28,24},{1,5},{5... | collective-permute-start | bytes 1572872 | tf_op jit(solution)/shard_map/ppermute | solution.py:222
  11.8 11.1 %collective-permute-start.1 = (f32[8,128,128]{2,1,0:T(8,128)S(1)}, f32[8,128,128]{2,1,0:T(8,128)S(1)}, u32[]{:S(2)}, u32[]{:S(2)}) collective-permute-start(f32[8,128,128]{2,1,0:T(8,128)S(1)} %add.24), channel_id=1, source_target_pairs={{0,8},{8,0},{16,24},{24,16},{4,20},{12,28},{1,9},{9,1},{17,25},{25... | collective-permute-start | bytes 1572872 | tf_op jit(solution)/shard_map/ppermute | solution.py:243
  22.9 2.2 %copy-start.9 = (f32[8,128,128]{2,1,0:T(8,128)}, f32[8,128,128]{2,1,0:T(8,128)S(1)}, u32[]{:S(2)}) copy-start(f32[8,128,128]{2,1,0:T(8,128)S(1)} %collective-permute-done.1) | copy-start | bytes 1572868
  23.8 33.9 %collective-permute-start.2 = (f32[8,128,128]{2,1,0:T(8,128)}, f32[8,128,128]{2,1,0:T(8,128)}, u32[]{:S(2)}, u32[]{:S(2)}) collective-permute-start(f32[8,128,128]{2,1,0:T(8,128)} %select_add_fusion.2), channel_id=1, source_target_pairs={{0,16},{8,24},{4,12},{20,28},{28,20},{1,17},{9,25},{5,13},{21,29},... | collective-permute-start | bytes 1572872 | tf_op jit(solution)/shard_map/ppermute | solution.py:247
  25.1 75.3 %collective-permute-start.7 = (f32[128,2048]{1,0:T(8,128)}, f32[128,2048]{1,0:T(8,128)S(1)}, u32[]{:S(2)}, u32[]{:S(2)}) collective-permute-start(f32[128,2048]{1,0:T(8,128)} %get-tuple-element.21), channel_id=1, source_target_pairs={{0,4},{4,8},{8,12},{12,16},{16,20},{20,24},{24,28},{1,5},{5,9},{9,... | collective-permute-start | bytes 3145736 | tf_op jit(solution)/shard_map/ppermute | solution.py:307
  28.2 72.3 %collective-permute-start.8 = (f32[128,2048]{1,0:T(8,128)}, f32[128,2048]{1,0:T(8,128)S(1)}, u32[]{:S(2)}, u32[]{:S(2)}) collective-permute-start(f32[128,2048]{1,0:T(8,128)} %copy-done.8), channel_id=1, source_target_pairs={{0,4},{4,8},{8,12},{12,16},{16,20},{20,24},{24,28},{1,5},{5,9},{9,... | collective-permute-start | bytes 3145736 | tf_op jit(solution)/shard_map/ppermute | solution.py:308
  59.0 31.9 %collective-permute-start.3 = (f32[8,128,128]{2,1,0:T(8,128)S(1)}, f32[8,128,128]{2,1,0:T(8,128)S(1)}, u32[]{:S(2)}, u32[]{:S(2)}) collective-permute-start(f32[8,128,128]{2,1,0:T(8,128)S(1)} %get-tuple-element.27), channel_id=1, source_target_pairs={{0,4},{4,0},{8,12},{12,8},{16,20},{20,16},{24,28},{28,24},{1,5},{5... | collective-permute-start | bytes 1572872 | tf_op jit(solution)/shard_map/ppermute | solution.py:222
  59.0 2.2 %copy-start = (f32[512,2048]{1,0:T(8,128)S(1)}, f32[512,2048]{1,0:T(8,128)}, u32[]{:S(2)}) copy-start(f32[512,2048]{1,0:T(8,128)} %q_ref.5) | copy-start | bytes 12582916
  61.2 2.2 %copy-start.2 = (f32[512,2048]{1,0:T(8,128)S(1)}, f32[512,2048]{1,0:T(8,128)}, u32[]{:S(2)}) copy-start(f32[512,2048]{1,0:T(8,128)} %k_ref.5) | copy-start | bytes 12582916
  63.4 2.2 %copy-start.5 = (f32[512,2048]{1,0:T(8,128)S(1)}, f32[512,2048]{1,0:T(8,128)}, u32[]{:S(2)}) copy-start(f32[512,2048]{1,0:T(8,128)} %v_ref.5) | copy-start | bytes 12582916
  90.8 9.6 %copy-start.3 = (f32[512,2048]{1,0:T(8,128)S(1)}, f32[512,2048]{1,0:T(8,128)}, u32[]{:S(2)}) copy-start(f32[512,2048]{1,0:T(8,128)} %k_ref.5) | copy-start | bytes 12582916
  90.8 9.6 %copy-start.6 = (f32[512,2048]{1,0:T(8,128)S(1)}, f32[512,2048]{1,0:T(8,128)}, u32[]{:S(2)}) copy-start(f32[512,2048]{1,0:T(8,128)} %v_ref.5) | copy-start | bytes 12582916
  95.8 17.3 %collective-permute-start.6 = (f32[8,512]{1,0:T(8,128)S(1)}, f32[8,512]{1,0:T(8,128)S(1)}, u32[]{:S(2)}, u32[]{:S(2)}) collective-permute-start(f32[8,512]{1,0:T(8,128)S(1)} %get-tuple-element.20.refs_0_), channel_id=1, source_target_pairs={{0,3},{1,0},{2,1},{3,2},{4,7},{5,4},{6,5},{7,6},{8,11},{9,8},{10,9... | collective-permute-start | bytes 49160 | tf_op jit(solution)/shard_map/ppermute | solution.py:228
  99.4 13.7 %collective-permute-start.5 = (f32[8,512]{1,0:T(8,128)S(1)}, f32[8,512]{1,0:T(8,128)S(1)}, u32[]{:S(2)}, u32[]{:S(2)}) collective-permute-start(f32[8,512]{1,0:T(8,128)S(1)} %get-tuple-element.20.refs_0_), channel_id=1, source_target_pairs={{0,2},{1,3},{2,0},{3,1},{4,6},{5,7},{6,4},{7,5},{8,10},{9,11},{10,... | collective-permute-start | bytes 49160 | tf_op jit(solution)/shard_map/ppermute | solution.py:228
  99.4 13.7 %collective-permute-start.4 = (f32[8,512]{1,0:T(8,128)S(1)}, f32[8,512]{1,0:T(8,128)S(1)}, u32[]{:S(2)}, u32[]{:S(2)}) collective-permute-start(f32[8,512]{1,0:T(8,128)S(1)} %get-tuple-element.20.refs_0_), channel_id=1, source_target_pairs={{0,1},{1,2},{2,3},{3,0},{4,5},{5,6},{6,7},{7,4},{8,9},{9,10},{10,1... | collective-permute-start | bytes 49160 | tf_op jit(solution)/shard_map/ppermute | solution.py:228
  109.1 6.5 %collective-permute-start.11 = (f32[8,128]{1,0:T(8,128)S(1)}, f32[8,128]{1,0:T(8,128)S(1)}, u32[]{:S(2)}, u32[]{:S(2)}) collective-permute-start(f32[8,128]{1,0:T(8,128)S(1)} %get-tuple-element.23.refs_4_), channel_id=1, source_target_pairs={{0,3},{1,0},{2,1},{3,2},{4,7},{5,4},{6,5},{7,6},{8,11},{9,8},{10,9... | collective-permute-start | bytes 12296 | tf_op jit(solution)/shard_map/ppermute | solution.py:228
  112.0 4.5 %collective-permute-start.10 = (f32[8,128]{1,0:T(8,128)S(1)}, f32[8,128]{1,0:T(8,128)S(1)}, u32[]{:S(2)}, u32[]{:S(2)}) collective-permute-start(f32[8,128]{1,0:T(8,128)S(1)} %get-tuple-element.23.refs_4_), channel_id=1, source_target_pairs={{0,2},{1,3},{2,0},{3,1},{4,6},{5,7},{6,4},{7,5},{8,10},{9,11},{10,... | collective-permute-start | bytes 12296 | tf_op jit(solution)/shard_map/ppermute | solution.py:228
  113.1 5.4 %collective-permute-start.9 = (f32[8,128]{1,0:T(8,128)S(1)}, f32[8,128]{1,0:T(8,128)S(1)}, u32[]{:S(2)}, u32[]{:S(2)}) collective-permute-start(f32[8,128]{1,0:T(8,128)S(1)} %get-tuple-element.23.refs_4_), channel_id=1, source_target_pairs={{0,1},{1,2},{2,3},{3,0},{4,5},{5,6},{6,7},{7,4},{8,9},{9,10},{10,1... | collective-permute-start | bytes 12296 | tf_op jit(solution)/shard_map/ppermute | solution.py:228
where the time goes:
time: 121 us; the launch traced here: 120 us
  Pallas kernels  47 us (39%)
  waiting for transfers between devices  39.6 us (33%)
  starting transfers between devices  18.8 us (16%)
  local copies, waits for them, and re-layouts  12 us (10%)
  other arithmetic  2.25 us (2%)
    ppermute x1, waiting for transfers between devices, earlier_states(): second = lax.ppermute(message, 'ctx', route)  27.1 us
    pallas_call x1, Pallas kernels, shards(): call(local_kernel, 'local', 24 * unit, 5 * size, grid=(steps,), in_specs=...  25.2 us
    unnamed x20, local copies, waits for them, and re-layouts  12 us
    ppermute x6, starting transfers between devices, everyone(): lax.ppermute(block, axis, [(i, (i + s) % count) for i in range(count)])  8.67 us
    pallas_call x1, Pallas kernels, shards(): call(first_tile_kernel, 'first_tile', 2 * unit, size, grid=(steps,), in_s...  8.62 us
    ppermute x1, waiting for transfers between devices, earlier_states(): first = lax.ppermute(chip, 'ctx', route)  7.65 us
    pallas_call x1, Pallas kernels, shards(): call(earlier_kernel, 'earlier', 3 * unit, 3 * size, grid=(steps,), in_spe...  4.92 us
    pallas_call x1, Pallas kernels, shards(): call(totals_kernel, 'totals', 4 * unit, 2 * size, grid=(steps,), in_specs...  4.47 us
  transfers between devices with their start and end apart: 12, of which 5 were waited for; matrix products, arithmetic and copies ran while one was open for 1% of the time, Pallas kernels for 34%

commit v1 on v0

v1 whole, which is shorter than its diff:
```python
import functools
import math

import jax
import jax.numpy as jnp
from jax import lax
from jax.experimental import pallas as pl
from jax.experimental.pallas import tpu as pltpu
from jax.sharding import PartitionSpec as P

HEADS = 64
HD = 128
WINDOW = 128
EPS = 1e-06
F32 = jnp.float32
BF16 = jnp.bfloat16
EXP2_SCALE = math.log2(math.e) / math.sqrt(HD)
VMEM_BYTES = 24 * 1024 * 1024


def halves(x):
    high = x.astype(BF16)
    low = (x - high.astype(F32)).astype(BF16)
    return high, low


def dot(a, b):
    return lax.dot_general(a, b, (((1,), (0,)), ((), ())), preferred_element_type=F32)


def dot_rows(a, b):
    return lax.dot_general(a, b, (((1,), (1,)), ((), ())), preferred_element_type=F32)


def dot_columns(a, b):
    return lax.dot_general(a, b, (((0,), (0,)), ((), ())), preferred_element_type=F32)


def side(a, b):
    return jnp.concatenate([a, b], axis=1)


def stack(a, b):
    return jnp.concatenate([a, b], axis=0)


def outer_state(k_high, k_low, v_high, v_low):
    grid = dot_columns(side(k_high, k_low), side(v_high, v_low))
    return grid[:HD, :HD] + (grid[:HD, HD:] + grid[HD:, :HD]) + grid[HD:, HD:]


def lower_mask():
    rows = lax.broadcasted_iota(jnp.int32, (WINDOW, WINDOW), 0)
    columns = lax.broadcasted_iota(jnp.int32, (WINDOW, WINDOW), 1)
    return rows >= columns


def row_sums(square):
    ones = jnp.ones((8, HD), BF16)
    high, low = halves(square)
    return dot_rows(ones, high) + dot_rows(ones, low)


def wide_keys(k_high, k_low):
    return stack(side(k_high, k_high), side(k_low, jnp.zeros_like(k_low)))


def wide_state(state):
    high, low = halves(state)
    return stack(side(high, low), side(high, jnp.zeros_like(high)))


def folded(wide):
    half = wide.shape[1] // 2
    return wide[:, :half] + wide[:, half:]


def totals_kernel(k_ref, v_ref, keep_ref, send_ref, half_ref, tail_k_ref, tail_v_ref):
    core = lax.axis_index("ctx") % 2
    rows = k_ref.shape[0]
    middle = rows // 2
    states = []
    for j in range(2):
        columns = slice(j * HD, (j + 1) * HD)
        k_high, k_low = halves(k_ref[:, columns])
        v_high, v_low = halves(v_ref[:, columns])
        first = outer_state(k_high[:middle], k_low[:middle], v_high[:middle], v_low[:middle])
        second = outer_state(k_high[middle:], k_low[middle:], v_high[middle:], v_low[middle:])
        half_ref[j] = first
        states.append(first + second)
    keep_ref[0] = jnp.where(core == 0, states[0], states[1])
    send_ref[0] = jnp.where(core == 0, states[1], states[0])
    tail_k_ref[...] = k_ref[rows - WINDOW :, :]
    tail_v_ref[...] = v_ref[rows - WINDOW :, :]


def weights_of(scores):
    biggest = jnp.max(scores, axis=1, keepdims=True)
    weights = jnp.exp2((scores - biggest) * EXP2_SCALE)
    return weights, jnp.sum(weights, axis=1, keepdims=True)


def masked_pair(weights, below, above):
    high, low = halves(weights)
    return side(high * above, high * below), side(low * above, low * below)


def local_kernel(gain_ref, q_ref, k_ref, v_ref, a_ref, b_ref, qq_ref, sum_ref, square_ref):
    step = pl.program_id(0)
    lower = lower_mask()
    below = jnp.where(lower, 1.0, 0.0).astype(BF16)
    above = jnp.where(lower, 0.0, 1.0).astype(BF16)
    rows = q_ref.shape[0]
    tiles = rows // WINDOW

    @pl.when(step == 0)
    def _():
        square_ref[...] = jnp.zeros_like(square_ref)

    def tile(n):
        return slice(n * WINDOW, (n + 1) * WINDOW)

    scores = []
    for j in range(2):
        columns = slice(j * HD, (j + 1) * HD)
        qq = side(*halves(q_ref[:, columns]))
        qq_ref[:, 2 * j * HD : 2 * (j + 1) * HD] = qq
        k_high, k_low = halves(k_ref[:, columns])
        now, before = [], [None]
        for n in range(tiles):
            keys = wide_keys(k_high[tile(n)], k_low[tile(n)])
            found = folded(dot_rows(qq[n * WINDOW : min((n + 2) * WINDOW, rows)], keys))
            now.append(found[:WINDOW])
            before.append(found[WINDOW:])
        scores.append((now, before))
    for j in range(2):
        columns = slice(j * HD, (j + 1) * HD)
        v_high, v_low = halves(v_ref[:, columns])
        vv = side(v_high, v_low)
        now, before = scores[j]
        gain_a = gain_ref[0, 2 * step + j]
        for n in range(tiles):
            inner_high, inner_low = halves(jnp.where(lower, now[n], 0.0))
            if n == 0:
                wide = dot(stack(inner_high, inner_low), vv[tile(0)])
                b_ref[tile(0), columns] = folded(wide[:WINDOW]) + wide[WINDOW:, :HD]
                a_ref[tile(0), columns] = jnp.zeros((WINDOW, HD), F32)
                continue
            weights, total = weights_of(jnp.where(lower, now[n], before[n]))
            pair_high, pair_low = masked_pair(weights, below, above)
            if n % 2:
                before_high, before_low = halves(before[n])
            else:
                before_high = before_low = jnp.zeros((WINDOW, HD), BF16)
            left = jnp.concatenate(
                [pair_high, pair_low, side(before_high, inner_high), side(before_low, inner_low)], axis=0
            )
            wide = dot(left, vv[(n - 1) * WINDOW : (n + 1) * WINDOW])
            a = (folded(wide[tile(0)]) + wide[tile(1), :HD]) * (gain_a / total)
            a_ref[tile(n), columns] = a
            square_ref[tile(n), :] += a * a
            b_ref[tile(n), columns] = folded(wide[tile(2)]) + wide[tile(3), :HD]

    @pl.when(step == pl.num_programs(0) - 1)
    def _():
        sum_ref[...] = row_sums(square_ref[...])


def message_kernel(first_ref, chip_ref, _, __, out_ref):
    index = lax.axis_index("ctx")
    added = (index % 2 == 0) | ((index >> 1) % 2 == 0)
    out_ref[...] = first_ref[...] + jnp.where(added, chip_ref[...], 0.0)


def prefix_kernel(first_ref, second_ref, keep_ref, beside_ref, mine_ref, other_ref):
    index = lax.axis_index("ctx")
    core = index % 2
    held = (core == 1) | ((index >> 1) % 2 == 1)
    earlier = jnp.where(held, first_ref[...], 0.0) + second_ref[...]
    mine_ref[...] = earlier + jnp.where(core == 1, beside_ref[...], 0.0)
    other_ref[...] = earlier + jnp.where(core == 0, keep_ref[...], 0.0)


def earlier_kernel(
    gain_ref, qq_ref, b_ref, half_ref, mine_ref, other_ref, sum_a_ref, out_ref, sums_ref, square_ref
):
    step = pl.program_id(0)
    core = lax.axis_index("ctx") % 2
    rows = qq_ref.shape[0]
    middle = rows // 2

    @pl.when(step == 0)
    def _():
        square_ref[...] = jnp.zeros_like(square_ref)

    for j in range(2):
        columns = slice(j * HD, (j + 1) * HD)
        state = jnp.where(core == j, mine_ref[0], other_ref[0])
        gain_b = gain_ref[1, 2 * step + j]
        for part, held in ((slice(0, middle), state), (slice(middle, rows), state + half_ref[j])):
            qq = qq_ref[part, 2 * j * HD : 2 * (j + 1) * HD]
            b = gain_b * (b_ref[part, columns] + folded(dot(qq, wide_state(held))))
            out_ref[part, columns] = b
            square_ref[part, :] += b * b

    @pl.when(step == pl.num_programs(0) - 1)
    def _():
        row = lax.broadcasted_iota(jnp.int32, sums_ref.shape, 0)
        sums_ref[...] = jnp.where(row == 0, sum_a_ref[...], row_sums(square_ref[...]))


def first_tile_kernel(gain_ref, q_ref, k_ref, v_ref, tail_k_ref, tail_v_ref, a_ref, sum_ref, square_ref):
    step = pl.program_id(0)
    count = q_ref.shape[1] // HD
    lower = lower_mask()
    below = jnp.where(lower, 1.0, 0.0).astype(BF16)
    above = jnp.where(lower, 0.0, 1.0).astype(BF16)
    reachable = jnp.logical_or(lower, lax.axis_index("ctx") > 0)

    @pl.when(step == 0)
    def _():
        square_ref[...] = jnp.zeros_like(square_ref)

    scores = []
    for j in range(count):
        columns = slice(j * HD, (j + 1) * HD)
        qq = side(*halves(q_ref[:, columns]))
        now = folded(dot_rows(qq, wide_keys(*halves(k_ref[:, columns]))))
        before = folded(dot_rows(qq, wide_keys(*halves(tail_k_ref[:, columns]))))
        scores.append(jnp.where(reachable, jnp.where(lower, now, before), -jnp.inf))
    for j in range(count):
        columns = slice(j * HD, (j + 1) * HD)
        gain_a = gain_ref[0, count * step + j]
        weights, total = weights_of(scores[j])
        pair_high, pair_low = masked_pair(weights, below, above)
        vv = side(*halves(stack(tail_v_ref[:, columns], v_ref[:, columns])))
        wide = dot(stack(pair_high, pair_low), vv)
        a = (folded(wide[:WINDOW]) + wide[WINDOW:, :HD]) * (gain_a / total)
        a_ref[:, columns] = a
        square_ref[...] += a * a

    @pl.when(step == pl.num_programs(0) - 1)
    def _():
        sum_ref[...] = row_sums(square_ref[...])


def inverse_norm(total):
    return 1.0 / jnp.sqrt(total / (HEADS * HD) + EPS)


def scale_kernel(parts, *refs):
    sums, (a_ref, b_ref, out_ref) = refs[:parts], refs[-3:]
    total = sums[0][...]
    for part in sums[1:parts]:
        total = total + part[...]
    columns = inverse_norm(total).T
    out_ref[...] = a_ref[...] * columns[:, 0:1] + b_ref[...] * columns[:, 1:2]


def first_scale_kernel(parts, *refs):
    sums_b, sums_a = refs[:parts], refs[parts : 2 * parts]
    a_ref, b_ref, _, out_ref = refs[-4:]
    total_a, total_b = sums_a[0][...], sums_b[0][...]
    for part_a, part_b in zip(sums_a[1:], sums_b[1:]):
        total_a, total_b = total_a + part_a[...], total_b + part_b[...]
    inverse_a = inverse_norm(total_a).T[:, 0:1]
    inverse_b = inverse_norm(total_b).T[:, 1:2]
    out_ref[...] = a_ref[...] * inverse_a + b_ref[...] * inverse_b


def swap(block, axis, bit):
    return lax.ppermute(block, axis, [(i, i ^ bit) for i in range(lax.axis_size(axis))])


def everyone(block, axis):
    count = lax.axis_size(axis)
    return [block] + [
        lax.ppermute(block, axis, [(i, (i + s) % count) for i in range(count)]) for s in range(1, count)
    ]


def chip_totals(keep, send):
    beside = swap(send, "ctx", 1)
    return beside, keep + beside


def first_phase(chip):
    route = [(i, i ^ 2) for i in range(8) if i % 2 == 0]
    route += [(i, i + 4) for i in range(8) if i % 2 == 1 and i < 4]
    return lax.ppermute(chip, "ctx", route)


def second_phase(message):
    route = [(i, i + 4) for i in range(8) if i % 2 == 0 and i < 4]
    route += [(i, i ^ 2) for i in range(8) if i % 2 == 1 and i != 3]
    return lax.ppermute(message, "ctx", route)


def doubled_prefix(chip):
    index = lax.axis_index("ctx")
    earlier = jnp.zeros_like(chip)
    running = chip
    bit = 2
    while bit < lax.axis_size("ctx"):
        partner = swap(running, "ctx", bit)
        earlier = earlier + jnp.where((index & bit) != 0, partner, 0.0)
        running = running + partner
        bit *= 2
    return earlier


def shards(queries, keys, values, head_gain):
    rows, width = queries.shape
    heads = head_gain.shape[1]
    steps = heads // 2
    parts = lax.axis_size("head")
    queries, keys, values = (
        pltpu.with_memory_space_constraint(x, pltpu.HBM) for x in (queries, keys, values)
    )
    smem = pl.BlockSpec(memory_space=pltpu.SMEM)
    anywhere = pl.BlockSpec(memory_space=pl.ANY)
    whole = pl.BlockSpec((rows, 2 * HD), lambda i: (0, i))
    top = pl.BlockSpec((WINDOW, 2 * HD), lambda i: (0, i))
    top_four = pl.BlockSpec((WINDOW, 4 * HD), lambda i: (0, i))
    doubled = pl.BlockSpec((rows, 4 * HD), lambda i: (0, i))
    state = pl.BlockSpec((1, HD, HD), lambda i: (i, 0, 0))
    state_pair = pl.BlockSpec((2, HD, HD), lambda i: (i, 0, 0))
    sums_block = pl.BlockSpec((8, rows), lambda i: (0, 0))
    first_sums_block = pl.BlockSpec((8, WINDOW), lambda i: (0, 0))

    def array(*shape):
        return jax.ShapeDtypeStruct(shape, F32)

    def call(kernel, name, flops, moved, **kwargs):
        return pl.pallas_call(
            kernel,
            name=name,
            compiler_params=pltpu.CompilerParams(vmem_limit_bytes=VMEM_BYTES),
            cost_estimate=pl.CostEstimate(flops=flops, bytes_accessed=moved, transcendentals=0),
            **kwargs,
        )

    size = rows * width * 4
    unit = 2 * rows * width * HD
    packed = array(steps, HD, HD)
    keep, send, half, tail_k, tail_v = call(
        totals_kernel,
        "totals",
        4 * unit,
        2 * size,
        grid=(steps,),
        in_specs=[whole, whole],
        out_specs=[state, state, state_pair, top, top],
        out_shape=[packed, packed, array(heads, HD, HD), array(WINDOW, width), array(WINDOW, width)],
    )(keys, values)

    route = [(i, i + 1) for i in range(lax.axis_size("ctx") - 1)]
    before_k = lax.ppermute(tail_k, "ctx", route)
    before_v = lax.ppermute(tail_v, "ctx", route)
    beside, chip = chip_totals(keep, send)

    window, linear, qq, sum_a = call(
        local_kernel,
        "local",
        24 * unit,
        5 * size,
        grid=(steps,),
        in_specs=[smem, whole, whole, whole],
        out_specs=[whole, whole, doubled, sums_block],
        out_shape=[
            array(rows, width),
            array(rows, width),
            jax.ShapeDtypeStruct((rows, 2 * width), BF16),
            array(8, rows),
        ],
        scratch_shapes=[pltpu.VMEM((rows, HD), F32)],
    )(head_gain, queries, keys, values)

    if lax.axis_size("ctx") == 8:
        first = first_phase(chip)
        message = call(
            message_kernel,
            "message",
            0,
            size // 4,
            in_specs=[pl.BlockSpec(), pl.BlockSpec(), anywhere, anywhere],
            out_shape=packed,
        )(first, chip, sum_a, before_k)
        second = second_phase(message)
        mine, other = call(
            prefix_kernel, "prefix", 0, size // 2, out_shape=[packed, packed]
        )(first, second, keep, beside)
    else:
        earlier = doubled_prefix(chip)
        core = lax.axis_index("ctx") % 2
        mine = earlier + jnp.where(core == 1, beside, 0.0)
        other = earlier + jnp.where(core == 0, keep, 0.0)
    other = swap(other, "ctx", 1)

    linear, sums = call(
        earlier_kernel,
        "earlier",
        3 * unit,
        3 * size,
        grid=(steps,),
        in_specs=[smem, doubled, whole, state_pair, state, state, sums_block],
        out_specs=[whole, sums_block],
        out_shape=[array(rows, width), array(8, rows)],
        scratch_shapes=[pltpu.VMEM((rows, HD), F32)],
    )(head_gain, qq, linear, half, mine, other, sum_a)
    all_sums = everyone(sums, "head")

    first_a, first_sum = call(
        first_tile_kernel,
        "first_tile",
        2 * unit,
        size,
        grid=(heads // 4,),
        in_specs=[smem] + [top_four] * 5,
        out_specs=[top_four, first_sums_block],
        out_shape=[array(WINDOW, width), array(8, WINDOW)],
        scratch_shapes=[pltpu.VMEM((WINDOW, HD), F32)],
    )(head_gain, queries, keys, values, before_k, before_v)
    all_first = everyone(first_sum, "head")

    row_block = pl.BlockSpec((WINDOW, width), lambda i: (i + 1, 0))
    first_block = pl.BlockSpec((WINDOW, width), lambda i: (0, 0))
    out = call(
        functools.partial(scale_kernel, parts),
        "scale",
        unit // 64,
        2 * size,
        grid=(rows // WINDOW - 1,),
        in_specs=[pl.BlockSpec((8, WINDOW), lambda i: (0, i + 1))] * parts + [row_block, row_block],
        out_specs=row_block,
        out_shape=array(rows, width),
    )(*all_sums, window, linear)
    return call(
        functools.partial(first_scale_kernel, parts),
        "first_scale",
        unit // 256,
        size // 2,
        grid=(1,),
        in_specs=[first_sums_block] * (2 * parts) + [first_block, first_block, anywhere],
        out_specs=first_block,
        out_shape=array(rows, width),
        input_output_aliases={2 * parts + 2: 0},
    )(*all_sums, *all_first, first_a, linear, out)


def solution(mesh):
    in_specs = (P("ctx", "head"), P("ctx", "head"), P("ctx", "head"), P(None, "head"))
    out_specs = P("ctx", "head")
    return jax.shard_map(shards, mesh=mesh, in_specs=in_specs, out_specs=out_specs, check_vma=False)
```

time: 121 us -> 80.3 us (0.66)
  Pallas kernels: 47 us -> 32.1 us
  local copies, waits for them, and re-layouts: 12 us -> 0.01 us
  waiting for transfers between devices: 39.6 us -> 28.5 us
  other arithmetic: 2.25 us -> 0.06 us
    ppermute x2, waiting for transfers between devices: 34.8 us -> 19.3 us  [the longest x1 18.4 us: second_phase(): return lax.ppermute(message, 'ctx', route)]
    pallas_call x1, Pallas kernels: 25.2 us -> 11.5 us  [shards(): call(local_kernel, 'local', 24 * unit, 5 * size, grid=(steps,), in_specs=...]
    unnamed x20 -> x2, local copies, waits for them, and re-layouts: 12 us -> 0.01 us
    ppermute x1, waiting for transfers between devices: 0.01 us -> 4.5 us  [shards(): before_k = lax.ppermute(tail_k, 'ctx', route)]
    pallas_call x1 -> x3, Pallas kernels: 8.62 us -> 5.27 us  [the longest x1 5.02 us: shards(): call(first_tile_kernel, 'first_tile', 2 * unit, size, grid=(heads // 4,),...]
    pallas_call x1, Pallas kernels: 4.47 us -> 7.01 us  [shards(): call(totals_kernel, 'totals', 4 * unit, 2 * size, grid=(steps,), in_specs...]
    add x3 -> x1, other arithmetic: 2.25 us -> 0.06 us  [chip_totals(): return (beside, keep + beside)]
  transfers between devices with their start and end apart: 12 -> 12, of which waited for: 5 -> 6; matrix products, arithmetic and copies ran while one was open for 1% -> 0% of each run, Pallas kernels for 34% -> 30%
where the time goes in v1:
time: 80.3 us; the launch traced here: 79.3 us
  Pallas kernels  32.1 us (40%)
  waiting for transfers between devices  28.5 us (35%)
  starting transfers between devices  18.4 us (23%)
    ppermute x1, waiting for transfers between devices, second_phase(): return lax.ppermute(message, 'ctx', route)  18.4 us
    pallas_call x1, Pallas kernels, shards(): call(local_kernel, 'local', 24 * unit, 5 * size, grid=(steps,), in_specs=...  11.5 us
    ppermute x6, starting transfers between devices, everyone(): lax.ppermute(block, axis, [(i, (i + s) % count) for i in range(count)])  8.61 us
    pallas_call x1, Pallas kernels, shards(): call(totals_kernel, 'totals', 4 * unit, 2 * size, grid=(steps,), in_specs...  7.01 us
    pallas_call x1, Pallas kernels, shards(): call(first_tile_kernel, 'first_tile', 2 * unit, size, grid=(heads // 4,),...  5.02 us
    pallas_call x1, Pallas kernels, shards(): call(earlier_kernel, 'earlier', 3 * unit, 3 * size, grid=(steps,), in_spe...  4.53 us
    ppermute x1, waiting for transfers between devices, shards(): before_k = lax.ppermute(tail_k, 'ctx', route)  4.5 us
    ppermute x1, starting transfers between devices, first_phase(): return lax.ppermute(chip, 'ctx', route)  3.4 us
  transfers between devices with their start and end apart: 12, of which 6 were waited for; matrix products, arithmetic and copies ran while one was open for 0% of the time, Pallas kernels for 30%

profile of v1, /device:TPU:4, one launch (start us, length us, event | category | flops | bytes accessed | tf_op | source)
XLA Modules:
  0.0 79.3 jit_solution(11229550452336152900)
XLA Ops:
  0.0 7.0 %totals.1 = (f32[8,128,128]{2,1,0:T(8,128)S(1)}, f32[8,128,128]{2,1,0:T(8,128)S(1)}, f32[16,128,128]{2,1,0:T(8,128)S(1)}, f32[128,2048]{1,0:T(8,128)S(1)}, f32[128,2048]{1,0:T(8,128)S(1)}) custom-call(f32[512,2048]{1,0:T(8,128)} %k_ref.5, f32[512,2048]{1,0:T(8,128)} %v_ref.5), custom_call_target="tpu_custom_call" | custom-call | flops 1073741824 | bytes 8388608 | tf_op jit(solution)/shard_map/totals/pallas_call | solution.py:346
  7.0 0.1 collective-permute-start
  7.1 2.4 %collective-permute-start.2 = (f32[128,2048]{1,0:T(8,128)S(1)}, f32[128,2048]{1,0:T(8,128)S(1)}, u32[]{:S(2)}, u32[]{:S(2)}) collective-permute-start(f32[128,2048]{1,0:T(8,128)S(1)} %get-tuple-element.26), channel_id=1, source_target_pairs={{0,4},{4,8},{8,12},{12,16},{16,20},{20,24},{24,28},{1,5},{5,9},{9,... | collective-permute-start | bytes 3145736 | tf_op jit(solution)/shard_map/ppermute | solution.py:358
  9.6 3.4 %collective-permute-start.1 = (f32[8,128,128]{2,1,0:T(8,128)S(1)}, f32[8,128,128]{2,1,0:T(8,128)S(1)}, u32[]{:S(2)}, u32[]{:S(2)}) collective-permute-start(f32[8,128,128]{2,1,0:T(8,128)S(1)} %add.3.chip_ref), channel_id=1, source_target_pairs={{0,8},{8,0},{16,24},{24,16},{4,20},{12,28},{1,9},{9,1},{17,25},{25... | collective-permute-start | bytes 1572872 | tf_op jit(solution)/shard_map/ppermute | solution.py:290
  13.0 11.5 %local.1 = (f32[512,2048]{1,0:T(8,128)S(1)}, f32[512,2048]{1,0:T(8,128)S(1)}, bf16[512,4096]{1,0:T(8,128)(2,1)S(1)}, f32[8,512]{1,0:T(8,128)S(1)}) custom-call(f32[2,16]{1,0:T(2,128)S(1)} %copy-done, f32[512,2048]{1,0:T(8,128)} %q_ref.3, f32[512,2048]{1,0:T(8,128)} %k_ref.5, f32[512,2048]{1,0:T(8,128)} %v_ref.5), custom_call_target="tpu_custom_call" | custom-call | flops 6442450944 | bytes 20971520 | tf_op jit(solution)/shard_map/local/pallas_call | solution.py:362
  24.5 0.9 %collective-permute-done.1.first_ref = f32[8,128,128]{2,1,0:T(8,128)S(1)} collective-permute-done((f32[8,128,128]{2,1,0:T(8,128)S(1)}, f32[8,128,128]{2,1,0:T(8,128)S(1)}, u32[]{:S(2)}, u32[]{:S(2)}) %collective-permute-start.1) | collective-permute-done | bytes 524320 | tf_op jit(solution)/shard_map/ppermute | solution.py:290
  25.3 4.5 %collective-permute-done.2.__.tail_k_ref = f32[128,2048]{1,0:T(8,128)S(1)} collective-permute-done((f32[128,2048]{1,0:T(8,128)S(1)}, f32[128,2048]{1,0:T(8,128)S(1)}, u32[]{:S(2)}, u32[]{:S(2)}) %collective-permute-start.2) | collective-permute-done | bytes 1048608 | tf_op jit(solution)/shard_map/ppermute | solution.py:358
  29.8 0.1 message.1
  29.9 1.3 %collective-permute-start.3 = (f32[8,128,128]{2,1,0:T(8,128)S(1)}, f32[8,128,128]{2,1,0:T(8,128)S(1)}, u32[]{:S(2)}, u32[]{:S(2)}) collective-permute-start(f32[8,128,128]{2,1,0:T(8,128)S(1)} %message.1), channel_id=1, source_target_pairs={{0,16},{8,24},{4,12},{20,28},{28,20},{1,17},{9,25},{5,13},{21,29},... | collective-permute-start | bytes 1572872 | tf_op jit(solution)/shard_map/ppermute | solution.py:296
  31.2 2.6 %collective-permute-start.8 = (f32[128,2048]{1,0:T(8,128)S(1)}, f32[128,2048]{1,0:T(8,128)S(1)}, u32[]{:S(2)}, u32[]{:S(2)}) collective-permute-start(f32[128,2048]{1,0:T(8,128)S(1)} %get-tuple-element.30), channel_id=1, source_target_pairs={{0,4},{4,8},{8,12},{12,16},{16,20},{20,24},{24,28},{1,5},{5,9},{9,... | collective-permute-start | bytes 3145736 | tf_op jit(solution)/shard_map/ppermute | solution.py:359
  33.8 18.4 %collective-permute-done.3.second_ref = f32[8,128,128]{2,1,0:T(8,128)S(1)} collective-permute-done((f32[8,128,128]{2,1,0:T(8,128)S(1)}, f32[8,128,128]{2,1,0:T(8,128)S(1)}, u32[]{:S(2)}, u32[]{:S(2)}) %collective-permute-start.3) | collective-permute-done | bytes 524320 | tf_op jit(solution)/shard_map/ppermute | solution.py:296
  52.2 0.2 prefix.1
  52.4 0.1 collective-permute-start.4
  52.5 1.9 %collective-permute-done.4.other_ref = f32[8,128,128]{2,1,0:T(8,128)S(1)} collective-permute-done((f32[8,128,128]{2,1,0:T(8,128)S(1)}, f32[8,128,128]{2,1,0:T(8,128)S(1)}, u32[]{:S(2)}, u32[]{:S(2)}) %collective-permute-start.4) | collective-permute-done | bytes 524320 | tf_op jit(solution)/shard_map/ppermute | solution.py:272
  54.4 4.5 %earlier.1 = (f32[512,2048]{1,0:T(8,128)S(1)}, f32[8,512]{1,0:T(8,128)S(1)}) custom-call(f32[2,16]{1,0:T(2,128)S(1)} %copy-done, bf16[512,4096]{1,0:T(8,128)(2,1)S(1)} %get-tuple-element.20.qq_ref, f32[512,2048]{1,0:T(8,128)S(1)} %get-tuple-element.21.b_ref, f32[16,128,128]{2,1,0:T(8,128)S(1)} %get-tuple-element.22.half_ref, ...), custom_call_target="tpu_custom_call" | custom-call | flops 805306368 | bytes 12582912 | tf_op jit(solution)/shard_map/earlier/pallas_call | solution.py:400
  58.9 3.6 %collective-permute-start.7 = (f32[8,512]{1,0:T(8,128)S(1)}, f32[8,512]{1,0:T(8,128)S(1)}, u32[]{:S(2)}, u32[]{:S(2)}) collective-permute-start(f32[8,512]{1,0:T(8,128)S(1)} %get-tuple-element.29.refs_0_), channel_id=1, source_target_pairs={{0,3},{1,0},{2,1},{3,2},{4,7},{5,4},{6,5},{7,6},{8,11},{9,8},{10,9... | collective-permute-start | bytes 49160 | tf_op jit(solution)/shard_map/ppermute | solution.py:278
  62.5 1.0 %collective-permute-start.5 = (f32[8,512]{1,0:T(8,128)S(1)}, f32[8,512]{1,0:T(8,128)S(1)}, u32[]{:S(2)}, u32[]{:S(2)}) collective-permute-start(f32[8,512]{1,0:T(8,128)S(1)} %get-tuple-element.29.refs_0_), channel_id=1, source_target_pairs={{0,1},{1,2},{2,3},{3,0},{4,5},{5,6},{6,7},{7,4},{8,9},{9,10},{10,1... | collective-permute-start | bytes 49160 | tf_op jit(solution)/shard_map/ppermute | solution.py:278
  63.5 5.0 %first_tile.1 = (f32[128,2048]{1,0:T(8,128)S(1)}, f32[8,128]{1,0:T(8,128)S(1)}) custom-call(f32[2,16]{1,0:T(2,128)S(1)} %copy-done, f32[512,2048]{1,0:T(8,128)} %q_ref.3, f32[512,2048]{1,0:T(8,128)} %k_ref.5, f32[512,2048]{1,0:T(8,128)} %v_ref.5, f32[128,2048]{1,0:T(8,128)S(1)} %collective-permute-done.2.__.tail_k_ref, ...), custom_call_target="tpu_custom_call" | custom-call | flops 536870912 | bytes 4194304 | tf_op jit(solution)/shard_map/first_tile/pallas_call | solution.py:413
  68.6 2.9 %collective-permute-start.11 = (f32[8,128]{1,0:T(8,128)S(1)}, f32[8,128]{1,0:T(8,128)S(1)}, u32[]{:S(2)}, u32[]{:S(2)}) collective-permute-start(f32[8,128]{1,0:T(8,128)S(1)} %get-tuple-element.31.refs_4_), channel_id=1, source_target_pairs={{0,3},{1,0},{2,1},{3,2},{4,7},{5,4},{6,5},{7,6},{8,11},{9,8},{10,9... | collective-permute-start | bytes 12296 | tf_op jit(solution)/shard_map/ppermute | solution.py:278
  71.4 1.1 %collective-permute-start.10 = (f32[8,128]{1,0:T(8,128)S(1)}, f32[8,128]{1,0:T(8,128)S(1)}, u32[]{:S(2)}, u32[]{:S(2)}) collective-permute-start(f32[8,128]{1,0:T(8,128)S(1)} %get-tuple-element.31.refs_4_), channel_id=1, source_target_pairs={{0,2},{1,3},{2,0},{3,1},{4,6},{5,7},{6,4},{7,5},{8,10},{9,11},{10,... | collective-permute-start | bytes 12296 | tf_op jit(solution)/shard_map/ppermute | solution.py:278
  72.6 2.5 %scale.1.refs_10_ = f32[512,2048]{1,0:T(8,128)} custom-call(f32[8,512]{1,0:T(8,128)S(1)} %get-tuple-element.29.refs_0_, f32[8,512]{1,0:T(8,128)S(1)} %collective-permute-done.5.refs_1_, f32[8,512]{1,0:T(8,128)S(1)} %collective-permute-done.6.refs_2_, f32[8,512]{1,0:T(8,128)S(1)} %collective-permute-done.7.refs_3_, ...), custom_call_target="tpu_custom_call" | custom-call | flops 4194304 | bytes 8388608 | tf_op jit(solution)/shard_map/scale/pallas_call | solution.py:428
  75.1 0.8 %collective-permute-done.10.refs_6_ = f32[8,128]{1,0:T(8,128)S(1)} collective-permute-done((f32[8,128]{1,0:T(8,128)S(1)}, f32[8,128]{1,0:T(8,128)S(1)}, u32[]{:S(2)}, u32[]{:S(2)}) %collective-permute-start.10) | collective-permute-done | bytes 4128 | tf_op jit(solution)/shard_map/ppermute | solution.py:278
  75.9 2.0 %collective-permute-done.9.refs_5_ = f32[8,128]{1,0:T(8,128)S(1)} collective-permute-done((f32[8,128]{1,0:T(8,128)S(1)}, f32[8,128]{1,0:T(8,128)S(1)}, u32[]{:S(2)}, u32[]{:S(2)}) %collective-permute-start.9) | collective-permute-done | bytes 4128 | tf_op jit(solution)/shard_map/ppermute | solution.py:278
  78.0 1.3 %first_scale.1 = f32[512,2048]{1,0:T(8,128)} custom-call(f32[8,512]{1,0:T(8,128)S(1)} %get-tuple-element.29.refs_0_, f32[8,512]{1,0:T(8,128)S(1)} %collective-permute-done.5.refs_1_, f32[8,512]{1,0:T(8,128)S(1)} %collective-permute-done.6.refs_2_, f32[8,512]{1,0:T(8,128)S(1)} %collective-permute-done.7.refs_3_, ...), custom_call_target="tpu_custom_call", output_to_operand_aliasing={{}: (10, {})} | custom-call | flops 1048576 | bytes 2097152 | tf_op jit(solution)/shard_map/first_scale/pallas_call | solution.py:438
  (11 shorter events, 0.1 us)
Async XLA Ops:
  0.0 13.0 %copy-start = (f32[2,16]{1,0:T(2,128)S(1)}, f32[2,16]{1,0:T(2,128)}, u32[]{:S(2)}) copy-start(f32[2,16]{1,0:T(2,128)} %gain_ref.5) | copy-start | bytes 388
  7.0 2.5 %collective-permute-start = (f32[8,128,128]{2,1,0:T(8,128)S(1)}, f32[8,128,128]{2,1,0:T(8,128)S(1)}, u32[]{:S(2)}, u32[]{:S(2)}) collective-permute-start(f32[8,128,128]{2,1,0:T(8,128)S(1)} %get-tuple-element.24), channel_id=1, source_target_pairs={{0,4},{4,0},{8,12},{12,8},{16,20},{20,16},{24,28},{28,24},{1,5},{5... | collective-permute-start | bytes 1572872 | tf_op jit(solution)/shard_map/ppermute | solution.py:272
  7.1 22.7 %collective-permute-start.2 = (f32[128,2048]{1,0:T(8,128)S(1)}, f32[128,2048]{1,0:T(8,128)S(1)}, u32[]{:S(2)}, u32[]{:S(2)}) collective-permute-start(f32[128,2048]{1,0:T(8,128)S(1)} %get-tuple-element.26), channel_id=1, source_target_pairs={{0,4},{4,8},{8,12},{12,16},{16,20},{20,24},{24,28},{1,5},{5,9},{9,... | collective-permute-start | bytes 3145736 | tf_op jit(solution)/shard_map/ppermute | solution.py:358
  9.6 15.8 %collective-permute-start.1 = (f32[8,128,128]{2,1,0:T(8,128)S(1)}, f32[8,128,128]{2,1,0:T(8,128)S(1)}, u32[]{:S(2)}, u32[]{:S(2)}) collective-permute-start(f32[8,128,128]{2,1,0:T(8,128)S(1)} %add.3.chip_ref), channel_id=1, source_target_pairs={{0,8},{8,0},{16,24},{24,16},{4,20},{12,28},{1,9},{9,1},{17,25},{25... | collective-permute-start | bytes 1572872 | tf_op jit(solution)/shard_map/ppermute | solution.py:290
  29.9 22.3 %collective-permute-start.3 = (f32[8,128,128]{2,1,0:T(8,128)S(1)}, f32[8,128,128]{2,1,0:T(8,128)S(1)}, u32[]{:S(2)}, u32[]{:S(2)}) collective-permute-start(f32[8,128,128]{2,1,0:T(8,128)S(1)} %message.1), channel_id=1, source_target_pairs={{0,16},{8,24},{4,12},{20,28},{28,20},{1,17},{9,25},{5,13},{21,29},... | collective-permute-start | bytes 1572872 | tf_op jit(solution)/shard_map/ppermute | solution.py:296
  31.2 32.3 %collective-permute-start.8 = (f32[128,2048]{1,0:T(8,128)S(1)}, f32[128,2048]{1,0:T(8,128)S(1)}, u32[]{:S(2)}, u32[]{:S(2)}) collective-permute-start(f32[128,2048]{1,0:T(8,128)S(1)} %get-tuple-element.30), channel_id=1, source_target_pairs={{0,4},{4,8},{8,12},{12,16},{16,20},{20,24},{24,28},{1,5},{5,9},{9,... | collective-permute-start | bytes 3145736 | tf_op jit(solution)/shard_map/ppermute | solution.py:359
  52.4 2.0 %collective-permute-start.4 = (f32[8,128,128]{2,1,0:T(8,128)S(1)}, f32[8,128,128]{2,1,0:T(8,128)S(1)}, u32[]{:S(2)}, u32[]{:S(2)}) collective-permute-start(f32[8,128,128]{2,1,0:T(8,128)S(1)} %get-tuple-element.28), channel_id=1, source_target_pairs={{0,4},{4,0},{8,12},{12,8},{16,20},{20,16},{24,28},{28,24},{1,5},{5... | collective-permute-start | bytes 1572872 | tf_op jit(solution)/shard_map/ppermute | solution.py:272
  58.9 13.6 %collective-permute-start.7 = (f32[8,512]{1,0:T(8,128)S(1)}, f32[8,512]{1,0:T(8,128)S(1)}, u32[]{:S(2)}, u32[]{:S(2)}) collective-permute-start(f32[8,512]{1,0:T(8,128)S(1)} %get-tuple-element.29.refs_0_), channel_id=1, source_target_pairs={{0,3},{1,0},{2,1},{3,2},{4,7},{5,4},{6,5},{7,6},{8,11},{9,8},{10,9... | collective-permute-start | bytes 49160 | tf_op jit(solution)/shard_map/ppermute | solution.py:278
  62.5 10.1 %collective-permute-start.6 = (f32[8,512]{1,0:T(8,128)S(1)}, f32[8,512]{1,0:T(8,128)S(1)}, u32[]{:S(2)}, u32[]{:S(2)}) collective-permute-start(f32[8,512]{1,0:T(8,128)S(1)} %get-tuple-element.29.refs_0_), channel_id=1, source_target_pairs={{0,2},{1,3},{2,0},{3,1},{4,6},{5,7},{6,4},{7,5},{8,10},{9,11},{10,... | collective-permute-start | bytes 49160 | tf_op jit(solution)/shard_map/ppermute | solution.py:278
  62.5 10.1 %collective-permute-start.5 = (f32[8,512]{1,0:T(8,128)S(1)}, f32[8,512]{1,0:T(8,128)S(1)}, u32[]{:S(2)}, u32[]{:S(2)}) collective-permute-start(f32[8,512]{1,0:T(8,128)S(1)} %get-tuple-element.29.refs_0_), channel_id=1, source_target_pairs={{0,1},{1,2},{2,3},{3,0},{4,5},{5,6},{6,7},{7,4},{8,9},{9,10},{10,1... | collective-permute-start | bytes 49160 | tf_op jit(solution)/shard_map/ppermute | solution.py:278
  68.6 6.5 %collective-permute-start.11 = (f32[8,128]{1,0:T(8,128)S(1)}, f32[8,128]{1,0:T(8,128)S(1)}, u32[]{:S(2)}, u32[]{:S(2)}) collective-permute-start(f32[8,128]{1,0:T(8,128)S(1)} %get-tuple-element.31.refs_4_), channel_id=1, source_target_pairs={{0,3},{1,0},{2,1},{3,2},{4,7},{5,4},{6,5},{7,6},{8,11},{9,8},{10,9... | collective-permute-start | bytes 12296 | tf_op jit(solution)/shard_map/ppermute | solution.py:278
  71.4 4.5 %collective-permute-start.10 = (f32[8,128]{1,0:T(8,128)S(1)}, f32[8,128]{1,0:T(8,128)S(1)}, u32[]{:S(2)}, u32[]{:S(2)}) collective-permute-start(f32[8,128]{1,0:T(8,128)S(1)} %get-tuple-element.31.refs_4_), channel_id=1, source_target_pairs={{0,2},{1,3},{2,0},{3,1},{4,6},{5,7},{6,4},{7,5},{8,10},{9,11},{10,... | collective-permute-start | bytes 12296 | tf_op jit(solution)/shard_map/ppermute | solution.py:278
  72.6 5.4 %collective-permute-start.9 = (f32[8,128]{1,0:T(8,128)S(1)}, f32[8,128]{1,0:T(8,128)S(1)}, u32[]{:S(2)}, u32[]{:S(2)}) collective-permute-start(f32[8,128]{1,0:T(8,128)S(1)} %get-tuple-element.31.refs_4_), channel_id=1, source_target_pairs={{0,1},{1,2},{2,3},{3,0},{4,5},{5,6},{6,7},{7,4},{8,9},{9,10},{10,1... | collective-permute-start | bytes 12296 | tf_op jit(solution)/shard_map/ppermute | solution.py:278

commit v2 on v1

v2 whole, which is shorter than its diff:
```python
import functools
import math

import jax
import jax.numpy as jnp
from jax import lax
from jax.experimental import pallas as pl
from jax.experimental.pallas import tpu as pltpu
from jax.sharding import PartitionSpec as P

HEADS = 64
HD = 128
WINDOW = 128
EPS = 1e-06
F32 = jnp.float32
BF16 = jnp.bfloat16
EXP2_SCALE = math.log2(math.e) / math.sqrt(HD)
VMEM_BYTES = 24 * 1024 * 1024


def halves(x):
    high = x.astype(BF16)
    low = (x - high.astype(F32)).astype(BF16)
    return high, low


def dot(a, b):
    return lax.dot_general(a, b, (((1,), (0,)), ((), ())), preferred_element_type=F32)


def dot_rows(a, b):
    return lax.dot_general(a, b, (((1,), (1,)), ((), ())), preferred_element_type=F32)


def dot_columns(a, b):
    return lax.dot_general(a, b, (((0,), (0,)), ((), ())), preferred_element_type=F32)


def side(a, b):
    return jnp.concatenate([a, b], axis=1)


def stack(a, b):
    return jnp.concatenate([a, b], axis=0)


def outer_state(k_high, k_low, v_high, v_low):
    grid = dot_columns(side(k_high, k_low), side(v_high, v_low))
    return grid[:HD, :HD] + (grid[:HD, HD:] + grid[HD:, :HD]) + grid[HD:, HD:]


def lower_mask():
    rows = lax.broadcasted_iota(jnp.int32, (WINDOW, WINDOW), 0)
    columns = lax.broadcasted_iota(jnp.int32, (WINDOW, WINDOW), 1)
    return rows >= columns


def row_sums(square):
    ones = jnp.ones((8, HD), BF16)
    high, low = halves(square)
    return dot_rows(ones, high) + dot_rows(ones, low)


def wide_keys(k_high, k_low):
    return stack(side(k_high, k_high), side(k_low, jnp.zeros_like(k_low)))


def wide_state(state):
    high, low = halves(state)
    return stack(side(high, low), side(high, jnp.zeros_like(high)))


def folded(wide):
    half = wide.shape[1] // 2
    return wide[:, :half] + wide[:, half:]


def totals_kernel(k_ref, v_ref, keep_ref, send_ref, half_ref, tail_v_ref):
    core = lax.axis_index("ctx") % 2
    rows = k_ref.shape[0]
    middle = rows // 2
    for i in range(k_ref.shape[1] // (2 * HD)):
        states = []
        for j in (2 * i, 2 * i + 1):
            columns = slice(j * HD, (j + 1) * HD)
            k_high, k_low = halves(k_ref[:, columns])
            v_high, v_low = halves(v_ref[:, columns])
            first = outer_state(k_high[:middle], k_low[:middle], v_high[:middle], v_low[:middle])
            second = outer_state(k_high[middle:], k_low[middle:], v_high[middle:], v_low[middle:])
            half_ref[j] = first
            states.append(first + second)
        keep_ref[i] = jnp.where(core == 0, states[0], states[1])
        send_ref[i] = jnp.where(core == 0, states[1], states[0])
    tail_v_ref[...] = v_ref[rows - WINDOW :, :]


def weights_of(scores):
    biggest = jnp.max(scores, axis=1, keepdims=True)
    weights = jnp.exp2((scores - biggest) * EXP2_SCALE)
    return weights, jnp.sum(weights, axis=1, keepdims=True)


def masked_pair(weights, below, above):
    high, low = halves(weights)
    return side(high * above, high * below), side(low * above, low * below)


def local_kernel(start, extra, gain_ref, q_ref, k_ref, v_ref, *refs):
    a_ref, b_ref, qq_ref, sum_ref, square_ref = refs[extra:]
    step = pl.program_id(0)
    lower = lower_mask()
    below = jnp.where(lower, 1.0, 0.0).astype(BF16)
    above = jnp.where(lower, 0.0, 1.0).astype(BF16)
    rows = q_ref.shape[0]
    tiles = rows // WINDOW
    head = start + 2 * step

    @pl.when(step == 0)
    def _():
        square_ref[...] = jnp.zeros_like(square_ref)

    def tile(n):
        return slice(n * WINDOW, (n + 1) * WINDOW)

    scores = []
    for j in range(2):
        columns = slice(j * HD, (j + 1) * HD)
        qq = side(*halves(q_ref[:, columns]))
        qq_ref[:, 2 * j * HD : 2 * (j + 1) * HD] = qq
        k_high, k_low = halves(k_ref[:, columns])
        now, before = [], [None]
        for n in range(tiles):
            keys = wide_keys(k_high[tile(n)], k_low[tile(n)])
            found = folded(dot_rows(qq[n * WINDOW : min((n + 2) * WINDOW, rows)], keys))
            now.append(found[:WINDOW])
            before.append(found[WINDOW:])
        scores.append((now, before))
    for j in range(2):
        columns = slice(j * HD, (j + 1) * HD)
        v_high, v_low = halves(v_ref[:, columns])
        vv = side(v_high, v_low)
        now, before = scores[j]
        gain_a = gain_ref[0, head + j]
        for n in range(tiles):
            inner_high, inner_low = halves(jnp.where(lower, now[n], 0.0))
            if n == 0:
                wide = dot(stack(inner_high, inner_low), vv[tile(0)])
                b_ref[tile(0), columns] = folded(wide[:WINDOW]) + wide[WINDOW:, :HD]
                a_ref[tile(0), columns] = jnp.zeros((WINDOW, HD), F32)
                continue
            weights, total = weights_of(jnp.where(lower, now[n], before[n]))
            pair_high, pair_low = masked_pair(weights, below, above)
            if n % 2:
                before_high, before_low = halves(before[n])
            else:
                before_high = before_low = jnp.zeros((WINDOW, HD), BF16)
            left = jnp.concatenate(
                [pair_high, pair_low, side(before_high, inner_high), side(before_low, inner_low)], axis=0
            )
            wide = dot(left, vv[(n - 1) * WINDOW : (n + 1) * WINDOW])
            a = (folded(wide[tile(0)]) + wide[tile(1), :HD]) * (gain_a / total)
            a_ref[tile(n), columns] = a
            square_ref[tile(n), :] += a * a
            b_ref[tile(n), columns] = folded(wide[tile(2)]) + wide[tile(3), :HD]

    @pl.when(step == pl.num_programs(0) - 1)
    def _():
        sum_ref[...] = row_sums(square_ref[...])


def message_kernel(first_ref, chip_ref, *refs):
    out_ref = refs[-2]
    index = lax.axis_index("ctx")
    core, x, y = index % 2, (index >> 1) % 2, index >> 2
    first = jnp.where((core == 0) | (y == 1), first_ref[...], 0.0)
    out_ref[...] = first + jnp.where((core == 0) | (x == 0), chip_ref[...], 0.0)


def prefix_kernel(first_ref, second_ref, keep_ref, beside_ref, *refs):
    mine_ref, other_ref = refs[-2:]
    index = lax.axis_index("ctx")
    core, x, y = index % 2, (index >> 1) % 2, index >> 2
    use_first = jnp.where(core == 0, x, y) == 1
    use_second = (core == 1) & ((x == 1) | (y == 1)) | (core == 0) & (y == 1)
    earlier = jnp.where(use_first, first_ref[...], 0.0) + jnp.where(use_second, second_ref[...], 0.0)
    mine_ref[...] = earlier + jnp.where(core == 1, beside_ref[...], 0.0)
    other_ref[...] = earlier + jnp.where(core == 0, keep_ref[...], 0.0)


def earlier_kernel(gain_ref, *refs):
    parts, (half_ref, mine_ref, other_ref, sum_low_ref, sum_high_ref), outs = refs[:4], refs[4:9], refs[9:]
    sums_ref, square_ref = outs[2:]
    core = lax.axis_index("ctx") % 2
    rows = parts[1].shape[0]
    middle = rows // 2
    begin = 0
    square_ref[...] = jnp.zeros_like(square_ref)
    for side_number in range(2):
        qq_ref, b_ref = parts[2 * side_number : 2 * side_number + 2]
        out_ref = outs[side_number]
        for j in range(b_ref.shape[1] // HD):
            head = begin + j
            columns = slice(j * HD, (j + 1) * HD)
            state = jnp.where(core == head % 2, mine_ref[head // 2], other_ref[head // 2])
            gain_b = gain_ref[1, head]
            for part, held in ((slice(0, middle), state), (slice(middle, rows), state + half_ref[head])):
                qq = qq_ref[part, 2 * j * HD : 2 * (j + 1) * HD]
                b = gain_b * (b_ref[part, columns] + folded(dot(qq, wide_state(held))))
                out_ref[part, columns] = b
                square_ref[part, :] += b * b
        begin += b_ref.shape[1] // HD
    row = lax.broadcasted_iota(jnp.int32, sums_ref.shape, 0)
    sums_ref[...] = jnp.where(row == 0, sum_low_ref[...] + sum_high_ref[...], row_sums(square_ref[...]))


def first_weights_kernel(gain_ref, q_ref, k_ref, v_ref, tail_k_ref, weights_ref, out_ref):
    step = pl.program_id(0)
    count = q_ref.shape[1] // HD
    lower = lower_mask()
    reachable = jnp.logical_or(lower, lax.axis_index("ctx") > 0)
    scores = []
    for j in range(count):
        columns = slice(j * HD, (j + 1) * HD)
        qq = side(*halves(q_ref[:, columns]))
        now = folded(dot_rows(qq, wide_keys(*halves(k_ref[:, columns]))))
        before = folded(dot_rows(qq, wide_keys(*halves(tail_k_ref[:, columns]))))
        scores.append(jnp.where(reachable, jnp.where(lower, now, before), -jnp.inf))
    for j in range(count):
        columns = slice(j * HD, (j + 1) * HD)
        weights, total = weights_of(scores[j])
        weights = weights * (gain_ref[0, count * step + j] / total)
        now_high, now_low = halves(jnp.where(lower, weights, 0.0))
        vv = side(*halves(v_ref[:, columns]))
        wide = dot(stack(now_high, now_low), vv)
        out_ref[:, columns] = folded(wide[:WINDOW]) + wide[WINDOW:, :HD]
        weights_ref[:, 2 * j * HD : 2 * (j + 1) * HD] = side(*halves(jnp.where(lower, 0.0, weights)))


def first_values_kernel(weights_ref, now_ref, tail_v_ref, a_ref, sum_ref):
    square = jnp.zeros((WINDOW, HD), F32)
    for j in range(now_ref.shape[1] // HD):
        columns = slice(j * HD, (j + 1) * HD)
        high = weights_ref[:, 2 * j * HD : (2 * j + 1) * HD]
        low = weights_ref[:, (2 * j + 1) * HD : 2 * (j + 1) * HD]
        wide = dot(stack(high, low), side(*halves(tail_v_ref[:, columns])))
        a = now_ref[:, columns] + (folded(wide[:WINDOW]) + wide[WINDOW:, :HD])
        a_ref[:, columns] = a
        square = square + a * a
    sum_ref[...] = row_sums(square)


def inverse_norm(total):
    return 1.0 / jnp.sqrt(total / (HEADS * HD) + EPS)


def scale_kernel(parts, *refs):
    sums, (a_low, a_high, b_low, b_high, out_ref) = refs[:parts], refs[-5:]
    total = sums[0][...]
    for part in sums[1:parts]:
        total = total + part[...]
    columns = inverse_norm(total).T
    half = a_low.shape[1]
    out_ref[:, :half] = a_low[...] * columns[:, 0:1] + b_low[...] * columns[:, 1:2]
    out_ref[:, half:] = a_high[...] * columns[:, 0:1] + b_high[...] * columns[:, 1:2]


def first_scale_kernel(parts, *refs):
    sums_b, sums_a = refs[:parts], refs[parts : 2 * parts]
    a_ref, b_low, b_high, _, out_ref = refs[-5:]
    total_a, total_b = sums_a[0][...], sums_b[0][...]
    for part_a, part_b in zip(sums_a[1:], sums_b[1:]):
        total_a, total_b = total_a + part_a[...], total_b + part_b[...]
    inverse_a = inverse_norm(total_a).T[:, 0:1]
    inverse_b = inverse_norm(total_b).T[:, 1:2]
    half = b_low.shape[1]
    out_ref[:, :half] = a_ref[:, :half] * inverse_a + b_low[...] * inverse_b
    out_ref[:, half:] = a_ref[:, half:] * inverse_a + b_high[...] * inverse_b


def swap(block, axis, bit):
    return lax.ppermute(block, axis, [(i, i ^ bit) for i in range(lax.axis_size(axis))])


def everyone(block, axis):
    return [block] + [swap(block, axis, bits) for bits in range(1, lax.axis_size(axis))]


def chip_totals(keep, send):
    beside = swap(send, "ctx", 1)
    return beside, keep + beside


def first_phase(chip):
    return lax.ppermute(chip, "ctx", [(i, i ^ (2 if i % 2 == 0 else 4)) for i in range(8)])


def second_phase(message):
    return lax.ppermute(message, "ctx", [(i, i ^ (4 if i % 2 == 0 else 2)) for i in range(8)])


def doubled_prefix(chip):
    index = lax.axis_index("ctx")
    earlier = jnp.zeros_like(chip)
    running = chip
    bit = 2
    while bit < lax.axis_size("ctx"):
        partner = swap(running, "ctx", bit)
        earlier = earlier + jnp.where((index & bit) != 0, partner, 0.0)
        running = running + partner
        bit *= 2
    return earlier


def shards(queries, keys, values, head_gain):
    rows, width = queries.shape
    heads = head_gain.shape[1]
    steps = heads // 2
    parts = lax.axis_size("head")
    tail_k = keys[rows - WINDOW :]
    queries, keys, values = (
        pltpu.with_memory_space_constraint(x, pltpu.HBM) for x in (queries, keys, values)
    )
    smem = pl.BlockSpec(memory_space=pltpu.SMEM)
    anywhere = pl.BlockSpec(memory_space=pl.ANY)
    whole = pl.BlockSpec((rows, 2 * HD), lambda i: (0, i))
    whole_four = pl.BlockSpec((rows, 4 * HD), lambda i: (0, i))
    top_four = pl.BlockSpec((WINDOW, 4 * HD), lambda i: (0, i))
    doubled = pl.BlockSpec((rows, 4 * HD), lambda i: (0, i))
    state_pair = pl.BlockSpec((2, HD, HD), lambda i: (i, 0, 0))
    state_four = pl.BlockSpec((4, HD, HD), lambda i: (i, 0, 0))
    sums_block = pl.BlockSpec((8, rows), lambda i: (0, 0))
    first_sums_block = pl.BlockSpec((8, WINDOW), lambda i: (0, 0))

    def array(*shape):
        return jax.ShapeDtypeStruct(shape, F32)

    def call(kernel, name, flops, moved, **kwargs):
        return pl.pallas_call(
            kernel,
            name=name,
            compiler_params=pltpu.CompilerParams(vmem_limit_bytes=VMEM_BYTES),
            cost_estimate=pl.CostEstimate(flops=flops, bytes_accessed=moved, transcendentals=0),
            **kwargs,
        )

    size = rows * width * 4
    unit = 2 * rows * width * HD
    packed = array(steps, HD, HD)
    route = [(i, i + 1) for i in range(lax.axis_size("ctx") - 1)]
    before_k = lax.ppermute(tail_k, "ctx", route)

    keep, send, half, tail_v = call(
        totals_kernel,
        "totals",
        4 * unit,
        2 * size,
        grid=(heads // 4,),
        in_specs=[whole_four, whole_four],
        out_specs=[state_pair, state_pair, state_four, top_four],
        out_shape=[packed, packed, array(heads, HD, HD), array(WINDOW, width)],
    )(keys, values)
    beside, chip = chip_totals(keep, send)

    first_weights, first_now = call(
        first_weights_kernel,
        "first_weights",
        4 * unit,
        size,
        grid=(heads // 4,),
        in_specs=[smem] + [top_four] * 4,
        out_specs=[pl.BlockSpec((WINDOW, 8 * HD), lambda i: (0, i)), top_four],
        out_shape=[jax.ShapeDtypeStruct((WINDOW, 2 * width), BF16), array(WINDOW, width)],
    )(head_gain, queries, keys, values, before_k)

    def local(begin, count, *after):
        block = pl.BlockSpec((rows, 2 * HD), lambda i: (0, i + begin))
        taken = 2 * count * HD
        return call(
            functools.partial(local_kernel, 2 * begin, len(after)),
            "local",
            3 * count * unit // 2,
            5 * size * count // steps,
            grid=(count,),
            in_specs=[smem, block, block, block] + [anywhere] * len(after),
            out_specs=[whole, whole, doubled, sums_block],
            out_shape=[
                array(rows, taken),
                array(rows, taken),
                jax.ShapeDtypeStruct((rows, 2 * taken), BF16),
                array(8, rows),
            ],
            scratch_shapes=[pltpu.VMEM((rows, HD), F32)],
        )(head_gain, queries, keys, values, *after)

    low_steps = 3 * steps // 8
    window_low, linear_low, qq_low, sum_low = local(0, low_steps, first_now)
    window_high, linear_high, qq_high, sum_high = local(low_steps, steps - low_steps)

    if lax.axis_size("ctx") == 8:
        first = first_phase(chip)
        message, tail_v = call(
            message_kernel,
            "message",
            0,
            size // 4,
            in_specs=[pl.BlockSpec(), pl.BlockSpec(), anywhere, anywhere],
            out_specs=[pl.BlockSpec(), anywhere],
            out_shape=[packed, array(WINDOW, width)],
            input_output_aliases={3: 1},
        )(first, chip, sum_low, tail_v)
        second = second_phase(message)
        mine, other = call(
            prefix_kernel,
            "prefix",
            0,
            size // 2,
            in_specs=[pl.BlockSpec()] * 4 + [anywhere],
            out_shape=[packed, packed],
        )(first, second, keep, beside, sum_high)
    else:
        earlier = doubled_prefix(chip)
        core = lax.axis_index("ctx") % 2
        mine = earlier + jnp.where(core == 1, beside, 0.0)
        other = earlier + jnp.where(core == 0, keep, 0.0)
    before_v = lax.ppermute(tail_v, "ctx", route)
    other = swap(other, "ctx", 1)

    linear_low, linear_high, sums = call(
        earlier_kernel,
        "earlier",
        3 * unit,
        3 * size,
        in_specs=[smem] + [pl.BlockSpec()] * 9,
        out_shape=[array(*linear_low.shape), array(*linear_high.shape), array(8, rows)],
        scratch_shapes=[pltpu.VMEM((rows, HD), F32)],
    )(head_gain, qq_low, linear_low, qq_high, linear_high, half, mine, other, sum_low, sum_high)
    all_sums = everyone(sums, "head")

    first_a, first_sum = call(
        first_values_kernel,
        "first_values",
        unit,
        size // 2,
        out_shape=[array(WINDOW, width), array(8, WINDOW)],
    )(first_weights, first_now, before_v)
    all_first = everyone(first_sum, "head")

    row_block = pl.BlockSpec((WINDOW, width), lambda i: (i + 1, 0))
    row_parts = [pl.BlockSpec((WINDOW, x.shape[1]), lambda i: (i + 1, 0)) for x in (window_low, window_high)]
    first_block = pl.BlockSpec((WINDOW, width), lambda i: (0, 0))
    first_parts = [pl.BlockSpec((WINDOW, x.shape[1]), lambda i: (0, 0)) for x in (window_low, window_high)]
    out = call(
        functools.partial(scale_kernel, parts),
        "scale",
        unit // 64,
        2 * size,
        grid=(rows // WINDOW - 1,),
        in_specs=[pl.BlockSpec((8, WINDOW), lambda i: (0, i + 1))] * parts + row_parts * 2,
        out_specs=row_block,
        out_shape=array(rows, width),
    )(*all_sums, window_low, window_high, linear_low, linear_high)
    return call(
        functools.partial(first_scale_kernel, parts),
        "first_scale",
        unit // 256,
        size // 2,
        grid=(1,),
        in_specs=[first_sums_block] * (2 * parts) + [first_block, *first_parts, anywhere],
        out_specs=first_block,
        out_shape=array(rows, width),
        input_output_aliases={2 * parts + 3: 0},
    )(*all_sums, *all_first, first_a, linear_low, linear_high, out)


def solution(mesh):
    in_specs = (P("ctx", "head"), P("ctx", "head"), P("ctx", "head"), P(None, "head"))
    out_specs = P("ctx", "head")
    return jax.shard_map(shards, mesh=mesh, in_specs=in_specs, out_specs=out_specs, check_vma=False)
```

time: 80.3 us -> 72 us (0.90)
  waiting for transfers between devices: 28.5 us -> 24.5 us
  starting transfers between devices: 18.4 us -> 14.8 us
  Pallas kernels: 32.1 us -> 30.3 us
  local copies, waits for them, and re-layouts: 0.01 us -> 1.32 us
    ppermute x8 -> x2, starting transfers between devices: 13.3 us -> 0.39 us  [the longest x1 0.32 us: first_phase(): lax.ppermute(chip, 'ctx', [(i, i ^ (2 if i % 2 == 0 else 4)) for i in ran...]
    ppermute x8 -> x2, waiting for transfers between devices: 22.1 us -> 10.8 us  [the longest x1 10.8 us: second_phase(): lax.ppermute(message, 'ctx', [(i, i ^ (4 if i % 2 == 0 else 2)) for i in...]
    ppermute x2 -> x8, starting transfers between devices: 0.14 us -> 10.5 us  [swap(): lax.ppermute(block, axis, [(i, i ^ bit) for i in range(lax.axis_size(axis...]
    ppermute x1, waiting for transfers between devices: 4.5 us -> 9.05 us  [shards(): before_k = lax.ppermute(tail_k, 'ctx', route)]
    ppermute x2 -> x8, waiting for transfers between devices: 1.9 us -> 4.69 us  [swap(): lax.ppermute(block, axis, [(i, i ^ bit) for i in range(lax.axis_size(axis...]
    pallas_call x5 -> x7, Pallas kernels: 28.2 us -> 26.4 us  [the longest x2 12.9 us: local(): call(functools.partial(local_kernel, 2 * begin, len(after)), 'local', 3 *...]
    slice x0 -> x1, local copies, waits for them, and re-layouts: none -> 1.31 us  [shards(): tail_k = keys[rows - WINDOW:]]
  transfers between devices with their start and end apart: 12 -> 12, of which waited for: 6 -> 5; matrix products, arithmetic and copies ran while one was open for 0% -> 0% of each run, Pallas kernels for 30% -> 41%
where the time goes in v2:
time: 72 us; the launch traced here: 71.1 us
  Pallas kernels  30.3 us (42%)
  waiting for transfers between devices  24.5 us (34%)
  starting transfers between devices  14.8 us (21%)
  local copies, waits for them, and re-layouts  1.32 us (2%)
    pallas_call x2, Pallas kernels, local(): call(functools.partial(local_kernel, 2 * begin, len(after)), 'local', 3 *...  12.9 us
    ppermute x1, waiting for transfers between devices, second_phase(): lax.ppermute(message, 'ctx', [(i, i ^ (4 if i % 2 == 0 else 2)) for i in...  10.8 us
    ppermute x8, starting transfers between devices, swap(): lax.ppermute(block, axis, [(i, i ^ bit) for i in range(lax.axis_size(axis...  10.5 us
    ppermute x1, waiting for transfers between devices, shards(): before_k = lax.ppermute(tail_k, 'ctx', route)  9.05 us
    pallas_call x1, Pallas kernels, shards(): call(totals_kernel, 'totals', 4 * unit, 2 * size, grid=(heads // 4,), in_...  5.31 us
    pallas_call x1, Pallas kernels, shards(): call(first_weights_kernel, 'first_weights', 4 * unit, size, grid=(heads /...  4.97 us
    ppermute x8, waiting for transfers between devices, swap(): lax.ppermute(block, axis, [(i, i ^ bit) for i in range(lax.axis_size(axis...  4.69 us
    pallas_call x1, Pallas kernels, shards(): call(functools.partial(scale_kernel, parts), 'scale', unit // 64, 2 * siz...  2.49 us
  transfers between devices with their start and end apart: 12, of which 5 were waited for; matrix products, arithmetic and copies ran while one was open for 0% of the time, Pallas kernels for 41%

profile of v2, /device:TPU:4, one launch (start us, length us, event | category | flops | bytes accessed | tf_op | source)
XLA Modules:
  0.0 71.1 jit_solution(13834906362109296386)
XLA Ops:
  0.0 1.3 %slice.3 = f32[128,2048]{1,0:T(8,128)S(1)} slice(f32[512,2048]{1,0:T(8,128)} %k_ref.7), slice={[384:512], [0:2048]} | slice | bytes 2097152 | tf_op jit(solution)/shard_map/slice | solution.py:319
  1.3 1.9 %collective-permute-start = (f32[128,2048]{1,0:T(8,128)S(1)}, f32[128,2048]{1,0:T(8,128)S(1)}, u32[]{:S(2)}, u32[]{:S(2)}) collective-permute-start(f32[128,2048]{1,0:T(8,128)S(1)} %slice.3), channel_id=1, source_target_pairs={{0,4},{4,8},{8,12},{12,16},{16,20},{20,24},{24,28},{1,5},{5,9},{9,... | collective-permute-start | bytes 3145736 | tf_op jit(solution)/shard_map/ppermute | solution.py:350
  3.3 5.3 %totals.1 = (f32[8,128,128]{2,1,0:T(8,128)S(1)}, f32[8,128,128]{2,1,0:T(8,128)S(1)}, f32[16,128,128]{2,1,0:T(8,128)S(1)}, f32[128,2048]{1,0:T(8,128)S(1)}) custom-call(f32[512,2048]{1,0:T(8,128)} %k_ref.7, f32[512,2048]{1,0:T(8,128)} %v_ref.7), custom_call_target="tpu_custom_call" | custom-call | flops 1073741824 | bytes 8388608 | tf_op jit(solution)/shard_map/totals/pallas_call | solution.py:352
  8.6 1.7 %collective-permute-start.1 = (f32[8,128,128]{2,1,0:T(8,128)S(1)}, f32[8,128,128]{2,1,0:T(8,128)S(1)}, u32[]{:S(2)}, u32[]{:S(2)}) collective-permute-start(f32[8,128,128]{2,1,0:T(8,128)S(1)} %get-tuple-element.35), channel_id=1, source_target_pairs={{0,4},{4,0},{8,12},{12,8},{16,20},{20,16},{24,28},{28,24},{1,5},{5... | collective-permute-start | bytes 1572872 | tf_op jit(solution)/shard_map/ppermute | solution.py:281
  10.2 1.5 %collective-permute-done.1.beside_ref = f32[8,128,128]{2,1,0:T(8,128)S(1)} collective-permute-done((f32[8,128,128]{2,1,0:T(8,128)S(1)}, f32[8,128,128]{2,1,0:T(8,128)S(1)}, u32[]{:S(2)}, u32[]{:S(2)}) %collective-permute-start.1) | collective-permute-done | bytes 524320 | tf_op jit(solution)/shard_map/ppermute | solution.py:281
  11.8 0.3 collective-permute-start.2
  12.2 9.0 %collective-permute-done.tail_k_ref = f32[128,2048]{1,0:T(8,128)S(1)} collective-permute-done((f32[128,2048]{1,0:T(8,128)S(1)}, f32[128,2048]{1,0:T(8,128)S(1)}, u32[]{:S(2)}, u32[]{:S(2)}) %collective-permute-start) | collective-permute-done | bytes 1048608 | tf_op jit(solution)/shard_map/ppermute | solution.py:350
  21.2 5.0 %first_weights.1 = (bf16[128,4096]{1,0:T(8,128)(2,1)S(1)}, f32[128,2048]{1,0:T(8,128)S(1)}) custom-call(f32[2,16]{1,0:T(2,128)S(1)} %copy-done, f32[512,2048]{1,0:T(8,128)} %q_ref.5, f32[512,2048]{1,0:T(8,128)} %k_ref.7, f32[512,2048]{1,0:T(8,128)} %v_ref.7, f32[128,2048]{1,0:T(8,128)S(1)} %collective-permute-done.tail_k_ref), custom_call_target="tpu_custom_call" | custom-call | flops 1073741824 | bytes 4194304 | tf_op jit(solution)/shard_map/first_weights/pallas_call | solution.py:364
  26.2 5.2 %local.2 = (f32[512,768]{1,0:T(8,128)S(1)}, f32[512,768]{1,0:T(8,128)S(1)}, bf16[512,1536]{1,0:T(8,128)(2,1)S(1)}, f32[8,512]{1,0:T(8,128)S(1)}) custom-call(f32[2,16]{1,0:T(2,128)S(1)} %copy-done, f32[512,2048]{1,0:T(8,128)} %q_ref.5, f32[512,2048]{1,0:T(8,128)} %k_ref.7, f32[512,2048]{1,0:T(8,128)} %v_ref.7, f32[128,2048]{1,0:T(8,128)S(1)} %get-tuple-element.28.refs_0_.now_ref), custom_call_target="tpu_custom_call" | custom-call | flops 1207959552 | bytes 7864320 | tf_op jit(solution)/shard_map/local/pallas_call | solution.py:378
  31.4 0.1 message.1
  31.6 1.9 %collective-permute-start.8 = (f32[128,2048]{1,0:T(8,128)S(1)}, f32[128,2048]{1,0:T(8,128)S(1)}, u32[]{:S(2)}, u32[]{:S(2)}) collective-permute-start(f32[128,2048]{1,0:T(8,128)S(1)} %get-tuple-element.44), channel_id=1, source_target_pairs={{0,4},{4,8},{8,12},{12,16},{16,20},{20,24},{24,28},{1,5},{5,9},{9,... | collective-permute-start | bytes 3145736 | tf_op jit(solution)/shard_map/ppermute | solution.py:425
  33.5 7.7 %local.3 = (f32[512,1280]{1,0:T(8,128)S(1)}, f32[512,1280]{1,0:T(8,128)S(1)}, bf16[512,2560]{1,0:T(8,128)(2,1)S(1)}, f32[8,512]{1,0:T(8,128)S(1)}) custom-call(f32[2,16]{1,0:T(2,128)S(1)} %copy-done, f32[512,2048]{1,0:T(8,128)} %q_ref.5, f32[512,2048]{1,0:T(8,128)} %k_ref.7, f32[512,2048]{1,0:T(8,128)} %v_ref.7), custom_call_target="tpu_custom_call" | custom-call | flops 2013265920 | bytes 13107200 | tf_op jit(solution)/shard_map/local/pallas_call | solution.py:378
  41.2 10.8 %collective-permute-done.3.second_ref = f32[8,128,128]{2,1,0:T(8,128)S(1)} collective-permute-done((f32[8,128,128]{2,1,0:T(8,128)S(1)}, f32[8,128,128]{2,1,0:T(8,128)S(1)}, u32[]{:S(2)}, u32[]{:S(2)}) %collective-permute-start.3) | collective-permute-done | bytes 524320 | tf_op jit(solution)/shard_map/ppermute | solution.py:298
  52.0 0.2 prefix.1
  52.3 1.9 %collective-permute-done.4.refs_6_ = f32[8,128,128]{2,1,0:T(8,128)S(1)} collective-permute-done((f32[8,128,128]{2,1,0:T(8,128)S(1)}, f32[8,128,128]{2,1,0:T(8,128)S(1)}, u32[]{:S(2)}, u32[]{:S(2)}) %collective-permute-start.4) | collective-permute-done | bytes 524320 | tf_op jit(solution)/shard_map/ppermute | solution.py:281
  54.2 2.2 %earlier.1 = (f32[512,768]{1,0:T(8,128)S(1)}, f32[512,1280]{1,0:T(8,128)S(1)}, f32[8,512]{1,0:T(8,128)S(1)}) custom-call(f32[2,16]{1,0:T(2,128)S(1)} %copy-done, bf16[512,1536]{1,0:T(8,128)(2,1)S(1)} %get-tuple-element.29.refs_0_, f32[512,768]{1,0:T(8,128)S(1)} %get-tuple-element.30.refs_1_, bf16[512,2560]{1,0:T(8,128)(2,1)S(1)} %get-tuple-element.31.refs_2_, ...), custom_call_target="tpu_custom_call" | custom-call | flops 805306368 | bytes 12582912 | tf_op jit(solution)/shard_map/earlier/pallas_call | solution.py:428
  56.4 3.7 %collective-permute-start.7 = (f32[8,512]{1,0:T(8,128)S(1)}, f32[8,512]{1,0:T(8,128)S(1)}, u32[]{:S(2)}, u32[]{:S(2)}) collective-permute-start(f32[8,512]{1,0:T(8,128)S(1)} %get-tuple-element.42.refs_0_), channel_id=1, source_target_pairs={{0,3},{1,2},{2,1},{3,0},{4,7},{5,6},{6,5},{7,4},{8,11},{9,10},{10,... | collective-permute-start | bytes 49160 | tf_op jit(solution)/shard_map/ppermute | solution.py:281
  60.1 0.7 %collective-permute-start.5 = (f32[8,512]{1,0:T(8,128)S(1)}, f32[8,512]{1,0:T(8,128)S(1)}, u32[]{:S(2)}, u32[]{:S(2)}) collective-permute-start(f32[8,512]{1,0:T(8,128)S(1)} %get-tuple-element.42.refs_0_), channel_id=1, source_target_pairs={{0,1},{1,0},{2,3},{3,2},{4,5},{5,4},{6,7},{7,6},{8,9},{9,8},{10,11... | collective-permute-start | bytes 49160 | tf_op jit(solution)/shard_map/ppermute | solution.py:281
  60.8 0.8 %first_values.1 = (f32[128,2048]{1,0:T(8,128)S(1)}, f32[8,128]{1,0:T(8,128)S(1)}) custom-call(bf16[128,4096]{1,0:T(8,128)(2,1)S(1)} %get-tuple-element.43.weights_ref, f32[128,2048]{1,0:T(8,128)S(1)} %get-tuple-element.28.refs_0_.now_ref, f32[128,2048]{1,0:T(8,128)S(1)} %collective-permute-done.8.tail_v_ref), custom_call_target="tpu_custom_call" | custom-call | flops 268435456 | bytes 2097152 | tf_op jit(solution)/shard_map/first_values/pallas_call | solution.py:439
  61.6 3.6 %collective-permute-start.11 = (f32[8,128]{1,0:T(8,128)S(1)}, f32[8,128]{1,0:T(8,128)S(1)}, u32[]{:S(2)}, u32[]{:S(2)}) collective-permute-start(f32[8,128]{1,0:T(8,128)S(1)} %get-tuple-element.45.refs_4_), channel_id=1, source_target_pairs={{0,3},{1,2},{2,1},{3,0},{4,7},{5,6},{6,5},{7,4},{8,11},{9,10},{10,... | collective-permute-start | bytes 12296 | tf_op jit(solution)/shard_map/ppermute | solution.py:281
  65.3 0.8 %collective-permute-start.9 = (f32[8,128]{1,0:T(8,128)S(1)}, f32[8,128]{1,0:T(8,128)S(1)}, u32[]{:S(2)}, u32[]{:S(2)}) collective-permute-start(f32[8,128]{1,0:T(8,128)S(1)} %get-tuple-element.45.refs_4_), channel_id=1, source_target_pairs={{0,1},{1,0},{2,3},{3,2},{4,5},{5,4},{6,7},{7,6},{8,9},{9,8},{10,11... | collective-permute-start | bytes 12296 | tf_op jit(solution)/shard_map/ppermute | solution.py:281
  66.0 2.5 %scale.1.refs_11_ = f32[512,2048]{1,0:T(8,128)} custom-call(f32[8,512]{1,0:T(8,128)S(1)} %get-tuple-element.42.refs_0_, f32[8,512]{1,0:T(8,128)S(1)} %collective-permute-done.5.refs_1_, f32[8,512]{1,0:T(8,128)S(1)} %collective-permute-done.6.refs_2_, f32[8,512]{1,0:T(8,128)S(1)} %collective-permute-done.7.refs_3_, f32[512,768]{1,0:T(8,128)S(1)} %get-tuple-element.49.refs_4_, ...), custom_call_target="tpu_custom_call" | custom-call | flops 4194304 | bytes 8388608 | tf_op jit(solution)/shard_map/scale/pallas_call | solution.py:452
  68.5 1.2 %collective-permute-done.10.refs_6_ = f32[8,128]{1,0:T(8,128)S(1)} collective-permute-done((f32[8,128]{1,0:T(8,128)S(1)}, f32[8,128]{1,0:T(8,128)S(1)}, u32[]{:S(2)}, u32[]{:S(2)}) %collective-permute-start.10) | collective-permute-done | bytes 4128 | tf_op jit(solution)/shard_map/ppermute | solution.py:281
  69.8 1.3 %first_scale.1 = f32[512,2048]{1,0:T(8,128)} custom-call(f32[8,512]{1,0:T(8,128)S(1)} %get-tuple-element.42.refs_0_, f32[8,512]{1,0:T(8,128)S(1)} %collective-permute-done.5.refs_1_, f32[8,512]{1,0:T(8,128)S(1)} %collective-permute-done.6.refs_2_, f32[8,512]{1,0:T(8,128)S(1)} %collective-permute-done.7.refs_3_, ...), custom_call_target="tpu_custom_call", output_to_operand_aliasing={{}: (11, {})} | custom-call | flops 1048576 | bytes 2097152 | tf_op jit(solution)/shard_map/first_scale/pallas_call | solution.py:462
  (14 shorter events, 0.2 us)
Async XLA Ops:
  1.3 19.9 %copy-start = (f32[2,16]{1,0:T(2,128)S(1)}, f32[2,16]{1,0:T(2,128)}, u32[]{:S(2)}) copy-start(f32[2,16]{1,0:T(2,128)} %gain_ref.7) | copy-start | bytes 388
  1.3 19.9 %collective-permute-start = (f32[128,2048]{1,0:T(8,128)S(1)}, f32[128,2048]{1,0:T(8,128)S(1)}, u32[]{:S(2)}, u32[]{:S(2)}) collective-permute-start(f32[128,2048]{1,0:T(8,128)S(1)} %slice.3), channel_id=1, source_target_pairs={{0,4},{4,8},{8,12},{12,16},{16,20},{20,24},{24,28},{1,5},{5,9},{9,... | collective-permute-start | bytes 3145736 | tf_op jit(solution)/shard_map/ppermute | solution.py:350
  8.6 3.2 %collective-permute-start.1 = (f32[8,128,128]{2,1,0:T(8,128)S(1)}, f32[8,128,128]{2,1,0:T(8,128)S(1)}, u32[]{:S(2)}, u32[]{:S(2)}) collective-permute-start(f32[8,128,128]{2,1,0:T(8,128)S(1)} %get-tuple-element.35), channel_id=1, source_target_pairs={{0,4},{4,0},{8,12},{12,8},{16,20},{20,16},{24,28},{28,24},{1,5},{5... | collective-permute-start | bytes 1572872 | tf_op jit(solution)/shard_map/ppermute | solution.py:281
  11.8 19.5 %collective-permute-start.2 = (f32[8,128,128]{2,1,0:T(8,128)S(1)}, f32[8,128,128]{2,1,0:T(8,128)S(1)}, u32[]{:S(2)}, u32[]{:S(2)}) collective-permute-start(f32[8,128,128]{2,1,0:T(8,128)S(1)} %add.3.chip_ref), channel_id=1, source_target_pairs={{0,8},{4,20},{8,0},{12,28},{16,24},{20,4},{24,16},{28,12},{1,9},{5... | collective-permute-start | bytes 1572872 | tf_op jit(solution)/shard_map/ppermute | solution.py:294
  31.5 20.5 %collective-permute-start.3 = (f32[8,128,128]{2,1,0:T(8,128)S(1)}, f32[8,128,128]{2,1,0:T(8,128)S(1)}, u32[]{:S(2)}, u32[]{:S(2)}) collective-permute-start(f32[8,128,128]{2,1,0:T(8,128)S(1)} %get-tuple-element.38), channel_id=1, source_target_pairs={{0,16},{4,12},{8,24},{12,4},{16,0},{20,28},{24,8},{28,20},{1,17},{... | collective-permute-start | bytes 1572872 | tf_op jit(solution)/shard_map/ppermute | solution.py:298
  31.6 29.2 %collective-permute-start.8 = (f32[128,2048]{1,0:T(8,128)S(1)}, f32[128,2048]{1,0:T(8,128)S(1)}, u32[]{:S(2)}, u32[]{:S(2)}) collective-permute-start(f32[128,2048]{1,0:T(8,128)S(1)} %get-tuple-element.44), channel_id=1, source_target_pairs={{0,4},{4,8},{8,12},{12,16},{16,20},{20,24},{24,28},{1,5},{5,9},{9,... | collective-permute-start | bytes 3145736 | tf_op jit(solution)/shard_map/ppermute | solution.py:425
  52.2 2.0 %collective-permute-start.4 = (f32[8,128,128]{2,1,0:T(8,128)S(1)}, f32[8,128,128]{2,1,0:T(8,128)S(1)}, u32[]{:S(2)}, u32[]{:S(2)}) collective-permute-start(f32[8,128,128]{2,1,0:T(8,128)S(1)} %get-tuple-element.41), channel_id=1, source_target_pairs={{0,4},{4,0},{8,12},{12,8},{16,20},{20,16},{24,28},{28,24},{1,5},{5... | collective-permute-start | bytes 1572872 | tf_op jit(solution)/shard_map/ppermute | solution.py:281
  56.4 8.9 %collective-permute-start.7 = (f32[8,512]{1,0:T(8,128)S(1)}, f32[8,512]{1,0:T(8,128)S(1)}, u32[]{:S(2)}, u32[]{:S(2)}) collective-permute-start(f32[8,512]{1,0:T(8,128)S(1)} %get-tuple-element.42.refs_0_), channel_id=1, source_target_pairs={{0,3},{1,2},{2,1},{3,0},{4,7},{5,6},{6,5},{7,4},{8,11},{9,10},{10,... | collective-permute-start | bytes 49160 | tf_op jit(solution)/shard_map/ppermute | solution.py:281
  60.0 6.0 %collective-permute-start.6 = (f32[8,512]{1,0:T(8,128)S(1)}, f32[8,512]{1,0:T(8,128)S(1)}, u32[]{:S(2)}, u32[]{:S(2)}) collective-permute-start(f32[8,512]{1,0:T(8,128)S(1)} %get-tuple-element.42.refs_0_), channel_id=1, source_target_pairs={{0,2},{1,3},{2,0},{3,1},{4,6},{5,7},{6,4},{7,5},{8,10},{9,11},{10,... | collective-permute-start | bytes 49160 | tf_op jit(solution)/shard_map/ppermute | solution.py:281
  60.1 6.0 %collective-permute-start.5 = (f32[8,512]{1,0:T(8,128)S(1)}, f32[8,512]{1,0:T(8,128)S(1)}, u32[]{:S(2)}, u32[]{:S(2)}) collective-permute-start(f32[8,512]{1,0:T(8,128)S(1)} %get-tuple-element.42.refs_0_), channel_id=1, source_target_pairs={{0,1},{1,0},{2,3},{3,2},{4,5},{5,4},{6,7},{7,6},{8,9},{9,8},{10,11... | collective-permute-start | bytes 49160 | tf_op jit(solution)/shard_map/ppermute | solution.py:281
  61.6 6.9 %collective-permute-start.11 = (f32[8,128]{1,0:T(8,128)S(1)}, f32[8,128]{1,0:T(8,128)S(1)}, u32[]{:S(2)}, u32[]{:S(2)}) collective-permute-start(f32[8,128]{1,0:T(8,128)S(1)} %get-tuple-element.45.refs_4_), channel_id=1, source_target_pairs={{0,3},{1,2},{2,1},{3,0},{4,7},{5,6},{6,5},{7,4},{8,11},{9,10},{10,... | collective-permute-start | bytes 12296 | tf_op jit(solution)/shard_map/ppermute | solution.py:281
  65.3 4.5 %collective-permute-start.10 = (f32[8,128]{1,0:T(8,128)S(1)}, f32[8,128]{1,0:T(8,128)S(1)}, u32[]{:S(2)}, u32[]{:S(2)}) collective-permute-start(f32[8,128]{1,0:T(8,128)S(1)} %get-tuple-element.45.refs_4_), channel_id=1, source_target_pairs={{0,2},{1,3},{2,0},{3,1},{4,6},{5,7},{6,4},{7,5},{8,10},{9,11},{10,... | collective-permute-start | bytes 12296 | tf_op jit(solution)/shard_map/ppermute | solution.py:281
  65.3 4.5 %collective-permute-start.9 = (f32[8,128]{1,0:T(8,128)S(1)}, f32[8,128]{1,0:T(8,128)S(1)}, u32[]{:S(2)}, u32[]{:S(2)}) collective-permute-start(f32[8,128]{1,0:T(8,128)S(1)} %get-tuple-element.45.refs_4_), channel_id=1, source_target_pairs={{0,1},{1,0},{2,3},{3,2},{4,5},{5,4},{6,7},{7,6},{8,9},{9,8},{10,11... | collective-permute-start | bytes 12296 | tf_op jit(solution)/shard_map/ppermute | solution.py:281

commit v3 on v2

v3 whole, which is shorter than its diff:
```python
import functools
import math

import jax
import jax.numpy as jnp
from jax import lax
from jax.experimental import pallas as pl
from jax.experimental.pallas import tpu as pltpu
from jax.sharding import PartitionSpec as P

HEADS = 64
HD = 128
WINDOW = 128
EPS = 1e-06
F32 = jnp.float32
BF16 = jnp.bfloat16
EXP2_SCALE = math.log2(math.e) / math.sqrt(HD)
VMEM_BYTES = 20 * 1024 * 1024
GROUP = 4


def halves(x):
    high = x.astype(BF16)
    low = (x - high.astype(F32)).astype(BF16)
    return high, low


def dot(a, b):
    return lax.dot_general(a, b, (((1,), (0,)), ((), ())), preferred_element_type=F32)


def dot_rows(a, b):
    return lax.dot_general(a, b, (((1,), (1,)), ((), ())), preferred_element_type=F32)


def dot_columns(a, b):
    return lax.dot_general(a, b, (((0,), (0,)), ((), ())), preferred_element_type=F32)


def side(a, b):
    return jnp.concatenate([a, b], axis=1)


def stack(a, b):
    return jnp.concatenate([a, b], axis=0)


def outer_state(k_high, k_low, v_high, v_low):
    grid = dot_columns(side(k_high, k_low), side(v_high, v_low))
    return grid[:HD, :HD] + (grid[:HD, HD:] + grid[HD:, :HD]) + grid[HD:, HD:]


def lower_mask():
    rows = lax.broadcasted_iota(jnp.int32, (WINDOW, WINDOW), 0)
    columns = lax.broadcasted_iota(jnp.int32, (WINDOW, WINDOW), 1)
    return rows >= columns


def row_sums(square):
    ones = jnp.ones((8, HD), BF16)
    high, low = halves(square)
    return dot_rows(ones, high) + dot_rows(ones, low)


def wide_keys(k_high, k_low):
    return stack(side(k_high, k_high), side(k_low, jnp.zeros_like(k_low)))


def wide_state(state):
    high, low = halves(state)
    return stack(side(high, low), side(high, jnp.zeros_like(high)))


def folded(wide):
    half = wide.shape[1] // 2
    return wide[:, :half] + wide[:, half:]


def head_columns(head, count=1, width=HD):
    return pl.ds(pl.multiple_of(head * width, width), count * width)


def tails_kernel(k_ref, v_ref, tail_k_ref, tail_v_ref, sems):
    rows = k_ref.shape[0]
    copies = [
        pltpu.make_async_copy(source.at[pl.ds(rows - WINDOW, WINDOW), :], target, sems.at[i])
        for i, (source, target) in enumerate(((k_ref, tail_k_ref), (v_ref, tail_v_ref)))
    ]
    for copy in copies:
        copy.start()
    for copy in copies:
        copy.wait()


def totals_kernel(k_hbm, v_hbm, keep_ref, send_ref, half_ref, k_ref, v_ref, sems):
    core = lax.axis_index("ctx") % 2
    rows, width = k_ref.shape
    middle = rows // 2
    groups = width // (GROUP * HD)

    def copies(group):
        columns = head_columns(group, 1, GROUP * HD)
        return [
            pltpu.make_async_copy(source.at[:, columns], target.at[:, columns], sems.at[i, group])
            for i, (source, target) in enumerate(((k_hbm, k_ref), (v_hbm, v_ref)))
        ]

    for group in range(groups):
        for copy in copies(group):
            copy.start()

    @pl.loop(0, groups)
    def _(group):
        for copy in copies(group):
            copy.wait()
        for i in range(GROUP // 2):
            states = []
            for j in (2 * i, 2 * i + 1):
                head = GROUP * group + j
                columns = head_columns(head)
                k_high, k_low = halves(k_ref[:, columns])
                v_high, v_low = halves(v_ref[:, columns])
                first = outer_state(k_high[:middle], k_low[:middle], v_high[:middle], v_low[:middle])
                second = outer_state(k_high[middle:], k_low[middle:], v_high[middle:], v_low[middle:])
                half_ref[head] = first
                states.append(first + second)
            pair = GROUP // 2 * group + i
            keep_ref[pair] = jnp.where(core == 0, states[0], states[1])
            send_ref[pair] = jnp.where(core == 0, states[1], states[0])


def weights_of(scores):
    biggest = jnp.max(scores, axis=1, keepdims=True)
    weights = jnp.exp2((scores - biggest) * EXP2_SCALE)
    return weights, jnp.sum(weights, axis=1, keepdims=True)


def masked_pair(weights, below, above):
    high, low = halves(weights)
    return side(high * above, high * below), side(low * above, low * below)


def local_kernel(begin, gain_ref, q_hbm, k_ref, v_ref, *refs):
    a_ref, b_ref, qq_ref, sum_ref, q_ref, square_ref, sems = refs[-7:]
    lower = lower_mask()
    below = jnp.where(lower, 1.0, 0.0).astype(BF16)
    above = jnp.where(lower, 0.0, 1.0).astype(BF16)
    rows, width = a_ref.shape
    tiles = rows // WINDOW
    groups = width // (GROUP * HD)

    def load(group):
        source = pl.ds(pl.multiple_of(begin * HD + group * (GROUP * HD), HD), GROUP * HD)
        target = head_columns(group, 1, GROUP * HD)
        return pltpu.make_async_copy(q_hbm.at[:, source], q_ref.at[:, target], sems.at[group])

    for group in range(groups):
        load(group).start()
    square_ref[...] = jnp.zeros_like(square_ref)

    def tile(n):
        return slice(n * WINDOW, (n + 1) * WINDOW)

    @pl.loop(0, groups)
    def _(group):
        load(group).wait()
        scores = []
        for j in range(GROUP):
            head = GROUP * group + j
            qq = side(*halves(q_ref[:, head_columns(head)]))
            qq_ref[:, head_columns(head, 1, 2 * HD)] = qq
            k_high, k_low = halves(k_ref[:, head_columns(begin + head)])
            now, before = [], [None]
            for n in range(tiles):
                keys = wide_keys(k_high[tile(n)], k_low[tile(n)])
                found = folded(dot_rows(qq[n * WINDOW : min((n + 2) * WINDOW, rows)], keys))
                now.append(found[:WINDOW])
                before.append(found[WINDOW:])
            scores.append((now, before))
        for j in range(GROUP):
            head = GROUP * group + j
            columns = head_columns(head)
            vv = side(*halves(v_ref[:, head_columns(begin + head)]))
            now, before = scores[j]
            gain_a = gain_ref[0, begin + head]
            for n in range(tiles):
                inner_high, inner_low = halves(jnp.where(lower, now[n], 0.0))
                if n == 0:
                    wide = dot(stack(inner_high, inner_low), vv[tile(0)])
                    b_ref[tile(0), columns] = folded(wide[:WINDOW]) + wide[WINDOW:, :HD]
                    a_ref[tile(0), columns] = jnp.zeros((WINDOW, HD), F32)
                    continue
                weights, total = weights_of(jnp.where(lower, now[n], before[n]))
                pair_high, pair_low = masked_pair(weights, below, above)
                if n % 2:
                    before_high, before_low = halves(before[n])
                else:
                    before_high = before_low = jnp.zeros((WINDOW, HD), BF16)
                left = jnp.concatenate(
                    [pair_high, pair_low, side(before_high, inner_high), side(before_low, inner_low)], axis=0
                )
                wide = dot(left, vv[(n - 1) * WINDOW : (n + 1) * WINDOW])
                a = (folded(wide[tile(0)]) + wide[tile(1), :HD]) * (gain_a / total)
                a_ref[tile(n), columns] = a
                square_ref[tile(n), :] += a * a
                b_ref[tile(n), columns] = folded(wide[tile(2)]) + wide[tile(3), :HD]

    sum_ref[...] = row_sums(square_ref[...])


def message_kernel(first_ref, chip_ref, *refs):
    out_ref = refs[-2]
    index = lax.axis_index("ctx")
    core, x, y = index % 2, (index >> 1) % 2, index >> 2
    first = jnp.where((core == 0) | (y == 1), first_ref[...], 0.0)
    out_ref[...] = first + jnp.where((core == 0) | (x == 0), chip_ref[...], 0.0)


def prefix_kernel(first_ref, second_ref, keep_ref, beside_ref, *refs):
    mine_ref, other_ref = refs[-2:]
    index = lax.axis_index("ctx")
    core, x, y = index % 2, (index >> 1) % 2, index >> 2
    use_first = jnp.where(core == 0, x, y) == 1
    use_second = (core == 1) & ((x == 1) | (y == 1)) | (core == 0) & (y == 1)
    earlier = jnp.where(use_first, first_ref[...], 0.0) + jnp.where(use_second, second_ref[...], 0.0)
    mine_ref[...] = earlier + jnp.where(core == 1, beside_ref[...], 0.0)
    other_ref[...] = earlier + jnp.where(core == 0, keep_ref[...], 0.0)


def earlier_kernel(gain_ref, *refs):
    parts, (half_ref, mine_ref, other_ref, sum_low_ref, sum_high_ref), outs = refs[:4], refs[4:9], refs[9:]
    sums_ref, square_ref = outs[2:]
    core = lax.axis_index("ctx") % 2
    rows = parts[1].shape[0]
    middle = rows // 2
    begin = 0
    square_ref[...] = jnp.zeros_like(square_ref)
    for side_number in range(2):
        qq_ref, b_ref = parts[2 * side_number : 2 * side_number + 2]
        out_ref = outs[side_number]
        for j in range(b_ref.shape[1] // HD):
            head = begin + j
            columns = slice(j * HD, (j + 1) * HD)
            state = jnp.where(core == head % 2, mine_ref[head // 2], other_ref[head // 2])
            gain_b = gain_ref[1, head]
            for part, held in ((slice(0, middle), state), (slice(middle, rows), state + half_ref[head])):
                qq = qq_ref[part, 2 * j * HD : 2 * (j + 1) * HD]
                b = gain_b * (b_ref[part, columns] + folded(dot(qq, wide_state(held))))
                out_ref[part, columns] = b
                square_ref[part, :] += b * b
        begin += b_ref.shape[1] // HD
    own = row_sums(square_ref[...])
    row = lax.broadcasted_iota(jnp.int32, own.shape, 0)
    own = jnp.where(row == 0, sum_low_ref[...] + sum_high_ref[...], own)
    for i in range(sums_ref.shape[0]):
        sums_ref[i] = own


def first_weights_kernel(gain_ref, qq_low_ref, qq_high_ref, k_ref, v_ref, tail_k_ref, weights_ref, out_ref):
    lower = lower_mask()
    reachable = jnp.logical_or(lower, lax.axis_index("ctx") > 0)
    top = slice(0, WINDOW)
    begin = 0
    for qq_ref in (qq_low_ref, qq_high_ref):
        count = qq_ref.shape[1] // (2 * HD)

        @pl.loop(0, count // GROUP)
        def _(group):
            scores = []
            for j in range(GROUP):
                head = GROUP * group + j
                columns = head_columns(begin + head)
                qq = qq_ref[top, head_columns(head, 1, 2 * HD)]
                now = folded(dot_rows(qq, wide_keys(*halves(k_ref[top, columns]))))
                before = folded(dot_rows(qq, wide_keys(*halves(tail_k_ref[:, columns]))))
                scores.append(jnp.where(reachable, jnp.where(lower, now, before), -jnp.inf))
            for j in range(GROUP):
                head = begin + GROUP * group + j
                columns = head_columns(head)
                weights, total = weights_of(scores[j])
                weights = weights * (gain_ref[0, head] / total)
                now_high, now_low = halves(jnp.where(lower, weights, 0.0))
                vv = side(*halves(v_ref[top, columns]))
                wide = dot(stack(now_high, now_low), vv)
                out_ref[:, columns] = folded(wide[:WINDOW]) + wide[WINDOW:, :HD]
                weights_ref[:, head_columns(head, 1, 2 * HD)] = side(*halves(jnp.where(lower, 0.0, weights)))

        begin += count


def first_values_kernel(weights_ref, now_ref, tail_v_ref, _, a_ref, sums_ref):
    square = jnp.zeros((WINDOW, HD), F32)
    for j in range(now_ref.shape[1] // HD):
        columns = slice(j * HD, (j + 1) * HD)
        high = weights_ref[:, 2 * j * HD : (2 * j + 1) * HD]
        low = weights_ref[:, (2 * j + 1) * HD : 2 * (j + 1) * HD]
        wide = dot(stack(high, low), side(*halves(tail_v_ref[:, columns])))
        a = now_ref[:, columns] + (folded(wide[:WINDOW]) + wide[WINDOW:, :HD])
        a_ref[:, columns] = a
        square = square + a * a
    own = row_sums(square)
    for i in range(sums_ref.shape[0]):
        sums_ref[i] = own


def inverse_norm(total):
    return 1.0 / jnp.sqrt(total / (HEADS * HD) + EPS)


def scale_kernel(sums_ref, a_low, a_high, b_low, b_high, out_hbm, written_ref, out_ref, sems):
    inverse = inverse_norm(jnp.sum(sums_ref[...], axis=0)).T
    middle = a_low.shape[1]
    written_ref[...] = inverse[:8]
    copies = []
    for n in range(out_ref.shape[0] // WINDOW):
        held = slice(n * WINDOW, (n + 1) * WINDOW)
        rows = slice((n + 1) * WINDOW, (n + 2) * WINDOW)
        inverse_a, inverse_b = inverse[rows, 0:1], inverse[rows, 1:2]
        out_ref[held, :middle] = a_low[rows, :] * inverse_a + b_low[rows, :] * inverse_b
        out_ref[held, middle:] = a_high[rows, :] * inverse_a + b_high[rows, :] * inverse_b
        copy = pltpu.make_async_copy(out_ref.at[held, :], out_hbm.at[rows, :], sems.at[n])
        copy.start()
        copies.append(copy)
    for copy in copies:
        copy.wait()


def first_scale_kernel(sums_b_ref, sums_a_ref, a_ref, b_low, b_high, _, out_hbm, out_ref, sems):
    inverse_a = inverse_norm(jnp.sum(sums_a_ref[...], axis=0)).T[:, 0:1]
    inverse_b = inverse_norm(jnp.sum(sums_b_ref[:, :, :WINDOW], axis=0)).T[:, 1:2]
    middle = b_low.shape[1]
    copies = []
    for n in range(sems.shape[0]):
        rows = slice(n * WINDOW // sems.shape[0], (n + 1) * WINDOW // sems.shape[0])
        scale_a, scale_b = inverse_a[rows], inverse_b[rows]
        out_ref[rows, :middle] = a_ref[rows, :middle] * scale_a + b_low[rows, :] * scale_b
        out_ref[rows, middle:] = a_ref[rows, middle:] * scale_a + b_high[rows, :] * scale_b
        copy = pltpu.make_async_copy(out_ref.at[rows, :], out_hbm.at[rows, :], sems.at[n])
        copy.start()
        copies.append(copy)
    for copy in copies:
        copy.wait()


def swap(block, axis, bit):
    return lax.ppermute(block, axis, [(i, i ^ bit) for i in range(lax.axis_size(axis))])


def chip_totals(keep, send):
    beside = swap(send, "ctx", 1)
    return beside, keep + beside


def first_phase(chip):
    return lax.ppermute(chip, "ctx", [(i, i ^ (2 if i % 2 == 0 else 4)) for i in range(8)])


def second_phase(message):
    return lax.ppermute(message, "ctx", [(i, i ^ (4 if i % 2 == 0 else 2)) for i in range(8)])


def doubled_prefix(chip):
    index = lax.axis_index("ctx")
    earlier = jnp.zeros_like(chip)
    running = chip
    bit = 2
    while bit < lax.axis_size("ctx"):
        partner = swap(running, "ctx", bit)
        earlier = earlier + jnp.where((index & bit) != 0, partner, 0.0)
        running = running + partner
        bit *= 2
    return earlier


def shards(queries, keys, values, head_gain):
    rows, width = queries.shape
    heads = head_gain.shape[1]
    parts = lax.axis_size("head")
    queries, keys, values = (
        pltpu.with_memory_space_constraint(x, pltpu.HBM) for x in (queries, keys, values)
    )
    smem = pl.BlockSpec(memory_space=pltpu.SMEM)
    anywhere = pl.BlockSpec(memory_space=pl.ANY)
    vmem = pl.BlockSpec()

    def array(*shape, dtype=F32):
        return jax.ShapeDtypeStruct(shape, dtype)

    def call(kernel, name, flops, moved, **kwargs):
        return pl.pallas_call(
            kernel,
            name=name,
            compiler_params=pltpu.CompilerParams(vmem_limit_bytes=VMEM_BYTES),
            cost_estimate=pl.CostEstimate(flops=flops, bytes_accessed=moved, transcendentals=0),
            **kwargs,
        )

    size = rows * width * 4
    unit = 2 * rows * width * HD
    packed = array(heads // 2, HD, HD)
    first_tile = array(WINDOW, width)
    dma = pltpu.SemaphoreType.DMA
    tail_k, tail_v = call(
        tails_kernel,
        "tails",
        0,
        size,
        in_specs=[anywhere, anywhere],
        out_shape=[first_tile, first_tile],
        scratch_shapes=[dma((2,))],
    )(keys, values)
    route = [(i, i + 1) for i in range(lax.axis_size("ctx") - 1)]
    before_k = lax.ppermute(tail_k, "ctx", route)

    keep, send, half, held_k, held_v = call(
        totals_kernel,
        "totals",
        4 * unit,
        2 * size,
        in_specs=[anywhere, anywhere],
        out_shape=[packed, packed, array(heads, HD, HD), array(rows, width), array(rows, width)],
        scratch_shapes=[dma((2, heads // GROUP))],
    )(keys, values)
    beside, chip = chip_totals(keep, send)

    def local(begin, count, *after):
        taken = count * HD
        return call(
            functools.partial(local_kernel, begin),
            "local",
            count * unit,
            4 * size * count // heads,
            in_specs=[smem, anywhere, vmem, vmem] + [anywhere] * len(after),
            out_shape=[
                array(rows, taken),
                array(rows, taken),
                array(rows, 2 * taken, dtype=BF16),
                array(8, rows),
            ],
            scratch_shapes=[
                pltpu.VMEM((rows, taken), F32),
                pltpu.VMEM((rows, HD), F32),
                dma((count // GROUP,)),
            ],
        )(head_gain, queries, held_k, held_v, *after)

    low_heads = heads // 8 * 4
    window_low, linear_low, qq_low, sum_low = local(0, low_heads, before_k)
    window_high, linear_high, qq_high, sum_high = local(low_heads, heads - low_heads)
    first_weights, first_now = call(
        first_weights_kernel,
        "first_weights",
        4 * unit,
        size,
        in_specs=[smem] + [vmem] * 5,
        out_shape=[array(WINDOW, 2 * width, dtype=BF16), first_tile],
    )(head_gain, qq_low, qq_high, held_k, held_v, before_k)

    if lax.axis_size("ctx") == 8:
        first = first_phase(chip)
        message, tail_v = call(
            message_kernel,
            "message",
            0,
            size // 4,
            in_specs=[vmem, vmem, anywhere, anywhere],
            out_specs=[vmem, anywhere],
            out_shape=[packed, first_tile],
            input_output_aliases={3: 1},
        )(first, chip, sum_low, tail_v)
        second = second_phase(message)
        mine, other = call(
            prefix_kernel,
            "prefix",
            0,
            size // 2,
            in_specs=[vmem] * 4 + [anywhere],
            out_shape=[packed, packed],
        )(first, second, keep, beside, first_now)
    else:
        earlier = doubled_prefix(chip)
        core = lax.axis_index("ctx") % 2
        mine = earlier + jnp.where(core == 1, beside, 0.0)
        other = earlier + jnp.where(core == 0, keep, 0.0)
    before_v = lax.ppermute(tail_v, "ctx", route)
    other = swap(other, "ctx", 1)

    linear_low, linear_high, sums = call(
        earlier_kernel,
        "earlier",
        3 * unit,
        3 * size,
        in_specs=[smem] + [vmem] * 9,
        out_shape=[array(*linear_low.shape), array(*linear_high.shape), array(parts, 8, rows)],
        scratch_shapes=[pltpu.VMEM((rows, HD), F32)],
    )(head_gain, qq_low, linear_low, qq_high, linear_high, half, mine, other, sum_low, sum_high)
    sums = lax.all_to_all(sums, "head", 0, 0)

    out, written = call(
        scale_kernel,
        "scale",
        unit // 64,
        2 * size,
        out_specs=[anywhere, vmem],
        out_shape=[array(rows, width), array(8, 8)],
        scratch_shapes=[pltpu.VMEM((rows - WINDOW, width), F32), dma((rows // WINDOW - 1,))],
    )(sums, window_low, window_high, linear_low, linear_high)

    first_a, first_sums = call(
        first_values_kernel,
        "first_values",
        unit,
        size // 2,
        in_specs=[vmem] * 3 + [anywhere],
        out_shape=[first_tile, array(parts, 8, WINDOW)],
    )(first_weights, first_now, before_v, written)
    first_sums = lax.all_to_all(first_sums, "head", 0, 0)
    return call(
        first_scale_kernel,
        "first_scale",
        unit // 256,
        size // 2,
        in_specs=[vmem] * 5 + [anywhere],
        out_specs=anywhere,
        out_shape=array(rows, width),
        scratch_shapes=[pltpu.VMEM((WINDOW, width), F32), dma((4,))],
        input_output_aliases={5: 0},
    )(sums, first_sums, first_a, linear_low, linear_high, out)


def solution(mesh):
    in_specs = (P("ctx", "head"), P("ctx", "head"), P("ctx", "head"), P(None, "head"))
    out_specs = P("ctx", "head")
    return jax.shard_map(shards, mesh=mesh, in_specs=in_specs, out_specs=out_specs, check_vma=False)
```

time: 72 us -> 76.9 us (1.068)
  blocking collectives: 0 us -> 18.4 us
  starting transfers between devices: 14.8 us -> 5.99 us
  Pallas kernels: 30.3 us -> 28 us
  local copies, waits for them, and re-layouts: 1.32 us -> 0.01 us
  waiting for transfers between devices: 24.5 us -> 23.5 us
    all_to_all x0 -> x2, blocking collectives: none -> 18.4 us  [the longest x1 10.4 us: shards(): sums = lax.all_to_all(sums, 'head', 0, 0)]
    ppermute x8 -> x2, starting transfers between devices: 10.5 us -> 1.75 us  [swap(): lax.ppermute(block, axis, [(i, i ^ bit) for i in range(lax.axis_size(axis...]
    pallas_call x10 -> x11, Pallas kernels: 30.3 us -> 28 us  [the longest x2 11.5 us: local(): call(functools.partial(local_kernel, begin), 'local', count * unit, 4 * s...]
    ppermute x1, waiting for transfers between devices: 9.05 us -> 11.2 us  [shards(): before_k = lax.ppermute(tail_k, 'ctx', route)]
    ppermute x1, waiting for transfers between devices: 10.8 us -> 8.81 us  [second_phase(): lax.ppermute(message, 'ctx', [(i, i ^ (4 if i % 2 == 0 else 2)) for i in...]
    slice x1 -> x0, local copies, waits for them, and re-layouts: 1.31 us -> none  [shards(): tail_k = keys[rows - WINDOW:]]
    ppermute x8 -> x2, waiting for transfers between devices: 4.69 us -> 3.43 us  [swap(): lax.ppermute(block, axis, [(i, i ^ bit) for i in range(lax.axis_size(axis...]
  transfers between devices with their start and end apart: 12 -> 6, of which waited for: 5 -> 4; matrix products, arithmetic and copies ran while one was open for 0% -> 0% of each run, Pallas kernels for 41% -> 32%
where the time goes in v3:
time: 76.9 us; the launch traced here: 76.1 us
  Pallas kernels  28 us (36%)
  waiting for transfers between devices  23.5 us (31%)
  blocking collectives  18.4 us (24%)
  starting transfers between devices  5.99 us (8%)
    pallas_call x2, Pallas kernels, local(): call(functools.partial(local_kernel, begin), 'local', count * unit, 4 * s...  11.5 us
    ppermute x1, waiting for transfers between devices, shards(): before_k = lax.ppermute(tail_k, 'ctx', route)  11.2 us
    all_to_all x1, blocking collectives, shards(): sums = lax.all_to_all(sums, 'head', 0, 0)  10.4 us
    ppermute x1, waiting for transfers between devices, second_phase(): lax.ppermute(message, 'ctx', [(i, i ^ (4 if i % 2 == 0 else 2)) for i in...  8.81 us
    all_to_all x1, blocking collectives, shards(): first_sums = lax.all_to_all(first_sums, 'head', 0, 0)  7.96 us
    pallas_call x1, Pallas kernels, shards(): call(totals_kernel, 'totals', 4 * unit, 2 * size, in_specs=[anywhere, any...  4.19 us
    pallas_call x1, Pallas kernels, shards(): call(first_weights_kernel, 'first_weights', 4 * unit, size, in_specs=[sme...  3.92 us
    ppermute x2, waiting for transfers between devices, swap(): lax.ppermute(block, axis, [(i, i ^ bit) for i in range(lax.axis_size(axis...  3.43 us
  transfers between devices with their start and end apart: 6, of which 4 were waited for; matrix products, arithmetic and copies ran while one was open for 0% of the time, Pallas kernels for 32%

profile of v3, /device:TPU:4, one launch (start us, length us, event | category | flops | bytes accessed | tf_op | source)
XLA Modules:
  0.0 76.1 jit_solution(14507065511059440026)
XLA Ops:
  0.0 1.6 %tails.1 = (f32[128,2048]{1,0:T(8,128)S(1)}, f32[128,2048]{1,0:T(8,128)S(1)}) custom-call(f32[512,2048]{1,0:T(8,128)} %k_ref.1, f32[512,2048]{1,0:T(8,128)} %v_ref.1), custom_call_target="tpu_custom_call" | custom-call | bytes 4194304 | tf_op jit(solution)/shard_map/tails/pallas_call | solution.py:403
  1.6 1.9 %collective-permute-start = (f32[128,2048]{1,0:T(8,128)S(1)}, f32[128,2048]{1,0:T(8,128)S(1)}, u32[]{:S(2)}, u32[]{:S(2)}) collective-permute-start(f32[128,2048]{1,0:T(8,128)S(1)} %get-tuple-element.35), channel_id=1, source_target_pairs={{0,4},{4,8},{8,12},{12,16},{16,20},{20,24},{24,28},{1,5},{5,9},{9,... | collective-permute-start | bytes 3145736 | tf_op jit(solution)/shard_map/ppermute | solution.py:413
  3.5 4.2 %totals.1 = (f32[8,128,128]{2,1,0:T(8,128)S(1)}, f32[8,128,128]{2,1,0:T(8,128)S(1)}, f32[16,128,128]{2,1,0:T(8,128)S(1)}, f32[512,2048]{1,0:T(8,128)S(1)}, f32[512,2048]{1,0:T(8,128)S(1)}) custom-call(f32[512,2048]{1,0:T(8,128)} %k_ref.1, f32[512,2048]{1,0:T(8,128)} %v_ref.1), custom_call_target="tpu_custom_call" | custom-call | flops 1073741824 | bytes 8388608 | tf_op jit(solution)/shard_map/totals/pallas_call | solution.py:415
  7.7 1.7 %collective-permute-start.1 = (f32[8,128,128]{2,1,0:T(8,128)S(1)}, f32[8,128,128]{2,1,0:T(8,128)S(1)}, u32[]{:S(2)}, u32[]{:S(2)}) collective-permute-start(f32[8,128,128]{2,1,0:T(8,128)S(1)} %get-tuple-element.42), channel_id=1, source_target_pairs={{0,4},{4,0},{8,12},{12,8},{16,20},{20,16},{24,28},{28,24},{1,5},{5... | collective-permute-start | bytes 1572872 | tf_op jit(solution)/shard_map/ppermute | solution.py:346
  9.4 1.5 %collective-permute-done.1.beside_ref = f32[8,128,128]{2,1,0:T(8,128)S(1)} collective-permute-done((f32[8,128,128]{2,1,0:T(8,128)S(1)}, f32[8,128,128]{2,1,0:T(8,128)S(1)}, u32[]{:S(2)}, u32[]{:S(2)}) %collective-permute-start.1) | collective-permute-done | bytes 524320 | tf_op jit(solution)/shard_map/ppermute | solution.py:346
  10.9 0.1 add.3.chip_ref
  11.0 0.3 collective-permute-start.2
  11.3 11.2 %collective-permute-done.refs_0_.tail_k_ref = f32[128,2048]{1,0:T(8,128)S(1)} collective-permute-done((f32[128,2048]{1,0:T(8,128)S(1)}, f32[128,2048]{1,0:T(8,128)S(1)}, u32[]{:S(2)}, u32[]{:S(2)}) %collective-permute-start) | collective-permute-done | bytes 1048608 | tf_op jit(solution)/shard_map/ppermute | solution.py:413
  22.6 5.7 %local.2 = (f32[512,1024]{1,0:T(8,128)S(1)}, f32[512,1024]{1,0:T(8,128)S(1)}, bf16[512,2048]{1,0:T(8,128)(2,1)S(1)}, f32[8,512]{1,0:T(8,128)S(1)}) custom-call(f32[2,16]{1,0:T(2,128)S(1)} %copy-done, f32[512,2048]{1,0:T(8,128)} %q_hbm.3, f32[512,2048]{1,0:T(8,128)S(1)} %get-tuple-element.33.k_ref, f32[512,2048]{1,0:T(8,128)S(1)} %get-tuple-element.34.v_ref, ...), custom_call_target="tpu_custom_call" | custom-call | flops 2147483648 | bytes 8388608 | tf_op jit(solution)/shard_map/local/pallas_call | solution.py:428
  28.3 0.1 message.1
  28.4 0.1 collective-permute-start.3
  28.5 1.9 %collective-permute-start.5 = (f32[128,2048]{1,0:T(8,128)S(1)}, f32[128,2048]{1,0:T(8,128)S(1)}, u32[]{:S(2)}, u32[]{:S(2)}) collective-permute-start(f32[128,2048]{1,0:T(8,128)S(1)} %get-tuple-element.52), channel_id=1, source_target_pairs={{0,4},{4,8},{8,12},{12,16},{16,20},{20,24},{24,28},{1,5},{5,9},{9,... | collective-permute-start | bytes 3145736 | tf_op jit(solution)/shard_map/ppermute | solution.py:485
  30.4 5.7 %local.3 = (f32[512,1024]{1,0:T(8,128)S(1)}, f32[512,1024]{1,0:T(8,128)S(1)}, bf16[512,2048]{1,0:T(8,128)(2,1)S(1)}, f32[8,512]{1,0:T(8,128)S(1)}) custom-call(f32[2,16]{1,0:T(2,128)S(1)} %copy-done, f32[512,2048]{1,0:T(8,128)} %q_hbm.3, f32[512,2048]{1,0:T(8,128)S(1)} %get-tuple-element.33.k_ref, f32[512,2048]{1,0:T(8,128)S(1)} %get-tuple-element.34.v_ref), custom_call_target="tpu_custom_call" | custom-call | flops 2147483648 | bytes 8388608 | tf_op jit(solution)/shard_map/local/pallas_call | solution.py:428
  36.2 3.9 %first_weights.1 = (bf16[128,4096]{1,0:T(8,128)(2,1)S(1)}, f32[128,2048]{1,0:T(8,128)S(1)}) custom-call(f32[2,16]{1,0:T(2,128)S(1)} %copy-done, bf16[512,2048]{1,0:T(8,128)(2,1)S(1)} %get-tuple-element.36.qq_low_ref.refs_0_, bf16[512,2048]{1,0:T(8,128)(2,1)S(1)} %get-tuple-element.38.qq_high_ref.refs_2_, f32[512,2048]{1,0:T(8,128)S(1)} %get-tuple-element.33.k_ref, ...), custom_call_target="tpu_custom_call" | custom-call | flops 1073741824 | bytes 4194304 | tf_op jit(solution)/shard_map/first_weights/pallas_call | solution.py:450
  40.1 8.8 %collective-permute-done.3.second_ref = f32[8,128,128]{2,1,0:T(8,128)S(1)} collective-permute-done((f32[8,128,128]{2,1,0:T(8,128)S(1)}, f32[8,128,128]{2,1,0:T(8,128)S(1)}, u32[]{:S(2)}, u32[]{:S(2)}) %collective-permute-start.3) | collective-permute-done | bytes 524320 | tf_op jit(solution)/shard_map/ppermute | solution.py:359
  48.9 0.2 prefix.1
  49.1 0.1 collective-permute-start.4
  49.2 1.9 %collective-permute-done.4.refs_6_ = f32[8,128,128]{2,1,0:T(8,128)S(1)} collective-permute-done((f32[8,128,128]{2,1,0:T(8,128)S(1)}, f32[8,128,128]{2,1,0:T(8,128)S(1)}, u32[]{:S(2)}, u32[]{:S(2)}) %collective-permute-start.4) | collective-permute-done | bytes 524320 | tf_op jit(solution)/shard_map/ppermute | solution.py:346
  51.1 2.3 %earlier.1 = (f32[512,1024]{1,0:T(8,128)S(1)}, f32[512,1024]{1,0:T(8,128)S(1)}, f32[4,8,512]{2,1,0:T(8,128)S(1)}) custom-call(f32[2,16]{1,0:T(2,128)S(1)} %copy-done, bf16[512,2048]{1,0:T(8,128)(2,1)S(1)} %get-tuple-element.36.qq_low_ref.refs_0_, f32[512,1024]{1,0:T(8,128)S(1)} %get-tuple-element.37.refs_1_, ...), custom_call_target="tpu_custom_call" | custom-call | flops 805306368 | bytes 12582912 | tf_op jit(solution)/shard_map/earlier/pallas_call | solution.py:488
  53.4 10.4 %all_to_all.10.sums_ref.sums_b_ref = f32[4,8,512]{2,1,0:T(8,128)S(1)} all-to-all(f32[4,8,512]{2,1,0:T(8,128)S(1)} %get-tuple-element.50), channel_id=1, replica_groups=mesh['ctx'=8,'head'=4] {'head'}, dimensions={0} | all-to-all | bytes 131072 | tf_op jit(solution)/shard_map/all_to_all | solution.py:497
  63.8 2.2 %scale.1 = (f32[512,2048]{1,0:T(8,128)}, f32[8,8]{1,0:T(8,128)S(1)}) custom-call(f32[4,8,512]{2,1,0:T(8,128)S(1)} %all_to_all.10.sums_ref.sums_b_ref, f32[512,1024]{1,0:T(8,128)S(1)} %get-tuple-element.53.a_low, f32[512,1024]{1,0:T(8,128)S(1)} %get-tuple-element.54.a_high, f32[512,1024]{1,0:T(8,128)S(1)} %get-tuple-element.55.b_low, ...), custom_call_target="tpu_custom_call" | custom-call | flops 4194304 | bytes 8388608 | tf_op jit(solution)/shard_map/scale/pallas_call | solution.py:499
  66.1 0.8 %first_values.1 = (f32[128,2048]{1,0:T(8,128)S(1)}, f32[4,8,128]{2,1,0:T(8,128)S(1)}) custom-call(bf16[128,4096]{1,0:T(8,128)(2,1)S(1)} %get-tuple-element.51.weights_ref, f32[128,2048]{1,0:T(8,128)S(1)} %get-tuple-element.46.refs_0_.now_ref, f32[128,2048]{1,0:T(8,128)S(1)} %collective-permute-done.5.tail_v_ref, f32[8,8]{1,0:T(8,128)S(1)} %get-tuple-element.57._), custom_call_target="tpu_custom_call" | custom-call | flops 268435456 | bytes 2097152 | tf_op jit(solution)/shard_map/first_values/pallas_call | solution.py:509
  66.9 8.0 %all_to_all.11.sums_a_ref = f32[4,8,128]{2,1,0:T(8,128)S(1)} all-to-all(f32[4,8,128]{2,1,0:T(8,128)S(1)} %get-tuple-element.58), channel_id=1, replica_groups=mesh['ctx'=8,'head'=4] {'head'}, dimensions={0} | all-to-all | bytes 32768 | tf_op jit(solution)/shard_map/all_to_all | solution.py:517
  74.8 1.2 %first_scale.1 = f32[512,2048]{1,0:T(8,128)} custom-call(f32[4,8,512]{2,1,0:T(8,128)S(1)} %all_to_all.10.sums_ref.sums_b_ref, f32[4,8,128]{2,1,0:T(8,128)S(1)} %all_to_all.11.sums_a_ref, f32[128,2048]{1,0:T(8,128)S(1)} %get-tuple-element.59.a_ref, f32[512,1024]{1,0:T(8,128)S(1)} %get-tuple-element.55.b_low, ...), custom_call_target="tpu_custom_call", output_to_operand_aliasing={{}: (5, {})} | custom-call | flops 1048576 | bytes 2097152 | tf_op jit(solution)/shard_map/first_scale/pallas_call | solution.py:518
  (4 shorter events, 0.0 us)
Async XLA Ops:
  1.6 21.0 %copy-start = (f32[2,16]{1,0:T(2,128)S(1)}, f32[2,16]{1,0:T(2,128)}, u32[]{:S(2)}) copy-start(f32[2,16]{1,0:T(2,128)} %gain_ref.7) | copy-start | bytes 388
  1.6 21.0 %collective-permute-start = (f32[128,2048]{1,0:T(8,128)S(1)}, f32[128,2048]{1,0:T(8,128)S(1)}, u32[]{:S(2)}, u32[]{:S(2)}) collective-permute-start(f32[128,2048]{1,0:T(8,128)S(1)} %get-tuple-element.35), channel_id=1, source_target_pairs={{0,4},{4,8},{8,12},{12,16},{16,20},{20,24},{24,28},{1,5},{5,9},{9,... | collective-permute-start | bytes 3145736 | tf_op jit(solution)/shard_map/ppermute | solution.py:413
  7.7 3.2 %collective-permute-start.1 = (f32[8,128,128]{2,1,0:T(8,128)S(1)}, f32[8,128,128]{2,1,0:T(8,128)S(1)}, u32[]{:S(2)}, u32[]{:S(2)}) collective-permute-start(f32[8,128,128]{2,1,0:T(8,128)S(1)} %get-tuple-element.42), channel_id=1, source_target_pairs={{0,4},{4,0},{8,12},{12,8},{16,20},{20,16},{24,28},{28,24},{1,5},{5... | collective-permute-start | bytes 1572872 | tf_op jit(solution)/shard_map/ppermute | solution.py:346
  11.0 17.3 %collective-permute-start.2 = (f32[8,128,128]{2,1,0:T(8,128)S(1)}, f32[8,128,128]{2,1,0:T(8,128)S(1)}, u32[]{:S(2)}, u32[]{:S(2)}) collective-permute-start(f32[8,128,128]{2,1,0:T(8,128)S(1)} %add.3.chip_ref), channel_id=1, source_target_pairs={{0,8},{4,20},{8,0},{12,28},{16,24},{20,4},{24,16},{28,12},{1,9},{5... | collective-permute-start | bytes 1572872 | tf_op jit(solution)/shard_map/ppermute | solution.py:355
  28.4 20.5 %collective-permute-start.3 = (f32[8,128,128]{2,1,0:T(8,128)S(1)}, f32[8,128,128]{2,1,0:T(8,128)S(1)}, u32[]{:S(2)}, u32[]{:S(2)}) collective-permute-start(f32[8,128,128]{2,1,0:T(8,128)S(1)} %get-tuple-element.45), channel_id=1, source_target_pairs={{0,16},{4,12},{8,24},{12,4},{16,0},{20,28},{24,8},{28,20},{1,17},{... | collective-permute-start | bytes 1572872 | tf_op jit(solution)/shard_map/ppermute | solution.py:359
  28.5 37.5 %collective-permute-start.5 = (f32[128,2048]{1,0:T(8,128)S(1)}, f32[128,2048]{1,0:T(8,128)S(1)}, u32[]{:S(2)}, u32[]{:S(2)}) collective-permute-start(f32[128,2048]{1,0:T(8,128)S(1)} %get-tuple-element.52), channel_id=1, source_target_pairs={{0,4},{4,8},{8,12},{12,16},{16,20},{20,24},{24,28},{1,5},{5,9},{9,... | collective-permute-start | bytes 3145736 | tf_op jit(solution)/shard_map/ppermute | solution.py:485
  49.1 2.0 %collective-permute-start.4 = (f32[8,128,128]{2,1,0:T(8,128)S(1)}, f32[8,128,128]{2,1,0:T(8,128)S(1)}, u32[]{:S(2)}, u32[]{:S(2)}) collective-permute-start(f32[8,128,128]{2,1,0:T(8,128)S(1)} %get-tuple-element.48), channel_id=1, source_target_pairs={{0,4},{4,0},{8,12},{12,8},{16,20},{20,16},{24,28},{28,24},{1,5},{5... | collective-permute-start | bytes 1572872 | tf_op jit(solution)/shard_map/ppermute | solution.py:346

commit v4 on v3

--- a/solution.py
+++ b/solution.py
@@ -80,19 +80,14 @@
     return pl.ds(pl.multiple_of(head * width, width), count * width)
 
 
-def tails_kernel(k_ref, v_ref, tail_k_ref, tail_v_ref, sems):
+def tail_kernel(k_ref, tail_ref, sem):
     rows = k_ref.shape[0]
-    copies = [
-        pltpu.make_async_copy(source.at[pl.ds(rows - WINDOW, WINDOW), :], target, sems.at[i])
-        for i, (source, target) in enumerate(((k_ref, tail_k_ref), (v_ref, tail_v_ref)))
-    ]
-    for copy in copies:
-        copy.start()
-    for copy in copies:
-        copy.wait()
-
-
-def totals_kernel(k_hbm, v_hbm, keep_ref, send_ref, half_ref, k_ref, v_ref, sems):
+    copy = pltpu.make_async_copy(k_ref.at[pl.ds(rows - WINDOW, WINDOW), :], tail_ref, sem)
+    copy.start()
+    copy.wait()
+
+
+def totals_kernel(k_hbm, v_hbm, keep_ref, send_ref, half_ref, k_ref, v_ref, tail_v_ref, sems):
     core = lax.axis_index("ctx") % 2
     rows, width = k_ref.shape
     middle = rows // 2
@@ -127,6 +122,8 @@
             pair = GROUP // 2 * group + i
             keep_ref[pair] = jnp.where(core == 0, states[0], states[1])
             send_ref[pair] = jnp.where(core == 0, states[1], states[0])
+        columns = head_columns(group, 1, GROUP * HD)
+        tail_v_ref[:, columns] = v_ref[rows - WINDOW :, columns]
 
 
 def weights_of(scores):
@@ -140,8 +137,9 @@
     return side(high * above, high * below), side(low * above, low * below)
 
 
-def local_kernel(begin, gain_ref, q_hbm, k_ref, v_ref, *refs):
-    a_ref, b_ref, qq_ref, sum_ref, q_ref, square_ref, sems = refs[-7:]
+def local_kernel(begin, extra, gain_ref, q_hbm, k_ref, v_ref, *refs):
+    a_ref, b_ref, qq_ref, sum_ref = refs[extra : extra + 4]
+    q_ref, square_ref, sems = refs[-3:]
     lower = lower_mask()
     below = jnp.where(lower, 1.0, 0.0).astype(BF16)
     above = jnp.where(lower, 0.0, 1.0).astype(BF16)
@@ -208,8 +206,7 @@
     sum_ref[...] = row_sums(square_ref[...])
 
 
-def message_kernel(first_ref, chip_ref, *refs):
-    out_ref = refs[-2]
+def message_kernel(first_ref, chip_ref, _, out_ref):
     index = lax.axis_index("ctx")
     core, x, y = index % 2, (index >> 1) % 2, index >> 2
     first = jnp.where((core == 0) | (y == 1), first_ref[...], 0.0)
@@ -227,19 +224,16 @@
     other_ref[...] = earlier + jnp.where(core == 0, keep_ref[...], 0.0)
 
 
-def earlier_kernel(gain_ref, *refs):
-    parts, (half_ref, mine_ref, other_ref, sum_low_ref, sum_high_ref), outs = refs[:4], refs[4:9], refs[9:]
-    sums_ref, square_ref = outs[2:]
+def earlier_kernel(count, gain_ref, half_ref, mine_ref, other_ref, *refs):
+    qq_refs, b_refs, sum_refs, out_refs = (refs[i * count : (i + 1) * count] for i in range(4))
+    sums_ref, square_ref = refs[4 * count :]
     core = lax.axis_index("ctx") % 2
-    rows = parts[1].shape[0]
+    rows = b_refs[0].shape[0]
     middle = rows // 2
-    begin = 0
+    head = 0
     square_ref[...] = jnp.zeros_like(square_ref)
-    for side_number in range(2):
-        qq_ref, b_ref = parts[2 * side_number : 2 * side_number + 2]
-        out_ref = outs[side_number]
+    for qq_ref, b_ref, out_ref in zip(qq_refs, b_refs, out_refs):
         for j in range(b_ref.shape[1] // HD):
-            head = begin + j
             columns = slice(j * HD, (j + 1) * HD)
             state = jnp.where(core == head % 2, mine_ref[head // 2], other_ref[head // 2])
             gain_b = gain_ref[1, head]
@@ -248,20 +242,19 @@
                 b = gain_b * (b_ref[part, columns] + folded(dot(qq, wide_state(held))))
                 out_ref[part, columns] = b
                 square_ref[part, :] += b * b
-        begin += b_ref.shape[1] // HD
-    own = row_sums(square_ref[...])
-    row = lax.broadcasted_iota(jnp.int32, own.shape, 0)
-    own = jnp.where(row == 0, sum_low_ref[...] + sum_high_ref[...], own)
-    for i in range(sums_ref.shape[0]):
-        sums_ref[i] = own
-
-
-def first_weights_kernel(gain_ref, qq_low_ref, qq_high_ref, k_ref, v_ref, tail_k_ref, weights_ref, out_ref):
+            head += 1
+    sums = row_sums(square_ref[...])
+    row = lax.broadcasted_iota(jnp.int32, sums.shape, 0)
+    sums_ref[...] = jnp.where(row == 0, sum(ref[...] for ref in sum_refs), sums)
+
+
+def first_weights_kernel(gain_ref, k_ref, v_ref, tail_k_ref, *refs):
+    qq_refs, (weights_ref, out_ref) = refs[:-2], refs[-2:]
     lower = lower_mask()
     reachable = jnp.logical_or(lower, lax.axis_index("ctx") > 0)
     top = slice(0, WINDOW)
     begin = 0
-    for qq_ref in (qq_low_ref, qq_high_ref):
+    for qq_ref in qq_refs:
         count = qq_ref.shape[1] // (2 * HD)
 
         @pl.loop(0, count // GROUP)
@@ -288,7 +281,7 @@
         begin += count
 
 
-def first_values_kernel(weights_ref, now_ref, tail_v_ref, _, a_ref, sums_ref):
+def first_values_kernel(weights_ref, now_ref, tail_v_ref, sums_ref, a_ref, out_ref):
     square = jnp.zeros((WINDOW, HD), F32)
     for j in range(now_ref.shape[1] // HD):
         columns = slice(j * HD, (j + 1) * HD)
@@ -299,47 +292,40 @@
         a_ref[:, columns] = a
         square = square + a * a
     own = row_sums(square)
-    for i in range(sums_ref.shape[0]):
-        sums_ref[i] = own
+    row = lax.broadcasted_iota(jnp.int32, own.shape, 0)
+    out_ref[:, :WINDOW] = jnp.where(row == 0, own, sums_ref[:, :WINDOW])
+    out_ref[:, WINDOW:] = sums_ref[:, WINDOW:]
 
 
 def inverse_norm(total):
     return 1.0 / jnp.sqrt(total / (HEADS * HD) + EPS)
 
 
-def scale_kernel(sums_ref, a_low, a_high, b_low, b_high, out_hbm, written_ref, out_ref, sems):
-    inverse = inverse_norm(jnp.sum(sums_ref[...], axis=0)).T
-    middle = a_low.shape[1]
-    written_ref[...] = inverse[:8]
+def scale_kernel(count, sums, first_ref, *refs):
+    a_refs, b_refs, (out_hbm, out_ref, sems) = refs[:count], refs[count : 2 * count], refs[2 * count :]
+    total = sums[0][...]
+    for part in sums[1:]:
+        total = total + part[...]
+    inverse = inverse_norm(total).T
     copies = []
     for n in range(out_ref.shape[0] // WINDOW):
-        held = slice(n * WINDOW, (n + 1) * WINDOW)
-        rows = slice((n + 1) * WINDOW, (n + 2) * WINDOW)
+        rows = slice(n * WINDOW, (n + 1) * WINDOW)
         inverse_a, inverse_b = inverse[rows, 0:1], inverse[rows, 1:2]
-        out_ref[held, :middle] = a_low[rows, :] * inverse_a + b_low[rows, :] * inverse_b
-        out_ref[held, middle:] = a_high[rows, :] * inverse_a + b_high[rows, :] * inverse_b
-        copy = pltpu.make_async_copy(out_ref.at[held, :], out_hbm.at[rows, :], sems.at[n])
-        copy.start()
-        copies.append(copy)
-    for copy in copies:
-        copy.wait()
-
-
-def first_scale_kernel(sums_b_ref, sums_a_ref, a_ref, b_low, b_high, _, out_hbm, out_ref, sems):
-    inverse_a = inverse_norm(jnp.sum(sums_a_ref[...], axis=0)).T[:, 0:1]
-    inverse_b = inverse_norm(jnp.sum(sums_b_ref[:, :, :WINDOW], axis=0)).T[:, 1:2]
-    middle = b_low.shape[1]
-    copies = []
-    for n in range(sems.shape[0]):
-        rows = slice(n * WINDOW // sems.shape[0], (n + 1) * WINDOW // sems.shape[0])
-        scale_a, scale_b = inverse_a[rows], inverse_b[rows]
-        out_ref[rows, :middle] = a_ref[rows, :middle] * scale_a + b_low[rows, :] * scale_b
-        out_ref[rows, middle:] = a_ref[rows, middle:] * scale_a + b_high[rows, :] * scale_b
+        begin = 0
+        for a_ref, b_ref in zip(a_refs, b_refs):
+            columns = slice(begin, begin + a_ref.shape[1])
+            a = a_ref[rows, :] if n else first_ref[:, columns]
+            out_ref[rows, columns] = a * inverse_a + b_ref[rows, :] * inverse_b
+            begin = columns.stop
         copy = pltpu.make_async_copy(out_ref.at[rows, :], out_hbm.at[rows, :], sems.at[n])
         copy.start()
         copies.append(copy)
     for copy in copies:
         copy.wait()
+
+
+def scale_first(parts, count, *refs):
+    scale_kernel(count, refs[:parts], *refs[parts:])
 
 
 def swap(block, axis, bit):
@@ -375,7 +361,6 @@
 def shards(queries, keys, values, head_gain):
     rows, width = queries.shape
     heads = head_gain.shape[1]
-    parts = lax.axis_size("head")
     queries, keys, values = (
         pltpu.with_memory_space_constraint(x, pltpu.HBM) for x in (queries, keys, values)
     )
@@ -400,25 +385,25 @@
     packed = array(heads // 2, HD, HD)
     first_tile = array(WINDOW, width)
     dma = pltpu.SemaphoreType.DMA
-    tail_k, tail_v = call(
-        tails_kernel,
-        "tails",
+    tail_k = call(
+        tail_kernel,
+        "tail",
         0,
-        size,
-        in_specs=[anywhere, anywhere],
-        out_shape=[first_tile, first_tile],
-        scratch_shapes=[dma((2,))],
-    )(keys, values)
+        size // 2,
+        in_specs=[anywhere],
+        out_shape=first_tile,
+        scratch_shapes=[dma],
+    )(keys)
     route = [(i, i + 1) for i in range(lax.axis_size("ctx") - 1)]
     before_k = lax.ppermute(tail_k, "ctx", route)
 
-    keep, send, half, held_k, held_v = call(
+    keep, send, half, held_k, held_v, tail_v = call(
         totals_kernel,
         "totals",
         4 * unit,
         2 * size,
         in_specs=[anywhere, anywhere],
-        out_shape=[packed, packed, array(heads, HD, HD), array(rows, width), array(rows, width)],
+        out_shape=[packed, packed, array(heads, HD, HD), array(rows, width), array(rows, width), first_tile],
         scratch_shapes=[dma((2, heads // GROUP))],
     )(keys, values)
     beside, chip = chip_totals(keep, send)
@@ -426,48 +411,57 @@
     def local(begin, count, *after):
         taken = count * HD
         return call(
-            functools.partial(local_kernel, begin),
+            functools.partial(local_kernel, begin, len(after)),
             "local",
-            count * unit,
-            4 * size * count // heads,
+            0,
+            0,
             in_specs=[smem, anywhere, vmem, vmem] + [anywhere] * len(after),
+            out_specs=[vmem] * 4 + [anywhere] * (len(after) // 2),
             out_shape=[
                 array(rows, taken),
                 array(rows, taken),
                 array(rows, 2 * taken, dtype=BF16),
                 array(8, rows),
-            ],
+            ]
+            + [first_tile] * (len(after) // 2),
             scratch_shapes=[
                 pltpu.VMEM((rows, taken), F32),
                 pltpu.VMEM((rows, HD), F32),
                 dma((count // GROUP,)),
             ],
+            input_output_aliases={5: 4} if after else {},
         )(head_gain, queries, held_k, held_v, *after)
 
-    low_heads = heads // 8 * 4
-    window_low, linear_low, qq_low, sum_low = local(0, low_heads, before_k)
-    window_high, linear_high, qq_high, sum_high = local(low_heads, heads - low_heads)
+    begin = heads // 2
+    parts = [local(0, begin)]
+    *part, before_k = local(begin, GROUP, parts[0][3], before_k)
+    parts.append(part)
+    message = None
+    if lax.axis_size("ctx") == 8:
+        first = first_phase(chip)
+        message = call(
+            message_kernel,
+            "message",
+            0,
+            size // 4,
+            in_specs=[vmem, vmem, anywhere],
+            out_shape=packed,
+        )(first, chip, parts[1][3])
+    after = parts[1][3] if message is None else message
+    for begin in range(begin + GROUP, heads, GROUP):
+        *part, tail_v = local(begin, GROUP, after, tail_v)
+        parts.append(part)
+    window, linear, qq, window_sums = zip(*parts)
     first_weights, first_now = call(
         first_weights_kernel,
         "first_weights",
         4 * unit,
         size,
-        in_specs=[smem] + [vmem] * 5,
+        in_specs=[smem] + [vmem] * (3 + len(qq)),
         out_shape=[array(WINDOW, 2 * width, dtype=BF16), first_tile],
-    )(head_gain, qq_low, qq_high, held_k, held_v, before_k)
-
-    if lax.axis_size("ctx") == 8:
-        first = first_phase(chip)
-        message, tail_v = call(
-            message_kernel,
-            "message",
-            0,
-            size // 4,
-            in_specs=[vmem, vmem, anywhere, anywhere],
-            out_specs=[vmem, anywhere],
-            out_shape=[packed, first_tile],
-            input_output_aliases={3: 1},
-        )(first, chip, sum_low, tail_v)
+    )(head_gain, held_k, held_v, before_k, *qq)
+
+    if message is not None:
         second = second_phase(message)
         mine, other = call(
             prefix_kernel,
@@ -485,47 +479,32 @@
     before_v = lax.ppermute(tail_v, "ctx", route)
     other = swap(other, "ctx", 1)
 
-    linear_low, linear_high, sums = call(
-        earlier_kernel,
+    *linear, sums = call(
+        functools.partial(earlier_kernel, len(parts)),
         "earlier",
         3 * unit,
         3 * size,
-        in_specs=[smem] + [vmem] * 9,
-        out_shape=[array(*linear_low.shape), array(*linear_high.shape), array(parts, 8, rows)],
+        in_specs=[smem] + [vmem] * (3 + 3 * len(parts)),
+        out_shape=[array(*x.shape) for x in linear] + [array(8, rows)],
         scratch_shapes=[pltpu.VMEM((rows, HD), F32)],
-    )(head_gain, qq_low, linear_low, qq_high, linear_high, half, mine, other, sum_low, sum_high)
-    sums = lax.all_to_all(sums, "head", 0, 0)
-
-    out, written = call(
-        scale_kernel,
-        "scale",
-        unit // 64,
-        2 * size,
-        out_specs=[anywhere, vmem],
-        out_shape=[array(rows, width), array(8, 8)],
-        scratch_shapes=[pltpu.VMEM((rows - WINDOW, width), F32), dma((rows // WINDOW - 1,))],
-    )(sums, window_low, window_high, linear_low, linear_high)
-
-    first_a, first_sums = call(
+    )(head_gain, half, mine, other, *qq, *linear, *window_sums)
+    first_a, sums = call(
         first_values_kernel,
         "first_values",
         unit,
         size // 2,
-        in_specs=[vmem] * 3 + [anywhere],
-        out_shape=[first_tile, array(parts, 8, WINDOW)],
-    )(first_weights, first_now, before_v, written)
-    first_sums = lax.all_to_all(first_sums, "head", 0, 0)
+        out_shape=[first_tile, array(8, rows)],
+    )(first_weights, first_now, before_v, sums)
+    all_sums = [sums] + [swap(sums, "head", bits) for bits in range(1, lax.axis_size("head"))]
     return call(
-        first_scale_kernel,
-        "first_scale",
-        unit // 256,
-        size // 2,
-        in_specs=[vmem] * 5 + [anywhere],
+        functools.partial(scale_first, len(all_sums), len(parts)),
+        "scale",
+        unit // 64,
+        2 * size,
         out_specs=anywhere,
         out_shape=array(rows, width),
-        scratch_shapes=[pltpu.VMEM((WINDOW, width), F32), dma((4,))],
-        input_output_aliases={5: 0},
-    )(sums, first_sums, first_a, linear_low, linear_high, out)
+        scratch_shapes=[pltpu.VMEM((rows, width), F32), dma((rows // WINDOW,))],
+    )(*all_sums, first_a, *window, *linear)
 
 
 def solution(mesh):

time: 76.9 us -> 65.3 us (0.85)
  blocking collectives: 18.4 us -> 0 us
  starting transfers between devices: 5.99 us -> 12 us
    all_to_all x2 -> x0, blocking collectives: 18.4 us -> none  [the longest x1 10.4 us: shards(): sums = lax.all_to_all(sums, 'head', 0, 0)]
    ppermute x1, waiting for transfers between devices: 8.81 us -> 0.01 us  [second_phase(): lax.ppermute(message, 'ctx', [(i, i ^ (4 if i % 2 == 0 else 2)) for i in...]
    ppermute x1, waiting for transfers between devices: 0.01 us -> 5.71 us  [shards(): before_v = lax.ppermute(tail_v, 'ctx', route)]
    ppermute x2 -> x5, starting transfers between devices: 1.75 us -> 5.91 us  [swap(): lax.ppermute(block, axis, [(i, i ^ bit) for i in range(lax.axis_size(axis...]
    ppermute x2 -> x5, waiting for transfers between devices: 3.43 us -> 5.58 us  [swap(): lax.ppermute(block, axis, [(i, i ^ bit) for i in range(lax.axis_size(axis...]
    ppermute x1, waiting for transfers between devices: 11.2 us -> 12.7 us  [shards(): before_k = lax.ppermute(tail_k, 'ctx', route)]
    ppermute x1, starting transfers between devices: 0.32 us -> 1.56 us  [first_phase(): lax.ppermute(chip, 'ctx', [(i, i ^ (2 if i % 2 == 0 else 4)) for i in ran...]
  transfers between devices with their start and end apart: 6 -> 9, of which waited for: 4 -> 5; matrix products, arithmetic and copies ran while one was open for 0% -> 0% of each run, Pallas kernels for 32% -> 32%
where the time goes in v4:
time: 65.3 us; the launch traced here: 65 us
  Pallas kernels  28.6 us (44%)
  waiting for transfers between devices  24 us (37%)
  starting transfers between devices  12 us (18%)
    pallas_call x3, Pallas kernels, local(): call(functools.partial(local_kernel, begin, len(after)), 'local', 0, 0, i...  13.3 us
    ppermute x1, waiting for transfers between devices, shards(): before_k = lax.ppermute(tail_k, 'ctx', route)  12.7 us
    ppermute x5, starting transfers between devices, swap(): lax.ppermute(block, axis, [(i, i ^ bit) for i in range(lax.axis_size(axis...  5.91 us
    ppermute x1, waiting for transfers between devices, shards(): before_v = lax.ppermute(tail_v, 'ctx', route)  5.71 us
    ppermute x5, waiting for transfers between devices, swap(): lax.ppermute(block, axis, [(i, i ^ bit) for i in range(lax.axis_size(axis...  5.58 us
    pallas_call x1, Pallas kernels, shards(): call(totals_kernel, 'totals', 4 * unit, 2 * size, in_specs=[anywhere, any...  4.24 us
    pallas_call x1, Pallas kernels, shards(): call(first_weights_kernel, 'first_weights', 4 * unit, size, in_specs=[sme...  3.73 us
    pallas_call x1, Pallas kernels, shards(): call(functools.partial(scale_first, len(all_sums), len(parts)), 'scale',...  2.63 us
  transfers between devices with their start and end apart: 9, of which 5 were waited for; matrix products, arithmetic and copies ran while one was open for 0% of the time, Pallas kernels for 32%

profile of v4, /device:TPU:4, one launch (start us, length us, event | category | flops | bytes accessed | tf_op | source)
XLA Modules:
  0.0 65.0 jit_solution(15213894367792683528)
XLA Ops:
  0.0 4.2 %totals.1 = (f32[8,128,128]{2,1,0:T(8,128)S(1)}, f32[8,128,128]{2,1,0:T(8,128)S(1)}, f32[16,128,128]{2,1,0:T(8,128)S(1)}, f32[512,2048]{1,0:T(8,128)S(1)}, f32[5...) custom-call(f32[512,2048]{1,0:T(8,128)} %k_ref.1, f32[512,2048]{1,0:T(8,128)} %v_hbm.1), custom_call_target="tpu_custom_call" | custom-call | flops 1073741824 | bytes 8388608 | tf_op jit(solution)/shard_map/totals/pallas_call | solution.py:400
  4.3 1.2 %tail.1 = f32[128,2048]{1,0:T(8,128)S(1)} custom-call(f32[512,2048]{1,0:T(8,128)} %k_ref.1), custom_call_target="tpu_custom_call" | custom-call | bytes 2097152 | tf_op jit(solution)/shard_map/tail/pallas_call | solution.py:388
  5.6 2.4 %collective-permute-start = (f32[128,2048]{1,0:T(8,128)S(1)}, f32[128,2048]{1,0:T(8,128)S(1)}, u32[]{:S(2)}, u32[]{:S(2)}) collective-permute-start(f32[128,2048]{1,0:T(8,128)S(1)} %tail.1), channel_id=1, source_target_pairs={{0,4},{4,8},{8,12},{12,16},{16,20},{20,24},{24,28},{1,5},{5,9},{9,... | collective-permute-start | bytes 3145736 | tf_op jit(solution)/shard_map/ppermute | solution.py:398
  8.0 0.1 add.3.chip_ref
  8.1 1.6 %collective-permute-start.2 = (f32[8,128,128]{2,1,0:T(8,128)S(1)}, f32[8,128,128]{2,1,0:T(8,128)S(1)}, u32[]{:S(2)}, u32[]{:S(2)}) collective-permute-start(f32[8,128,128]{2,1,0:T(8,128)S(1)} %add.3.chip_ref), channel_id=1, source_target_pairs={{0,8},{4,20},{8,0},{12,28},{16,24},{20,4},{24,16},{28,12},{1,9},{5... | collective-permute-start | bytes 1572872 | tf_op jit(solution)/shard_map/ppermute | solution.py:341
  9.6 5.7 %local.3 = (f32[512,1024]{1,0:T(8,128)S(1)}, f32[512,1024]{1,0:T(8,128)S(1)}, bf16[512,2048]{1,0:T(8,128)(2,1)S(1)}, f32[8,512]{1,0:T(8,128)S(1)}) custom-call(f32[2,16]{1,0:T(2,128)S(1)} %copy-done, f32[512,2048]{1,0:T(8,128)} %q_hbm.5, f32[512,2048]{1,0:T(8,128)S(1)} %get-tuple-element.35.k_ref, f32[512,2048]{1,0:T(8,128)S(1)} %get-tuple-element.36.v_ref), custom_call_target="tpu_custom_call" | custom-call | tf_op jit(solution)/shard_map/local/pallas_call | solution.py:413
  15.4 12.7 %collective-permute-done.refs_1_ = f32[128,2048]{1,0:T(8,128)S(1)} collective-permute-done((f32[128,2048]{1,0:T(8,128)S(1)}, f32[128,2048]{1,0:T(8,128)S(1)}, u32[]{:S(2)}, u32[]{:S(2)}) %collective-permute-start) | collective-permute-done | bytes 1048608 | tf_op jit(solution)/shard_map/ppermute | solution.py:398
  28.1 3.8 %local.4 = (f32[512,512]{1,0:T(8,128)S(1)}, f32[512,512]{1,0:T(8,128)S(1)}, bf16[512,1024]{1,0:T(8,128)(2,1)S(1)}, f32[8,512]{1,0:T(8,128)S(1)}, f32[128,2048]{1,0:T(8,128)S(1)}) custom-call(f32[2,16]{1,0:T(2,128)S(1)} %copy-done, f32[512,2048]{1,0:T(8,128)} %q_hbm.5, f32[512,2048]{1,0:T(8,128)S(1)} %get-tuple-element.35.k_ref, ...), custom_call_target="tpu_custom_call", output_to_operand_aliasing={{4}: (5, {})} | custom-call | tf_op jit(solution)/shard_map/local/pallas_call | solution.py:413
  31.9 0.1 message.1.refs_0_
  32.0 0.1 collective-permute-start.4
  32.1 3.8 %local.5 = (f32[512,512]{1,0:T(8,128)S(1)}, f32[512,512]{1,0:T(8,128)S(1)}, bf16[512,1024]{1,0:T(8,128)(2,1)S(1)}, f32[8,512]{1,0:T(8,128)S(1)}, f32[128,2048]{1,0:T(8,128)S(1)}) custom-call(f32[2,16]{1,0:T(2,128)S(1)} %copy-done, f32[512,2048]{1,0:T(8,128)} %q_hbm.5, f32[512,2048]{1,0:T(8,128)S(1)} %get-tuple-element.35.k_ref, ...), custom_call_target="tpu_custom_call", output_to_operand_aliasing={{4}: (5, {})} | custom-call | tf_op jit(solution)/shard_map/local/pallas_call | solution.py:413
  35.9 2.1 %collective-permute-start.3 = (f32[128,2048]{1,0:T(8,128)S(1)}, f32[128,2048]{1,0:T(8,128)S(1)}, u32[]{:S(2)}, u32[]{:S(2)}) collective-permute-start(f32[128,2048]{1,0:T(8,128)S(1)} %get-tuple-element.48), channel_id=1, source_target_pairs={{0,4},{4,8},{8,12},{12,16},{16,20},{20,24},{24,28},{1,5},{5,9},{9,... | collective-permute-start | bytes 3145736 | tf_op jit(solution)/shard_map/ppermute | solution.py:479
  38.0 3.7 %first_weights.1 = (bf16[128,4096]{1,0:T(8,128)(2,1)S(1)}, f32[128,2048]{1,0:T(8,128)S(1)}) custom-call(f32[2,16]{1,0:T(2,128)S(1)} %copy-done, f32[512,2048]{1,0:T(8,128)S(1)} %get-tuple-element.35.k_ref, f32[512,2048]{1,0:T(8,128)S(1)} %get-tuple-element.36.v_ref, f32[128,2048]{1,0:T(8,128)S(1)} %get-tuple-element.38.tail_k_ref, ...), custom_call_target="tpu_custom_call" | custom-call | flops 1073741824 | bytes 4194304 | tf_op jit(solution)/shard_map/first_weights/pallas_call | solution.py:455
  41.7 0.2 prefix.1
  42.0 1.4 %collective-permute-start.5 = (f32[8,128,128]{2,1,0:T(8,128)S(1)}, f32[8,128,128]{2,1,0:T(8,128)S(1)}, u32[]{:S(2)}, u32[]{:S(2)}) collective-permute-start(f32[8,128,128]{2,1,0:T(8,128)S(1)} %get-tuple-element.51), channel_id=1, source_target_pairs={{0,4},{4,0},{8,12},{12,8},{16,20},{20,16},{24,28},{28,24},{1,5},{5... | collective-permute-start | bytes 1572872 | tf_op jit(solution)/shard_map/ppermute | solution.py:332
  43.3 1.5 %collective-permute-done.5.other_ref = f32[8,128,128]{2,1,0:T(8,128)S(1)} collective-permute-done((f32[8,128,128]{2,1,0:T(8,128)S(1)}, f32[8,128,128]{2,1,0:T(8,128)S(1)}, u32[]{:S(2)}, u32[]{:S(2)}) %collective-permute-start.5) | collective-permute-done | bytes 524320 | tf_op jit(solution)/shard_map/ppermute | solution.py:332
  44.9 2.3 %earlier.1 = (f32[512,1024]{1,0:T(8,128)S(1)}, f32[512,512]{1,0:T(8,128)S(1)}, f32[512,512]{1,0:T(8,128)S(1)}, f32[8,512]{1,0:T(8,128)S(1)}) custom-call(f32[2,16]{1,0:T(2,128)S(1)} %copy-done, f32[16,128,128]{2,1,0:T(8,128)S(1)} %get-tuple-element.49.half_ref, f32[8,128,128]{2,1,0:T(8,128)S(1)} %get-tuple-element.50.mine_ref, ...), custom_call_target="tpu_custom_call" | custom-call | flops 805306368 | bytes 12582912 | tf_op jit(solution)/shard_map/earlier/pallas_call | solution.py:482
  47.2 5.7 %collective-permute-done.3.tail_v_ref = f32[128,2048]{1,0:T(8,128)S(1)} collective-permute-done((f32[128,2048]{1,0:T(8,128)S(1)}, f32[128,2048]{1,0:T(8,128)S(1)}, u32[]{:S(2)}, u32[]{:S(2)}) %collective-permute-start.3) | collective-permute-done | bytes 1048608 | tf_op jit(solution)/shard_map/ppermute | solution.py:479
  52.9 0.8 %first_values.1 = (f32[128,2048]{1,0:T(8,128)S(1)}, f32[8,512]{1,0:T(8,128)S(1)}) custom-call(bf16[128,4096]{1,0:T(8,128)(2,1)S(1)} %get-tuple-element.46.weights_ref, f32[128,2048]{1,0:T(8,128)S(1)} %get-tuple-element.47.refs_0_.now_ref, f32[128,2048]{1,0:T(8,128)S(1)} %collective-permute-done.3.tail_v_ref, f32[8,512]{1,0:T(8,128)S(1)} %get-tuple-element.56.sums_ref), custom_call_target="tpu_custom_call" | custom-call | flops 268435456 | bytes 2097152 | tf_op jit(solution)/shard_map/first_values/pallas_call | solution.py:491
  53.7 3.9 %collective-permute-start.8 = (f32[8,512]{1,0:T(8,128)S(1)}, f32[8,512]{1,0:T(8,128)S(1)}, u32[]{:S(2)}, u32[]{:S(2)}) collective-permute-start(f32[8,512]{1,0:T(8,128)S(1)} %get-tuple-element.57.refs_0_), channel_id=1, source_target_pairs={{0,3},{1,2},{2,1},{3,0},{4,7},{5,6},{6,5},{7,4},{8,11},{9,10},{10,... | collective-permute-start | bytes 49160 | tf_op jit(solution)/shard_map/ppermute | solution.py:332
  57.6 0.6 collective-permute-start.6
  58.2 1.1 %collective-permute-done.8.refs_3_ = f32[8,512]{1,0:T(8,128)S(1)} collective-permute-done((f32[8,512]{1,0:T(8,128)S(1)}, f32[8,512]{1,0:T(8,128)S(1)}, u32[]{:S(2)}, u32[]{:S(2)}) %collective-permute-start.8) | collective-permute-done | bytes 16416 | tf_op jit(solution)/shard_map/ppermute | solution.py:332
  59.3 2.9 %collective-permute-done.7.refs_2_ = f32[8,512]{1,0:T(8,128)S(1)} collective-permute-done((f32[8,512]{1,0:T(8,128)S(1)}, f32[8,512]{1,0:T(8,128)S(1)}, u32[]{:S(2)}, u32[]{:S(2)}) %collective-permute-start.7) | collective-permute-done | bytes 16416 | tf_op jit(solution)/shard_map/ppermute | solution.py:332
  62.2 2.6 %scale.1 = f32[512,2048]{1,0:T(8,128)} custom-call(f32[8,512]{1,0:T(8,128)S(1)} %get-tuple-element.57.refs_0_, f32[8,512]{1,0:T(8,128)S(1)} %collective-permute-done.6.refs_1_, f32[8,512]{1,0:T(8,128)S(1)} %collective-permute-done.7.refs_2_, f32[8,512]{1,0:T(8,128)S(1)} %collective-permute-done.8.refs_3_, f32[128,2048]{1,0:T(8,128)S(1)} %get-tuple-element.58.refs_4_, ...), custom_call_target="tpu_custom_call" | custom-call | flops 4194304 | bytes 8388608 | tf_op jit(solution)/shard_map/scale/pallas_call | solution.py:499
  (8 shorter events, 0.1 us)
Async XLA Ops:
  4.2 5.4 %copy-start = (f32[2,16]{1,0:T(2,128)S(1)}, f32[2,16]{1,0:T(2,128)}, u32[]{:S(2)}) copy-start(f32[2,16]{1,0:T(2,128)} %gain_ref.9) | copy-start | bytes 388
  4.3 3.7 %collective-permute-start.1 = (f32[8,128,128]{2,1,0:T(8,128)S(1)}, f32[8,128,128]{2,1,0:T(8,128)S(1)}, u32[]{:S(2)}, u32[]{:S(2)}) collective-permute-start(f32[8,128,128]{2,1,0:T(8,128)S(1)} %get-tuple-element.42), channel_id=1, source_target_pairs={{0,4},{4,0},{8,12},{12,8},{16,20},{20,16},{24,28},{28,24},{1,5},{5... | collective-permute-start | bytes 1572872 | tf_op jit(solution)/shard_map/ppermute | solution.py:332
  5.6 22.5 %collective-permute-start = (f32[128,2048]{1,0:T(8,128)S(1)}, f32[128,2048]{1,0:T(8,128)S(1)}, u32[]{:S(2)}, u32[]{:S(2)}) collective-permute-start(f32[128,2048]{1,0:T(8,128)S(1)} %tail.1), channel_id=1, source_target_pairs={{0,4},{4,8},{8,12},{12,16},{16,20},{20,24},{24,28},{1,5},{5,9},{9,... | collective-permute-start | bytes 3145736 | tf_op jit(solution)/shard_map/ppermute | solution.py:398
  8.1 23.8 %collective-permute-start.2 = (f32[8,128,128]{2,1,0:T(8,128)S(1)}, f32[8,128,128]{2,1,0:T(8,128)S(1)}, u32[]{:S(2)}, u32[]{:S(2)}) collective-permute-start(f32[8,128,128]{2,1,0:T(8,128)S(1)} %add.3.chip_ref), channel_id=1, source_target_pairs={{0,8},{4,20},{8,0},{12,28},{16,24},{20,4},{24,16},{28,12},{1,9},{5... | collective-permute-start | bytes 1572872 | tf_op jit(solution)/shard_map/ppermute | solution.py:341
  32.0 9.7 %collective-permute-start.4 = (f32[8,128,128]{2,1,0:T(8,128)S(1)}, f32[8,128,128]{2,1,0:T(8,128)S(1)}, u32[]{:S(2)}, u32[]{:S(2)}) collective-permute-start(f32[8,128,128]{2,1,0:T(8,128)S(1)} %message.1.refs_0_), channel_id=1, source_target_pairs={{0,16},{4,12},{8,24},{12,4},{16,0},{20,28},{24,8},{28,20},{1,17},{... | collective-permute-start | bytes 1572872 | tf_op jit(solution)/shard_map/ppermute | solution.py:345
  35.9 17.0 %collective-permute-start.3 = (f32[128,2048]{1,0:T(8,128)S(1)}, f32[128,2048]{1,0:T(8,128)S(1)}, u32[]{:S(2)}, u32[]{:S(2)}) collective-permute-start(f32[128,2048]{1,0:T(8,128)S(1)} %get-tuple-element.48), channel_id=1, source_target_pairs={{0,4},{4,8},{8,12},{12,16},{16,20},{20,24},{24,28},{1,5},{5,9},{9,... | collective-permute-start | bytes 3145736 | tf_op jit(solution)/shard_map/ppermute | solution.py:479
  42.0 2.9 %collective-permute-start.5 = (f32[8,128,128]{2,1,0:T(8,128)S(1)}, f32[8,128,128]{2,1,0:T(8,128)S(1)}, u32[]{:S(2)}, u32[]{:S(2)}) collective-permute-start(f32[8,128,128]{2,1,0:T(8,128)S(1)} %get-tuple-element.51), channel_id=1, source_target_pairs={{0,4},{4,0},{8,12},{12,8},{16,20},{20,16},{24,28},{28,24},{1,5},{5... | collective-permute-start | bytes 1572872 | tf_op jit(solution)/shard_map/ppermute | solution.py:332
  53.7 5.6 %collective-permute-start.8 = (f32[8,512]{1,0:T(8,128)S(1)}, f32[8,512]{1,0:T(8,128)S(1)}, u32[]{:S(2)}, u32[]{:S(2)}) collective-permute-start(f32[8,512]{1,0:T(8,128)S(1)} %get-tuple-element.57.refs_0_), channel_id=1, source_target_pairs={{0,3},{1,2},{2,1},{3,0},{4,7},{5,6},{6,5},{7,4},{8,11},{9,10},{10,... | collective-permute-start | bytes 49160 | tf_op jit(solution)/shard_map/ppermute | solution.py:332
  57.6 4.6 %collective-permute-start.7 = (f32[8,512]{1,0:T(8,128)S(1)}, f32[8,512]{1,0:T(8,128)S(1)}, u32[]{:S(2)}, u32[]{:S(2)}) collective-permute-start(f32[8,512]{1,0:T(8,128)S(1)} %get-tuple-element.57.refs_0_), channel_id=1, source_target_pairs={{0,2},{1,3},{2,0},{3,1},{4,6},{5,7},{6,4},{7,5},{8,10},{9,11},{10,... | collective-permute-start | bytes 49160 | tf_op jit(solution)/shard_map/ppermute | solution.py:332
  57.6 4.6 %collective-permute-start.6 = (f32[8,512]{1,0:T(8,128)S(1)}, f32[8,512]{1,0:T(8,128)S(1)}, u32[]{:S(2)}, u32[]{:S(2)}) collective-permute-start(f32[8,512]{1,0:T(8,128)S(1)} %get-tuple-element.57.refs_0_), channel_id=1, source_target_pairs={{0,1},{1,0},{2,3},{3,2},{4,5},{5,4},{6,7},{7,6},{8,9},{9,8},{10,11... | collective-permute-start | bytes 49160 | tf_op jit(solution)/shard_map/ppermute | solution.py:332

commit v5 on v4

--- a/solution.py
+++ b/solution.py
@@ -80,11 +80,35 @@
     return pl.ds(pl.multiple_of(head * width, width), count * width)
 
 
-def tail_kernel(k_ref, tail_ref, sem):
-    rows = k_ref.shape[0]
-    copy = pltpu.make_async_copy(k_ref.at[pl.ds(rows - WINDOW, WINDOW), :], tail_ref, sem)
-    copy.start()
-    copy.wait()
+def tail_kernel(k_ref, low_ref, high_ref, sems):
+    rows, width = k_ref.shape
+    middle = width // 2
+    copies = [
+        pltpu.make_async_copy(
+            k_ref.at[pl.ds(rows - WINDOW, WINDOW), pl.ds(i * middle, middle)], target, sems.at[i]
+        )
+        for i, target in enumerate((low_ref, high_ref))
+    ]
+    for copy in copies:
+        copy.start()
+    for copy in copies:
+        copy.wait()
+
+
+def load_kernel(q_hbm, q_ref, sems):
+    width = q_ref.shape[1] // sems.shape[0]
+    copies = []
+    for i in range(sems.shape[0]):
+        columns = pl.ds(i * width, width)
+        copies.append(pltpu.make_async_copy(q_hbm.at[:, columns], q_ref.at[:, columns], sems.at[i]))
+    for copy in copies:
+        copy.start()
+    for copy in copies:
+        copy.wait()
+
+
+def chip_kernel(keep_ref, beside_ref, _, out_ref):
+    out_ref[...] = keep_ref[...] + beside_ref[...]
 
 
 def totals_kernel(k_hbm, v_hbm, keep_ref, send_ref, half_ref, k_ref, v_ref, tail_v_ref, sems):
@@ -137,23 +161,15 @@
     return side(high * above, high * below), side(low * above, low * below)
 
 
-def local_kernel(begin, extra, gain_ref, q_hbm, k_ref, v_ref, *refs):
-    a_ref, b_ref, qq_ref, sum_ref = refs[extra : extra + 4]
-    q_ref, square_ref, sems = refs[-3:]
+def local_kernel(begin, extra, gain_ref, q_ref, k_ref, v_ref, *refs):
+    a_ref, b_ref, sum_ref = refs[extra : extra + 3]
+    square_ref = refs[-1]
     lower = lower_mask()
     below = jnp.where(lower, 1.0, 0.0).astype(BF16)
     above = jnp.where(lower, 0.0, 1.0).astype(BF16)
     rows, width = a_ref.shape
     tiles = rows // WINDOW
     groups = width // (GROUP * HD)
-
-    def load(group):
-        source = pl.ds(pl.multiple_of(begin * HD + group * (GROUP * HD), HD), GROUP * HD)
-        target = head_columns(group, 1, GROUP * HD)
-        return pltpu.make_async_copy(q_hbm.at[:, source], q_ref.at[:, target], sems.at[group])
-
-    for group in range(groups):
-        load(group).start()
     square_ref[...] = jnp.zeros_like(square_ref)
 
     def tile(n):
@@ -161,13 +177,11 @@
 
     @pl.loop(0, groups)
     def _(group):
-        load(group).wait()
         scores = []
         for j in range(GROUP):
-            head = GROUP * group + j
-            qq = side(*halves(q_ref[:, head_columns(head)]))
-            qq_ref[:, head_columns(head, 1, 2 * HD)] = qq
-            k_high, k_low = halves(k_ref[:, head_columns(begin + head)])
+            columns = head_columns(begin + GROUP * group + j)
+            qq = side(*halves(q_ref[:, columns]))
+            k_high, k_low = halves(k_ref[:, columns])
             now, before = [], [None]
             for n in range(tiles):
                 keys = wide_keys(k_high[tile(n)], k_low[tile(n)])
@@ -224,21 +238,21 @@
     other_ref[...] = earlier + jnp.where(core == 0, keep_ref[...], 0.0)
 
 
-def earlier_kernel(count, gain_ref, half_ref, mine_ref, other_ref, *refs):
-    qq_refs, b_refs, sum_refs, out_refs = (refs[i * count : (i + 1) * count] for i in range(4))
-    sums_ref, square_ref = refs[4 * count :]
+def earlier_kernel(count, gain_ref, half_ref, mine_ref, other_ref, q_ref, *refs):
+    b_refs, sum_refs, out_refs = (refs[i * count : (i + 1) * count] for i in range(3))
+    sums_ref, square_ref = refs[3 * count :]
     core = lax.axis_index("ctx") % 2
     rows = b_refs[0].shape[0]
     middle = rows // 2
     head = 0
     square_ref[...] = jnp.zeros_like(square_ref)
-    for qq_ref, b_ref, out_ref in zip(qq_refs, b_refs, out_refs):
+    for b_ref, out_ref in zip(b_refs, out_refs):
         for j in range(b_ref.shape[1] // HD):
             columns = slice(j * HD, (j + 1) * HD)
             state = jnp.where(core == head % 2, mine_ref[head // 2], other_ref[head // 2])
             gain_b = gain_ref[1, head]
             for part, held in ((slice(0, middle), state), (slice(middle, rows), state + half_ref[head])):
-                qq = qq_ref[part, 2 * j * HD : 2 * (j + 1) * HD]
+                qq = side(*halves(q_ref[part, head * HD : (head + 1) * HD]))
                 b = gain_b * (b_ref[part, columns] + folded(dot(qq, wide_state(held))))
                 out_ref[part, columns] = b
                 square_ref[part, :] += b * b
@@ -248,40 +262,32 @@
     sums_ref[...] = jnp.where(row == 0, sum(ref[...] for ref in sum_refs), sums)
 
 
-def first_weights_kernel(gain_ref, k_ref, v_ref, tail_k_ref, *refs):
-    qq_refs, (weights_ref, out_ref) = refs[:-2], refs[-2:]
+def first_weights_kernel(gain_ref, q_ref, k_ref, v_ref, low_ref, high_ref, weights_ref, out_ref):
     lower = lower_mask()
     reachable = jnp.logical_or(lower, lax.axis_index("ctx") > 0)
     top = slice(0, WINDOW)
-    begin = 0
-    for qq_ref in qq_refs:
-        count = qq_ref.shape[1] // (2 * HD)
-
-        @pl.loop(0, count // GROUP)
-        def _(group):
-            scores = []
-            for j in range(GROUP):
-                head = GROUP * group + j
-                columns = head_columns(begin + head)
-                qq = qq_ref[top, head_columns(head, 1, 2 * HD)]
-                now = folded(dot_rows(qq, wide_keys(*halves(k_ref[top, columns]))))
-                before = folded(dot_rows(qq, wide_keys(*halves(tail_k_ref[:, columns]))))
-                scores.append(jnp.where(reachable, jnp.where(lower, now, before), -jnp.inf))
-            for j in range(GROUP):
-                head = begin + GROUP * group + j
-                columns = head_columns(head)
-                weights, total = weights_of(scores[j])
-                weights = weights * (gain_ref[0, head] / total)
-                now_high, now_low = halves(jnp.where(lower, weights, 0.0))
-                vv = side(*halves(v_ref[top, columns]))
-                wide = dot(stack(now_high, now_low), vv)
-                out_ref[:, columns] = folded(wide[:WINDOW]) + wide[WINDOW:, :HD]
-                weights_ref[:, head_columns(head, 1, 2 * HD)] = side(*halves(jnp.where(lower, 0.0, weights)))
-
-        begin += count
-
-
-def first_values_kernel(weights_ref, now_ref, tail_v_ref, sums_ref, a_ref, out_ref):
+    count = low_ref.shape[1] // HD
+    for part, tail_ref in enumerate((low_ref, high_ref)):
+        scores = []
+        for j in range(count):
+            columns = slice((part * count + j) * HD, (part * count + j + 1) * HD)
+            qq = side(*halves(q_ref[top, columns]))
+            now = folded(dot_rows(qq, wide_keys(*halves(k_ref[top, columns]))))
+            before = folded(dot_rows(qq, wide_keys(*halves(tail_ref[:, j * HD : (j + 1) * HD]))))
+            scores.append(jnp.where(reachable, jnp.where(lower, now, before), -jnp.inf))
+        for j in range(count):
+            head = part * count + j
+            columns = slice(head * HD, (head + 1) * HD)
+            weights, total = weights_of(scores[j])
+            weights = weights * (gain_ref[0, head] / total)
+            now_high, now_low = halves(jnp.where(lower, weights, 0.0))
+            vv = side(*halves(v_ref[top, columns]))
+            wide = dot(stack(now_high, now_low), vv)
+            out_ref[:, columns] = folded(wide[:WINDOW]) + wide[WINDOW:, :HD]
+            weights_ref[:, 2 * head * HD : 2 * (head + 1) * HD] = side(*halves(jnp.where(lower, 0.0, weights)))
+
+
+def first_values_kernel(weights_ref, now_ref, tail_v_ref, a_ref, sums_ref):
     square = jnp.zeros((WINDOW, HD), F32)
     for j in range(now_ref.shape[1] // HD):
         columns = slice(j * HD, (j + 1) * HD)
@@ -291,31 +297,47 @@
         a = now_ref[:, columns] + (folded(wide[:WINDOW]) + wide[WINDOW:, :HD])
         a_ref[:, columns] = a
         square = square + a * a
-    own = row_sums(square)
-    row = lax.broadcasted_iota(jnp.int32, own.shape, 0)
-    out_ref[:, :WINDOW] = jnp.where(row == 0, own, sums_ref[:, :WINDOW])
-    out_ref[:, WINDOW:] = sums_ref[:, WINDOW:]
+    sums_ref[...] = row_sums(square)
 
 
 def inverse_norm(total):
     return 1.0 / jnp.sqrt(total / (HEADS * HD) + EPS)
 
 
-def scale_kernel(count, sums, first_ref, *refs):
+def scale_kernel(count, sums_ref, _, *refs):
     a_refs, b_refs, (out_hbm, out_ref, sems) = refs[:count], refs[count : 2 * count], refs[2 * count :]
-    total = sums[0][...]
-    for part in sums[1:]:
-        total = total + part[...]
-    inverse = inverse_norm(total).T
+    inverse = inverse_norm(jnp.sum(sums_ref[...], axis=0)).T
     copies = []
     for n in range(out_ref.shape[0] // WINDOW):
-        rows = slice(n * WINDOW, (n + 1) * WINDOW)
+        held = slice(n * WINDOW, (n + 1) * WINDOW)
+        rows = slice((n + 1) * WINDOW, (n + 2) * WINDOW)
         inverse_a, inverse_b = inverse[rows, 0:1], inverse[rows, 1:2]
         begin = 0
         for a_ref, b_ref in zip(a_refs, b_refs):
             columns = slice(begin, begin + a_ref.shape[1])
-            a = a_ref[rows, :] if n else first_ref[:, columns]
-            out_ref[rows, columns] = a * inverse_a + b_ref[rows, :] * inverse_b
+            out_ref[held, columns] = a_ref[rows, :] * inverse_a + b_ref[rows, :] * inverse_b
+            begin = columns.stop
+        copy = pltpu.make_async_copy(out_ref.at[held, :], out_hbm.at[rows, :], sems.at[n])
+        copy.start()
+        copies.append(copy)
+    for copy in copies:
+        copy.wait()
+
+
+def first_scale_kernel(count, parts, sums_ref, a_ref, _, *refs):
+    b_refs, sums, (out_hbm, out_ref, sems) = refs[:count], refs[count : count + parts], refs[count + parts :]
+    total = sums[0][...]
+    for part in sums[1:]:
+        total = total + part[...]
+    inverse_a = inverse_norm(total).T[:, 0:1]
+    inverse_b = inverse_norm(jnp.sum(sums_ref[:, :, :WINDOW], axis=0)).T[:, 1:2]
+    copies = []
+    for n in range(sems.shape[0]):
+        rows = slice(n * WINDOW // sems.shape[0], (n + 1) * WINDOW // sems.shape[0])
+        begin = 0
+        for b_ref in b_refs:
+            columns = slice(begin, begin + b_ref.shape[1])
+            out_ref[rows, columns] = a_ref[rows, columns] * inverse_a[rows] + b_ref[rows, :] * inverse_b[rows]
             begin = columns.stop
         copy = pltpu.make_async_copy(out_ref.at[rows, :], out_hbm.at[rows, :], sems.at[n])
         copy.start()
@@ -324,17 +346,8 @@
         copy.wait()
 
 
-def scale_first(parts, count, *refs):
-    scale_kernel(count, refs[:parts], *refs[parts:])
-
-
 def swap(block, axis, bit):
     return lax.ppermute(block, axis, [(i, i ^ bit) for i in range(lax.axis_size(axis))])
-
-
-def chip_totals(keep, send):
-    beside = swap(send, "ctx", 1)
-    return beside, keep + beside
 
 
 def first_phase(chip):
@@ -385,17 +398,18 @@
     packed = array(heads // 2, HD, HD)
     first_tile = array(WINDOW, width)
     dma = pltpu.SemaphoreType.DMA
-    tail_k = call(
+    tail_low, tail_high = call(
         tail_kernel,
         "tail",
         0,
         size // 2,
         in_specs=[anywhere],
-        out_shape=first_tile,
-        scratch_shapes=[dma],
+        out_shape=[array(WINDOW, width // 2)] * 2,
+        scratch_shapes=[dma((2,))],
     )(keys)
     route = [(i, i + 1) for i in range(lax.axis_size("ctx") - 1)]
-    before_k = lax.ppermute(tail_k, "ctx", route)
+    before_low = lax.ppermute(tail_low, "ctx", route)
+    before_high = lax.ppermute(tail_high, "ctx", route)
 
     keep, send, half, held_k, held_v, tail_v = call(
         totals_kernel,
@@ -406,36 +420,41 @@
         out_shape=[packed, packed, array(heads, HD, HD), array(rows, width), array(rows, width), first_tile],
         scratch_shapes=[dma((2, heads // GROUP))],
     )(keys, values)
-    beside, chip = chip_totals(keep, send)
-
-    def local(begin, count, *after):
+    held_q = call(
+        load_kernel,
+        "load",
+        0,
+        2 * size,
+        in_specs=[anywhere],
+        out_shape=array(rows, width),
+        scratch_shapes=[dma((4,))],
+    )(queries)
+    beside = swap(send, "ctx", 1)
+    chip = call(
+        chip_kernel,
+        "chip",
+        0,
+        size // 4,
+        in_specs=[vmem, vmem, anywhere],
+        out_shape=packed,
+    )(keep, beside, held_q)
+
+    def local(begin, count, after, *passed):
         taken = count * HD
         return call(
-            functools.partial(local_kernel, begin, len(after)),
+            functools.partial(local_kernel, begin, 1 + len(passed)),
             "local",
             0,
             0,
-            in_specs=[smem, anywhere, vmem, vmem] + [anywhere] * len(after),
-            out_specs=[vmem] * 4 + [anywhere] * (len(after) // 2),
-            out_shape=[
-                array(rows, taken),
-                array(rows, taken),
-                array(rows, 2 * taken, dtype=BF16),
-                array(8, rows),
-            ]
-            + [first_tile] * (len(after) // 2),
-            scratch_shapes=[
-                pltpu.VMEM((rows, taken), F32),
-                pltpu.VMEM((rows, HD), F32),
-                dma((count // GROUP,)),
-            ],
-            input_output_aliases={5: 4} if after else {},
-        )(head_gain, queries, held_k, held_v, *after)
-
-    begin = heads // 2
-    parts = [local(0, begin)]
-    *part, before_k = local(begin, GROUP, parts[0][3], before_k)
-    parts.append(part)
+            in_specs=[smem, vmem, vmem, vmem] + [anywhere] * (1 + len(passed)),
+            out_specs=[vmem] * 3 + [anywhere] * len(passed),
+            out_shape=[array(rows, taken), array(rows, taken), array(8, rows)] + [first_tile] * len(passed),
+            scratch_shapes=[pltpu.VMEM((rows, HD), F32)],
+            input_output_aliases={5: 3} if passed else {},
+        )(head_gain, held_q, held_k, held_v, after, *passed)
+
+    begin = heads * 3 // 4 // GROUP * GROUP
+    parts = [local(0, begin, before_low)]
     message = None
     if lax.axis_size("ctx") == 8:
         first = first_phase(chip)
@@ -446,20 +465,19 @@
             size // 4,
             in_specs=[vmem, vmem, anywhere],
             out_shape=packed,
-        )(first, chip, parts[1][3])
-    after = parts[1][3] if message is None else message
-    for begin in range(begin + GROUP, heads, GROUP):
-        *part, tail_v = local(begin, GROUP, after, tail_v)
-        parts.append(part)
-    window, linear, qq, window_sums = zip(*parts)
+        )(first, chip, parts[0][2])
+    *part, tail_v = local(begin, heads - begin, parts[0][2] if message is None else message, tail_v)
+    parts.append(part)
+    window, linear, window_sums = zip(*parts)
+    before_v = lax.ppermute(tail_v, "ctx", route)
     first_weights, first_now = call(
         first_weights_kernel,
         "first_weights",
         4 * unit,
         size,
-        in_specs=[smem] + [vmem] * (3 + len(qq)),
+        in_specs=[smem] + [vmem] * 5,
         out_shape=[array(WINDOW, 2 * width, dtype=BF16), first_tile],
-    )(head_gain, held_k, held_v, before_k, *qq)
+    )(head_gain, held_q, held_k, held_v, before_low, before_high)
 
     if message is not None:
         second = second_phase(message)
@@ -476,7 +494,6 @@
         core = lax.axis_index("ctx") % 2
         mine = earlier + jnp.where(core == 1, beside, 0.0)
         other = earlier + jnp.where(core == 0, keep, 0.0)
-    before_v = lax.ppermute(tail_v, "ctx", route)
     other = swap(other, "ctx", 1)
 
     *linear, sums = call(
@@ -484,27 +501,40 @@
         "earlier",
         3 * unit,
         3 * size,
-        in_specs=[smem] + [vmem] * (3 + 3 * len(parts)),
+        in_specs=[smem] + [vmem] * (4 + 2 * len(parts)),
         out_shape=[array(*x.shape) for x in linear] + [array(8, rows)],
         scratch_shapes=[pltpu.VMEM((rows, HD), F32)],
-    )(head_gain, half, mine, other, *qq, *linear, *window_sums)
-    first_a, sums = call(
+    )(head_gain, half, mine, other, held_q, *linear, *window_sums)
+    sums = lax.all_gather(sums, "head")
+    first_a, first_sums = call(
         first_values_kernel,
         "first_values",
         unit,
         size // 2,
-        out_shape=[first_tile, array(8, rows)],
-    )(first_weights, first_now, before_v, sums)
-    all_sums = [sums] + [swap(sums, "head", bits) for bits in range(1, lax.axis_size("head"))]
-    return call(
-        functools.partial(scale_first, len(all_sums), len(parts)),
+        out_shape=[first_tile, array(8, WINDOW)],
+    )(first_weights, first_now, before_v)
+    first_sums = [first_sums] + [swap(first_sums, "head", bits) for bits in range(1, lax.axis_size("head"))]
+    out = call(
+        functools.partial(scale_kernel, len(parts)),
         "scale",
         unit // 64,
         2 * size,
+        in_specs=[vmem, anywhere] + [vmem] * (2 * len(parts)),
         out_specs=anywhere,
         out_shape=array(rows, width),
-        scratch_shapes=[pltpu.VMEM((rows, width), F32), dma((rows // WINDOW,))],
-    )(*all_sums, first_a, *window, *linear)
+        scratch_shapes=[pltpu.VMEM((rows - WINDOW, width), F32), dma((rows // WINDOW - 1,))],
+    )(sums, first_sums[0], *window, *linear)
+    return call(
+        functools.partial(first_scale_kernel, len(parts), len(first_sums)),
+        "first_scale",
+        unit // 256,
+        size // 2,
+        in_specs=[vmem, vmem, anywhere] + [vmem] * (len(parts) + len(first_sums)),
+        out_specs=anywhere,
+        out_shape=array(rows, width),
+        scratch_shapes=[pltpu.VMEM((WINDOW, width), F32), dma((4,))],
+        input_output_aliases={2: 0},
+    )(sums, first_a, out, *linear, *first_sums)
 
 
 def solution(mesh):

time: 65.3 us -> 78.4 us (1.20); the launches traced: 65 us -> 76.9 us
  blocking collectives: 0 us -> 13.2 us
  Pallas kernels: 28.6 us -> 26.6 us
  starting transfers between devices: 12 us -> 13.8 us
  waiting for transfers between devices: 24 us -> 23.1 us
    ppermute x1, waiting for transfers between devices: 0.01 us -> 16.4 us  [second_phase(): lax.ppermute(message, 'ctx', [(i, i ^ (4 if i % 2 == 0 else 2)) for i in...]
    all_gather x0 -> x1, blocking collectives: none -> 13.2 us  [shards(): sums = lax.all_gather(sums, 'head')]
    ppermute x1 -> x2, waiting for transfers between devices: 12.7 us -> 6.77 us  [the longest x1 6.76 us: shards(): before_low = lax.ppermute(tail_low, 'ctx', route)]
    ppermute x1, waiting for transfers between devices: 5.71 us -> 0.01 us  [shards(): before_v = lax.ppermute(tail_v, 'ctx', route)]
    ppermute x5, waiting for transfers between devices: 5.58 us -> 0.01 us  [swap(): lax.ppermute(block, axis, [(i, i ^ bit) for i in range(lax.axis_size(axis...]
    ppermute x1 -> x2, starting transfers between devices: 2.4 us -> 4.31 us  [the longest x1 2.4 us: shards(): before_low = lax.ppermute(tail_low, 'ctx', route)]
    ppermute x5, starting transfers between devices: 5.91 us -> 4.54 us  [swap(): lax.ppermute(block, axis, [(i, i ^ bit) for i in range(lax.axis_size(axis...]
    pallas_call x5 -> x7, Pallas kernels: 17.1 us -> 15.9 us  [the longest x2 8.94 us: local(): call(functools.partial(local_kernel, begin, 1 + len(passed)), 'local', 0,...]
  transfers between devices with their start and end apart: 9 -> 10, of which waited for: 5 -> 2; matrix products, arithmetic and copies ran while one was open for 0% -> 0% of each run, Pallas kernels for 32% -> 28%
where the time goes in v5:
time: 78.4 us; the launch traced here: 76.9 us
  Pallas kernels  26.6 us (34%)
  waiting for transfers between devices  23.1 us (29%)
  starting transfers between devices  13.8 us (18%)
  blocking collectives  13.2 us (17%)
    ppermute x1, waiting for transfers between devices, second_phase(): lax.ppermute(message, 'ctx', [(i, i ^ (4 if i % 2 == 0 else 2)) for i in...  16.4 us
    all_gather x1, blocking collectives, shards(): sums = lax.all_gather(sums, 'head')  13.2 us
    pallas_call x2, Pallas kernels, local(): call(functools.partial(local_kernel, begin, 1 + len(passed)), 'local', 0,...  8.94 us
    ppermute x1, waiting for transfers between devices, shards(): before_low = lax.ppermute(tail_low, 'ctx', route)  6.76 us
    ppermute x5, starting transfers between devices, swap(): lax.ppermute(block, axis, [(i, i ^ bit) for i in range(lax.axis_size(axis...  4.54 us
    pallas_call x1, Pallas kernels, shards(): call(totals_kernel, 'totals', 4 * unit, 2 * size, in_specs=[anywhere, any...  4.23 us
    ppermute x1, starting transfers between devices, shards(): before_v = lax.ppermute(tail_v, 'ctx', route)  3.31 us
    pallas_call x1, Pallas kernels, shards(): call(first_weights_kernel, 'first_weights', 4 * unit, size, in_specs=[sme...  2.86 us
  transfers between devices with their start and end apart: 10, of which 2 were waited for; matrix products, arithmetic and copies ran while one was open for 0% of the time, Pallas kernels for 28%

profile of v5, /device:TPU:4, one launch (start us, length us, event | category | flops | bytes accessed | tf_op | source)
XLA Modules:
  0.0 76.9 jit_solution(7666485282821168691)
XLA Ops:
  0.0 4.2 %totals.1 = (f32[8,128,128]{2,1,0:T(8,128)S(1)}, f32[8,128,128]{2,1,0:T(8,128)S(1)}, f32[16,128,128]{2,1,0:T(8,128)S(1)}, f32[512,2048]{1,0:T(8,128)S(1)}, f32[5...) custom-call(f32[512,2048]{1,0:T(8,128)} %k_ref.1, f32[512,2048]{1,0:T(8,128)} %v_hbm.1), custom_call_target="tpu_custom_call" | custom-call | flops 1073741824 | bytes 8388608 | tf_op jit(solution)/shard_map/totals/pallas_call | solution.py:414
  4.2 0.1 collective-permute-start
  4.3 1.2 %tail.1 = (f32[128,1024]{1,0:T(8,128)S(1)}, f32[128,1024]{1,0:T(8,128)S(1)}) custom-call(f32[512,2048]{1,0:T(8,128)} %k_ref.1), custom_call_target="tpu_custom_call" | custom-call | bytes 2097152 | tf_op jit(solution)/shard_map/tail/pallas_call | solution.py:401
  5.5 2.4 %collective-permute-start.2 = (f32[128,1024]{1,0:T(8,128)S(1)}, f32[128,1024]{1,0:T(8,128)S(1)}, u32[]{:S(2)}, u32[]{:S(2)}) collective-permute-start(f32[128,1024]{1,0:T(8,128)S(1)} %get-tuple-element.34), channel_id=1, source_target_pairs={{0,4},{4,8},{8,12},{12,16},{16,20},{20,24},{24,28},{1,5},{5,9},{9,... | collective-permute-start | bytes 1572872 | tf_op jit(solution)/shard_map/ppermute | solution.py:411
  8.0 2.2 %load.1._.q_ref = f32[512,2048]{1,0:T(8,128)S(1)} custom-call(f32[512,2048]{1,0:T(8,128)} %q_hbm.1), custom_call_target="tpu_custom_call" | custom-call | bytes 8388608 | tf_op jit(solution)/shard_map/load/pallas_call | solution.py:423
  10.3 1.6 %collective-permute-start.1 = (f32[8,128,128]{2,1,0:T(8,128)S(1)}, f32[8,128,128]{2,1,0:T(8,128)S(1)}, u32[]{:S(2)}, u32[]{:S(2)}) collective-permute-start(f32[8,128,128]{2,1,0:T(8,128)S(1)} %chip.1.chip_ref), channel_id=1, source_target_pairs={{0,8},{4,20},{8,0},{12,28},{16,24},{20,4},{24,16},{28,12},{1,9},{5... | collective-permute-start | bytes 1572872 | tf_op jit(solution)/shard_map/ppermute | solution.py:354
  11.8 1.9 %collective-permute-start.4 = (f32[128,1024]{1,0:T(8,128)S(1)}, f32[128,1024]{1,0:T(8,128)S(1)}, u32[]{:S(2)}, u32[]{:S(2)}) collective-permute-start(f32[128,1024]{1,0:T(8,128)S(1)} %get-tuple-element.36), channel_id=1, source_target_pairs={{0,4},{4,8},{8,12},{12,16},{16,20},{20,24},{24,28},{1,5},{5,9},{9,... | collective-permute-start | bytes 1572872 | tf_op jit(solution)/shard_map/ppermute | solution.py:412
  13.8 6.8 %collective-permute-done.2.refs_0_.low_ref = f32[128,1024]{1,0:T(8,128)S(1)} collective-permute-done((f32[128,1024]{1,0:T(8,128)S(1)}, f32[128,1024]{1,0:T(8,128)S(1)}, u32[]{:S(2)}, u32[]{:S(2)}) %collective-permute-start.2) | collective-permute-done | bytes 524320 | tf_op jit(solution)/shard_map/ppermute | solution.py:411
  20.5 6.4 %local.2 = (f32[512,1536]{1,0:T(8,128)S(1)}, f32[512,1536]{1,0:T(8,128)S(1)}, f32[8,512]{1,0:T(8,128)S(1)}) custom-call(f32[2,16]{1,0:T(2,128)S(1)} %copy-done, f32[512,2048]{1,0:T(8,128)S(1)} %load.1._.q_ref, f32[512,2048]{1,0:T(8,128)S(1)} %get-tuple-element.32.k_ref, f32[512,2048]{1,0:T(8,128)S(1)} %get-tuple-element.33.v_ref, ...), custom_call_target="tpu_custom_call" | custom-call | tf_op jit(solution)/shard_map/local/pallas_call | solution.py:444
  26.9 0.1 message.1.refs_0_
  27.1 2.5 %local.3 = (f32[512,512]{1,0:T(8,128)S(1)}, f32[512,512]{1,0:T(8,128)S(1)}, f32[8,512]{1,0:T(8,128)S(1)}, f32[128,2048]{1,0:T(8,128)S(1)}) custom-call(f32[2,16]{1,0:T(2,128)S(1)} %copy-done, f32[512,2048]{1,0:T(8,128)S(1)} %load.1._.q_ref, f32[512,2048]{1,0:T(8,128)S(1)} %get-tuple-element.32.k_ref, ...), custom_call_target="tpu_custom_call", output_to_operand_aliasing={{3}: (5, {})} | custom-call | tf_op jit(solution)/shard_map/local/pallas_call | solution.py:444
  29.6 3.3 %collective-permute-start.6 = (f32[128,2048]{1,0:T(8,128)S(1)}, f32[128,2048]{1,0:T(8,128)S(1)}, u32[]{:S(2)}, u32[]{:S(2)}) collective-permute-start(f32[128,2048]{1,0:T(8,128)S(1)} %get-tuple-element.46), channel_id=1, source_target_pairs={{0,4},{4,8},{8,12},{12,16},{16,20},{20,24},{24,28},{1,5},{5,9},{9,... | collective-permute-start | bytes 3145736 | tf_op jit(solution)/shard_map/ppermute | solution.py:472
  32.9 0.1 collective-permute-start.3
  33.0 2.9 %first_weights.1 = (bf16[128,4096]{1,0:T(8,128)(2,1)S(1)}, f32[128,2048]{1,0:T(8,128)S(1)}) custom-call(f32[2,16]{1,0:T(2,128)S(1)} %copy-done, f32[512,2048]{1,0:T(8,128)S(1)} %load.1._.q_ref, f32[512,2048]{1,0:T(8,128)S(1)} %get-tuple-element.32.k_ref, f32[512,2048]{1,0:T(8,128)S(1)} %get-tuple-element.33.v_ref, ...), custom_call_target="tpu_custom_call" | custom-call | flops 1073741824 | bytes 4194304 | tf_op jit(solution)/shard_map/first_weights/pallas_call | solution.py:473
  35.9 16.4 %collective-permute-done.3.second_ref = f32[8,128,128]{2,1,0:T(8,128)S(1)} collective-permute-done((f32[8,128,128]{2,1,0:T(8,128)S(1)}, f32[8,128,128]{2,1,0:T(8,128)S(1)}, u32[]{:S(2)}, u32[]{:S(2)}) %collective-permute-start.3) | collective-permute-done | bytes 524320 | tf_op jit(solution)/shard_map/ppermute | solution.py:358
  52.2 0.2 prefix.1
  52.5 0.8 %first_values.1 = (f32[128,2048]{1,0:T(8,128)S(1)}, f32[8,128]{1,0:T(8,128)S(1)}) custom-call(bf16[128,4096]{1,0:T(8,128)(2,1)S(1)} %get-tuple-element.45.weights_ref, f32[128,2048]{1,0:T(8,128)S(1)} %get-tuple-element.37.refs_0_.now_ref, f32[128,2048]{1,0:T(8,128)S(1)} %collective-permute-done.6.tail_v_ref), custom_call_target="tpu_custom_call" | custom-call | flops 268435456 | bytes 2097152 | tf_op jit(solution)/shard_map/first_values/pallas_call | solution.py:509
  53.4 0.8 %collective-permute-start.7 = (f32[8,128]{1,0:T(8,128)S(1)}, f32[8,128]{1,0:T(8,128)S(1)}, u32[]{:S(2)}, u32[]{:S(2)}) collective-permute-start(f32[8,128]{1,0:T(8,128)S(1)} %get-tuple-element.48._.refs_2_), channel_id=1, source_target_pairs={{0,1},{1,0},{2,3},{3,2},{4,5},{5,4},{6,7},{7,6},{8,9},{9,8},{10,11... | collective-permute-start | bytes 12296 | tf_op jit(solution)/shard_map/ppermute | solution.py:350
  54.2 2.6 %collective-permute-start.8 = (f32[8,128]{1,0:T(8,128)S(1)}, f32[8,128]{1,0:T(8,128)S(1)}, u32[]{:S(2)}, u32[]{:S(2)}) collective-permute-start(f32[8,128]{1,0:T(8,128)S(1)} %get-tuple-element.48._.refs_2_), channel_id=1, source_target_pairs={{0,2},{1,3},{2,0},{3,1},{4,6},{5,7},{6,4},{7,5},{8,10},{9,11},{10,... | collective-permute-start | bytes 12296 | tf_op jit(solution)/shard_map/ppermute | solution.py:350
  56.8 1.0 %collective-permute-start.9 = (f32[8,128]{1,0:T(8,128)S(1)}, f32[8,128]{1,0:T(8,128)S(1)}, u32[]{:S(2)}, u32[]{:S(2)}) collective-permute-start(f32[8,128]{1,0:T(8,128)S(1)} %get-tuple-element.48._.refs_2_), channel_id=1, source_target_pairs={{0,3},{1,2},{2,1},{3,0},{4,7},{5,6},{6,5},{7,4},{8,11},{9,10},{10,... | collective-permute-start | bytes 12296 | tf_op jit(solution)/shard_map/ppermute | solution.py:350
  57.8 2.5 %earlier.1 = (f32[512,1536]{1,0:T(8,128)S(1)}, f32[512,512]{1,0:T(8,128)S(1)}, f32[8,512]{1,0:T(8,128)S(1)}) custom-call(f32[2,16]{1,0:T(2,128)S(1)} %copy-done, f32[16,128,128]{2,1,0:T(8,128)S(1)} %get-tuple-element.29.half_ref, f32[8,128,128]{2,1,0:T(8,128)S(1)} %get-tuple-element.38.mine_ref, f32[8,128,128]{2,1,0:T(8,128)S(1)} %collective-permute-done.5.other_ref, ...), custom_call_target="tpu_custom_call" | custom-call | flops 805306368 | bytes 12582912 | tf_op jit(solution)/shard_map/earlier/pallas_call | solution.py:499
  60.3 13.2 %all-gather = f32[32,512]{1,0:T(8,128)S(1)} all-gather(f32[8,512]{1,0:T(8,128)S(1)} %get-tuple-element.44), channel_id=2, replica_groups=mesh['ctx'=8,'head'=4] {'head'}, dimensions={0}, use_global_device_ids=true | all-gather | bytes 81920 | tf_op jit(solution)/shard_map/all_gather | solution.py:508
  73.4 2.2 %scale.1._ = f32[512,2048]{1,0:T(8,128)} custom-call(f32[4,8,512]{2,1,0:T(8,128)S(1)} %bitcast.1, f32[8,128]{1,0:T(8,128)S(1)} %get-tuple-element.48._.refs_2_, f32[512,1536]{1,0:T(8,128)S(1)} %get-tuple-element.49.refs_0_, f32[512,512]{1,0:T(8,128)S(1)} %get-tuple-element.50.refs_1_, f32[512,1536]{1,0:T(8,128)S(1)} %get-tuple-element.51.refs_2_.refs_0_, ...), custom_call_target="tpu_custom_call" | custom-call | flops 4194304 | bytes 8388608 | tf_op jit(solution)/shard_map/scale/pallas_call | solution.py:517
  75.7 1.2 %first_scale.1 = f32[512,2048]{1,0:T(8,128)} custom-call(f32[4,8,512]{2,1,0:T(8,128)S(1)} %bitcast.2, f32[128,2048]{1,0:T(8,128)S(1)} %get-tuple-element.47.a_ref, f32[512,2048]{1,0:T(8,128)} %scale.1._, f32[512,1536]{1,0:T(8,128)S(1)} %get-tuple-element.51.refs_2_.refs_0_, ...), custom_call_target="tpu_custom_call", output_to_operand_aliasing={{}: (2, {})} | custom-call | flops 1048576 | bytes 2097152 | tf_op jit(solution)/shard_map/first_scale/pallas_call | solution.py:527
  (12 shorter events, 0.2 us)
Async XLA Ops:
  4.2 6.0 %collective-permute-start = (f32[8,128,128]{2,1,0:T(8,128)S(1)}, f32[8,128,128]{2,1,0:T(8,128)S(1)}, u32[]{:S(2)}, u32[]{:S(2)}) collective-permute-start(f32[8,128,128]{2,1,0:T(8,128)S(1)} %get-tuple-element.31), channel_id=1, source_target_pairs={{0,4},{4,0},{8,12},{12,8},{16,20},{20,16},{24,28},{28,24},{1,5},{5... | collective-permute-start | bytes 1572872 | tf_op jit(solution)/shard_map/ppermute | solution.py:350
  5.5 15.0 %collective-permute-start.2 = (f32[128,1024]{1,0:T(8,128)S(1)}, f32[128,1024]{1,0:T(8,128)S(1)}, u32[]{:S(2)}, u32[]{:S(2)}) collective-permute-start(f32[128,1024]{1,0:T(8,128)S(1)} %get-tuple-element.34), channel_id=1, source_target_pairs={{0,4},{4,8},{8,12},{12,16},{16,20},{20,24},{24,28},{1,5},{5,9},{9,... | collective-permute-start | bytes 1572872 | tf_op jit(solution)/shard_map/ppermute | solution.py:411
  10.2 10.3 %copy-start = (f32[2,16]{1,0:T(2,128)S(1)}, f32[2,16]{1,0:T(2,128)}, u32[]{:S(2)}) copy-start(f32[2,16]{1,0:T(2,128)} %gain_ref.7) | copy-start | bytes 388
  10.3 16.7 %collective-permute-start.1 = (f32[8,128,128]{2,1,0:T(8,128)S(1)}, f32[8,128,128]{2,1,0:T(8,128)S(1)}, u32[]{:S(2)}, u32[]{:S(2)}) collective-permute-start(f32[8,128,128]{2,1,0:T(8,128)S(1)} %chip.1.chip_ref), channel_id=1, source_target_pairs={{0,8},{4,20},{8,0},{12,28},{16,24},{20,4},{24,16},{28,12},{1,9},{5... | collective-permute-start | bytes 1572872 | tf_op jit(solution)/shard_map/ppermute | solution.py:354
  11.8 21.2 %collective-permute-start.4 = (f32[128,1024]{1,0:T(8,128)S(1)}, f32[128,1024]{1,0:T(8,128)S(1)}, u32[]{:S(2)}, u32[]{:S(2)}) collective-permute-start(f32[128,1024]{1,0:T(8,128)S(1)} %get-tuple-element.36), channel_id=1, source_target_pairs={{0,4},{4,8},{8,12},{12,16},{16,20},{20,24},{24,28},{1,5},{5,9},{9,... | collective-permute-start | bytes 1572872 | tf_op jit(solution)/shard_map/ppermute | solution.py:412
  29.6 22.9 %collective-permute-start.6 = (f32[128,2048]{1,0:T(8,128)S(1)}, f32[128,2048]{1,0:T(8,128)S(1)}, u32[]{:S(2)}, u32[]{:S(2)}) collective-permute-start(f32[128,2048]{1,0:T(8,128)S(1)} %get-tuple-element.46), channel_id=1, source_target_pairs={{0,4},{4,8},{8,12},{12,16},{16,20},{20,24},{24,28},{1,5},{5,9},{9,... | collective-permute-start | bytes 3145736 | tf_op jit(solution)/shard_map/ppermute | solution.py:472
  32.9 19.3 %collective-permute-start.3 = (f32[8,128,128]{2,1,0:T(8,128)S(1)}, f32[8,128,128]{2,1,0:T(8,128)S(1)}, u32[]{:S(2)}, u32[]{:S(2)}) collective-permute-start(f32[8,128,128]{2,1,0:T(8,128)S(1)} %message.1.refs_0_), channel_id=1, source_target_pairs={{0,16},{4,12},{8,24},{12,4},{16,0},{20,28},{24,8},{28,20},{1,17},{... | collective-permute-start | bytes 1572872 | tf_op jit(solution)/shard_map/ppermute | solution.py:358
  52.4 5.3 %collective-permute-start.5 = (f32[8,128,128]{2,1,0:T(8,128)S(1)}, f32[8,128,128]{2,1,0:T(8,128)S(1)}, u32[]{:S(2)}, u32[]{:S(2)}) collective-permute-start(f32[8,128,128]{2,1,0:T(8,128)S(1)} %get-tuple-element.39), channel_id=1, source_target_pairs={{0,4},{4,0},{8,12},{12,8},{16,20},{20,16},{24,28},{28,24},{1,5},{5... | collective-permute-start | bytes 1572872 | tf_op jit(solution)/shard_map/ppermute | solution.py:350
  53.4 22.3 %collective-permute-start.7 = (f32[8,128]{1,0:T(8,128)S(1)}, f32[8,128]{1,0:T(8,128)S(1)}, u32[]{:S(2)}, u32[]{:S(2)}) collective-permute-start(f32[8,128]{1,0:T(8,128)S(1)} %get-tuple-element.48._.refs_2_), channel_id=1, source_target_pairs={{0,1},{1,0},{2,3},{3,2},{4,5},{5,4},{6,7},{7,6},{8,9},{9,8},{10,11... | collective-permute-start | bytes 12296 | tf_op jit(solution)/shard_map/ppermute | solution.py:350
  54.2 21.4 %collective-permute-start.8 = (f32[8,128]{1,0:T(8,128)S(1)}, f32[8,128]{1,0:T(8,128)S(1)}, u32[]{:S(2)}, u32[]{:S(2)}) collective-permute-start(f32[8,128]{1,0:T(8,128)S(1)} %get-tuple-element.48._.refs_2_), channel_id=1, source_target_pairs={{0,2},{1,3},{2,0},{3,1},{4,6},{5,7},{6,4},{7,5},{8,10},{9,11},{10,... | collective-permute-start | bytes 12296 | tf_op jit(solution)/shard_map/ppermute | solution.py:350
  56.8 18.9 %collective-permute-start.9 = (f32[8,128]{1,0:T(8,128)S(1)}, f32[8,128]{1,0:T(8,128)S(1)}, u32[]{:S(2)}, u32[]{:S(2)}) collective-permute-start(f32[8,128]{1,0:T(8,128)S(1)} %get-tuple-element.48._.refs_2_), channel_id=1, source_target_pairs={{0,3},{1,2},{2,1},{3,0},{4,7},{5,6},{6,5},{7,4},{8,11},{9,10},{10,... | collective-permute-start | bytes 12296 | tf_op jit(solution)/shard_map/ppermute | solution.py:350

commit v6 on v5

--- a/solution.py
+++ b/solution.py
@@ -80,22 +80,7 @@
     return pl.ds(pl.multiple_of(head * width, width), count * width)
 
 
-def tail_kernel(k_ref, low_ref, high_ref, sems):
-    rows, width = k_ref.shape
-    middle = width // 2
-    copies = [
-        pltpu.make_async_copy(
-            k_ref.at[pl.ds(rows - WINDOW, WINDOW), pl.ds(i * middle, middle)], target, sems.at[i]
-        )
-        for i, target in enumerate((low_ref, high_ref))
-    ]
-    for copy in copies:
-        copy.start()
-    for copy in copies:
-        copy.wait()
-
-
-def load_kernel(q_hbm, q_ref, sems):
+def load_kernel(q_hbm, _, q_ref, sems):
     width = q_ref.shape[1] // sems.shape[0]
     copies = []
     for i in range(sems.shape[0]):
@@ -107,11 +92,15 @@
         copy.wait()
 
 
-def chip_kernel(keep_ref, beside_ref, _, out_ref):
+def pass_kernel(*_):
+    pass
+
+
+def chip_kernel(keep_ref, beside_ref, _, out_ref, __):
     out_ref[...] = keep_ref[...] + beside_ref[...]
 
 
-def totals_kernel(k_hbm, v_hbm, keep_ref, send_ref, half_ref, k_ref, v_ref, tail_v_ref, sems):
+def totals_kernel(k_hbm, v_hbm, keep_ref, send_ref, half_ref, k_ref, v_ref, tail_k_ref, tail_v_ref, sems):
     core = lax.axis_index("ctx") % 2
     rows, width = k_ref.shape
     middle = rows // 2
@@ -147,6 +136,7 @@
             keep_ref[pair] = jnp.where(core == 0, states[0], states[1])
             send_ref[pair] = jnp.where(core == 0, states[1], states[0])
         columns = head_columns(group, 1, GROUP * HD)
+        tail_k_ref[:, columns] = k_ref[rows - WINDOW :, columns]
         tail_v_ref[:, columns] = v_ref[rows - WINDOW :, columns]
 
 
@@ -162,8 +152,7 @@
 
 
 def local_kernel(begin, extra, gain_ref, q_ref, k_ref, v_ref, *refs):
-    a_ref, b_ref, sum_ref = refs[extra : extra + 3]
-    square_ref = refs[-1]
+    a_ref, b_ref, sum_ref, square_ref = refs[extra:]
     lower = lower_mask()
     below = jnp.where(lower, 1.0, 0.0).astype(BF16)
     above = jnp.where(lower, 0.0, 1.0).astype(BF16)
@@ -262,18 +251,18 @@
     sums_ref[...] = jnp.where(row == 0, sum(ref[...] for ref in sum_refs), sums)
 
 
-def first_weights_kernel(gain_ref, q_ref, k_ref, v_ref, low_ref, high_ref, weights_ref, out_ref):
+def first_weights_kernel(gain_ref, q_ref, k_ref, v_ref, tail_ref, weights_ref, out_ref):
     lower = lower_mask()
     reachable = jnp.logical_or(lower, lax.axis_index("ctx") > 0)
     top = slice(0, WINDOW)
-    count = low_ref.shape[1] // HD
-    for part, tail_ref in enumerate((low_ref, high_ref)):
+    count = tail_ref.shape[1] // (2 * HD)
+    for part in range(2):
         scores = []
         for j in range(count):
             columns = slice((part * count + j) * HD, (part * count + j + 1) * HD)
             qq = side(*halves(q_ref[top, columns]))
             now = folded(dot_rows(qq, wide_keys(*halves(k_ref[top, columns]))))
-            before = folded(dot_rows(qq, wide_keys(*halves(tail_ref[:, j * HD : (j + 1) * HD]))))
+            before = folded(dot_rows(qq, wide_keys(*halves(tail_ref[:, columns]))))
             scores.append(jnp.where(reachable, jnp.where(lower, now, before), -jnp.inf))
         for j in range(count):
             head = part * count + j
@@ -287,7 +276,7 @@
             weights_ref[:, 2 * head * HD : 2 * (head + 1) * HD] = side(*halves(jnp.where(lower, 0.0, weights)))
 
 
-def first_values_kernel(weights_ref, now_ref, tail_v_ref, a_ref, sums_ref):
+def first_values_kernel(weights_ref, now_ref, tail_v_ref, _, a_ref, sums_ref):
     square = jnp.zeros((WINDOW, HD), F32)
     for j in range(now_ref.shape[1] // HD):
         columns = slice(j * HD, (j + 1) * HD)
@@ -304,9 +293,17 @@
     return 1.0 / jnp.sqrt(total / (HEADS * HD) + EPS)
 
 
-def scale_kernel(count, sums_ref, _, *refs):
+def added(refs):
+    total = refs[0][...]
+    for ref in refs[1:]:
+        total = total + ref[...]
+    return total
+
+
+def scale_kernel(count, parts, _, *refs):
+    sums, refs = refs[:parts], refs[parts:]
     a_refs, b_refs, (out_hbm, out_ref, sems) = refs[:count], refs[count : 2 * count], refs[2 * count :]
-    inverse = inverse_norm(jnp.sum(sums_ref[...], axis=0)).T
+    inverse = inverse_norm(added(sums)).T
     copies = []
     for n in range(out_ref.shape[0] // WINDOW):
         held = slice(n * WINDOW, (n + 1) * WINDOW)
@@ -324,13 +321,11 @@
         copy.wait()
 
 
-def first_scale_kernel(count, parts, sums_ref, a_ref, _, *refs):
-    b_refs, sums, (out_hbm, out_ref, sems) = refs[:count], refs[count : count + parts], refs[count + parts :]
-    total = sums[0][...]
-    for part in sums[1:]:
-        total = total + part[...]
-    inverse_a = inverse_norm(total).T[:, 0:1]
-    inverse_b = inverse_norm(jnp.sum(sums_ref[:, :, :WINDOW], axis=0)).T[:, 1:2]
+def first_scale_kernel(count, parts, a_ref, _, *refs):
+    b_refs, refs = refs[:count], refs[count:]
+    sums, first_sums, (out_hbm, out_ref, sems) = refs[:parts], refs[parts : 2 * parts], refs[2 * parts :]
+    inverse_a = inverse_norm(added(first_sums)).T[:, 0:1]
+    inverse_b = inverse_norm(added(sums)[:, :WINDOW]).T[:, 1:2]
     copies = []
     for n in range(sems.shape[0]):
         rows = slice(n * WINDOW // sems.shape[0], (n + 1) * WINDOW // sems.shape[0])
@@ -350,6 +345,10 @@
     return lax.ppermute(block, axis, [(i, i ^ bit) for i in range(lax.axis_size(axis))])
 
 
+def everyone(block, axis):
+    return [block] + [swap(block, axis, bits) for bits in range(1, lax.axis_size(axis))]
+
+
 def first_phase(chip):
     return lax.ppermute(chip, "ctx", [(i, i ^ (2 if i % 2 == 0 else 4)) for i in range(8)])
 
@@ -384,108 +383,99 @@
     def array(*shape, dtype=F32):
         return jax.ShapeDtypeStruct(shape, dtype)
 
-    def call(kernel, name, flops, moved, **kwargs):
+    def call(kernel, name, **kwargs):
         return pl.pallas_call(
             kernel,
             name=name,
             compiler_params=pltpu.CompilerParams(vmem_limit_bytes=VMEM_BYTES),
-            cost_estimate=pl.CostEstimate(flops=flops, bytes_accessed=moved, transcendentals=0),
+            cost_estimate=pl.CostEstimate(flops=0, bytes_accessed=0, transcendentals=0),
             **kwargs,
         )
 
-    size = rows * width * 4
-    unit = 2 * rows * width * HD
     packed = array(heads // 2, HD, HD)
     first_tile = array(WINDOW, width)
     dma = pltpu.SemaphoreType.DMA
-    tail_low, tail_high = call(
-        tail_kernel,
-        "tail",
-        0,
-        size // 2,
-        in_specs=[anywhere],
-        out_shape=[array(WINDOW, width // 2)] * 2,
-        scratch_shapes=[dma((2,))],
-    )(keys)
-    route = [(i, i + 1) for i in range(lax.axis_size("ctx") - 1)]
-    before_low = lax.ppermute(tail_low, "ctx", route)
-    before_high = lax.ppermute(tail_high, "ctx", route)
-
-    keep, send, half, held_k, held_v, tail_v = call(
+    keep, send, half, held_k, held_v, tail_k, tail_v = call(
         totals_kernel,
         "totals",
-        4 * unit,
-        2 * size,
         in_specs=[anywhere, anywhere],
-        out_shape=[packed, packed, array(heads, HD, HD), array(rows, width), array(rows, width), first_tile],
+        out_shape=[
+            packed,
+            packed,
+            array(heads, HD, HD),
+            array(rows, width),
+            array(rows, width),
+            first_tile,
+            first_tile,
+        ],
         scratch_shapes=[dma((2, heads // GROUP))],
     )(keys, values)
+    beside = swap(send, "ctx", 1)
+    chip, tail_k = call(
+        chip_kernel,
+        "chip",
+        in_specs=[vmem, vmem, anywhere],
+        out_specs=[vmem, anywhere],
+        out_shape=[packed, first_tile],
+        input_output_aliases={2: 1},
+    )(keep, beside, tail_k)
     held_q = call(
         load_kernel,
         "load",
-        0,
-        2 * size,
-        in_specs=[anywhere],
+        in_specs=[anywhere, anywhere],
         out_shape=array(rows, width),
         scratch_shapes=[dma((4,))],
-    )(queries)
-    beside = swap(send, "ctx", 1)
-    chip = call(
-        chip_kernel,
-        "chip",
-        0,
-        size // 4,
-        in_specs=[vmem, vmem, anywhere],
-        out_shape=packed,
-    )(keep, beside, held_q)
-
-    def local(begin, count, after, *passed):
+    )(queries, chip)
+    route = [(i, i + 1) for i in range(lax.axis_size("ctx") - 1)]
+    before_k = lax.ppermute(tail_k, "ctx", route)
+
+    def local(begin, count, after):
         taken = count * HD
+        after = [] if after is None else [after]
         return call(
-            functools.partial(local_kernel, begin, 1 + len(passed)),
+            functools.partial(local_kernel, begin, len(after)),
             "local",
-            0,
-            0,
-            in_specs=[smem, vmem, vmem, vmem] + [anywhere] * (1 + len(passed)),
-            out_specs=[vmem] * 3 + [anywhere] * len(passed),
-            out_shape=[array(rows, taken), array(rows, taken), array(8, rows)] + [first_tile] * len(passed),
+            in_specs=[smem, vmem, vmem, vmem] + [anywhere] * len(after),
+            out_shape=[array(rows, taken), array(rows, taken), array(8, rows)],
             scratch_shapes=[pltpu.VMEM((rows, HD), F32)],
-            input_output_aliases={5: 3} if passed else {},
-        )(head_gain, held_q, held_k, held_v, after, *passed)
+        )(head_gain, held_q, held_k, held_v, *after)
+
+    def pass_on(array_now, after):
+        return call(
+            pass_kernel,
+            "pass",
+            in_specs=[anywhere, anywhere],
+            out_specs=anywhere,
+            out_shape=array(*array_now.shape),
+            input_output_aliases={0: 0},
+        )(array_now, after)
 
     begin = heads * 3 // 4 // GROUP * GROUP
-    parts = [local(0, begin, before_low)]
+    parts = [local(0, begin, None)]
     message = None
     if lax.axis_size("ctx") == 8:
         first = first_phase(chip)
         message = call(
             message_kernel,
             "message",
-            0,
-            size // 4,
             in_specs=[vmem, vmem, anywhere],
             out_shape=packed,
         )(first, chip, parts[0][2])
-    *part, tail_v = local(begin, heads - begin, parts[0][2] if message is None else message, tail_v)
-    parts.append(part)
+    parts.append(local(begin, heads - begin, message))
     window, linear, window_sums = zip(*parts)
-    before_v = lax.ppermute(tail_v, "ctx", route)
+    before_v = lax.ppermute(pass_on(tail_v, window_sums[1]), "ctx", route)
     first_weights, first_now = call(
         first_weights_kernel,
         "first_weights",
-        4 * unit,
-        size,
-        in_specs=[smem] + [vmem] * 5,
+        in_specs=[smem] + [vmem] * 4,
         out_shape=[array(WINDOW, 2 * width, dtype=BF16), first_tile],
-    )(head_gain, held_q, held_k, held_v, before_low, before_high)
+    )(head_gain, held_q, held_k, held_v, before_k)
 
     if message is not None:
         second = second_phase(message)
         mine, other = call(
             prefix_kernel,
             "prefix",
-            0,
-            size // 2,
             in_specs=[vmem] * 4 + [anywhere],
             out_shape=[packed, packed],
         )(first, second, keep, beside, first_now)
@@ -499,42 +489,35 @@
     *linear, sums = call(
         functools.partial(earlier_kernel, len(parts)),
         "earlier",
-        3 * unit,
-        3 * size,
         in_specs=[smem] + [vmem] * (4 + 2 * len(parts)),
         out_shape=[array(*x.shape) for x in linear] + [array(8, rows)],
         scratch_shapes=[pltpu.VMEM((rows, HD), F32)],
     )(head_gain, half, mine, other, held_q, *linear, *window_sums)
-    sums = lax.all_gather(sums, "head")
+    sums = everyone(sums, "head")
     first_a, first_sums = call(
         first_values_kernel,
         "first_values",
-        unit,
-        size // 2,
+        in_specs=[vmem] * 3 + [anywhere],
         out_shape=[first_tile, array(8, WINDOW)],
-    )(first_weights, first_now, before_v)
-    first_sums = [first_sums] + [swap(first_sums, "head", bits) for bits in range(1, lax.axis_size("head"))]
+    )(first_weights, first_now, before_v, sums[0])
+    first_sums = everyone(first_sums, "head")
     out = call(
-        functools.partial(scale_kernel, len(parts)),
+        functools.partial(scale_kernel, len(parts), len(sums)),
         "scale",
-        unit // 64,
-        2 * size,
-        in_specs=[vmem, anywhere] + [vmem] * (2 * len(parts)),
+        in_specs=[anywhere] + [vmem] * (2 * len(parts) + len(sums)),
         out_specs=anywhere,
         out_shape=array(rows, width),
         scratch_shapes=[pltpu.VMEM((rows - WINDOW, width), F32), dma((rows // WINDOW - 1,))],
-    )(sums, first_sums[0], *window, *linear)
+    )(first_sums[0], *sums, *window, *linear)
     return call(
-        functools.partial(first_scale_kernel, len(parts), len(first_sums)),
+        functools.partial(first_scale_kernel, len(parts), len(sums)),
         "first_scale",
-        unit // 256,
-        size // 2,
-        in_specs=[vmem, vmem, anywhere] + [vmem] * (len(parts) + len(first_sums)),
+        in_specs=[vmem, anywhere] + [vmem] * (len(parts) + 2 * len(sums)),
         out_specs=anywhere,
         out_shape=array(rows, width),
         scratch_shapes=[pltpu.VMEM((WINDOW, width), F32), dma((4,))],
-        input_output_aliases={2: 0},
-    )(sums, first_a, out, *linear, *first_sums)
+        input_output_aliases={1: 0},
+    )(first_a, out, *linear, *sums, *first_sums)
 
 
 def solution(mesh):

time: 78.4 us -> 53.8 us (0.69); the launches traced: 76.9 us -> 53.6 us
  blocking collectives: 13.2 us -> 0 us
  waiting for transfers between devices: 23.1 us -> 12.4 us
  starting transfers between devices: 13.8 us -> 15.9 us
  Pallas kernels: 26.6 us -> 25.3 us
    ppermute x1, waiting for transfers between devices: 16.4 us -> 2.65 us  [second_phase(): lax.ppermute(message, 'ctx', [(i, i ^ (4 if i % 2 == 0 else 2)) for i in...]
    all_gather x1 -> x0, blocking collectives: 13.2 us -> none  [shards(): sums = lax.all_gather(sums, 'head')]
    ppermute x5 -> x8, waiting for transfers between devices: 0.01 us -> 5.43 us  [swap(): lax.ppermute(block, axis, [(i, i ^ bit) for i in range(lax.axis_size(axis...]
    ppermute x5 -> x8, starting transfers between devices: 4.54 us -> 9.57 us  [swap(): lax.ppermute(block, axis, [(i, i ^ bit) for i in range(lax.axis_size(axis...]
    ppermute x3 -> x2, starting transfers between devices: 7.62 us -> 3.97 us  [the longest x1 2.04 us: shards(): before_k = lax.ppermute(tail_k, 'ctx', route)]
    ppermute x3 -> x2, waiting for transfers between devices: 6.77 us -> 4.27 us  [the longest x1 2.38 us: shards(): before_k = lax.ppermute(tail_k, 'ctx', route)]
    pallas_call x13, Pallas kernels: 26.6 us -> 25.3 us  [the longest x2 8.94 us: local(): call(functools.partial(local_kernel, begin, len(after)), 'local', in_spec...]
  transfers between devices with their start and end apart: 10 -> 12, of which waited for: 2 -> 6; matrix products, arithmetic and copies ran while one was open for 0% -> 0% of each run, Pallas kernels for 28% -> 37%
where the time goes in v6:
time: 53.8 us; the launch traced here: 53.6 us
  Pallas kernels  25.3 us (47%)
  starting transfers between devices  15.9 us (30%)
  waiting for transfers between devices  12.4 us (23%)
    ppermute x8, starting transfers between devices, swap(): lax.ppermute(block, axis, [(i, i ^ bit) for i in range(lax.axis_size(axis...  9.57 us
    pallas_call x2, Pallas kernels, local(): call(functools.partial(local_kernel, begin, len(after)), 'local', in_spec...  8.94 us
    ppermute x8, waiting for transfers between devices, swap(): lax.ppermute(block, axis, [(i, i ^ bit) for i in range(lax.axis_size(axis...  5.43 us
    pallas_call x1, Pallas kernels, shards(): call(totals_kernel, 'totals', in_specs=[anywhere, anywhere], out_shape=[p...  4.16 us
    pallas_call x1, Pallas kernels, shards(): call(first_weights_kernel, 'first_weights', in_specs=[smem] + [vmem] * 4,...  2.85 us
    ppermute x1, waiting for transfers between devices, second_phase(): lax.ppermute(message, 'ctx', [(i, i ^ (4 if i % 2 == 0 else 2)) for i in...  2.65 us
    pallas_call x1, Pallas kernels, shards(): call(functools.partial(earlier_kernel, len(parts)), 'earlier', in_specs=[...  2.47 us
    ppermute x1, waiting for transfers between devices, shards(): before_k = lax.ppermute(tail_k, 'ctx', route)  2.38 us
  transfers between devices with their start and end apart: 12, of which 6 were waited for; matrix products, arithmetic and copies ran while one was open for 0% of the time, Pallas kernels for 37%

profile of v6, /device:TPU:4, one launch (start us, length us, event | category | flops | bytes accessed | tf_op | source)
XLA Modules:
  0.0 53.6 jit_solution(12148496499934845156)
XLA Ops:
  0.0 4.2 %totals.1 = (f32[8,128,128]{2,1,0:T(8,128)S(1)}, f32[8,128,128]{2,1,0:T(8,128)S(1)}, f32[16,128,128]{2,1,0:T(8,128)S(1)}, f32[512,2048]{1,0:T(8,128)S(1)}, f32[5...) custom-call(f32[512,2048]{1,0:T(8,128)} %k_hbm.1, f32[512,2048]{1,0:T(8,128)} %v_hbm.1), custom_call_target="tpu_custom_call" | custom-call | tf_op jit(solution)/shard_map/totals/pallas_call | solution.py:398
  4.2 1.9 %collective-permute-done.beside_ref = f32[8,128,128]{2,1,0:T(8,128)S(1)} collective-permute-done((f32[8,128,128]{2,1,0:T(8,128)S(1)}, f32[8,128,128]{2,1,0:T(8,128)S(1)}, u32[]{:S(2)}, u32[]{:S(2)}) %collective-permute-start) | collective-permute-done | bytes 524320 | tf_op jit(solution)/shard_map/ppermute | solution.py:345
  6.2 1.6 %collective-permute-start.2 = (f32[8,128,128]{2,1,0:T(8,128)S(1)}, f32[8,128,128]{2,1,0:T(8,128)S(1)}, u32[]{:S(2)}, u32[]{:S(2)}) collective-permute-start(f32[8,128,128]{2,1,0:T(8,128)S(1)} %get-tuple-element.32._.chip_ref), channel_id=1, source_target_pairs={{0,8},{4,20},{8,0},{12,28},{16,24},{20,4},{24,16},{28,12},{1,9},{5... | collective-permute-start | bytes 1572872 | tf_op jit(solution)/shard_map/ppermute | solution.py:353
  7.8 2.0 %collective-permute-start.1 = (f32[128,2048]{1,0:T(8,128)S(1)}, f32[128,2048]{1,0:T(8,128)S(1)}, u32[]{:S(2)}, u32[]{:S(2)}) collective-permute-start(f32[128,2048]{1,0:T(8,128)S(1)} %get-tuple-element.35), channel_id=1, source_target_pairs={{0,4},{4,8},{8,12},{12,16},{16,20},{20,24},{24,28},{1,5},{5,9},{9,... | collective-permute-start | bytes 3145736 | tf_op jit(solution)/shard_map/ppermute | solution.py:430
  9.8 2.2 %load.1.q_ref = f32[512,2048]{1,0:T(8,128)S(1)} custom-call(f32[512,2048]{1,0:T(8,128)} %q_hbm.1, f32[8,128,128]{2,1,0:T(8,128)S(1)} %get-tuple-element.32._.chip_ref), custom_call_target="tpu_custom_call" | custom-call | tf_op jit(solution)/shard_map/load/pallas_call | solution.py:422
  12.1 6.4 %local.2 = (f32[512,1536]{1,0:T(8,128)S(1)}, f32[512,1536]{1,0:T(8,128)S(1)}, f32[8,512]{1,0:T(8,128)S(1)}) custom-call(f32[2,16]{1,0:T(2,128)S(1)} %copy-done, f32[512,2048]{1,0:T(8,128)S(1)} %load.1.q_ref, f32[512,2048]{1,0:T(8,128)S(1)} %get-tuple-element.33.k_ref, f32[512,2048]{1,0:T(8,128)S(1)} %get-tuple-element.34.v_ref), custom_call_target="tpu_custom_call" | custom-call | tf_op jit(solution)/shard_map/local/pallas_call | solution.py:435
  18.6 0.8 %collective-permute-start.4 = (f32[8,128,128]{2,1,0:T(8,128)S(1)}, f32[8,128,128]{2,1,0:T(8,128)S(1)}, u32[]{:S(2)}, u32[]{:S(2)}) collective-permute-start(f32[8,128,128]{2,1,0:T(8,128)S(1)} %message.1.refs_0_), channel_id=1, source_target_pairs={{0,16},{4,12},{8,24},{12,4},{16,0},{20,28},{24,8},{28,20},{1,17},{... | collective-permute-start | bytes 1572872 | tf_op jit(solution)/shard_map/ppermute | solution.py:357
  19.4 2.5 %local.3 = (f32[512,512]{1,0:T(8,128)S(1)}, f32[512,512]{1,0:T(8,128)S(1)}, f32[8,512]{1,0:T(8,128)S(1)}) custom-call(f32[2,16]{1,0:T(2,128)S(1)} %copy-done, f32[512,2048]{1,0:T(8,128)S(1)} %load.1.q_ref, f32[512,2048]{1,0:T(8,128)S(1)} %get-tuple-element.33.k_ref, f32[512,2048]{1,0:T(8,128)S(1)} %get-tuple-element.34.v_ref, f32[8,128,128]{2,1,0:T(8,128)S(1)} %message.1.refs_0_), custom_call_target="tpu_custom_call" | custom-call | tf_op jit(solution)/shard_map/local/pallas_call | solution.py:435
  21.9 1.9 %collective-permute-start.3 = (f32[128,2048]{1,0:T(8,128)S(1)}, f32[128,2048]{1,0:T(8,128)S(1)}, u32[]{:S(2)}, u32[]{:S(2)}) collective-permute-start(f32[128,2048]{1,0:T(8,128)S(1)} %pass.1), channel_id=1, source_target_pairs={{0,4},{4,8},{8,12},{12,16},{16,20},{20,24},{24,28},{1,5},{5,9},{9,... | collective-permute-start | bytes 3145736 | tf_op jit(solution)/shard_map/ppermute | solution.py:466
  23.8 2.4 %collective-permute-done.1.tail_ref = f32[128,2048]{1,0:T(8,128)S(1)} collective-permute-done((f32[128,2048]{1,0:T(8,128)S(1)}, f32[128,2048]{1,0:T(8,128)S(1)}, u32[]{:S(2)}, u32[]{:S(2)}) %collective-permute-start.1) | collective-permute-done | bytes 1048608 | tf_op jit(solution)/shard_map/ppermute | solution.py:430
  26.2 2.9 %first_weights.1 = (bf16[128,4096]{1,0:T(8,128)(2,1)S(1)}, f32[128,2048]{1,0:T(8,128)S(1)}) custom-call(f32[2,16]{1,0:T(2,128)S(1)} %copy-done, f32[512,2048]{1,0:T(8,128)S(1)} %load.1.q_ref, f32[512,2048]{1,0:T(8,128)S(1)} %get-tuple-element.33.k_ref, f32[512,2048]{1,0:T(8,128)S(1)} %get-tuple-element.34.v_ref, f32[128,2048]{1,0:T(8,128)S(1)} %collective-permute-done.1.tail_ref), custom_call_target="tpu_custom_call" | custom-call | tf_op jit(solution)/shard_map/first_weights/pallas_call | solution.py:467
  29.1 2.7 %collective-permute-done.4.second_ref = f32[8,128,128]{2,1,0:T(8,128)S(1)} collective-permute-done((f32[8,128,128]{2,1,0:T(8,128)S(1)}, f32[8,128,128]{2,1,0:T(8,128)S(1)}, u32[]{:S(2)}, u32[]{:S(2)}) %collective-permute-start.4) | collective-permute-done | bytes 524320 | tf_op jit(solution)/shard_map/ppermute | solution.py:357
  32.0 1.9 %collective-permute-done.5.other_ref = f32[8,128,128]{2,1,0:T(8,128)S(1)} collective-permute-done((f32[8,128,128]{2,1,0:T(8,128)S(1)}, f32[8,128,128]{2,1,0:T(8,128)S(1)}, u32[]{:S(2)}, u32[]{:S(2)}) %collective-permute-start.5) | collective-permute-done | bytes 524320 | tf_op jit(solution)/shard_map/ppermute | solution.py:345
  33.9 2.5 %earlier.1 = (f32[512,1536]{1,0:T(8,128)S(1)}, f32[512,512]{1,0:T(8,128)S(1)}, f32[8,512]{1,0:T(8,128)S(1)}) custom-call(f32[2,16]{1,0:T(2,128)S(1)} %copy-done, f32[16,128,128]{2,1,0:T(8,128)S(1)} %get-tuple-element.41.half_ref, f32[8,128,128]{2,1,0:T(8,128)S(1)} %get-tuple-element.42.mine_ref, f32[8,128,128]{2,1,0:T(8,128)S(1)} %collective-permute-done.5.other_ref, ...), custom_call_target="tpu_custom_call" | custom-call | tf_op jit(solution)/shard_map/earlier/pallas_call | solution.py:489
  36.4 2.1 %collective-permute-start.6 = (f32[8,512]{1,0:T(8,128)S(1)}, f32[8,512]{1,0:T(8,128)S(1)}, u32[]{:S(2)}, u32[]{:S(2)}) collective-permute-start(f32[8,512]{1,0:T(8,128)S(1)} %get-tuple-element.46._.refs_0_.refs_2_), channel_id=1, source_target_pairs={{0,1},{1,0},{2,3},{3,2},{4,5},{5,4},{6,7},{7,6},{8,9},{9,8},{10,11... | collective-permute-start | bytes 49160 | tf_op jit(solution)/shard_map/ppermute | solution.py:345
  38.5 2.6 %collective-permute-start.7 = (f32[8,512]{1,0:T(8,128)S(1)}, f32[8,512]{1,0:T(8,128)S(1)}, u32[]{:S(2)}, u32[]{:S(2)}) collective-permute-start(f32[8,512]{1,0:T(8,128)S(1)} %get-tuple-element.46._.refs_0_.refs_2_), channel_id=1, source_target_pairs={{0,2},{1,3},{2,0},{3,1},{4,6},{5,7},{6,4},{7,5},{8,10},{9,11},{10,... | collective-permute-start | bytes 49160 | tf_op jit(solution)/shard_map/ppermute | solution.py:345
  41.1 1.9 %collective-permute-done.3.tail_v_ref = f32[128,2048]{1,0:T(8,128)S(1)} collective-permute-done((f32[128,2048]{1,0:T(8,128)S(1)}, f32[128,2048]{1,0:T(8,128)S(1)}, u32[]{:S(2)}, u32[]{:S(2)}) %collective-permute-start.3) | collective-permute-done | bytes 1048608 | tf_op jit(solution)/shard_map/ppermute | solution.py:466
  43.0 0.8 %first_values.1 = (f32[128,2048]{1,0:T(8,128)S(1)}, f32[8,128]{1,0:T(8,128)S(1)}) custom-call(bf16[128,4096]{1,0:T(8,128)(2,1)S(1)} %get-tuple-element.36.weights_ref, f32[128,2048]{1,0:T(8,128)S(1)} %get-tuple-element.37.refs_0_.now_ref, f32[128,2048]{1,0:T(8,128)S(1)} %collective-permute-done.3.tail_v_ref, f32[8,512]{1,0:T(8,128)S(1)} %get-tuple-element.46._.refs_0_.refs_2_), custom_call_target="tpu_custom_call" | custom-call | tf_op jit(solution)/shard_map/first_values/pallas_call | solution.py:497
  43.8 3.1 %collective-permute-start.10 = (f32[8,128]{1,0:T(8,128)S(1)}, f32[8,128]{1,0:T(8,128)S(1)}, u32[]{:S(2)}, u32[]{:S(2)}) collective-permute-start(f32[8,128]{1,0:T(8,128)S(1)} %get-tuple-element.48._.refs_6_), channel_id=1, source_target_pairs={{0,2},{1,3},{2,0},{3,1},{4,6},{5,7},{6,4},{7,5},{8,10},{9,11},{10,... | collective-permute-start | bytes 12296 | tf_op jit(solution)/shard_map/ppermute | solution.py:345
  47.0 1.3 %collective-permute-start.11 = (f32[8,128]{1,0:T(8,128)S(1)}, f32[8,128]{1,0:T(8,128)S(1)}, u32[]{:S(2)}, u32[]{:S(2)}) collective-permute-start(f32[8,128]{1,0:T(8,128)S(1)} %get-tuple-element.48._.refs_6_), channel_id=1, source_target_pairs={{0,3},{1,2},{2,1},{3,0},{4,7},{5,6},{6,5},{7,4},{8,11},{9,10},{10,... | collective-permute-start | bytes 12296 | tf_op jit(solution)/shard_map/ppermute | solution.py:345
  48.3 0.2 collective-permute-start.9
  48.6 2.2 %scale.1._ = f32[512,2048]{1,0:T(8,128)} custom-call(f32[8,128]{1,0:T(8,128)S(1)} %get-tuple-element.48._.refs_6_, f32[8,512]{1,0:T(8,128)S(1)} %get-tuple-element.46._.refs_0_.refs_2_, f32[8,512]{1,0:T(8,128)S(1)} %collective-permute-done.6.refs_1_.refs_3_, f32[8,512]{1,0:T(8,128)S(1)} %collective-permute-done.7.refs_2_.refs_4_, ...), custom_call_target="tpu_custom_call" | custom-call | tf_op jit(solution)/shard_map/scale/pallas_call | solution.py:504
  50.8 1.6 %collective-permute-done.11.refs_9_ = f32[8,128]{1,0:T(8,128)S(1)} collective-permute-done((f32[8,128]{1,0:T(8,128)S(1)}, f32[8,128]{1,0:T(8,128)S(1)}, u32[]{:S(2)}, u32[]{:S(2)}) %collective-permute-start.11) | collective-permute-done | bytes 4128 | tf_op jit(solution)/shard_map/ppermute | solution.py:345
  52.4 1.2 %first_scale.1 = f32[512,2048]{1,0:T(8,128)} custom-call(f32[128,2048]{1,0:T(8,128)S(1)} %get-tuple-element.47.a_ref, f32[512,2048]{1,0:T(8,128)} %scale.1._, f32[512,1536]{1,0:T(8,128)S(1)} %get-tuple-element.51.refs_6_.refs_0_, f32[512,512]{1,0:T(8,128)S(1)} %get-tuple-element.52.refs_7_.refs_1_, ...), custom_call_target="tpu_custom_call", output_to_operand_aliasing={{}: (1, {})} | custom-call | tf_op jit(solution)/shard_map/first_scale/pallas_call | solution.py:512
  (15 shorter events, 0.6 us)
Async XLA Ops:
  4.2 2.0 %collective-permute-start = (f32[8,128,128]{2,1,0:T(8,128)S(1)}, f32[8,128,128]{2,1,0:T(8,128)S(1)}, u32[]{:S(2)}, u32[]{:S(2)}) collective-permute-start(f32[8,128,128]{2,1,0:T(8,128)S(1)} %get-tuple-element.30), channel_id=1, source_target_pairs={{0,4},{4,0},{8,12},{12,8},{16,20},{20,16},{24,28},{28,24},{1,5},{5... | collective-permute-start | bytes 1572872 | tf_op jit(solution)/shard_map/ppermute | solution.py:345
  6.2 12.3 %collective-permute-start.2 = (f32[8,128,128]{2,1,0:T(8,128)S(1)}, f32[8,128,128]{2,1,0:T(8,128)S(1)}, u32[]{:S(2)}, u32[]{:S(2)}) collective-permute-start(f32[8,128,128]{2,1,0:T(8,128)S(1)} %get-tuple-element.32._.chip_ref), channel_id=1, source_target_pairs={{0,8},{4,20},{8,0},{12,28},{16,24},{20,4},{24,16},{28,12},{1,9},{5... | collective-permute-start | bytes 1572872 | tf_op jit(solution)/shard_map/ppermute | solution.py:353
  7.8 4.3 %copy-start = (f32[2,16]{1,0:T(2,128)S(1)}, f32[2,16]{1,0:T(2,128)}, u32[]{:S(2)}) copy-start(f32[2,16]{1,0:T(2,128)} %gain_ref.7) | copy-start | bytes 388
  7.8 18.4 %collective-permute-start.1 = (f32[128,2048]{1,0:T(8,128)S(1)}, f32[128,2048]{1,0:T(8,128)S(1)}, u32[]{:S(2)}, u32[]{:S(2)}) collective-permute-start(f32[128,2048]{1,0:T(8,128)S(1)} %get-tuple-element.35), channel_id=1, source_target_pairs={{0,4},{4,8},{8,12},{12,16},{16,20},{20,24},{24,28},{1,5},{5,9},{9,... | collective-permute-start | bytes 3145736 | tf_op jit(solution)/shard_map/ppermute | solution.py:430
  18.6 13.1 %collective-permute-start.4 = (f32[8,128,128]{2,1,0:T(8,128)S(1)}, f32[8,128,128]{2,1,0:T(8,128)S(1)}, u32[]{:S(2)}, u32[]{:S(2)}) collective-permute-start(f32[8,128,128]{2,1,0:T(8,128)S(1)} %message.1.refs_0_), channel_id=1, source_target_pairs={{0,16},{4,12},{8,24},{12,4},{16,0},{20,28},{24,8},{28,20},{1,17},{... | collective-permute-start | bytes 1572872 | tf_op jit(solution)/shard_map/ppermute | solution.py:357
  21.9 21.1 %collective-permute-start.3 = (f32[128,2048]{1,0:T(8,128)S(1)}, f32[128,2048]{1,0:T(8,128)S(1)}, u32[]{:S(2)}, u32[]{:S(2)}) collective-permute-start(f32[128,2048]{1,0:T(8,128)S(1)} %pass.1), channel_id=1, source_target_pairs={{0,4},{4,8},{8,12},{12,16},{16,20},{20,24},{24,28},{1,5},{5,9},{9,... | collective-permute-start | bytes 3145736 | tf_op jit(solution)/shard_map/ppermute | solution.py:466
  32.0 2.0 %collective-permute-start.5 = (f32[8,128,128]{2,1,0:T(8,128)S(1)}, f32[8,128,128]{2,1,0:T(8,128)S(1)}, u32[]{:S(2)}, u32[]{:S(2)}) collective-permute-start(f32[8,128,128]{2,1,0:T(8,128)S(1)} %get-tuple-element.43), channel_id=1, source_target_pairs={{0,4},{4,0},{8,12},{12,8},{16,20},{20,16},{24,28},{28,24},{1,5},{5... | collective-permute-start | bytes 1572872 | tf_op jit(solution)/shard_map/ppermute | solution.py:345
  36.4 11.9 %collective-permute-start.6 = (f32[8,512]{1,0:T(8,128)S(1)}, f32[8,512]{1,0:T(8,128)S(1)}, u32[]{:S(2)}, u32[]{:S(2)}) collective-permute-start(f32[8,512]{1,0:T(8,128)S(1)} %get-tuple-element.46._.refs_0_.refs_2_), channel_id=1, source_target_pairs={{0,1},{1,0},{2,3},{3,2},{4,5},{5,4},{6,7},{7,6},{8,9},{9,8},{10,11... | collective-permute-start | bytes 49160 | tf_op jit(solution)/shard_map/ppermute | solution.py:345
  38.5 10.0 %collective-permute-start.7 = (f32[8,512]{1,0:T(8,128)S(1)}, f32[8,512]{1,0:T(8,128)S(1)}, u32[]{:S(2)}, u32[]{:S(2)}) collective-permute-start(f32[8,512]{1,0:T(8,128)S(1)} %get-tuple-element.46._.refs_0_.refs_2_), channel_id=1, source_target_pairs={{0,2},{1,3},{2,0},{3,1},{4,6},{5,7},{6,4},{7,5},{8,10},{9,11},{10,... | collective-permute-start | bytes 49160 | tf_op jit(solution)/shard_map/ppermute | solution.py:345
  41.1 7.4 %collective-permute-start.8 = (f32[8,512]{1,0:T(8,128)S(1)}, f32[8,512]{1,0:T(8,128)S(1)}, u32[]{:S(2)}, u32[]{:S(2)}) collective-permute-start(f32[8,512]{1,0:T(8,128)S(1)} %get-tuple-element.46._.refs_0_.refs_2_), channel_id=1, source_target_pairs={{0,3},{1,2},{2,1},{3,0},{4,7},{5,6},{6,5},{7,4},{8,11},{9,10},{10,... | collective-permute-start | bytes 49160 | tf_op jit(solution)/shard_map/ppermute | solution.py:345
  43.8 6.9 %collective-permute-start.10 = (f32[8,128]{1,0:T(8,128)S(1)}, f32[8,128]{1,0:T(8,128)S(1)}, u32[]{:S(2)}, u32[]{:S(2)}) collective-permute-start(f32[8,128]{1,0:T(8,128)S(1)} %get-tuple-element.48._.refs_6_), channel_id=1, source_target_pairs={{0,2},{1,3},{2,0},{3,1},{4,6},{5,7},{6,4},{7,5},{8,10},{9,11},{10,... | collective-permute-start | bytes 12296 | tf_op jit(solution)/shard_map/ppermute | solution.py:345
  47.0 5.4 %collective-permute-start.11 = (f32[8,128]{1,0:T(8,128)S(1)}, f32[8,128]{1,0:T(8,128)S(1)}, u32[]{:S(2)}, u32[]{:S(2)}) collective-permute-start(f32[8,128]{1,0:T(8,128)S(1)} %get-tuple-element.48._.refs_6_), channel_id=1, source_target_pairs={{0,3},{1,2},{2,1},{3,0},{4,7},{5,6},{6,5},{7,4},{8,11},{9,10},{10,... | collective-permute-start | bytes 12296 | tf_op jit(solution)/shard_map/ppermute | solution.py:345
  48.3 4.1 %collective-permute-start.9 = (f32[8,128]{1,0:T(8,128)S(1)}, f32[8,128]{1,0:T(8,128)S(1)}, u32[]{:S(2)}, u32[]{:S(2)}) collective-permute-start(f32[8,128]{1,0:T(8,128)S(1)} %get-tuple-element.48._.refs_6_), channel_id=1, source_target_pairs={{0,1},{1,0},{2,3},{3,2},{4,5},{5,4},{6,7},{7,6},{8,9},{9,8},{10,11... | collective-permute-start | bytes 12296 | tf_op jit(solution)/shard_map/ppermute | solution.py:345

commit v7 on v6

v7 whole, which is shorter than its diff:
```python
import functools
import math

import jax
import jax.numpy as jnp
from jax import lax
from jax.experimental import pallas as pl
from jax.experimental.pallas import tpu as pltpu
from jax.sharding import PartitionSpec as P

HEADS = 64
HD = 128
WINDOW = 128
EPS = 1e-06
F32 = jnp.float32
BF16 = jnp.bfloat16
EXP2_SCALE = math.log2(math.e) / math.sqrt(HD)
VMEM_BYTES = 20 * 1024 * 1024
GROUP = 4


def halves(x):
    high = x.astype(BF16)
    low = (x - high.astype(F32)).astype(BF16)
    return high, low


def dot(a, b):
    return lax.dot_general(a, b, (((1,), (0,)), ((), ())), preferred_element_type=F32)


def dot_rows(a, b):
    return lax.dot_general(a, b, (((1,), (1,)), ((), ())), preferred_element_type=F32)


def dot_columns(a, b):
    return lax.dot_general(a, b, (((0,), (0,)), ((), ())), preferred_element_type=F32)


def side(a, b):
    return jnp.concatenate([a, b], axis=1)


def stack(a, b):
    return jnp.concatenate([a, b], axis=0)


def outer_state(k_high, k_low, v_high, v_low):
    grid = dot_columns(side(k_high, k_low), side(v_high, v_low))
    return grid[:HD, :HD] + (grid[:HD, HD:] + grid[HD:, :HD]) + grid[HD:, HD:]


def lower_mask():
    rows = lax.broadcasted_iota(jnp.int32, (WINDOW, WINDOW), 0)
    columns = lax.broadcasted_iota(jnp.int32, (WINDOW, WINDOW), 1)
    return rows >= columns


def row_sums(square):
    ones = jnp.ones((8, HD), BF16)
    high, low = halves(square)
    return dot_rows(ones, high) + dot_rows(ones, low)


def wide_keys(k_high, k_low):
    return stack(side(k_high, k_high), side(k_low, jnp.zeros_like(k_low)))


def wide_state(state):
    high, low = halves(state)
    return stack(side(high, low), side(high, jnp.zeros_like(high)))


def folded(wide):
    half = wide.shape[1] // 2
    return wide[:, :half] + wide[:, half:]


def head_columns(head, count=1, width=HD):
    return pl.ds(pl.multiple_of(head * width, width), count * width)


def first_head(part, heads):
    core = lax.axis_index("ctx") % 2
    return jnp.where(core == part, heads // 2, 0)


def column_copies(part, sources, targets, sems):
    begin = first_head(part, sources[0].shape[1] // HD) * HD
    width = GROUP * HD
    copies = []
    for group in range(targets[0].shape[1] // width):
        there = pl.ds(pl.multiple_of(begin + group * width, HD), width)
        here = pl.ds(group * width, width)
        copies.append(
            [
                pltpu.make_async_copy(source.at[:, there], target.at[:, here], sems.at[i, group])
                for i, (source, target) in enumerate(zip(sources, targets))
            ]
        )
    return copies


def totals_kernel(part, k_hbm, v_hbm, _, total_ref, half_ref, k_ref, v_ref, sems):
    middle = k_ref.shape[0] // 2
    copies = column_copies(part, (k_hbm, v_hbm), (k_ref, v_ref), sems)
    for group in copies:
        for copy in group:
            copy.start()
    for i, group in enumerate(copies):
        for copy in group:
            copy.wait()
        for head in range(i * GROUP, (i + 1) * GROUP):
            columns = slice(head * HD, (head + 1) * HD)
            k_high, k_low = halves(k_ref[:, columns])
            v_high, v_low = halves(v_ref[:, columns])
            first = outer_state(k_high[:middle], k_low[:middle], v_high[:middle], v_low[:middle])
            second = outer_state(k_high[middle:], k_low[middle:], v_high[middle:], v_low[middle:])
            half_ref[head] = first
            total_ref[head] = first + second


def chip_kernel(keep_ref, beside_ref, out_ref):
    out_ref[...] = keep_ref[...] + beside_ref[...]


def tail_kernel(first_ref, second_ref, _, tail_ref):
    rows, width = first_ref.shape
    for part, ref in enumerate((first_ref, second_ref)):
        begin = first_head(part, 2 * width // HD) * HD
        tail_ref[:, pl.ds(pl.multiple_of(begin, HD), width)] = ref[rows - WINDOW :, :]


def weights_of(scores):
    biggest = jnp.max(scores, axis=1, keepdims=True)
    weights = jnp.exp2((scores - biggest) * EXP2_SCALE)
    return weights, jnp.sum(weights, axis=1, keepdims=True)


def masked_pair(weights, below, above):
    high, low = halves(weights)
    return side(high * above, high * below), side(low * above, low * below)


def local_kernel(part, gain_ref, q_hbm, k_ref, v_ref, _, a_ref, b_ref, sum_ref, q_ref, square_ref, sems):
    lower = lower_mask()
    below = jnp.where(lower, 1.0, 0.0).astype(BF16)
    above = jnp.where(lower, 0.0, 1.0).astype(BF16)
    rows, width = a_ref.shape
    tiles = rows // WINDOW
    groups = width // (GROUP * HD)
    begin = first_head(part, 2 * width // HD)

    def load(group):
        there = pl.ds(pl.multiple_of((begin + group * GROUP) * HD, HD), GROUP * HD)
        here = head_columns(group, 1, GROUP * HD)
        return pltpu.make_async_copy(q_hbm.at[:, there], q_ref.at[:, here], sems.at[group])

    for group in range(groups):
        load(group).start()
    square_ref[...] = jnp.zeros_like(square_ref)

    def tile(n):
        return slice(n * WINDOW, (n + 1) * WINDOW)

    @pl.loop(0, groups)
    def _(group):
        load(group).wait()
        scores = []
        for j in range(GROUP):
            columns = head_columns(GROUP * group + j)
            qq = side(*halves(q_ref[:, columns]))
            k_high, k_low = halves(k_ref[:, columns])
            now, before = [], [None]
            for n in range(tiles):
                keys = wide_keys(k_high[tile(n)], k_low[tile(n)])
                found = folded(dot_rows(qq[n * WINDOW : min((n + 2) * WINDOW, rows)], keys))
                now.append(found[:WINDOW])
                before.append(found[WINDOW:])
            scores.append((now, before))
        for j in range(GROUP):
            head = GROUP * group + j
            columns = head_columns(head)
            vv = side(*halves(v_ref[:, columns]))
            now, before = scores[j]
            gain_a = gain_ref[0, begin + head]
            for n in range(tiles):
                inner_high, inner_low = halves(jnp.where(lower, now[n], 0.0))
                if n == 0:
                    wide = dot(stack(inner_high, inner_low), vv[tile(0)])
                    b_ref[tile(0), columns] = folded(wide[:WINDOW]) + wide[WINDOW:, :HD]
                    a_ref[tile(0), columns] = jnp.zeros((WINDOW, HD), F32)
                    continue
                weights, total = weights_of(jnp.where(lower, now[n], before[n]))
                pair_high, pair_low = masked_pair(weights, below, above)
                if n % 2:
                    before_high, before_low = halves(before[n])
                else:
                    before_high = before_low = jnp.zeros((WINDOW, HD), BF16)
                left = jnp.concatenate(
                    [pair_high, pair_low, side(before_high, inner_high), side(before_low, inner_low)], axis=0
                )
                wide = dot(left, vv[(n - 1) * WINDOW : (n + 1) * WINDOW])
                a = (folded(wide[tile(0)]) + wide[tile(1), :HD]) * (gain_a / total)
                a_ref[tile(n), columns] = a
                square_ref[tile(n), :] += a * a
                b_ref[tile(n), columns] = folded(wide[tile(2)]) + wide[tile(3), :HD]

    sum_ref[...] = row_sums(square_ref[...])


def message_kernel(first_ref, chip_ref, _, out_ref):
    index = lax.axis_index("ctx")
    core, x, y = index % 2, (index >> 1) % 2, index >> 2
    first = jnp.where((core == 0) | (y == 1), first_ref[...], 0.0)
    out_ref[...] = first + jnp.where((core == 0) | (x == 0), chip_ref[...], 0.0)


def prefix_kernel(first_ref, second_ref, keep_ref, beside_ref, mine_ref, other_ref):
    index = lax.axis_index("ctx")
    core, x, y = index % 2, (index >> 1) % 2, index >> 2
    use_first = jnp.where(core == 0, x, y) == 1
    use_second = (core == 1) & ((x == 1) | (y == 1)) | (core == 0) & (y == 1)
    earlier = jnp.where(use_first, first_ref[...], 0.0) + jnp.where(use_second, second_ref[...], 0.0)
    mine_ref[...] = earlier + jnp.where(core == 1, beside_ref[...], 0.0)
    other_ref[...] = earlier + jnp.where(core == 0, keep_ref[...], 0.0)


def earlier_kernel(gain_ref, _, *refs):
    state_refs, half_refs, q_refs, b_refs, sum_refs, out_refs = (refs[2 * i : 2 * i + 2] for i in range(6))
    sums_ref, square_ref = refs[12:]
    rows, width = b_refs[0].shape
    middle = rows // 2
    square_ref[...] = jnp.zeros_like(square_ref)
    for part in range(2):
        begin = first_head(part, 2 * width // HD)
        for head in range(width // HD):
            columns = slice(head * HD, (head + 1) * HD)
            state = state_refs[part][head]
            gain_b = gain_ref[1, begin + head]
            for span, held in ((slice(0, middle), state), (slice(middle, rows), state + half_refs[part][head])):
                qq = side(*halves(q_refs[part][span, columns]))
                b = gain_b * (b_refs[part][span, columns] + folded(dot(qq, wide_state(held))))
                out_refs[part][span, columns] = b
                square_ref[span, :] += b * b
    sums = row_sums(square_ref[...])
    row = lax.broadcasted_iota(jnp.int32, sums.shape, 0)
    sums_ref[...] = jnp.where(row == 0, sum(ref[...] for ref in sum_refs), sums)


def first_weights_kernel(gain_ref, *refs):
    q_refs, k_refs, v_refs = (refs[2 * i : 2 * i + 2] for i in range(3))
    tail_ref, weights_ref, out_ref = refs[6:]
    lower = lower_mask()
    reachable = jnp.logical_or(lower, lax.axis_index("ctx") > 0)
    top = slice(0, WINDOW)
    width = q_refs[0].shape[1]
    for part in range(2):
        begin = first_head(part, 2 * width // HD)
        scores = []
        for head in range(width // HD):
            columns = slice(head * HD, (head + 1) * HD)
            qq = side(*halves(q_refs[part][top, columns]))
            now = folded(dot_rows(qq, wide_keys(*halves(k_refs[part][top, columns]))))
            before = folded(dot_rows(qq, wide_keys(*halves(tail_ref[:, head_columns(begin + head)]))))
            scores.append(jnp.where(reachable, jnp.where(lower, now, before), -jnp.inf))
        for head in range(width // HD):
            columns = slice(head * HD, (head + 1) * HD)
            weights, total = weights_of(scores[head])
            weights = weights * (gain_ref[0, begin + head] / total)
            now_high, now_low = halves(jnp.where(lower, weights, 0.0))
            vv = side(*halves(v_refs[part][top, columns]))
            wide = dot(stack(now_high, now_low), vv)
            out_ref[:, part * width + head * HD : part * width + (head + 1) * HD] = (
                folded(wide[:WINDOW]) + wide[WINDOW:, :HD]
            )
            held = slice(2 * (part * width + head * HD), 2 * (part * width + (head + 1) * HD))
            weights_ref[:, held] = side(*halves(jnp.where(lower, 0.0, weights)))


def first_values_kernel(weights_ref, now_ref, tail_ref, _, a_ref, sums_ref):
    square = jnp.zeros((WINDOW, HD), F32)
    heads = now_ref.shape[1] // HD
    for part in range(2):
        begin = first_head(part, heads)
        for head in range(heads // 2):
            j = part * (heads // 2) + head
            columns = slice(j * HD, (j + 1) * HD)
            high = weights_ref[:, 2 * j * HD : (2 * j + 1) * HD]
            low = weights_ref[:, (2 * j + 1) * HD : 2 * (j + 1) * HD]
            wide = dot(stack(high, low), side(*halves(tail_ref[:, head_columns(begin + head)])))
            a = now_ref[:, columns] + (folded(wide[:WINDOW]) + wide[WINDOW:, :HD])
            a_ref[:, columns] = a
            square = square + a * a
    sums_ref[...] = row_sums(square)


def inverse_norm(total):
    return 1.0 / jnp.sqrt(total / (HEADS * HD) + EPS)


def added(refs):
    total = refs[0][...]
    for ref in refs[1:]:
        total = total + ref[...]
    return total


def write(part, rows, held, out_ref, out_hbm, sem):
    width = out_ref.shape[1] // 2
    begin = first_head(part, 2 * width // HD) * HD
    there = pl.ds(pl.multiple_of(begin, HD), width)
    copy = pltpu.make_async_copy(
        out_ref.at[held, pl.ds(part * width, width)], out_hbm.at[rows, there], sem
    )
    copy.start()
    return copy


def scale_kernel(parts, _, *refs):
    sums, refs = refs[:parts], refs[parts:]
    a_refs, b_refs, (out_hbm, out_ref, sems) = refs[:2], refs[2:4], refs[4:]
    inverse = inverse_norm(added(sums)).T
    width = a_refs[0].shape[1]
    copies = []
    for n in range(out_ref.shape[0] // WINDOW):
        held = slice(n * WINDOW, (n + 1) * WINDOW)
        rows = slice((n + 1) * WINDOW, (n + 2) * WINDOW)
        inverse_a, inverse_b = inverse[rows, 0:1], inverse[rows, 1:2]
        for part in range(2):
            columns = slice(part * width, (part + 1) * width)
            out_ref[held, columns] = a_refs[part][rows, :] * inverse_a + b_refs[part][rows, :] * inverse_b
            copies.append(write(part, rows, held, out_ref, out_hbm, sems.at[n, part]))
    for copy in copies:
        copy.wait()


def first_scale_kernel(parts, a_ref, _, *refs):
    b_refs, refs = refs[:2], refs[2:]
    sums, first_sums, (out_hbm, out_ref, sems) = refs[:parts], refs[parts : 2 * parts], refs[2 * parts :]
    inverse_a = inverse_norm(added(first_sums)).T[:, 0:1]
    inverse_b = inverse_norm(added(sums)[:, :WINDOW]).T[:, 1:2]
    width = b_refs[0].shape[1]
    copies = []
    pieces = sems.shape[0]
    for n in range(pieces):
        rows = slice(n * WINDOW // pieces, (n + 1) * WINDOW // pieces)
        for part in range(2):
            columns = slice(part * width, (part + 1) * width)
            out_ref[rows, columns] = (
                a_ref[rows, columns] * inverse_a[rows] + b_refs[part][rows, :] * inverse_b[rows]
            )
            copies.append(write(part, rows, rows, out_ref, out_hbm, sems.at[n, part]))
    for copy in copies:
        copy.wait()


def swap(block, axis, bit):
    return lax.ppermute(block, axis, [(i, i ^ bit) for i in range(lax.axis_size(axis))])


def everyone(block, axis):
    return [block] + [swap(block, axis, bits) for bits in range(1, lax.axis_size(axis))]


def first_phase(chip):
    return lax.ppermute(chip, "ctx", [(i, i ^ (2 if i % 2 == 0 else 4)) for i in range(8)])


def second_phase(message):
    return lax.ppermute(message, "ctx", [(i, i ^ (4 if i % 2 == 0 else 2)) for i in range(8)])


def doubled_prefix(chip):
    index = lax.axis_index("ctx")
    earlier = jnp.zeros_like(chip)
    running = chip
    bit = 2
    while bit < lax.axis_size("ctx"):
        partner = swap(running, "ctx", bit)
        earlier = earlier + jnp.where((index & bit) != 0, partner, 0.0)
        running = running + partner
        bit *= 2
    return earlier


def shards(queries, keys, values, head_gain):
    rows, width = queries.shape
    heads = head_gain.shape[1]
    queries, keys, values = (
        pltpu.with_memory_space_constraint(x, pltpu.HBM) for x in (queries, keys, values)
    )
    smem = pl.BlockSpec(memory_space=pltpu.SMEM)
    anywhere = pl.BlockSpec(memory_space=pl.ANY)
    vmem = pl.BlockSpec()

    def array(*shape, dtype=F32):
        return jax.ShapeDtypeStruct(shape, dtype)

    def call(kernel, name, **kwargs):
        return pl.pallas_call(
            kernel,
            name=name,
            compiler_params=pltpu.CompilerParams(vmem_limit_bytes=VMEM_BYTES),
            cost_estimate=pl.CostEstimate(flops=0, bytes_accessed=0, transcendentals=0),
            **kwargs,
        )

    packed = array(heads // 2, HD, HD)
    half = array(rows, width // 2)
    first_tile = array(WINDOW, width)
    dma = pltpu.SemaphoreType.DMA
    groups = heads // (2 * GROUP)

    def totals(part, after):
        return call(
            functools.partial(totals_kernel, part),
            "totals",
            in_specs=[anywhere] * 3,
            out_shape=[packed, packed, half, half],
            scratch_shapes=[dma((2, groups))],
        )(keys, values, after)

    def local(part, after):
        return call(
            functools.partial(local_kernel, part),
            "local",
            in_specs=[smem, anywhere, vmem, vmem, anywhere],
            out_shape=[half, half, array(8, rows), half],
            scratch_shapes=[pltpu.VMEM((rows, HD), F32), dma((groups,))],
        )(head_gain, queries, held_k[part], held_v[part], after)

    def tail(held, after):
        return call(
            tail_kernel, "tail", in_specs=[vmem, vmem, anywhere], out_shape=first_tile
        )(*held, after)

    route = [(i, i + 1) for i in range(lax.axis_size("ctx") - 1)]
    send, *held_0 = totals(0, queries)
    beside = swap(send, "ctx", 1)
    keep, *held_1 = totals(1, send)
    early, held_k, held_v = zip(held_0, held_1)
    chip = call(chip_kernel, "chip", in_specs=[vmem, vmem], out_shape=packed)(keep, beside)
    before_k = lax.ppermute(tail(held_k, chip), "ctx", route)
    local_0 = local(0, chip)
    message = local_0[2]
    if lax.axis_size("ctx") == 8:
        first = first_phase(chip)
        message = call(
            message_kernel,
            "message",
            in_specs=[vmem, vmem, anywhere],
            out_shape=packed,
        )(first, chip, message)
    window, linear, window_sums, held_q = zip(local_0, local(1, message))
    before_v = lax.ppermute(tail(held_v, window_sums[1]), "ctx", route)
    first_weights, first_now = call(
        first_weights_kernel,
        "first_weights",
        in_specs=[smem] + [vmem] * 7,
        out_shape=[array(WINDOW, 2 * width, dtype=BF16), first_tile],
    )(head_gain, *held_q, *held_k, *held_v, before_k)

    if lax.axis_size("ctx") == 8:
        second = second_phase(message)
        mine, other = call(
            prefix_kernel,
            "prefix",
            out_shape=[packed, packed],
        )(first, second, keep, beside)
    else:
        earlier = doubled_prefix(chip)
        core = lax.axis_index("ctx") % 2
        mine = earlier + jnp.where(core == 1, beside, 0.0)
        other = earlier + jnp.where(core == 0, keep, 0.0)
    other = swap(other, "ctx", 1)

    *linear, sums = call(
        earlier_kernel,
        "earlier",
        in_specs=[smem, anywhere] + [vmem] * 10,
        out_shape=[half, half, array(8, rows)],
        scratch_shapes=[pltpu.VMEM((rows, HD), F32)],
    )(head_gain, first_now, other, mine, *early, *held_q, *linear, *window_sums)
    sums = everyone(sums, "head")
    first_a, first_sums = call(
        first_values_kernel,
        "first_values",
        in_specs=[vmem] * 3 + [anywhere],
        out_shape=[first_tile, array(8, WINDOW)],
    )(first_weights, first_now, before_v, sums[0])
    first_sums = everyone(first_sums, "head")
    out = call(
        functools.partial(scale_kernel, len(sums)),
        "scale",
        in_specs=[anywhere] + [vmem] * (4 + len(sums)),
        out_specs=anywhere,
        out_shape=array(rows, width),
        scratch_shapes=[pltpu.VMEM((rows - WINDOW, width), F32), dma((rows // WINDOW - 1, 2))],
    )(first_sums[0], *sums, *window, *linear)
    return call(
        functools.partial(first_scale_kernel, len(sums)),
        "first_scale",
        in_specs=[vmem, anywhere] + [vmem] * (2 + 2 * len(sums)),
        out_specs=anywhere,
        out_shape=array(rows, width),
        scratch_shapes=[pltpu.VMEM((WINDOW, width), F32), dma((4, 2))],
        input_output_aliases={1: 0},
    )(first_a, out, *linear, *sums, *first_sums)


def solution(mesh):
    in_specs = (P("ctx", "head"), P("ctx", "head"), P("ctx", "head"), P(None, "head"))
    out_specs = P("ctx", "head")
    return jax.shard_map(shards, mesh=mesh, in_specs=in_specs, out_specs=out_specs, check_vma=False)
```

time: 53.8 us -> 53.9 us (level)
  waiting for transfers between devices: 12.4 us -> 9.91 us
  Pallas kernels: 25.3 us -> 27.4 us
    ppermute x8, waiting for transfers between devices: 5.43 us -> 1.71 us  [swap(): lax.ppermute(block, axis, [(i, i ^ bit) for i in range(lax.axis_size(axis...]
    ppermute x2, waiting for transfers between devices: 4.27 us -> 1.07 us  [the longest x1 1.07 us: shards(): before_v = lax.ppermute(tail(held_v, window_sums[1]), 'ctx', route)]
    ppermute x1, waiting for transfers between devices: 0.01 us -> 2.46 us  [first_phase(): lax.ppermute(chip, 'ctx', [(i, i ^ (2 if i % 2 == 0 else 4)) for i in ran...]
    pallas_call x11 -> x12, Pallas kernels: 24.3 us -> 26.4 us  [the longest x2 11.6 us: local(): call(functools.partial(local_kernel, part), 'local', in_specs=[smem, anyw...]
    ppermute x1, waiting for transfers between devices: 2.65 us -> 4.67 us  [second_phase(): lax.ppermute(message, 'ctx', [(i, i ^ (4 if i % 2 == 0 else 2)) for i in...]
  transfers between devices with their start and end apart: 12 -> 12, of which waited for: 6 -> 4; matrix products, arithmetic and copies ran while one was open for 0% -> 0% of each run, Pallas kernels for 37% -> 43%
where the time goes in v7:
time: 53.9 us; the launch traced here: 53.6 us
  Pallas kernels  27.4 us (51%)
  starting transfers between devices  16 us (30%)
  waiting for transfers between devices  9.91 us (18%)
    pallas_call x2, Pallas kernels, local(): call(functools.partial(local_kernel, part), 'local', in_specs=[smem, anyw...  11.6 us
    ppermute x8, starting transfers between devices, swap(): lax.ppermute(block, axis, [(i, i ^ bit) for i in range(lax.axis_size(axis...  9.48 us
    pallas_call x2, Pallas kernels, totals(): call(functools.partial(totals_kernel, part), 'totals', in_specs=[anywhere...  5.75 us
    ppermute x1, waiting for transfers between devices, second_phase(): lax.ppermute(message, 'ctx', [(i, i ^ (4 if i % 2 == 0 else 2)) for i in...  4.67 us
    pallas_call x1, Pallas kernels, shards(): call(first_weights_kernel, 'first_weights', in_specs=[smem] + [vmem] * 7,...  2.77 us
    ppermute x1, waiting for transfers between devices, first_phase(): lax.ppermute(chip, 'ctx', [(i, i ^ (2 if i % 2 == 0 else 4)) for i in ran...  2.46 us
    pallas_call x1, Pallas kernels, shards(): call(earlier_kernel, 'earlier', in_specs=[smem, anywhere] + [vmem] * 10,...  2.42 us
    pallas_call x1, Pallas kernels, shards(): call(functools.partial(scale_kernel, len(sums)), 'scale', in_specs=[anywh...  2.19 us
  transfers between devices with their start and end apart: 12, of which 4 were waited for; matrix products, arithmetic and copies ran while one was open for 0% of the time, Pallas kernels for 43%

profile of v7, /device:TPU:4, one launch (start us, length us, event | category | flops | bytes accessed | tf_op | source)
XLA Modules:
  0.0 53.6 jit_solution(9251674902645234840)
XLA Ops:
  0.0 2.9 %totals.2 = (f32[8,128,128]{2,1,0:T(8,128)S(1)}, f32[8,128,128]{2,1,0:T(8,128)S(1)}, f32[512,1024]{1,0:T(8,128)S(1)}, f32[512,1024]{1,0:T(8,128)S(1)}) custom-call(f32[512,2048]{1,0:T(8,128)} %k_hbm.3, f32[512,2048]{1,0:T(8,128)} %v_hbm.3, f32[512,2048]{1,0:T(8,128)} %q_hbm.3), custom_call_target="tpu_custom_call" | custom-call | tf_op jit(solution)/shard_map/totals/pallas_call | solution.py:416
  3.0 2.9 %totals.3 = (f32[8,128,128]{2,1,0:T(8,128)S(1)}, f32[8,128,128]{2,1,0:T(8,128)S(1)}, f32[512,1024]{1,0:T(8,128)S(1)}, f32[512,1024]{1,0:T(8,128)S(1)}) custom-call(f32[512,2048]{1,0:T(8,128)} %k_hbm.3, f32[512,2048]{1,0:T(8,128)} %v_hbm.3, f32[8,128,128]{2,1,0:T(8,128)S(1)} %get-tuple-element.32._), custom_call_target="tpu_custom_call" | custom-call | tf_op jit(solution)/shard_map/totals/pallas_call | solution.py:416
  5.9 1.6 %collective-permute-start.1 = (f32[8,128,128]{2,1,0:T(8,128)S(1)}, f32[8,128,128]{2,1,0:T(8,128)S(1)}, u32[]{:S(2)}, u32[]{:S(2)}) collective-permute-start(f32[8,128,128]{2,1,0:T(8,128)S(1)} %chip.1._.chip_ref), channel_id=1, source_target_pairs={{0,8},{4,20},{8,0},{12,28},{16,24},{20,4},{24,16},{28,12},{1,9},{5... | collective-permute-start | bytes 1572872 | tf_op jit(solution)/shard_map/ppermute | solution.py:367
  7.6 1.9 %collective-permute-start.2 = (f32[128,2048]{1,0:T(8,128)S(1)}, f32[128,2048]{1,0:T(8,128)S(1)}, u32[]{:S(2)}, u32[]{:S(2)}) collective-permute-start(f32[128,2048]{1,0:T(8,128)S(1)} %tail.2), channel_id=1, source_target_pairs={{0,4},{4,8},{8,12},{12,16},{16,20},{20,24},{24,28},{1,5},{5,9},{9,... | collective-permute-start | bytes 3145736 | tf_op jit(solution)/shard_map/ppermute | solution.py:444
  9.5 5.8 %local.2 = (f32[512,1024]{1,0:T(8,128)S(1)}, f32[512,1024]{1,0:T(8,128)S(1)}, f32[8,512]{1,0:T(8,128)S(1)}, f32[512,1024]{1,0:T(8,128)S(1)}) custom-call(f32[2,16]{1,0:T(2,128)S(1)} %copy-done, f32[512,2048]{1,0:T(8,128)} %q_hbm.3, f32[512,1024]{1,0:T(8,128)S(1)} %get-tuple-element.30.k_ref.first_ref.refs_2_, ...), custom_call_target="tpu_custom_call" | custom-call | tf_op jit(solution)/shard_map/local/pallas_call | solution.py:425
  15.3 2.5 %collective-permute-done.1.first_ref = f32[8,128,128]{2,1,0:T(8,128)S(1)} collective-permute-done((f32[8,128,128]{2,1,0:T(8,128)S(1)}, f32[8,128,128]{2,1,0:T(8,128)S(1)}, u32[]{:S(2)}, u32[]{:S(2)}) %collective-permute-start.1) | collective-permute-done | bytes 524320 | tf_op jit(solution)/shard_map/ppermute | solution.py:367
  17.8 0.1 message.1._
  17.9 1.0 %collective-permute-start.4 = (f32[8,128,128]{2,1,0:T(8,128)S(1)}, f32[8,128,128]{2,1,0:T(8,128)S(1)}, u32[]{:S(2)}, u32[]{:S(2)}) collective-permute-start(f32[8,128,128]{2,1,0:T(8,128)S(1)} %message.1._), channel_id=1, source_target_pairs={{0,16},{4,12},{8,24},{12,4},{16,0},{20,28},{24,8},{28,20},{1,17},{... | collective-permute-start | bytes 1572872 | tf_op jit(solution)/shard_map/ppermute | solution.py:371
  18.9 5.8 %local.3 = (f32[512,1024]{1,0:T(8,128)S(1)}, f32[512,1024]{1,0:T(8,128)S(1)}, f32[8,512]{1,0:T(8,128)S(1)}, f32[512,1024]{1,0:T(8,128)S(1)}) custom-call(f32[2,16]{1,0:T(2,128)S(1)} %copy-done, f32[512,2048]{1,0:T(8,128)} %q_hbm.3, f32[512,1024]{1,0:T(8,128)S(1)} %get-tuple-element.35.k_ref.second_ref.refs_3_, ...), custom_call_target="tpu_custom_call" | custom-call | tf_op jit(solution)/shard_map/local/pallas_call | solution.py:425
  24.7 0.1 tail.3
  24.8 2.1 %collective-permute-start.3 = (f32[128,2048]{1,0:T(8,128)S(1)}, f32[128,2048]{1,0:T(8,128)S(1)}, u32[]{:S(2)}, u32[]{:S(2)}) collective-permute-start(f32[128,2048]{1,0:T(8,128)S(1)} %tail.3), channel_id=1, source_target_pairs={{0,4},{4,8},{8,12},{12,16},{16,20},{20,24},{24,28},{1,5},{5,9},{9,... | collective-permute-start | bytes 3145736 | tf_op jit(solution)/shard_map/ppermute | solution.py:456
  26.9 4.7 %collective-permute-done.4.second_ref = f32[8,128,128]{2,1,0:T(8,128)S(1)} collective-permute-done((f32[8,128,128]{2,1,0:T(8,128)S(1)}, f32[8,128,128]{2,1,0:T(8,128)S(1)}, u32[]{:S(2)}, u32[]{:S(2)}) %collective-permute-start.4) | collective-permute-done | bytes 524320 | tf_op jit(solution)/shard_map/ppermute | solution.py:371
  31.5 0.2 prefix.1
  31.9 2.8 %first_weights.1 = (bf16[128,4096]{1,0:T(8,128)(2,1)S(1)}, f32[128,2048]{1,0:T(8,128)S(1)}) custom-call(f32[2,16]{1,0:T(2,128)S(1)} %copy-done, f32[512,1024]{1,0:T(8,128)S(1)} %get-tuple-element.34.refs_0_.refs_4_, f32[512,1024]{1,0:T(8,128)S(1)} %get-tuple-element.38.refs_1_.refs_5_, f32[512,1024]{1,0:T(8,128)S(1)} %get-tuple-element.30.k_ref.first_ref.refs_2_, ...), custom_call_target="tpu_custom_call" | custom-call | tf_op jit(solution)/shard_map/first_weights/pallas_call | solution.py:457
  34.6 2.4 %earlier.1 = (f32[512,1024]{1,0:T(8,128)S(1)}, f32[512,1024]{1,0:T(8,128)S(1)}, f32[8,512]{1,0:T(8,128)S(1)}) custom-call(f32[2,16]{1,0:T(2,128)S(1)} %copy-done, f32[128,2048]{1,0:T(8,128)S(1)} %get-tuple-element.40._.now_ref, f32[8,128,128]{2,1,0:T(8,128)S(1)} %collective-permute-done.5.refs_0_, f32[8,128,128]{2,1,0:T(8,128)S(1)} %get-tuple-element.43.refs_1_, ...), custom_call_target="tpu_custom_call" | custom-call | tf_op jit(solution)/shard_map/earlier/pallas_call | solution.py:478
  37.1 4.0 %collective-permute-start.8 = (f32[8,512]{1,0:T(8,128)S(1)}, f32[8,512]{1,0:T(8,128)S(1)}, u32[]{:S(2)}, u32[]{:S(2)}) collective-permute-start(f32[8,512]{1,0:T(8,128)S(1)} %get-tuple-element.48._.refs_0_.refs_2_), channel_id=1, source_target_pairs={{0,3},{1,2},{2,1},{3,0},{4,7},{5,6},{6,5},{7,4},{8,11},{9,10},{10,... | collective-permute-start | bytes 49160 | tf_op jit(solution)/shard_map/ppermute | solution.py:359
  41.1 0.6 %collective-permute-start.6 = (f32[8,512]{1,0:T(8,128)S(1)}, f32[8,512]{1,0:T(8,128)S(1)}, u32[]{:S(2)}, u32[]{:S(2)}) collective-permute-start(f32[8,512]{1,0:T(8,128)S(1)} %get-tuple-element.48._.refs_0_.refs_2_), channel_id=1, source_target_pairs={{0,1},{1,0},{2,3},{3,2},{4,5},{5,4},{6,7},{7,6},{8,9},{9,8},{10,11... | collective-permute-start | bytes 49160 | tf_op jit(solution)/shard_map/ppermute | solution.py:359
  41.7 1.1 %collective-permute-done.3.tail_ref = f32[128,2048]{1,0:T(8,128)S(1)} collective-permute-done((f32[128,2048]{1,0:T(8,128)S(1)}, f32[128,2048]{1,0:T(8,128)S(1)}, u32[]{:S(2)}, u32[]{:S(2)}) %collective-permute-start.3) | collective-permute-done | bytes 1048608 | tf_op jit(solution)/shard_map/ppermute | solution.py:456
  42.8 0.8 %first_values.1 = (f32[128,2048]{1,0:T(8,128)S(1)}, f32[8,128]{1,0:T(8,128)S(1)}) custom-call(bf16[128,4096]{1,0:T(8,128)(2,1)S(1)} %get-tuple-element.39.weights_ref, f32[128,2048]{1,0:T(8,128)S(1)} %get-tuple-element.40._.now_ref, f32[128,2048]{1,0:T(8,128)S(1)} %collective-permute-done.3.tail_ref, f32[8,512]{1,0:T(8,128)S(1)} %get-tuple-element.48._.refs_0_.refs_2_), custom_call_target="tpu_custom_call" | custom-call | tf_op jit(solution)/shard_map/first_values/pallas_call | solution.py:486
  43.6 4.1 %collective-permute-start.11 = (f32[8,128]{1,0:T(8,128)S(1)}, f32[8,128]{1,0:T(8,128)S(1)}, u32[]{:S(2)}, u32[]{:S(2)}) collective-permute-start(f32[8,128]{1,0:T(8,128)S(1)} %get-tuple-element.50._.refs_6_), channel_id=1, source_target_pairs={{0,3},{1,2},{2,1},{3,0},{4,7},{5,6},{6,5},{7,4},{8,11},{9,10},{10,... | collective-permute-start | bytes 12296 | tf_op jit(solution)/shard_map/ppermute | solution.py:359
  47.7 0.6 %collective-permute-start.9 = (f32[8,128]{1,0:T(8,128)S(1)}, f32[8,128]{1,0:T(8,128)S(1)}, u32[]{:S(2)}, u32[]{:S(2)}) collective-permute-start(f32[8,128]{1,0:T(8,128)S(1)} %get-tuple-element.50._.refs_6_), channel_id=1, source_target_pairs={{0,1},{1,0},{2,3},{3,2},{4,5},{5,4},{6,7},{7,6},{8,9},{9,8},{10,11... | collective-permute-start | bytes 12296 | tf_op jit(solution)/shard_map/ppermute | solution.py:359
  48.3 2.2 %scale.1._ = f32[512,2048]{1,0:T(8,128)} custom-call(f32[8,128]{1,0:T(8,128)S(1)} %get-tuple-element.50._.refs_6_, f32[8,512]{1,0:T(8,128)S(1)} %get-tuple-element.48._.refs_0_.refs_2_, f32[8,512]{1,0:T(8,128)S(1)} %collective-permute-done.6.refs_1_.refs_3_, f32[8,512]{1,0:T(8,128)S(1)} %collective-permute-done.7.refs_2_.refs_4_, ...), custom_call_target="tpu_custom_call" | custom-call | tf_op jit(solution)/shard_map/scale/pallas_call | solution.py:493
  50.5 1.7 %collective-permute-done.10.refs_8_ = f32[8,128]{1,0:T(8,128)S(1)} collective-permute-done((f32[8,128]{1,0:T(8,128)S(1)}, f32[8,128]{1,0:T(8,128)S(1)}, u32[]{:S(2)}, u32[]{:S(2)}) %collective-permute-start.10) | collective-permute-done | bytes 4128 | tf_op jit(solution)/shard_map/ppermute | solution.py:359
  52.2 1.3 %first_scale.1 = f32[512,2048]{1,0:T(8,128)} custom-call(f32[128,2048]{1,0:T(8,128)S(1)} %get-tuple-element.49.a_ref, f32[512,2048]{1,0:T(8,128)} %scale.1._, f32[512,1024]{1,0:T(8,128)S(1)} %get-tuple-element.53.refs_6_.refs_0_, f32[512,1024]{1,0:T(8,128)S(1)} %get-tuple-element.54.refs_7_.refs_1_, ...), custom_call_target="tpu_custom_call", output_to_operand_aliasing={{}: (1, {})} | custom-call | tf_op jit(solution)/shard_map/first_scale/pallas_call | solution.py:501
  (16 shorter events, 0.3 us)
Async XLA Ops:
  2.9 3.0 %collective-permute-start = (f32[8,128,128]{2,1,0:T(8,128)S(1)}, f32[8,128,128]{2,1,0:T(8,128)S(1)}, u32[]{:S(2)}, u32[]{:S(2)}) collective-permute-start(f32[8,128,128]{2,1,0:T(8,128)S(1)} %get-tuple-element.32._), channel_id=1, source_target_pairs={{0,4},{4,0},{8,12},{12,8},{16,20},{20,16},{24,28},{28,24},{1,5},{5... | collective-permute-start | bytes 1572872 | tf_op jit(solution)/shard_map/ppermute | solution.py:359
  5.9 11.8 %collective-permute-start.1 = (f32[8,128,128]{2,1,0:T(8,128)S(1)}, f32[8,128,128]{2,1,0:T(8,128)S(1)}, u32[]{:S(2)}, u32[]{:S(2)}) collective-permute-start(f32[8,128,128]{2,1,0:T(8,128)S(1)} %chip.1._.chip_ref), channel_id=1, source_target_pairs={{0,8},{4,20},{8,0},{12,28},{16,24},{20,4},{24,16},{28,12},{1,9},{5... | collective-permute-start | bytes 1572872 | tf_op jit(solution)/shard_map/ppermute | solution.py:367
  7.5 2.0 %copy-start = (f32[2,16]{1,0:T(2,128)S(1)}, f32[2,16]{1,0:T(2,128)}, u32[]{:S(2)}) copy-start(f32[2,16]{1,0:T(2,128)} %gain_ref.7) | copy-start | bytes 388
  7.6 24.3 %collective-permute-start.2 = (f32[128,2048]{1,0:T(8,128)S(1)}, f32[128,2048]{1,0:T(8,128)S(1)}, u32[]{:S(2)}, u32[]{:S(2)}) collective-permute-start(f32[128,2048]{1,0:T(8,128)S(1)} %tail.2), channel_id=1, source_target_pairs={{0,4},{4,8},{8,12},{12,16},{16,20},{20,24},{24,28},{1,5},{5,9},{9,... | collective-permute-start | bytes 3145736 | tf_op jit(solution)/shard_map/ppermute | solution.py:444
  17.9 13.7 %collective-permute-start.4 = (f32[8,128,128]{2,1,0:T(8,128)S(1)}, f32[8,128,128]{2,1,0:T(8,128)S(1)}, u32[]{:S(2)}, u32[]{:S(2)}) collective-permute-start(f32[8,128,128]{2,1,0:T(8,128)S(1)} %message.1._), channel_id=1, source_target_pairs={{0,16},{4,12},{8,24},{12,4},{16,0},{20,28},{24,8},{28,20},{1,17},{... | collective-permute-start | bytes 1572872 | tf_op jit(solution)/shard_map/ppermute | solution.py:371
  24.8 18.0 %collective-permute-start.3 = (f32[128,2048]{1,0:T(8,128)S(1)}, f32[128,2048]{1,0:T(8,128)S(1)}, u32[]{:S(2)}, u32[]{:S(2)}) collective-permute-start(f32[128,2048]{1,0:T(8,128)S(1)} %tail.3), channel_id=1, source_target_pairs={{0,4},{4,8},{8,12},{12,16},{16,20},{20,24},{24,28},{1,5},{5,9},{9,... | collective-permute-start | bytes 3145736 | tf_op jit(solution)/shard_map/ppermute | solution.py:456
  31.8 2.9 %collective-permute-start.5 = (f32[8,128,128]{2,1,0:T(8,128)S(1)}, f32[8,128,128]{2,1,0:T(8,128)S(1)}, u32[]{:S(2)}, u32[]{:S(2)}) collective-permute-start(f32[8,128,128]{2,1,0:T(8,128)S(1)} %get-tuple-element.42), channel_id=1, source_target_pairs={{0,4},{4,0},{8,12},{12,8},{16,20},{20,16},{24,28},{28,24},{1,5},{5... | collective-permute-start | bytes 1572872 | tf_op jit(solution)/shard_map/ppermute | solution.py:359
  37.1 10.7 %collective-permute-start.8 = (f32[8,512]{1,0:T(8,128)S(1)}, f32[8,512]{1,0:T(8,128)S(1)}, u32[]{:S(2)}, u32[]{:S(2)}) collective-permute-start(f32[8,512]{1,0:T(8,128)S(1)} %get-tuple-element.48._.refs_0_.refs_2_), channel_id=1, source_target_pairs={{0,3},{1,2},{2,1},{3,0},{4,7},{5,6},{6,5},{7,4},{8,11},{9,10},{10,... | collective-permute-start | bytes 49160 | tf_op jit(solution)/shard_map/ppermute | solution.py:359
  41.1 7.2 %collective-permute-start.7 = (f32[8,512]{1,0:T(8,128)S(1)}, f32[8,512]{1,0:T(8,128)S(1)}, u32[]{:S(2)}, u32[]{:S(2)}) collective-permute-start(f32[8,512]{1,0:T(8,128)S(1)} %get-tuple-element.48._.refs_0_.refs_2_), channel_id=1, source_target_pairs={{0,2},{1,3},{2,0},{3,1},{4,6},{5,7},{6,4},{7,5},{8,10},{9,11},{10,... | collective-permute-start | bytes 49160 | tf_op jit(solution)/shard_map/ppermute | solution.py:359
  41.1 7.2 %collective-permute-start.6 = (f32[8,512]{1,0:T(8,128)S(1)}, f32[8,512]{1,0:T(8,128)S(1)}, u32[]{:S(2)}, u32[]{:S(2)}) collective-permute-start(f32[8,512]{1,0:T(8,128)S(1)} %get-tuple-element.48._.refs_0_.refs_2_), channel_id=1, source_target_pairs={{0,1},{1,0},{2,3},{3,2},{4,5},{5,4},{6,7},{7,6},{8,9},{9,8},{10,11... | collective-permute-start | bytes 49160 | tf_op jit(solution)/shard_map/ppermute | solution.py:359
  43.6 6.9 %collective-permute-start.11 = (f32[8,128]{1,0:T(8,128)S(1)}, f32[8,128]{1,0:T(8,128)S(1)}, u32[]{:S(2)}, u32[]{:S(2)}) collective-permute-start(f32[8,128]{1,0:T(8,128)S(1)} %get-tuple-element.50._.refs_6_), channel_id=1, source_target_pairs={{0,3},{1,2},{2,1},{3,0},{4,7},{5,6},{6,5},{7,4},{8,11},{9,10},{10,... | collective-permute-start | bytes 12296 | tf_op jit(solution)/shard_map/ppermute | solution.py:359
  47.7 4.5 %collective-permute-start.10 = (f32[8,128]{1,0:T(8,128)S(1)}, f32[8,128]{1,0:T(8,128)S(1)}, u32[]{:S(2)}, u32[]{:S(2)}) collective-permute-start(f32[8,128]{1,0:T(8,128)S(1)} %get-tuple-element.50._.refs_6_), channel_id=1, source_target_pairs={{0,2},{1,3},{2,0},{3,1},{4,6},{5,7},{6,4},{7,5},{8,10},{9,11},{10,... | collective-permute-start | bytes 12296 | tf_op jit(solution)/shard_map/ppermute | solution.py:359
  47.7 4.5 %collective-permute-start.9 = (f32[8,128]{1,0:T(8,128)S(1)}, f32[8,128]{1,0:T(8,128)S(1)}, u32[]{:S(2)}, u32[]{:S(2)}) collective-permute-start(f32[8,128]{1,0:T(8,128)S(1)} %get-tuple-element.50._.refs_6_), channel_id=1, source_target_pairs={{0,1},{1,0},{2,3},{3,2},{4,5},{5,4},{6,7},{7,6},{8,9},{9,8},{10,11... | collective-permute-start | bytes 12296 | tf_op jit(solution)/shard_map/ppermute | solution.py:359

commit v8 on v7

--- a/solution.py
+++ b/solution.py
@@ -101,7 +101,7 @@
     return copies
 
 
-def totals_kernel(part, k_hbm, v_hbm, _, total_ref, half_ref, k_ref, v_ref, sems):
+def totals_kernel(part, k_hbm, v_hbm, _, total_ref, half_ref, k_ref, v_ref, tail_ref, sems):
     middle = k_ref.shape[0] // 2
     copies = column_copies(part, (k_hbm, v_hbm), (k_ref, v_ref), sems)
     for group in copies:
@@ -118,17 +118,17 @@
             second = outer_state(k_high[middle:], k_low[middle:], v_high[middle:], v_low[middle:])
             half_ref[head] = first
             total_ref[head] = first + second
-
-
-def chip_kernel(keep_ref, beside_ref, out_ref):
+    tail_ref[...] = k_ref[k_ref.shape[0] - WINDOW :, :]
+
+
+def chip_kernel(keep_ref, beside_ref, _, out_ref, __):
     out_ref[...] = keep_ref[...] + beside_ref[...]
 
 
 def tail_kernel(first_ref, second_ref, _, tail_ref):
     rows, width = first_ref.shape
-    for part, ref in enumerate((first_ref, second_ref)):
-        begin = first_head(part, 2 * width // HD) * HD
-        tail_ref[:, pl.ds(pl.multiple_of(begin, HD), width)] = ref[rows - WINDOW :, :]
+    tail_ref[:, :width] = first_ref[rows - WINDOW :, :]
+    tail_ref[:, width:] = second_ref[rows - WINDOW :, :]
 
 
 def weights_of(scores):
@@ -142,7 +142,9 @@
     return side(high * above, high * below), side(low * above, low * below)
 
 
-def local_kernel(part, gain_ref, q_hbm, k_ref, v_ref, _, a_ref, b_ref, sum_ref, q_ref, square_ref, sems):
+def local_kernel(part, gain_ref, q_in_ref, k_ref, v_ref, *refs):
+    a_ref, b_ref, sum_ref = refs[2:5]
+    square_ref = refs[-2]
     lower = lower_mask()
     below = jnp.where(lower, 1.0, 0.0).astype(BF16)
     above = jnp.where(lower, 0.0, 1.0).astype(BF16)
@@ -150,14 +152,23 @@
     tiles = rows // WINDOW
     groups = width // (GROUP * HD)
     begin = first_head(part, 2 * width // HD)
-
-    def load(group):
-        there = pl.ds(pl.multiple_of((begin + group * GROUP) * HD, HD), GROUP * HD)
-        here = head_columns(group, 1, GROUP * HD)
-        return pltpu.make_async_copy(q_hbm.at[:, there], q_ref.at[:, here], sems.at[group])
-
-    for group in range(groups):
-        load(group).start()
+    if part == 0:
+        q_refs, sems = refs[5:7], refs[-1]
+        q_ref = q_refs[0]
+
+        def load(number, group):
+            there = pl.ds(pl.multiple_of((first_head(number, 2 * width // HD) + group * GROUP) * HD, HD), GROUP * HD)
+            here = head_columns(group, 1, GROUP * HD)
+            return pltpu.make_async_copy(
+                q_in_ref.at[:, there], q_refs[number].at[:, here], sems.at[number, group]
+            )
+
+        for number in range(2):
+            for group in range(groups):
+                load(number, group).start()
+    else:
+        q_ref = q_in_ref
+        square_ref = refs[-1]
     square_ref[...] = jnp.zeros_like(square_ref)
 
     def tile(n):
@@ -165,7 +176,8 @@
 
     @pl.loop(0, groups)
     def _(group):
-        load(group).wait()
+        if part == 0:
+            load(0, group).wait()
         scores = []
         for j in range(GROUP):
             columns = head_columns(GROUP * group + j)
@@ -206,6 +218,9 @@
                 square_ref[tile(n), :] += a * a
                 b_ref[tile(n), columns] = folded(wide[tile(2)]) + wide[tile(3), :HD]
 
+    if part == 0:
+        for group in range(groups):
+            load(1, group).wait()
     sum_ref[...] = row_sums(square_ref[...])
 
 
@@ -216,7 +231,7 @@
     out_ref[...] = first + jnp.where((core == 0) | (x == 0), chip_ref[...], 0.0)
 
 
-def prefix_kernel(first_ref, second_ref, keep_ref, beside_ref, mine_ref, other_ref):
+def prefix_kernel(first_ref, second_ref, keep_ref, beside_ref, _, mine_ref, other_ref):
     index = lax.axis_index("ctx")
     core, x, y = index % 2, (index >> 1) % 2, index >> 2
     use_first = jnp.where(core == 0, x, y) == 1
@@ -226,7 +241,7 @@
     other_ref[...] = earlier + jnp.where(core == 0, keep_ref[...], 0.0)
 
 
-def earlier_kernel(gain_ref, _, *refs):
+def earlier_kernel(gain_ref, *refs):
     state_refs, half_refs, q_refs, b_refs, sum_refs, out_refs = (refs[2 * i : 2 * i + 2] for i in range(6))
     sums_ref, square_ref = refs[12:]
     rows, width = b_refs[0].shape
@@ -250,7 +265,7 @@
 
 def first_weights_kernel(gain_ref, *refs):
     q_refs, k_refs, v_refs = (refs[2 * i : 2 * i + 2] for i in range(3))
-    tail_ref, weights_ref, out_ref = refs[6:]
+    *tail_refs, weights_ref, out_ref = refs[6:]
     lower = lower_mask()
     reachable = jnp.logical_or(lower, lax.axis_index("ctx") > 0)
     top = slice(0, WINDOW)
@@ -262,7 +277,7 @@
             columns = slice(head * HD, (head + 1) * HD)
             qq = side(*halves(q_refs[part][top, columns]))
             now = folded(dot_rows(qq, wide_keys(*halves(k_refs[part][top, columns]))))
-            before = folded(dot_rows(qq, wide_keys(*halves(tail_ref[:, head_columns(begin + head)]))))
+            before = folded(dot_rows(qq, wide_keys(*halves(tail_refs[part][:, columns]))))
             scores.append(jnp.where(reachable, jnp.where(lower, now, before), -jnp.inf))
         for head in range(width // HD):
             columns = slice(head * HD, (head + 1) * HD)
@@ -282,13 +297,13 @@
     square = jnp.zeros((WINDOW, HD), F32)
     heads = now_ref.shape[1] // HD
     for part in range(2):
-        begin = first_head(part, heads)
         for head in range(heads // 2):
             j = part * (heads // 2) + head
+            sent = (1 - part) * (heads // 2) + head
             columns = slice(j * HD, (j + 1) * HD)
             high = weights_ref[:, 2 * j * HD : (2 * j + 1) * HD]
             low = weights_ref[:, (2 * j + 1) * HD : 2 * (j + 1) * HD]
-            wide = dot(stack(high, low), side(*halves(tail_ref[:, head_columns(begin + head)])))
+            wide = dot(stack(high, low), side(*halves(tail_ref[:, sent * HD : (sent + 1) * HD])))
             a = now_ref[:, columns] + (folded(wide[:WINDOW]) + wide[WINDOW:, :HD])
             a_ref[:, columns] = a
             square = square + a * a
@@ -410,6 +425,7 @@
     half = array(rows, width // 2)
     first_tile = array(WINDOW, width)
     dma = pltpu.SemaphoreType.DMA
+    half_tile = array(WINDOW, width // 2)
     groups = heads // (2 * GROUP)
 
     def totals(part, after):
@@ -417,32 +433,35 @@
             functools.partial(totals_kernel, part),
             "totals",
             in_specs=[anywhere] * 3,
-            out_shape=[packed, packed, half, half],
+            out_shape=[packed, packed, half, half, half_tile],
             scratch_shapes=[dma((2, groups))],
         )(keys, values, after)
 
-    def local(part, after):
+    def local(part, query_source, *after):
         return call(
             functools.partial(local_kernel, part),
             "local",
-            in_specs=[smem, anywhere, vmem, vmem, anywhere],
-            out_shape=[half, half, array(8, rows), half],
-            scratch_shapes=[pltpu.VMEM((rows, HD), F32), dma((groups,))],
-        )(head_gain, queries, held_k[part], held_v[part], after)
-
-    def tail(held, after):
-        return call(
-            tail_kernel, "tail", in_specs=[vmem, vmem, anywhere], out_shape=first_tile
-        )(*held, after)
+            in_specs=[smem, vmem if part else anywhere, vmem, vmem, anywhere, anywhere],
+            out_shape=[half, half, array(8, rows)] + ([] if part else [half, half]),
+            scratch_shapes=[pltpu.VMEM((rows, HD), F32)] + ([] if part else [dma((2, groups))]),
+        )(head_gain, query_source, held_k[part], held_v[part], *after)
 
     route = [(i, i + 1) for i in range(lax.axis_size("ctx") - 1)]
-    send, *held_0 = totals(0, queries)
+    send, *held_0, tail_0 = totals(0, queries)
     beside = swap(send, "ctx", 1)
-    keep, *held_1 = totals(1, send)
+    before_1 = lax.ppermute(tail_0, "ctx", route)
+    keep, *held_1, tail_1 = totals(1, send)
     early, held_k, held_v = zip(held_0, held_1)
-    chip = call(chip_kernel, "chip", in_specs=[vmem, vmem], out_shape=packed)(keep, beside)
-    before_k = lax.ppermute(tail(held_k, chip), "ctx", route)
-    local_0 = local(0, chip)
+    chip, tail_1 = call(
+        chip_kernel,
+        "chip",
+        in_specs=[vmem, vmem, anywhere],
+        out_specs=[vmem, anywhere],
+        out_shape=[packed, half_tile],
+        input_output_aliases={2: 1},
+    )(keep, beside, tail_1)
+    before_0 = lax.ppermute(tail_1, "ctx", route)
+    *local_0, query_0, query_1 = local(0, queries, chip, before_1)
     message = local_0[2]
     if lax.axis_size("ctx") == 8:
         first = first_phase(chip)
@@ -452,22 +471,27 @@
             in_specs=[vmem, vmem, anywhere],
             out_shape=packed,
         )(first, chip, message)
-    window, linear, window_sums, held_q = zip(local_0, local(1, message))
-    before_v = lax.ppermute(tail(held_v, window_sums[1]), "ctx", route)
+    held_q = query_0, query_1
+    window, linear, window_sums = zip(local_0, local(1, query_1, message, message))
+    tail_v = call(
+        tail_kernel, "tail", in_specs=[vmem, vmem, anywhere], out_shape=first_tile
+    )(*held_v, window_sums[1])
+    before_v = lax.ppermute(tail_v, "ctx", route)
     first_weights, first_now = call(
         first_weights_kernel,
         "first_weights",
-        in_specs=[smem] + [vmem] * 7,
+        in_specs=[smem] + [vmem] * 8,
         out_shape=[array(WINDOW, 2 * width, dtype=BF16), first_tile],
-    )(head_gain, *held_q, *held_k, *held_v, before_k)
+    )(head_gain, *held_q, *held_k, *held_v, before_0, before_1)
 
     if lax.axis_size("ctx") == 8:
         second = second_phase(message)
         mine, other = call(
             prefix_kernel,
             "prefix",
+            in_specs=[vmem] * 4 + [anywhere],
             out_shape=[packed, packed],
-        )(first, second, keep, beside)
+        )(first, second, keep, beside, first_now)
     else:
         earlier = doubled_prefix(chip)
         core = lax.axis_index("ctx") % 2
@@ -478,10 +502,10 @@
     *linear, sums = call(
         earlier_kernel,
         "earlier",
-        in_specs=[smem, anywhere] + [vmem] * 10,
+        in_specs=[smem] + [vmem] * 10,
         out_shape=[half, half, array(8, rows)],
         scratch_shapes=[pltpu.VMEM((rows, HD), F32)],
-    )(head_gain, first_now, other, mine, *early, *held_q, *linear, *window_sums)
+    )(head_gain, other, mine, *early, *held_q, *linear, *window_sums)
     sums = everyone(sums, "head")
     first_a, first_sums = call(
         first_values_kernel,

time: 53.9 us -> 57 us (1.058); the launches traced: 53.6 us -> 56.1 us
  starting transfers between devices: 16 us -> 20.2 us
  Pallas kernels: 27.4 us -> 26.1 us
    ppermute x2 -> x3, starting transfers between devices: 4.02 us -> 8.95 us  [the longest x1 4.53 us: shards(): before_v = lax.ppermute(tail_v, 'ctx', route)]
    ppermute x2 -> x3, waiting for transfers between devices: 1.07 us -> 5.83 us  [the longest x1 5.29 us: shards(): before_1 = lax.ppermute(tail_0, 'ctx', route)]
    ppermute x1, waiting for transfers between devices: 4.67 us -> 0.01 us  [second_phase(): lax.ppermute(message, 'ctx', [(i, i ^ (4 if i % 2 == 0 else 2)) for i in...]
    ppermute x1, waiting for transfers between devices: 2.46 us -> 0.01 us  [first_phase(): lax.ppermute(chip, 'ctx', [(i, i ^ (2 if i % 2 == 0 else 4)) for i in ran...]
    ppermute x8, waiting for transfers between devices: 1.71 us -> 3.6 us  [swap(): lax.ppermute(block, axis, [(i, i ^ bit) for i in range(lax.axis_size(axis...]
    pallas_call x8 -> x7, Pallas kernels: 17.2 us -> 16 us  [the longest x2 10.4 us: local(): call(functools.partial(local_kernel, part), 'local', in_specs=[smem, vmem...]
    ppermute x1, starting transfers between devices: 0.99 us -> 0.35 us  [second_phase(): lax.ppermute(message, 'ctx', [(i, i ^ (4 if i % 2 == 0 else 2)) for i in...]
  transfers between devices with their start and end apart: 12 -> 13, of which waited for: 4 -> 4; matrix products, arithmetic and copies ran while one was open for 0% -> 0% of each run, Pallas kernels for 43% -> 39%
where the time goes in v8:
time: 57 us; the launch traced here: 56.1 us
  Pallas kernels  26.1 us (46%)
  starting transfers between devices  20.2 us (35%)
  waiting for transfers between devices  9.43 us (17%)
    pallas_call x2, Pallas kernels, local(): call(functools.partial(local_kernel, part), 'local', in_specs=[smem, vmem...  10.4 us
    ppermute x8, starting transfers between devices, swap(): lax.ppermute(block, axis, [(i, i ^ bit) for i in range(lax.axis_size(axis...  9.32 us
    pallas_call x2, Pallas kernels, totals(): call(functools.partial(totals_kernel, part), 'totals', in_specs=[anywhere...  5.72 us
    ppermute x1, waiting for transfers between devices, shards(): before_1 = lax.ppermute(tail_0, 'ctx', route)  5.29 us
    ppermute x1, starting transfers between devices, shards(): before_v = lax.ppermute(tail_v, 'ctx', route)  4.53 us
    ppermute x8, waiting for transfers between devices, swap(): lax.ppermute(block, axis, [(i, i ^ bit) for i in range(lax.axis_size(axis...  3.6 us
    pallas_call x1, Pallas kernels, shards(): call(first_weights_kernel, 'first_weights', in_specs=[smem] + [vmem] * 8,...  2.86 us
    ppermute x1, starting transfers between devices, shards(): before_1 = lax.ppermute(tail_0, 'ctx', route)  2.51 us
  transfers between devices with their start and end apart: 13, of which 4 were waited for; matrix products, arithmetic and copies ran while one was open for 0% of the time, Pallas kernels for 39%

profile of v8, /device:TPU:4, one launch (start us, length us, event | category | flops | bytes accessed | tf_op | source)
XLA Modules:
  0.0 56.1 jit_solution(562035424226310484)
XLA Ops:
  0.0 2.9 %totals.2 = (f32[8,128,128]{2,1,0:T(8,128)S(1)}, f32[8,128,128]{2,1,0:T(8,128)S(1)}, f32[512,1024]{1,0:T(8,128)S(1)}, f32[512,1024]{1,0:T(8,128)S(1)}, f32[128,1024]{1,0:T(8,128)S(1)}) custom-call(f32[512,2048]{1,0:T(8,128)} %k_hbm.3, f32[512,2048]{1,0:T(8,128)} %v_hbm.3, f32[512,2048]{1,0:T(8,128)} %q_in_ref.1), custom_call_target="tpu_custom_call" | custom-call | tf_op jit(solution)/shard_map/totals/pallas_call | solution.py:432
  3.0 2.5 %collective-permute-start.1 = (f32[128,1024]{1,0:T(8,128)S(1)}, f32[128,1024]{1,0:T(8,128)S(1)}, u32[]{:S(2)}, u32[]{:S(2)}) collective-permute-start(f32[128,1024]{1,0:T(8,128)S(1)} %get-tuple-element.40), channel_id=1, source_target_pairs={{0,4},{4,8},{8,12},{12,16},{16,20},{20,24},{24,28},{1,5},{5,9},{9,... | collective-permute-start | bytes 1572872 | tf_op jit(solution)/shard_map/ppermute | solution.py:452
  5.5 2.9 %totals.3 = (f32[8,128,128]{2,1,0:T(8,128)S(1)}, f32[8,128,128]{2,1,0:T(8,128)S(1)}, f32[512,1024]{1,0:T(8,128)S(1)}, f32[512,1024]{1,0:T(8,128)S(1)}, f32[128,1024]{1,0:T(8,128)S(1)}) custom-call(f32[512,2048]{1,0:T(8,128)} %k_hbm.3, f32[512,2048]{1,0:T(8,128)} %v_hbm.3, f32[8,128,128]{2,1,0:T(8,128)S(1)} %get-tuple-element.36._), custom_call_target="tpu_custom_call" | custom-call | tf_op jit(solution)/shard_map/totals/pallas_call | solution.py:432
  8.4 1.6 %collective-permute-start.3 = (f32[8,128,128]{2,1,0:T(8,128)S(1)}, f32[8,128,128]{2,1,0:T(8,128)S(1)}, u32[]{:S(2)}, u32[]{:S(2)}) collective-permute-start(f32[8,128,128]{2,1,0:T(8,128)S(1)} %get-tuple-element.39.refs_0_.chip_ref), channel_id=1, source_target_pairs={{0,8},{4,20},{8,0},{12,28},{16,24},{20,4},{24,16},{28,12},{1,9},{5... | collective-permute-start | bytes 1572872 | tf_op jit(solution)/shard_map/ppermute | solution.py:382
  10.0 1.9 %collective-permute-start.2 = (f32[128,1024]{1,0:T(8,128)S(1)}, f32[128,1024]{1,0:T(8,128)S(1)}, u32[]{:S(2)}, u32[]{:S(2)}) collective-permute-start(f32[128,1024]{1,0:T(8,128)S(1)} %get-tuple-element.45), channel_id=1, source_target_pairs={{0,4},{4,8},{8,12},{12,16},{16,20},{20,24},{24,28},{1,5},{5,9},{9,... | collective-permute-start | bytes 1572872 | tf_op jit(solution)/shard_map/ppermute | solution.py:463
  11.9 5.3 %collective-permute-done.1.refs_1_.refs_7_ = f32[128,1024]{1,0:T(8,128)S(1)} collective-permute-done((f32[128,1024]{1,0:T(8,128)S(1)}, f32[128,1024]{1,0:T(8,128)S(1)}, u32[]{:S(2)}, u32[]{:S(2)}) %collective-permute-start.1) | collective-permute-done | bytes 524320 | tf_op jit(solution)/shard_map/ppermute | solution.py:452
  17.2 5.8 %local.2 = (f32[512,1024]{1,0:T(8,128)S(1)}, f32[512,1024]{1,0:T(8,128)S(1)}, f32[8,512]{1,0:T(8,128)S(1)}, f32[512,1024]{1,0:T(8,128)S(1)}, f32[512,1024]{1,0:T(8,128)S(1)}) custom-call(f32[2,16]{1,0:T(2,128)S(1)} %copy-done, f32[512,2048]{1,0:T(8,128)} %q_in_ref.1, f32[512,1024]{1,0:T(8,128)S(1)} %get-tuple-element.34.k_ref.refs_2_, ...), custom_call_target="tpu_custom_call" | custom-call | tf_op jit(solution)/shard_map/local/pallas_call | solution.py:441
  23.0 0.1 message.1.refs_0_.refs_1_
  23.1 0.3 collective-permute-start.5
  23.5 4.5 %local.3 = (f32[512,1024]{1,0:T(8,128)S(1)}, f32[512,1024]{1,0:T(8,128)S(1)}, f32[8,512]{1,0:T(8,128)S(1)}) custom-call(f32[2,16]{1,0:T(2,128)S(1)} %copy-done, f32[512,1024]{1,0:T(8,128)S(1)} %get-tuple-element.42.refs_1_.q_in_ref.refs_5_, f32[512,1024]{1,0:T(8,128)S(1)} %get-tuple-element.43.refs_3_.k_ref, ...), custom_call_target="tpu_custom_call" | custom-call | tf_op jit(solution)/shard_map/local/pallas_call | solution.py:441
  28.1 4.5 %collective-permute-start.4 = (f32[128,2048]{1,0:T(8,128)S(1)}, f32[128,2048]{1,0:T(8,128)S(1)}, u32[]{:S(2)}, u32[]{:S(2)}) collective-permute-start(f32[128,2048]{1,0:T(8,128)S(1)} %tail.1), channel_id=1, source_target_pairs={{0,4},{4,8},{8,12},{12,16},{16,20},{20,24},{24,28},{1,5},{5,9},{9,... | collective-permute-start | bytes 3145736 | tf_op jit(solution)/shard_map/ppermute | solution.py:479
  32.7 2.9 %first_weights.1 = (bf16[128,4096]{1,0:T(8,128)(2,1)S(1)}, f32[128,2048]{1,0:T(8,128)S(1)}) custom-call(f32[2,16]{1,0:T(2,128)S(1)} %copy-done, f32[512,1024]{1,0:T(8,128)S(1)} %get-tuple-element.41.refs_0_.refs_4_, f32[512,1024]{1,0:T(8,128)S(1)} %get-tuple-element.42.refs_1_.q_in_ref.refs_5_, f32[512,1024]{1,0:T(8,128)S(1)} %get-tuple-element.34.k_ref.refs_2_, ...), custom_call_target="tpu_custom_call" | custom-call | tf_op jit(solution)/shard_map/first_weights/pallas_call | solution.py:480
  35.6 0.2 prefix.1
  35.9 1.9 %collective-permute-done.6.refs_0_ = f32[8,128,128]{2,1,0:T(8,128)S(1)} collective-permute-done((f32[8,128,128]{2,1,0:T(8,128)S(1)}, f32[8,128,128]{2,1,0:T(8,128)S(1)}, u32[]{:S(2)}, u32[]{:S(2)}) %collective-permute-start.6) | collective-permute-done | bytes 524320 | tf_op jit(solution)/shard_map/ppermute | solution.py:374
  37.8 2.4 %earlier.1 = (f32[512,1024]{1,0:T(8,128)S(1)}, f32[512,1024]{1,0:T(8,128)S(1)}, f32[8,512]{1,0:T(8,128)S(1)}) custom-call(f32[2,16]{1,0:T(2,128)S(1)} %copy-done, f32[8,128,128]{2,1,0:T(8,128)S(1)} %collective-permute-done.6.refs_0_, f32[8,128,128]{2,1,0:T(8,128)S(1)} %get-tuple-element.51.refs_1_, f32[8,128,128]{2,1,0:T(8,128)S(1)} %get-tuple-element.52.refs_2_, ...), custom_call_target="tpu_custom_call" | custom-call | tf_op jit(solution)/shard_map/earlier/pallas_call | solution.py:502
  40.2 3.0 %collective-permute-start.9 = (f32[8,512]{1,0:T(8,128)S(1)}, f32[8,512]{1,0:T(8,128)S(1)}, u32[]{:S(2)}, u32[]{:S(2)}) collective-permute-start(f32[8,512]{1,0:T(8,128)S(1)} %get-tuple-element.56._.refs_0_.refs_2_), channel_id=1, source_target_pairs={{0,3},{1,2},{2,1},{3,0},{4,7},{5,6},{6,5},{7,4},{8,11},{9,10},{10,... | collective-permute-start | bytes 49160 | tf_op jit(solution)/shard_map/ppermute | solution.py:374
  43.2 1.4 %collective-permute-start.7 = (f32[8,512]{1,0:T(8,128)S(1)}, f32[8,512]{1,0:T(8,128)S(1)}, u32[]{:S(2)}, u32[]{:S(2)}) collective-permute-start(f32[8,512]{1,0:T(8,128)S(1)} %get-tuple-element.56._.refs_0_.refs_2_), channel_id=1, source_target_pairs={{0,1},{1,0},{2,3},{3,2},{4,5},{5,4},{6,7},{7,6},{8,9},{9,8},{10,11... | collective-permute-start | bytes 49160 | tf_op jit(solution)/shard_map/ppermute | solution.py:374
  44.6 0.5 collective-permute-done.4.tail_ref
  45.2 0.8 %first_values.1 = (f32[128,2048]{1,0:T(8,128)S(1)}, f32[8,128]{1,0:T(8,128)S(1)}) custom-call(bf16[128,4096]{1,0:T(8,128)(2,1)S(1)} %get-tuple-element.46.weights_ref, f32[128,2048]{1,0:T(8,128)S(1)} %get-tuple-element.47._.now_ref, f32[128,2048]{1,0:T(8,128)S(1)} %collective-permute-done.4.tail_ref, f32[8,512]{1,0:T(8,128)S(1)} %get-tuple-element.56._.refs_0_.refs_2_), custom_call_target="tpu_custom_call" | custom-call | tf_op jit(solution)/shard_map/first_values/pallas_call | solution.py:510
  46.0 4.2 %collective-permute-start.12 = (f32[8,128]{1,0:T(8,128)S(1)}, f32[8,128]{1,0:T(8,128)S(1)}, u32[]{:S(2)}, u32[]{:S(2)}) collective-permute-start(f32[8,128]{1,0:T(8,128)S(1)} %get-tuple-element.58._.refs_6_), channel_id=1, source_target_pairs={{0,3},{1,2},{2,1},{3,0},{4,7},{5,6},{6,5},{7,4},{8,11},{9,10},{10,... | collective-permute-start | bytes 12296 | tf_op jit(solution)/shard_map/ppermute | solution.py:374
  50.2 0.6 %collective-permute-start.10 = (f32[8,128]{1,0:T(8,128)S(1)}, f32[8,128]{1,0:T(8,128)S(1)}, u32[]{:S(2)}, u32[]{:S(2)}) collective-permute-start(f32[8,128]{1,0:T(8,128)S(1)} %get-tuple-element.58._.refs_6_), channel_id=1, source_target_pairs={{0,1},{1,0},{2,3},{3,2},{4,5},{5,4},{6,7},{7,6},{8,9},{9,8},{10,11... | collective-permute-start | bytes 12296 | tf_op jit(solution)/shard_map/ppermute | solution.py:374
  50.8 2.2 %scale.1._ = f32[512,2048]{1,0:T(8,128)} custom-call(f32[8,128]{1,0:T(8,128)S(1)} %get-tuple-element.58._.refs_6_, f32[8,512]{1,0:T(8,128)S(1)} %get-tuple-element.56._.refs_0_.refs_2_, f32[8,512]{1,0:T(8,128)S(1)} %collective-permute-done.7.refs_1_.refs_3_, f32[8,512]{1,0:T(8,128)S(1)} %collective-permute-done.8.refs_2_.refs_4_, ...), custom_call_target="tpu_custom_call" | custom-call | tf_op jit(solution)/shard_map/scale/pallas_call | solution.py:517
  53.0 1.7 %collective-permute-done.11.refs_8_ = f32[8,128]{1,0:T(8,128)S(1)} collective-permute-done((f32[8,128]{1,0:T(8,128)S(1)}, f32[8,128]{1,0:T(8,128)S(1)}, u32[]{:S(2)}, u32[]{:S(2)}) %collective-permute-start.11) | collective-permute-done | bytes 4128 | tf_op jit(solution)/shard_map/ppermute | solution.py:374
  54.7 1.3 %first_scale.1 = f32[512,2048]{1,0:T(8,128)} custom-call(f32[128,2048]{1,0:T(8,128)S(1)} %get-tuple-element.57.a_ref, f32[512,2048]{1,0:T(8,128)} %scale.1._, f32[512,1024]{1,0:T(8,128)S(1)} %get-tuple-element.61.refs_6_.refs_0_, f32[512,1024]{1,0:T(8,128)S(1)} %get-tuple-element.62.refs_7_.refs_1_, ...), custom_call_target="tpu_custom_call", output_to_operand_aliasing={{}: (1, {})} | custom-call | tf_op jit(solution)/shard_map/first_scale/pallas_call | solution.py:525
  (17 shorter events, 0.3 us)
Async XLA Ops:
  2.9 5.5 %collective-permute-start = (f32[8,128,128]{2,1,0:T(8,128)S(1)}, f32[8,128,128]{2,1,0:T(8,128)S(1)}, u32[]{:S(2)}, u32[]{:S(2)}) collective-permute-start(f32[8,128,128]{2,1,0:T(8,128)S(1)} %get-tuple-element.36._), channel_id=1, source_target_pairs={{0,4},{4,0},{8,12},{12,8},{16,20},{20,16},{24,28},{28,24},{1,5},{5... | collective-permute-start | bytes 1572872 | tf_op jit(solution)/shard_map/ppermute | solution.py:374
  2.9 14.2 %copy-start = (f32[2,16]{1,0:T(2,128)S(1)}, f32[2,16]{1,0:T(2,128)}, u32[]{:S(2)}) copy-start(f32[2,16]{1,0:T(2,128)} %gain_ref.7) | copy-start | bytes 388
  3.0 14.2 %collective-permute-start.1 = (f32[128,1024]{1,0:T(8,128)S(1)}, f32[128,1024]{1,0:T(8,128)S(1)}, u32[]{:S(2)}, u32[]{:S(2)}) collective-permute-start(f32[128,1024]{1,0:T(8,128)S(1)} %get-tuple-element.40), channel_id=1, source_target_pairs={{0,4},{4,8},{8,12},{12,16},{16,20},{20,24},{24,28},{1,5},{5,9},{9,... | collective-permute-start | bytes 1572872 | tf_op jit(solution)/shard_map/ppermute | solution.py:452
  8.4 14.6 %collective-permute-start.3 = (f32[8,128,128]{2,1,0:T(8,128)S(1)}, f32[8,128,128]{2,1,0:T(8,128)S(1)}, u32[]{:S(2)}, u32[]{:S(2)}) collective-permute-start(f32[8,128,128]{2,1,0:T(8,128)S(1)} %get-tuple-element.39.refs_0_.chip_ref), channel_id=1, source_target_pairs={{0,8},{4,20},{8,0},{12,28},{16,24},{20,4},{24,16},{28,12},{1,9},{5... | collective-permute-start | bytes 1572872 | tf_op jit(solution)/shard_map/ppermute | solution.py:382
  10.0 22.7 %collective-permute-start.2 = (f32[128,1024]{1,0:T(8,128)S(1)}, f32[128,1024]{1,0:T(8,128)S(1)}, u32[]{:S(2)}, u32[]{:S(2)}) collective-permute-start(f32[128,1024]{1,0:T(8,128)S(1)} %get-tuple-element.45), channel_id=1, source_target_pairs={{0,4},{4,8},{8,12},{12,16},{16,20},{20,24},{24,28},{1,5},{5,9},{9,... | collective-permute-start | bytes 1572872 | tf_op jit(solution)/shard_map/ppermute | solution.py:463
  23.1 12.4 %collective-permute-start.5 = (f32[8,128,128]{2,1,0:T(8,128)S(1)}, f32[8,128,128]{2,1,0:T(8,128)S(1)}, u32[]{:S(2)}, u32[]{:S(2)}) collective-permute-start(f32[8,128,128]{2,1,0:T(8,128)S(1)} %message.1.refs_0_.refs_1_), channel_id=1, source_target_pairs={{0,16},{4,12},{8,24},{12,4},{16,0},{20,28},{24,8},{28,20},{1,17},{... | collective-permute-start | bytes 1572872 | tf_op jit(solution)/shard_map/ppermute | solution.py:386
  28.1 17.0 %collective-permute-start.4 = (f32[128,2048]{1,0:T(8,128)S(1)}, f32[128,2048]{1,0:T(8,128)S(1)}, u32[]{:S(2)}, u32[]{:S(2)}) collective-permute-start(f32[128,2048]{1,0:T(8,128)S(1)} %tail.1), channel_id=1, source_target_pairs={{0,4},{4,8},{8,12},{12,16},{16,20},{20,24},{24,28},{1,5},{5,9},{9,... | collective-permute-start | bytes 3145736 | tf_op jit(solution)/shard_map/ppermute | solution.py:479
  35.8 2.0 %collective-permute-start.6 = (f32[8,128,128]{2,1,0:T(8,128)S(1)}, f32[8,128,128]{2,1,0:T(8,128)S(1)}, u32[]{:S(2)}, u32[]{:S(2)}) collective-permute-start(f32[8,128,128]{2,1,0:T(8,128)S(1)} %get-tuple-element.50), channel_id=1, source_target_pairs={{0,4},{4,0},{8,12},{12,8},{16,20},{20,16},{24,28},{28,24},{1,5},{5... | collective-permute-start | bytes 1572872 | tf_op jit(solution)/shard_map/ppermute | solution.py:374
  40.2 9.9 %collective-permute-start.9 = (f32[8,512]{1,0:T(8,128)S(1)}, f32[8,512]{1,0:T(8,128)S(1)}, u32[]{:S(2)}, u32[]{:S(2)}) collective-permute-start(f32[8,512]{1,0:T(8,128)S(1)} %get-tuple-element.56._.refs_0_.refs_2_), channel_id=1, source_target_pairs={{0,3},{1,2},{2,1},{3,0},{4,7},{5,6},{6,5},{7,4},{8,11},{9,10},{10,... | collective-permute-start | bytes 49160 | tf_op jit(solution)/shard_map/ppermute | solution.py:374
  43.2 7.6 %collective-permute-start.8 = (f32[8,512]{1,0:T(8,128)S(1)}, f32[8,512]{1,0:T(8,128)S(1)}, u32[]{:S(2)}, u32[]{:S(2)}) collective-permute-start(f32[8,512]{1,0:T(8,128)S(1)} %get-tuple-element.56._.refs_0_.refs_2_), channel_id=1, source_target_pairs={{0,2},{1,3},{2,0},{3,1},{4,6},{5,7},{6,4},{7,5},{8,10},{9,11},{10,... | collective-permute-start | bytes 49160 | tf_op jit(solution)/shard_map/ppermute | solution.py:374
  43.2 7.6 %collective-permute-start.7 = (f32[8,512]{1,0:T(8,128)S(1)}, f32[8,512]{1,0:T(8,128)S(1)}, u32[]{:S(2)}, u32[]{:S(2)}) collective-permute-start(f32[8,512]{1,0:T(8,128)S(1)} %get-tuple-element.56._.refs_0_.refs_2_), channel_id=1, source_target_pairs={{0,1},{1,0},{2,3},{3,2},{4,5},{5,4},{6,7},{7,6},{8,9},{9,8},{10,11... | collective-permute-start | bytes 49160 | tf_op jit(solution)/shard_map/ppermute | solution.py:374
  46.0 7.0 %collective-permute-start.12 = (f32[8,128]{1,0:T(8,128)S(1)}, f32[8,128]{1,0:T(8,128)S(1)}, u32[]{:S(2)}, u32[]{:S(2)}) collective-permute-start(f32[8,128]{1,0:T(8,128)S(1)} %get-tuple-element.58._.refs_6_), channel_id=1, source_target_pairs={{0,3},{1,2},{2,1},{3,0},{4,7},{5,6},{6,5},{7,4},{8,11},{9,10},{10,... | collective-permute-start | bytes 12296 | tf_op jit(solution)/shard_map/ppermute | solution.py:374
  50.1 4.5 %collective-permute-start.11 = (f32[8,128]{1,0:T(8,128)S(1)}, f32[8,128]{1,0:T(8,128)S(1)}, u32[]{:S(2)}, u32[]{:S(2)}) collective-permute-start(f32[8,128]{1,0:T(8,128)S(1)} %get-tuple-element.58._.refs_6_), channel_id=1, source_target_pairs={{0,2},{1,3},{2,0},{3,1},{4,6},{5,7},{6,4},{7,5},{8,10},{9,11},{10,... | collective-permute-start | bytes 12296 | tf_op jit(solution)/shard_map/ppermute | solution.py:374
  50.2 4.5 %collective-permute-start.10 = (f32[8,128]{1,0:T(8,128)S(1)}, f32[8,128]{1,0:T(8,128)S(1)}, u32[]{:S(2)}, u32[]{:S(2)}) collective-permute-start(f32[8,128]{1,0:T(8,128)S(1)} %get-tuple-element.58._.refs_6_), channel_id=1, source_target_pairs={{0,1},{1,0},{2,3},{3,2},{4,5},{5,4},{6,7},{7,6},{8,9},{9,8},{10,11... | collective-permute-start | bytes 12296 | tf_op jit(solution)/shard_map/ppermute | solution.py:374

commit v9 on v6

--- a/solution.py
+++ b/solution.py
@@ -92,15 +92,22 @@
         copy.wait()
 
 
+def tail_kernel(k_ref, tail_ref, sem):
+    rows = k_ref.shape[0]
+    copy = pltpu.make_async_copy(k_ref.at[pl.ds(rows - WINDOW, WINDOW), :], tail_ref, sem)
+    copy.start()
+    copy.wait()
+
+
 def pass_kernel(*_):
     pass
 
 
-def chip_kernel(keep_ref, beside_ref, _, out_ref, __):
+def chip_kernel(keep_ref, beside_ref, out_ref):
     out_ref[...] = keep_ref[...] + beside_ref[...]
 
 
-def totals_kernel(k_hbm, v_hbm, keep_ref, send_ref, half_ref, k_ref, v_ref, tail_k_ref, tail_v_ref, sems):
+def totals_kernel(k_hbm, v_hbm, keep_ref, send_ref, half_ref, k_ref, v_ref, tail_v_ref, sems):
     core = lax.axis_index("ctx") % 2
     rows, width = k_ref.shape
     middle = rows // 2
@@ -136,7 +143,6 @@
             keep_ref[pair] = jnp.where(core == 0, states[0], states[1])
             send_ref[pair] = jnp.where(core == 0, states[1], states[0])
         columns = head_columns(group, 1, GROUP * HD)
-        tail_k_ref[:, columns] = k_ref[rows - WINDOW :, columns]
         tail_v_ref[:, columns] = v_ref[rows - WINDOW :, columns]
 
 
@@ -395,7 +401,12 @@
     packed = array(heads // 2, HD, HD)
     first_tile = array(WINDOW, width)
     dma = pltpu.SemaphoreType.DMA
-    keep, send, half, held_k, held_v, tail_k, tail_v = call(
+    route = [(i, i + 1) for i in range(lax.axis_size("ctx") - 1)]
+    tail_k = call(
+        tail_kernel, "tail", in_specs=[anywhere], out_shape=first_tile, scratch_shapes=[dma]
+    )(keys)
+    before_k = lax.ppermute(tail_k, "ctx", route)
+    keep, send, half, held_k, held_v, tail_v = call(
         totals_kernel,
         "totals",
         in_specs=[anywhere, anywhere],
@@ -406,19 +417,11 @@
             array(rows, width),
             array(rows, width),
             first_tile,
-            first_tile,
         ],
         scratch_shapes=[dma((2, heads // GROUP))],
     )(keys, values)
     beside = swap(send, "ctx", 1)
-    chip, tail_k = call(
-        chip_kernel,
-        "chip",
-        in_specs=[vmem, vmem, anywhere],
-        out_specs=[vmem, anywhere],
-        out_shape=[packed, first_tile],
-        input_output_aliases={2: 1},
-    )(keep, beside, tail_k)
+    chip = call(chip_kernel, "chip", in_specs=[vmem, vmem], out_shape=packed)(keep, beside)
     held_q = call(
         load_kernel,
         "load",
@@ -426,8 +429,6 @@
         out_shape=array(rows, width),
         scratch_shapes=[dma((4,))],
     )(queries, chip)
-    route = [(i, i + 1) for i in range(lax.axis_size("ctx") - 1)]
-    before_k = lax.ppermute(tail_k, "ctx", route)
 
     def local(begin, count, after):
         taken = count * HD
@@ -450,8 +451,8 @@
             input_output_aliases={0: 0},
         )(array_now, after)
 
-    begin = heads * 3 // 4 // GROUP * GROUP
-    parts = [local(0, begin, None)]
+    begin = heads // 2
+    parts = [local(0, begin, before_k)]
     message = None
     if lax.axis_size("ctx") == 8:
         first = first_phase(chip)

time: 53.8 us -> 58.7 us (1.091)
  waiting for transfers between devices: 12.4 us -> 16.1 us
  Pallas kernels: 25.3 us -> 26.8 us
    ppermute x1, waiting for transfers between devices: 2.38 us -> 8.93 us  [shards(): before_k = lax.ppermute(tail_k, 'ctx', route)]
    ppermute x1, waiting for transfers between devices: 2.65 us -> 0.01 us  [second_phase(): lax.ppermute(message, 'ctx', [(i, i ^ (4 if i % 2 == 0 else 2)) for i in...]
    ppermute x8, starting transfers between devices: 9.57 us -> 11.3 us  [swap(): lax.ppermute(block, axis, [(i, i ^ bit) for i in range(lax.axis_size(axis...]
    pallas_call x1 -> x2, Pallas kernels: 0.08 us -> 1.29 us  [the longest x1 1.23 us: shards(): call(tail_kernel, 'tail', in_specs=[anywhere], out_shape=first_tile, scra...]
    ppermute x1, starting transfers between devices: 1.55 us -> 0.34 us  [first_phase(): lax.ppermute(chip, 'ctx', [(i, i ^ (2 if i % 2 == 0 else 4)) for i in ran...]
    ppermute x8, waiting for transfers between devices: 5.43 us -> 4.69 us  [swap(): lax.ppermute(block, axis, [(i, i ^ bit) for i in range(lax.axis_size(axis...]
    ppermute x1, starting transfers between devices: 0.77 us -> 0.07 us  [second_phase(): lax.ppermute(message, 'ctx', [(i, i ^ (4 if i % 2 == 0 else 2)) for i in...]
    ppermute x1, waiting for transfers between devices: 1.89 us -> 2.49 us  [shards(): before_v = lax.ppermute(pass_on(tail_v, window_sums[1]), 'ctx', route)]
  transfers between devices with their start and end apart: 12 -> 12, of which waited for: 6 -> 5; matrix products, arithmetic and copies ran while one was open for 0% -> 0% of each run, Pallas kernels for 37% -> 41%
where the time goes in v9:
time: 58.7 us; the launch traced here: 58.6 us
  Pallas kernels  26.8 us (46%)
  waiting for transfers between devices  16.1 us (27%)
  starting transfers between devices  15.5 us (26%)
    ppermute x8, starting transfers between devices, swap(): lax.ppermute(block, axis, [(i, i ^ bit) for i in range(lax.axis_size(axis...  11.3 us
    pallas_call x2, Pallas kernels, local(): call(functools.partial(local_kernel, begin, len(after)), 'local', in_spec...  9.06 us
    ppermute x1, waiting for transfers between devices, shards(): before_k = lax.ppermute(tail_k, 'ctx', route)  8.93 us
    ppermute x8, waiting for transfers between devices, swap(): lax.ppermute(block, axis, [(i, i ^ bit) for i in range(lax.axis_size(axis...  4.69 us
    pallas_call x1, Pallas kernels, shards(): call(totals_kernel, 'totals', in_specs=[anywhere, anywhere], out_shape=[p...  4.24 us
    pallas_call x1, Pallas kernels, shards(): call(first_weights_kernel, 'first_weights', in_specs=[smem] + [vmem] * 4,...  2.85 us
    pallas_call x1, Pallas kernels, shards(): call(functools.partial(earlier_kernel, len(parts)), 'earlier', in_specs=[...  2.5 us
    ppermute x1, waiting for transfers between devices, shards(): before_v = lax.ppermute(pass_on(tail_v, window_sums[1]), 'ctx', route)  2.49 us
  transfers between devices with their start and end apart: 12, of which 5 were waited for; matrix products, arithmetic and copies ran while one was open for 0% of the time, Pallas kernels for 41%

profile of v9, /device:TPU:4, one launch (start us, length us, event | category | flops | bytes accessed | tf_op | source)
XLA Modules:
  0.0 58.6 jit_solution(1589888973771639279)
XLA Ops:
  0.0 1.2 %tail.1 = f32[128,2048]{1,0:T(8,128)S(1)} custom-call(f32[512,2048]{1,0:T(8,128)} %k_ref.1), custom_call_target="tpu_custom_call" | custom-call | tf_op jit(solution)/shard_map/tail/pallas_call | solution.py:405
  1.2 1.9 %collective-permute-start.1 = (f32[128,2048]{1,0:T(8,128)S(1)}, f32[128,2048]{1,0:T(8,128)S(1)}, u32[]{:S(2)}, u32[]{:S(2)}) collective-permute-start(f32[128,2048]{1,0:T(8,128)S(1)} %tail.1), channel_id=1, source_target_pairs={{0,4},{4,8},{8,12},{12,16},{16,20},{20,24},{24,28},{1,5},{5,9},{9,... | collective-permute-start | bytes 3145736 | tf_op jit(solution)/shard_map/ppermute | solution.py:408
  3.2 4.2 %totals.1 = (f32[8,128,128]{2,1,0:T(8,128)S(1)}, f32[8,128,128]{2,1,0:T(8,128)S(1)}, f32[16,128,128]{2,1,0:T(8,128)S(1)}, f32[512,2048]{1,0:T(8,128)S(1)}, f32[5...) custom-call(f32[512,2048]{1,0:T(8,128)} %k_ref.1, f32[512,2048]{1,0:T(8,128)} %v_hbm.1), custom_call_target="tpu_custom_call" | custom-call | tf_op jit(solution)/shard_map/totals/pallas_call | solution.py:409
  7.4 1.7 %collective-permute-start = (f32[8,128,128]{2,1,0:T(8,128)S(1)}, f32[8,128,128]{2,1,0:T(8,128)S(1)}, u32[]{:S(2)}, u32[]{:S(2)}) collective-permute-start(f32[8,128,128]{2,1,0:T(8,128)S(1)} %get-tuple-element.27), channel_id=1, source_target_pairs={{0,4},{4,0},{8,12},{12,8},{16,20},{20,16},{24,28},{28,24},{1,5},{5... | collective-permute-start | bytes 1572872 | tf_op jit(solution)/shard_map/ppermute | solution.py:351
  9.1 1.5 %collective-permute-done.beside_ref = f32[8,128,128]{2,1,0:T(8,128)S(1)} collective-permute-done((f32[8,128,128]{2,1,0:T(8,128)S(1)}, f32[8,128,128]{2,1,0:T(8,128)S(1)}, u32[]{:S(2)}, u32[]{:S(2)}) %collective-permute-start) | collective-permute-done | bytes 524320 | tf_op jit(solution)/shard_map/ppermute | solution.py:351
  10.7 0.3 collective-permute-start.2
  11.0 2.2 %load.1.q_ref = f32[512,2048]{1,0:T(8,128)S(1)} custom-call(f32[512,2048]{1,0:T(8,128)} %q_hbm.1, f32[8,128,128]{2,1,0:T(8,128)S(1)} %chip.1._.chip_ref), custom_call_target="tpu_custom_call" | custom-call | tf_op jit(solution)/shard_map/load/pallas_call | solution.py:425
  13.3 8.9 %collective-permute-done.1.tail_ref.refs_0_ = f32[128,2048]{1,0:T(8,128)S(1)} collective-permute-done((f32[128,2048]{1,0:T(8,128)S(1)}, f32[128,2048]{1,0:T(8,128)S(1)}, u32[]{:S(2)}, u32[]{:S(2)}) %collective-permute-start.1) | collective-permute-done | bytes 1048608 | tf_op jit(solution)/shard_map/ppermute | solution.py:408
  22.2 4.5 %local.2 = (f32[512,1024]{1,0:T(8,128)S(1)}, f32[512,1024]{1,0:T(8,128)S(1)}, f32[8,512]{1,0:T(8,128)S(1)}) custom-call(f32[2,16]{1,0:T(2,128)S(1)} %copy-done, f32[512,2048]{1,0:T(8,128)S(1)} %load.1.q_ref, f32[512,2048]{1,0:T(8,128)S(1)} %get-tuple-element.28.k_ref, f32[512,2048]{1,0:T(8,128)S(1)} %get-tuple-element.29.v_ref, ...), custom_call_target="tpu_custom_call" | custom-call | tf_op jit(solution)/shard_map/local/pallas_call | solution.py:436
  26.9 4.5 %local.3 = (f32[512,1024]{1,0:T(8,128)S(1)}, f32[512,1024]{1,0:T(8,128)S(1)}, f32[8,512]{1,0:T(8,128)S(1)}) custom-call(f32[2,16]{1,0:T(2,128)S(1)} %copy-done, f32[512,2048]{1,0:T(8,128)S(1)} %load.1.q_ref, f32[512,2048]{1,0:T(8,128)S(1)} %get-tuple-element.28.k_ref, f32[512,2048]{1,0:T(8,128)S(1)} %get-tuple-element.29.v_ref, ...), custom_call_target="tpu_custom_call" | custom-call | tf_op jit(solution)/shard_map/local/pallas_call | solution.py:436
  31.5 1.9 %collective-permute-start.3 = (f32[128,2048]{1,0:T(8,128)S(1)}, f32[128,2048]{1,0:T(8,128)S(1)}, u32[]{:S(2)}, u32[]{:S(2)}) collective-permute-start(f32[128,2048]{1,0:T(8,128)S(1)} %pass.1), channel_id=1, source_target_pairs={{0,4},{4,8},{8,12},{12,16},{16,20},{20,24},{24,28},{1,5},{5,9},{9,... | collective-permute-start | bytes 3145736 | tf_op jit(solution)/shard_map/ppermute | solution.py:467
  33.4 2.9 %first_weights.1 = (bf16[128,4096]{1,0:T(8,128)(2,1)S(1)}, f32[128,2048]{1,0:T(8,128)S(1)}) custom-call(f32[2,16]{1,0:T(2,128)S(1)} %copy-done, f32[512,2048]{1,0:T(8,128)S(1)} %load.1.q_ref, f32[512,2048]{1,0:T(8,128)S(1)} %get-tuple-element.28.k_ref, f32[512,2048]{1,0:T(8,128)S(1)} %get-tuple-element.29.v_ref, ...), custom_call_target="tpu_custom_call" | custom-call | tf_op jit(solution)/shard_map/first_weights/pallas_call | solution.py:468
  36.5 1.0 %collective-permute-start.5 = (f32[8,128,128]{2,1,0:T(8,128)S(1)}, f32[8,128,128]{2,1,0:T(8,128)S(1)}, u32[]{:S(2)}, u32[]{:S(2)}) collective-permute-start(f32[8,128,128]{2,1,0:T(8,128)S(1)} %get-tuple-element.37), channel_id=1, source_target_pairs={{0,4},{4,0},{8,12},{12,8},{16,20},{20,16},{24,28},{28,24},{1,5},{5... | collective-permute-start | bytes 1572872 | tf_op jit(solution)/shard_map/ppermute | solution.py:351
  37.5 1.5 %collective-permute-done.5.other_ref = f32[8,128,128]{2,1,0:T(8,128)S(1)} collective-permute-done((f32[8,128,128]{2,1,0:T(8,128)S(1)}, f32[8,128,128]{2,1,0:T(8,128)S(1)}, u32[]{:S(2)}, u32[]{:S(2)}) %collective-permute-start.5) | collective-permute-done | bytes 524320 | tf_op jit(solution)/shard_map/ppermute | solution.py:351
  39.1 2.5 %earlier.1 = (f32[512,1024]{1,0:T(8,128)S(1)}, f32[512,1024]{1,0:T(8,128)S(1)}, f32[8,512]{1,0:T(8,128)S(1)}) custom-call(f32[2,16]{1,0:T(2,128)S(1)} %copy-done, f32[16,128,128]{2,1,0:T(8,128)S(1)} %get-tuple-element.35.half_ref, f32[8,128,128]{2,1,0:T(8,128)S(1)} %get-tuple-element.36.mine_ref, f32[8,128,128]{2,1,0:T(8,128)S(1)} %collective-permute-done.5.other_ref, ...), custom_call_target="tpu_custom_call" | custom-call | tf_op jit(solution)/shard_map/earlier/pallas_call | solution.py:490
  41.6 1.6 %collective-permute-start.6 = (f32[8,512]{1,0:T(8,128)S(1)}, f32[8,512]{1,0:T(8,128)S(1)}, u32[]{:S(2)}, u32[]{:S(2)}) collective-permute-start(f32[8,512]{1,0:T(8,128)S(1)} %get-tuple-element.40._.refs_0_.refs_2_), channel_id=1, source_target_pairs={{0,1},{1,0},{2,3},{3,2},{4,5},{5,4},{6,7},{7,6},{8,9},{9,8},{10,11... | collective-permute-start | bytes 49160 | tf_op jit(solution)/shard_map/ppermute | solution.py:351
  43.2 2.6 %collective-permute-start.7 = (f32[8,512]{1,0:T(8,128)S(1)}, f32[8,512]{1,0:T(8,128)S(1)}, u32[]{:S(2)}, u32[]{:S(2)}) collective-permute-start(f32[8,512]{1,0:T(8,128)S(1)} %get-tuple-element.40._.refs_0_.refs_2_), channel_id=1, source_target_pairs={{0,2},{1,3},{2,0},{3,1},{4,6},{5,7},{6,4},{7,5},{8,10},{9,11},{10,... | collective-permute-start | bytes 49160 | tf_op jit(solution)/shard_map/ppermute | solution.py:351
  46.0 2.5 %collective-permute-done.3.tail_v_ref = f32[128,2048]{1,0:T(8,128)S(1)} collective-permute-done((f32[128,2048]{1,0:T(8,128)S(1)}, f32[128,2048]{1,0:T(8,128)S(1)}, u32[]{:S(2)}, u32[]{:S(2)}) %collective-permute-start.3) | collective-permute-done | bytes 1048608 | tf_op jit(solution)/shard_map/ppermute | solution.py:467
  48.5 0.8 %first_values.1 = (f32[128,2048]{1,0:T(8,128)S(1)}, f32[8,128]{1,0:T(8,128)S(1)}) custom-call(bf16[128,4096]{1,0:T(8,128)(2,1)S(1)} %get-tuple-element.30.weights_ref, f32[128,2048]{1,0:T(8,128)S(1)} %get-tuple-element.31.refs_0_.now_ref, f32[128,2048]{1,0:T(8,128)S(1)} %collective-permute-done.3.tail_v_ref, f32[8,512]{1,0:T(8,128)S(1)} %get-tuple-element.40._.refs_0_.refs_2_), custom_call_target="tpu_custom_call" | custom-call | tf_op jit(solution)/shard_map/first_values/pallas_call | solution.py:498
  49.3 2.6 %collective-permute-start.10 = (f32[8,128]{1,0:T(8,128)S(1)}, f32[8,128]{1,0:T(8,128)S(1)}, u32[]{:S(2)}, u32[]{:S(2)}) collective-permute-start(f32[8,128]{1,0:T(8,128)S(1)} %get-tuple-element.42._.refs_6_), channel_id=1, source_target_pairs={{0,2},{1,3},{2,0},{3,1},{4,6},{5,7},{6,4},{7,5},{8,10},{9,11},{10,... | collective-permute-start | bytes 12296 | tf_op jit(solution)/shard_map/ppermute | solution.py:351
  51.9 1.4 %collective-permute-start.11 = (f32[8,128]{1,0:T(8,128)S(1)}, f32[8,128]{1,0:T(8,128)S(1)}, u32[]{:S(2)}, u32[]{:S(2)}) collective-permute-start(f32[8,128]{1,0:T(8,128)S(1)} %get-tuple-element.42._.refs_6_), channel_id=1, source_target_pairs={{0,3},{1,2},{2,1},{3,0},{4,7},{5,6},{6,5},{7,4},{8,11},{9,10},{10,... | collective-permute-start | bytes 12296 | tf_op jit(solution)/shard_map/ppermute | solution.py:351
  53.5 2.2 %scale.1._ = f32[512,2048]{1,0:T(8,128)} custom-call(f32[8,128]{1,0:T(8,128)S(1)} %get-tuple-element.42._.refs_6_, f32[8,512]{1,0:T(8,128)S(1)} %get-tuple-element.40._.refs_0_.refs_2_, f32[8,512]{1,0:T(8,128)S(1)} %collective-permute-done.6.refs_1_.refs_3_, f32[8,512]{1,0:T(8,128)S(1)} %collective-permute-done.7.refs_2_.refs_4_, ...), custom_call_target="tpu_custom_call" | custom-call | tf_op jit(solution)/shard_map/scale/pallas_call | solution.py:505
  55.7 1.6 %collective-permute-done.11.refs_9_ = f32[8,128]{1,0:T(8,128)S(1)} collective-permute-done((f32[8,128]{1,0:T(8,128)S(1)}, f32[8,128]{1,0:T(8,128)S(1)}, u32[]{:S(2)}, u32[]{:S(2)}) %collective-permute-start.11) | collective-permute-done | bytes 4128 | tf_op jit(solution)/shard_map/ppermute | solution.py:351
  57.3 1.2 %first_scale.1 = f32[512,2048]{1,0:T(8,128)} custom-call(f32[128,2048]{1,0:T(8,128)S(1)} %get-tuple-element.41.a_ref, f32[512,2048]{1,0:T(8,128)} %scale.1._, f32[512,1024]{1,0:T(8,128)S(1)} %get-tuple-element.45.refs_6_.refs_0_, f32[512,1024]{1,0:T(8,128)S(1)} %get-tuple-element.46.refs_7_.refs_1_, ...), custom_call_target="tpu_custom_call", output_to_operand_aliasing={{}: (1, {})} | custom-call | tf_op jit(solution)/shard_map/first_scale/pallas_call | solution.py:513
  (16 shorter events, 1.0 us)
Async XLA Ops:
  1.2 20.9 %collective-permute-start.1 = (f32[128,2048]{1,0:T(8,128)S(1)}, f32[128,2048]{1,0:T(8,128)S(1)}, u32[]{:S(2)}, u32[]{:S(2)}) collective-permute-start(f32[128,2048]{1,0:T(8,128)S(1)} %tail.1), channel_id=1, source_target_pairs={{0,4},{4,8},{8,12},{12,16},{16,20},{20,24},{24,28},{1,5},{5,9},{9,... | collective-permute-start | bytes 3145736 | tf_op jit(solution)/shard_map/ppermute | solution.py:408
  7.4 3.2 %collective-permute-start = (f32[8,128,128]{2,1,0:T(8,128)S(1)}, f32[8,128,128]{2,1,0:T(8,128)S(1)}, u32[]{:S(2)}, u32[]{:S(2)}) collective-permute-start(f32[8,128,128]{2,1,0:T(8,128)S(1)} %get-tuple-element.27), channel_id=1, source_target_pairs={{0,4},{4,0},{8,12},{12,8},{16,20},{20,16},{24,28},{28,24},{1,5},{5... | collective-permute-start | bytes 1572872 | tf_op jit(solution)/shard_map/ppermute | solution.py:351
  10.7 11.5 %copy-start = (f32[2,16]{1,0:T(2,128)S(1)}, f32[2,16]{1,0:T(2,128)}, u32[]{:S(2)}) copy-start(f32[2,16]{1,0:T(2,128)} %gain_ref.7) | copy-start | bytes 388
  10.7 16.0 %collective-permute-start.2 = (f32[8,128,128]{2,1,0:T(8,128)S(1)}, f32[8,128,128]{2,1,0:T(8,128)S(1)}, u32[]{:S(2)}, u32[]{:S(2)}) collective-permute-start(f32[8,128,128]{2,1,0:T(8,128)S(1)} %chip.1._.chip_ref), channel_id=1, source_target_pairs={{0,8},{4,20},{8,0},{12,28},{16,24},{20,4},{24,16},{28,12},{1,9},{5... | collective-permute-start | bytes 1572872 | tf_op jit(solution)/shard_map/ppermute | solution.py:359
  26.8 9.4 %collective-permute-start.4 = (f32[8,128,128]{2,1,0:T(8,128)S(1)}, f32[8,128,128]{2,1,0:T(8,128)S(1)}, u32[]{:S(2)}, u32[]{:S(2)}) collective-permute-start(f32[8,128,128]{2,1,0:T(8,128)S(1)} %message.1.refs_0_), channel_id=1, source_target_pairs={{0,16},{4,12},{8,24},{12,4},{16,0},{20,28},{24,8},{28,20},{1,17},{... | collective-permute-start | bytes 1572872 | tf_op jit(solution)/shard_map/ppermute | solution.py:363
  31.5 17.0 %collective-permute-start.3 = (f32[128,2048]{1,0:T(8,128)S(1)}, f32[128,2048]{1,0:T(8,128)S(1)}, u32[]{:S(2)}, u32[]{:S(2)}) collective-permute-start(f32[128,2048]{1,0:T(8,128)S(1)} %pass.1), channel_id=1, source_target_pairs={{0,4},{4,8},{8,12},{12,16},{16,20},{20,24},{24,28},{1,5},{5,9},{9,... | collective-permute-start | bytes 3145736 | tf_op jit(solution)/shard_map/ppermute | solution.py:467
  36.5 2.6 %collective-permute-start.5 = (f32[8,128,128]{2,1,0:T(8,128)S(1)}, f32[8,128,128]{2,1,0:T(8,128)S(1)}, u32[]{:S(2)}, u32[]{:S(2)}) collective-permute-start(f32[8,128,128]{2,1,0:T(8,128)S(1)} %get-tuple-element.37), channel_id=1, source_target_pairs={{0,4},{4,0},{8,12},{12,8},{16,20},{20,16},{24,28},{28,24},{1,5},{5... | collective-permute-start | bytes 1572872 | tf_op jit(solution)/shard_map/ppermute | solution.py:351
  41.6 11.7 %collective-permute-start.6 = (f32[8,512]{1,0:T(8,128)S(1)}, f32[8,512]{1,0:T(8,128)S(1)}, u32[]{:S(2)}, u32[]{:S(2)}) collective-permute-start(f32[8,512]{1,0:T(8,128)S(1)} %get-tuple-element.40._.refs_0_.refs_2_), channel_id=1, source_target_pairs={{0,1},{1,0},{2,3},{3,2},{4,5},{5,4},{6,7},{7,6},{8,9},{9,8},{10,11... | collective-permute-start | bytes 49160 | tf_op jit(solution)/shard_map/ppermute | solution.py:351
  43.2 10.3 %collective-permute-start.7 = (f32[8,512]{1,0:T(8,128)S(1)}, f32[8,512]{1,0:T(8,128)S(1)}, u32[]{:S(2)}, u32[]{:S(2)}) collective-permute-start(f32[8,512]{1,0:T(8,128)S(1)} %get-tuple-element.40._.refs_0_.refs_2_), channel_id=1, source_target_pairs={{0,2},{1,3},{2,0},{3,1},{4,6},{5,7},{6,4},{7,5},{8,10},{9,11},{10,... | collective-permute-start | bytes 49160 | tf_op jit(solution)/shard_map/ppermute | solution.py:351
  45.8 7.7 %collective-permute-start.8 = (f32[8,512]{1,0:T(8,128)S(1)}, f32[8,512]{1,0:T(8,128)S(1)}, u32[]{:S(2)}, u32[]{:S(2)}) collective-permute-start(f32[8,512]{1,0:T(8,128)S(1)} %get-tuple-element.40._.refs_0_.refs_2_), channel_id=1, source_target_pairs={{0,3},{1,2},{2,1},{3,0},{4,7},{5,6},{6,5},{7,4},{8,11},{9,10},{10,... | collective-permute-start | bytes 49160 | tf_op jit(solution)/shard_map/ppermute | solution.py:351
  49.3 6.4 %collective-permute-start.10 = (f32[8,128]{1,0:T(8,128)S(1)}, f32[8,128]{1,0:T(8,128)S(1)}, u32[]{:S(2)}, u32[]{:S(2)}) collective-permute-start(f32[8,128]{1,0:T(8,128)S(1)} %get-tuple-element.42._.refs_6_), channel_id=1, source_target_pairs={{0,2},{1,3},{2,0},{3,1},{4,6},{5,7},{6,4},{7,5},{8,10},{9,11},{10,... | collective-permute-start | bytes 12296 | tf_op jit(solution)/shard_map/ppermute | solution.py:351
  51.9 5.4 %collective-permute-start.11 = (f32[8,128]{1,0:T(8,128)S(1)}, f32[8,128]{1,0:T(8,128)S(1)}, u32[]{:S(2)}, u32[]{:S(2)}) collective-permute-start(f32[8,128]{1,0:T(8,128)S(1)} %get-tuple-element.42._.refs_6_), channel_id=1, source_target_pairs={{0,3},{1,2},{2,1},{3,0},{4,7},{5,6},{6,5},{7,4},{8,11},{9,10},{10,... | collective-permute-start | bytes 12296 | tf_op jit(solution)/shard_map/ppermute | solution.py:351
  53.3 4.0 %collective-permute-start.9 = (f32[8,128]{1,0:T(8,128)S(1)}, f32[8,128]{1,0:T(8,128)S(1)}, u32[]{:S(2)}, u32[]{:S(2)}) collective-permute-start(f32[8,128]{1,0:T(8,128)S(1)} %get-tuple-element.42._.refs_6_), channel_id=1, source_target_pairs={{0,1},{1,0},{2,3},{3,2},{4,5},{5,4},{6,7},{7,6},{8,9},{9,8},{10,11... | collective-permute-start | bytes 12296 | tf_op jit(solution)/shard_map/ppermute | solution.py:351

commit v10 on v8

--- a/solution.py
+++ b/solution.py
@@ -101,7 +101,7 @@
     return copies
 
 
-def totals_kernel(part, k_hbm, v_hbm, _, total_ref, half_ref, k_ref, v_ref, tail_ref, sems):
+def totals_kernel(part, k_hbm, v_hbm, _, total_ref, half_ref, k_ref, v_ref, sems):
     middle = k_ref.shape[0] // 2
     copies = column_copies(part, (k_hbm, v_hbm), (k_ref, v_ref), sems)
     for group in copies:
@@ -118,11 +118,13 @@
             second = outer_state(k_high[middle:], k_low[middle:], v_high[middle:], v_low[middle:])
             half_ref[head] = first
             total_ref[head] = first + second
-    tail_ref[...] = k_ref[k_ref.shape[0] - WINDOW :, :]
-
-
-def chip_kernel(keep_ref, beside_ref, _, out_ref, __):
+
+
+def chip_kernel(keep_ref, beside_ref, first_ref, second_ref, out_ref, tail_ref):
     out_ref[...] = keep_ref[...] + beside_ref[...]
+    rows, width = first_ref.shape
+    tail_ref[:, :width] = first_ref[rows - WINDOW :, :]
+    tail_ref[:, width:] = second_ref[rows - WINDOW :, :]
 
 
 def tail_kernel(first_ref, second_ref, _, tail_ref):
@@ -143,7 +145,7 @@
 
 
 def local_kernel(part, gain_ref, q_in_ref, k_ref, v_ref, *refs):
-    a_ref, b_ref, sum_ref = refs[2:5]
+    a_ref, b_ref, sum_ref = refs[1:4]
     square_ref = refs[-2]
     lower = lower_mask()
     below = jnp.where(lower, 1.0, 0.0).astype(BF16)
@@ -153,7 +155,7 @@
     groups = width // (GROUP * HD)
     begin = first_head(part, 2 * width // HD)
     if part == 0:
-        q_refs, sems = refs[5:7], refs[-1]
+        q_refs, sems = refs[4:6], refs[-1]
         q_ref = q_refs[0]
 
         def load(number, group):
@@ -265,7 +267,7 @@
 
 def first_weights_kernel(gain_ref, *refs):
     q_refs, k_refs, v_refs = (refs[2 * i : 2 * i + 2] for i in range(3))
-    *tail_refs, weights_ref, out_ref = refs[6:]
+    tail_ref, weights_ref, out_ref = refs[6:]
     lower = lower_mask()
     reachable = jnp.logical_or(lower, lax.axis_index("ctx") > 0)
     top = slice(0, WINDOW)
@@ -275,9 +277,10 @@
         scores = []
         for head in range(width // HD):
             columns = slice(head * HD, (head + 1) * HD)
+            sent = (1 - part) * width + head * HD
             qq = side(*halves(q_refs[part][top, columns]))
             now = folded(dot_rows(qq, wide_keys(*halves(k_refs[part][top, columns]))))
-            before = folded(dot_rows(qq, wide_keys(*halves(tail_refs[part][:, columns]))))
+            before = folded(dot_rows(qq, wide_keys(*halves(tail_ref[:, sent : sent + HD]))))
             scores.append(jnp.where(reachable, jnp.where(lower, now, before), -jnp.inf))
         for head in range(width // HD):
             columns = slice(head * HD, (head + 1) * HD)
@@ -425,7 +428,6 @@
     half = array(rows, width // 2)
     first_tile = array(WINDOW, width)
     dma = pltpu.SemaphoreType.DMA
-    half_tile = array(WINDOW, width // 2)
     groups = heads // (2 * GROUP)
 
     def totals(part, after):
@@ -433,35 +435,27 @@
             functools.partial(totals_kernel, part),
             "totals",
             in_specs=[anywhere] * 3,
-            out_shape=[packed, packed, half, half, half_tile],
+            out_shape=[packed, packed, half, half],
             scratch_shapes=[dma((2, groups))],
         )(keys, values, after)
 
-    def local(part, query_source, *after):
+    def local(part, query_source, after):
         return call(
             functools.partial(local_kernel, part),
             "local",
-            in_specs=[smem, vmem if part else anywhere, vmem, vmem, anywhere, anywhere],
+            in_specs=[smem, vmem if part else anywhere, vmem, vmem, anywhere],
             out_shape=[half, half, array(8, rows)] + ([] if part else [half, half]),
             scratch_shapes=[pltpu.VMEM((rows, HD), F32)] + ([] if part else [dma((2, groups))]),
-        )(head_gain, query_source, held_k[part], held_v[part], *after)
+        )(head_gain, query_source, held_k[part], held_v[part], after)
 
     route = [(i, i + 1) for i in range(lax.axis_size("ctx") - 1)]
-    send, *held_0, tail_0 = totals(0, queries)
+    send, *held_0 = totals(0, queries)
     beside = swap(send, "ctx", 1)
-    before_1 = lax.ppermute(tail_0, "ctx", route)
-    keep, *held_1, tail_1 = totals(1, send)
+    keep, *held_1 = totals(1, send)
     early, held_k, held_v = zip(held_0, held_1)
-    chip, tail_1 = call(
-        chip_kernel,
-        "chip",
-        in_specs=[vmem, vmem, anywhere],
-        out_specs=[vmem, anywhere],
-        out_shape=[packed, half_tile],
-        input_output_aliases={2: 1},
-    )(keep, beside, tail_1)
-    before_0 = lax.ppermute(tail_1, "ctx", route)
-    *local_0, query_0, query_1 = local(0, queries, chip, before_1)
+    chip, tail_k = call(chip_kernel, "chip", out_shape=[packed, first_tile])(keep, beside, *held_k)
+    before_k = lax.ppermute(tail_k, "ctx", route)
+    *local_0, query_0, query_1 = local(0, queries, chip)
     message = local_0[2]
     if lax.axis_size("ctx") == 8:
         first = first_phase(chip)
@@ -472,7 +466,7 @@
             out_shape=packed,
         )(first, chip, message)
     held_q = query_0, query_1
-    window, linear, window_sums = zip(local_0, local(1, query_1, message, message))
+    window, linear, window_sums = zip(local_0, local(1, query_1, message))
     tail_v = call(
         tail_kernel, "tail", in_specs=[vmem, vmem, anywhere], out_shape=first_tile
     )(*held_v, window_sums[1])
@@ -480,9 +474,9 @@
     first_weights, first_now = call(
         first_weights_kernel,
         "first_weights",
-        in_specs=[smem] + [vmem] * 8,
+        in_specs=[smem] + [vmem] * 7,
         out_shape=[array(WINDOW, 2 * width, dtype=BF16), first_tile],
-    )(head_gain, *held_q, *held_k, *held_v, before_0, before_1)
+    )(head_gain, *held_q, *held_k, *held_v, before_k)
 
     if lax.axis_size("ctx") == 8:
         second = second_phase(message)

time: 57 us -> 53.9 us (0.946); the launches traced: 56.1 us -> 53.7 us
  starting transfers between devices: 20.2 us -> 16 us
  waiting for transfers between devices: 9.43 us -> 11.2 us
    ppermute x2 -> x1, waiting for transfers between devices: 5.29 us -> 0.21 us  [shards(): before_k = lax.ppermute(tail_k, 'ctx', route)]
    ppermute x1, waiting for transfers between devices: 0.01 us -> 2.76 us  [second_phase(): lax.ppermute(message, 'ctx', [(i, i ^ (4 if i % 2 == 0 else 2)) for i in...]
    ppermute x1, waiting for transfers between devices: 0.01 us -> 2.65 us  [first_phase(): lax.ppermute(chip, 'ctx', [(i, i ^ (2 if i % 2 == 0 else 4)) for i in ran...]
    ppermute x2 -> x1, starting transfers between devices: 4.42 us -> 1.91 us  [shards(): before_k = lax.ppermute(tail_k, 'ctx', route)]
    ppermute x1, starting transfers between devices: 4.53 us -> 2.1 us  [shards(): before_v = lax.ppermute(tail_v, 'ctx', route)]
    ppermute x1, waiting for transfers between devices: 0.54 us -> 1.97 us  [shards(): before_v = lax.ppermute(tail_v, 'ctx', route)]
    ppermute x1, starting transfers between devices: 0.35 us -> 1 us  [second_phase(): lax.ppermute(message, 'ctx', [(i, i ^ (4 if i % 2 == 0 else 2)) for i in...]
  transfers between devices with their start and end apart: 13 -> 12, of which waited for: 4 -> 6; matrix products, arithmetic and copies ran while one was open for 0% -> 0% of each run, Pallas kernels for 39% -> 41%
where the time goes in v10:
time: 53.9 us; the launch traced here: 53.7 us
  Pallas kernels  26.2 us (49%)
  starting transfers between devices  16 us (30%)
  waiting for transfers between devices  11.2 us (21%)
    pallas_call x2, Pallas kernels, local(): call(functools.partial(local_kernel, part), 'local', in_specs=[smem, vmem...  10.3 us
    ppermute x8, starting transfers between devices, swap(): lax.ppermute(block, axis, [(i, i ^ bit) for i in range(lax.axis_size(axis...  9.48 us
    pallas_call x2, Pallas kernels, totals(): call(functools.partial(totals_kernel, part), 'totals', in_specs=[anywhere...  5.75 us
    ppermute x8, waiting for transfers between devices, swap(): lax.ppermute(block, axis, [(i, i ^ bit) for i in range(lax.axis_size(axis...  3.6 us
    pallas_call x1, Pallas kernels, shards(): call(first_weights_kernel, 'first_weights', in_specs=[smem] + [vmem] * 7,...  2.85 us
    ppermute x1, waiting for transfers between devices, second_phase(): lax.ppermute(message, 'ctx', [(i, i ^ (4 if i % 2 == 0 else 2)) for i in...  2.76 us
    ppermute x1, waiting for transfers between devices, first_phase(): lax.ppermute(chip, 'ctx', [(i, i ^ (2 if i % 2 == 0 else 4)) for i in ran...  2.65 us
    pallas_call x1, Pallas kernels, shards(): call(earlier_kernel, 'earlier', in_specs=[smem] + [vmem] * 10, out_shape=...  2.41 us
  transfers between devices with their start and end apart: 12, of which 6 were waited for; matrix products, arithmetic and copies ran while one was open for 0% of the time, Pallas kernels for 41%

profile of v10, /device:TPU:4, one launch (start us, length us, event | category | flops | bytes accessed | tf_op | source)
XLA Modules:
  0.0 53.7 jit_solution(12267806356439656253)
XLA Ops:
  0.0 2.9 %totals.2 = (f32[8,128,128]{2,1,0:T(8,128)S(1)}, f32[8,128,128]{2,1,0:T(8,128)S(1)}, f32[512,1024]{1,0:T(8,128)S(1)}, f32[512,1024]{1,0:T(8,128)S(1)}) custom-call(f32[512,2048]{1,0:T(8,128)} %k_hbm.3, f32[512,2048]{1,0:T(8,128)} %v_hbm.3, f32[512,2048]{1,0:T(8,128)} %q_in_ref.1), custom_call_target="tpu_custom_call" | custom-call | tf_op jit(solution)/shard_map/totals/pallas_call | solution.py:434
  3.0 2.9 %totals.3 = (f32[8,128,128]{2,1,0:T(8,128)S(1)}, f32[8,128,128]{2,1,0:T(8,128)S(1)}, f32[512,1024]{1,0:T(8,128)S(1)}, f32[512,1024]{1,0:T(8,128)S(1)}) custom-call(f32[512,2048]{1,0:T(8,128)} %k_hbm.3, f32[512,2048]{1,0:T(8,128)} %v_hbm.3, f32[8,128,128]{2,1,0:T(8,128)S(1)} %get-tuple-element.34._), custom_call_target="tpu_custom_call" | custom-call | tf_op jit(solution)/shard_map/totals/pallas_call | solution.py:434
  6.0 1.6 %collective-permute-start.2 = (f32[8,128,128]{2,1,0:T(8,128)S(1)}, f32[8,128,128]{2,1,0:T(8,128)S(1)}, u32[]{:S(2)}, u32[]{:S(2)}) collective-permute-start(f32[8,128,128]{2,1,0:T(8,128)S(1)} %get-tuple-element.37.refs_0_.chip_ref), channel_id=1, source_target_pairs={{0,8},{4,20},{8,0},{12,28},{16,24},{20,4},{24,16},{28,12},{1,9},{5... | collective-permute-start | bytes 1572872 | tf_op jit(solution)/shard_map/ppermute | solution.py:385
  7.6 1.9 %collective-permute-start.1 = (f32[128,2048]{1,0:T(8,128)S(1)}, f32[128,2048]{1,0:T(8,128)S(1)}, u32[]{:S(2)}, u32[]{:S(2)}) collective-permute-start(f32[128,2048]{1,0:T(8,128)S(1)} %get-tuple-element.41), channel_id=1, source_target_pairs={{0,4},{4,8},{8,12},{12,16},{16,20},{20,24},{24,28},{1,5},{5,9},{9,... | collective-permute-start | bytes 3145736 | tf_op jit(solution)/shard_map/ppermute | solution.py:457
  9.5 5.8 %local.2 = (f32[512,1024]{1,0:T(8,128)S(1)}, f32[512,1024]{1,0:T(8,128)S(1)}, f32[8,512]{1,0:T(8,128)S(1)}, f32[512,1024]{1,0:T(8,128)S(1)}, f32[512,1024]{1,0:T(8,128)S(1)}) custom-call(f32[2,16]{1,0:T(2,128)S(1)} %copy-done, f32[512,2048]{1,0:T(8,128)} %q_in_ref.1, f32[512,1024]{1,0:T(8,128)S(1)} %get-tuple-element.32.first_ref.k_ref.refs_2_, ...), custom_call_target="tpu_custom_call" | custom-call | tf_op jit(solution)/shard_map/local/pallas_call | solution.py:443
  15.3 2.7 %collective-permute-done.2.first_ref = f32[8,128,128]{2,1,0:T(8,128)S(1)} collective-permute-done((f32[8,128,128]{2,1,0:T(8,128)S(1)}, f32[8,128,128]{2,1,0:T(8,128)S(1)}, u32[]{:S(2)}, u32[]{:S(2)}) %collective-permute-start.2) | collective-permute-done | bytes 524320 | tf_op jit(solution)/shard_map/ppermute | solution.py:385
  18.1 1.0 %collective-permute-start.4 = (f32[8,128,128]{2,1,0:T(8,128)S(1)}, f32[8,128,128]{2,1,0:T(8,128)S(1)}, u32[]{:S(2)}, u32[]{:S(2)}) collective-permute-start(f32[8,128,128]{2,1,0:T(8,128)S(1)} %message.1.refs_0_), channel_id=1, source_target_pairs={{0,16},{4,12},{8,24},{12,4},{16,0},{20,28},{24,8},{28,20},{1,17},{... | collective-permute-start | bytes 1572872 | tf_op jit(solution)/shard_map/ppermute | solution.py:389
  19.1 4.5 %local.3 = (f32[512,1024]{1,0:T(8,128)S(1)}, f32[512,1024]{1,0:T(8,128)S(1)}, f32[8,512]{1,0:T(8,128)S(1)}) custom-call(f32[2,16]{1,0:T(2,128)S(1)} %copy-done, f32[512,1024]{1,0:T(8,128)S(1)} %get-tuple-element.39.refs_1_.q_in_ref.refs_5_, f32[512,1024]{1,0:T(8,128)S(1)} %get-tuple-element.36.second_ref.refs_3_.k_ref, ...), custom_call_target="tpu_custom_call" | custom-call | tf_op jit(solution)/shard_map/local/pallas_call | solution.py:443
  23.7 2.1 %collective-permute-start.3 = (f32[128,2048]{1,0:T(8,128)S(1)}, f32[128,2048]{1,0:T(8,128)S(1)}, u32[]{:S(2)}, u32[]{:S(2)}) collective-permute-start(f32[128,2048]{1,0:T(8,128)S(1)} %tail.1), channel_id=1, source_target_pairs={{0,4},{4,8},{8,12},{12,16},{16,20},{20,24},{24,28},{1,5},{5,9},{9,... | collective-permute-start | bytes 3145736 | tf_op jit(solution)/shard_map/ppermute | solution.py:473
  25.8 0.2 collective-permute-done.1.refs_6_
  26.0 2.9 %first_weights.1 = (bf16[128,4096]{1,0:T(8,128)(2,1)S(1)}, f32[128,2048]{1,0:T(8,128)S(1)}) custom-call(f32[2,16]{1,0:T(2,128)S(1)} %copy-done, f32[512,1024]{1,0:T(8,128)S(1)} %get-tuple-element.38.refs_0_.refs_4_, f32[512,1024]{1,0:T(8,128)S(1)} %get-tuple-element.39.refs_1_.q_in_ref.refs_5_, f32[512,1024]{1,0:T(8,128)S(1)} %get-tuple-element.32.first_ref.k_ref.refs_2_, ...), custom_call_target="tpu_custom_call" | custom-call | tf_op jit(solution)/shard_map/first_weights/pallas_call | solution.py:474
  28.9 2.8 %collective-permute-done.4.second_ref = f32[8,128,128]{2,1,0:T(8,128)S(1)} collective-permute-done((f32[8,128,128]{2,1,0:T(8,128)S(1)}, f32[8,128,128]{2,1,0:T(8,128)S(1)}, u32[]{:S(2)}, u32[]{:S(2)}) %collective-permute-start.4) | collective-permute-done | bytes 524320 | tf_op jit(solution)/shard_map/ppermute | solution.py:389
  31.6 0.2 prefix.1
  31.9 1.9 %collective-permute-done.5.refs_0_ = f32[8,128,128]{2,1,0:T(8,128)S(1)} collective-permute-done((f32[8,128,128]{2,1,0:T(8,128)S(1)}, f32[8,128,128]{2,1,0:T(8,128)S(1)}, u32[]{:S(2)}, u32[]{:S(2)}) %collective-permute-start.5) | collective-permute-done | bytes 524320 | tf_op jit(solution)/shard_map/ppermute | solution.py:377
  33.8 2.4 %earlier.1 = (f32[512,1024]{1,0:T(8,128)S(1)}, f32[512,1024]{1,0:T(8,128)S(1)}, f32[8,512]{1,0:T(8,128)S(1)}) custom-call(f32[2,16]{1,0:T(2,128)S(1)} %copy-done, f32[8,128,128]{2,1,0:T(8,128)S(1)} %collective-permute-done.5.refs_0_, f32[8,128,128]{2,1,0:T(8,128)S(1)} %get-tuple-element.47.refs_1_, f32[8,128,128]{2,1,0:T(8,128)S(1)} %get-tuple-element.48.refs_2_, ...), custom_call_target="tpu_custom_call" | custom-call | tf_op jit(solution)/shard_map/earlier/pallas_call | solution.py:496
  36.2 4.0 %collective-permute-start.8 = (f32[8,512]{1,0:T(8,128)S(1)}, f32[8,512]{1,0:T(8,128)S(1)}, u32[]{:S(2)}, u32[]{:S(2)}) collective-permute-start(f32[8,512]{1,0:T(8,128)S(1)} %get-tuple-element.52._.refs_0_.refs_2_), channel_id=1, source_target_pairs={{0,3},{1,2},{2,1},{3,0},{4,7},{5,6},{6,5},{7,4},{8,11},{9,10},{10,... | collective-permute-start | bytes 49160 | tf_op jit(solution)/shard_map/ppermute | solution.py:377
  40.3 0.6 %collective-permute-start.6 = (f32[8,512]{1,0:T(8,128)S(1)}, f32[8,512]{1,0:T(8,128)S(1)}, u32[]{:S(2)}, u32[]{:S(2)}) collective-permute-start(f32[8,512]{1,0:T(8,128)S(1)} %get-tuple-element.52._.refs_0_.refs_2_), channel_id=1, source_target_pairs={{0,1},{1,0},{2,3},{3,2},{4,5},{5,4},{6,7},{7,6},{8,9},{9,8},{10,11... | collective-permute-start | bytes 49160 | tf_op jit(solution)/shard_map/ppermute | solution.py:377
  40.9 2.0 %collective-permute-done.3.tail_ref = f32[128,2048]{1,0:T(8,128)S(1)} collective-permute-done((f32[128,2048]{1,0:T(8,128)S(1)}, f32[128,2048]{1,0:T(8,128)S(1)}, u32[]{:S(2)}, u32[]{:S(2)}) %collective-permute-start.3) | collective-permute-done | bytes 1048608 | tf_op jit(solution)/shard_map/ppermute | solution.py:473
  42.8 0.8 %first_values.1 = (f32[128,2048]{1,0:T(8,128)S(1)}, f32[8,128]{1,0:T(8,128)S(1)}) custom-call(bf16[128,4096]{1,0:T(8,128)(2,1)S(1)} %get-tuple-element.42.weights_ref, f32[128,2048]{1,0:T(8,128)S(1)} %get-tuple-element.43._.now_ref, f32[128,2048]{1,0:T(8,128)S(1)} %collective-permute-done.3.tail_ref, f32[8,512]{1,0:T(8,128)S(1)} %get-tuple-element.52._.refs_0_.refs_2_), custom_call_target="tpu_custom_call" | custom-call | tf_op jit(solution)/shard_map/first_values/pallas_call | solution.py:504
  43.7 4.1 %collective-permute-start.11 = (f32[8,128]{1,0:T(8,128)S(1)}, f32[8,128]{1,0:T(8,128)S(1)}, u32[]{:S(2)}, u32[]{:S(2)}) collective-permute-start(f32[8,128]{1,0:T(8,128)S(1)} %get-tuple-element.54._.refs_6_), channel_id=1, source_target_pairs={{0,3},{1,2},{2,1},{3,0},{4,7},{5,6},{6,5},{7,4},{8,11},{9,10},{10,... | collective-permute-start | bytes 12296 | tf_op jit(solution)/shard_map/ppermute | solution.py:377
  47.8 0.6 %collective-permute-start.9 = (f32[8,128]{1,0:T(8,128)S(1)}, f32[8,128]{1,0:T(8,128)S(1)}, u32[]{:S(2)}, u32[]{:S(2)}) collective-permute-start(f32[8,128]{1,0:T(8,128)S(1)} %get-tuple-element.54._.refs_6_), channel_id=1, source_target_pairs={{0,1},{1,0},{2,3},{3,2},{4,5},{5,4},{6,7},{7,6},{8,9},{9,8},{10,11... | collective-permute-start | bytes 12296 | tf_op jit(solution)/shard_map/ppermute | solution.py:377
  48.4 2.2 %scale.1._ = f32[512,2048]{1,0:T(8,128)} custom-call(f32[8,128]{1,0:T(8,128)S(1)} %get-tuple-element.54._.refs_6_, f32[8,512]{1,0:T(8,128)S(1)} %get-tuple-element.52._.refs_0_.refs_2_, f32[8,512]{1,0:T(8,128)S(1)} %collective-permute-done.6.refs_1_.refs_3_, f32[8,512]{1,0:T(8,128)S(1)} %collective-permute-done.7.refs_2_.refs_4_, ...), custom_call_target="tpu_custom_call" | custom-call | tf_op jit(solution)/shard_map/scale/pallas_call | solution.py:511
  50.6 1.7 %collective-permute-done.10.refs_8_ = f32[8,128]{1,0:T(8,128)S(1)} collective-permute-done((f32[8,128]{1,0:T(8,128)S(1)}, f32[8,128]{1,0:T(8,128)S(1)}, u32[]{:S(2)}, u32[]{:S(2)}) %collective-permute-start.10) | collective-permute-done | bytes 4128 | tf_op jit(solution)/shard_map/ppermute | solution.py:377
  52.3 1.3 %first_scale.1 = f32[512,2048]{1,0:T(8,128)} custom-call(f32[128,2048]{1,0:T(8,128)S(1)} %get-tuple-element.53.a_ref, f32[512,2048]{1,0:T(8,128)} %scale.1._, f32[512,1024]{1,0:T(8,128)S(1)} %get-tuple-element.57.refs_6_.refs_0_, f32[512,1024]{1,0:T(8,128)S(1)} %get-tuple-element.58.refs_7_.refs_1_, ...), custom_call_target="tpu_custom_call", output_to_operand_aliasing={{}: (1, {})} | custom-call | tf_op jit(solution)/shard_map/first_scale/pallas_call | solution.py:519
  (15 shorter events, 0.5 us)
Async XLA Ops:
  2.9 3.0 %collective-permute-start = (f32[8,128,128]{2,1,0:T(8,128)S(1)}, f32[8,128,128]{2,1,0:T(8,128)S(1)}, u32[]{:S(2)}, u32[]{:S(2)}) collective-permute-start(f32[8,128,128]{2,1,0:T(8,128)S(1)} %get-tuple-element.34._), channel_id=1, source_target_pairs={{0,4},{4,0},{8,12},{12,8},{16,20},{20,16},{24,28},{28,24},{1,5},{5... | collective-permute-start | bytes 1572872 | tf_op jit(solution)/shard_map/ppermute | solution.py:377
  5.9 3.6 %copy-start = (f32[2,16]{1,0:T(2,128)S(1)}, f32[2,16]{1,0:T(2,128)}, u32[]{:S(2)}) copy-start(f32[2,16]{1,0:T(2,128)} %gain_ref.7) | copy-start | bytes 388
  6.0 12.0 %collective-permute-start.2 = (f32[8,128,128]{2,1,0:T(8,128)S(1)}, f32[8,128,128]{2,1,0:T(8,128)S(1)}, u32[]{:S(2)}, u32[]{:S(2)}) collective-permute-start(f32[8,128,128]{2,1,0:T(8,128)S(1)} %get-tuple-element.37.refs_0_.chip_ref), channel_id=1, source_target_pairs={{0,8},{4,20},{8,0},{12,28},{16,24},{20,4},{24,16},{28,12},{1,9},{5... | collective-permute-start | bytes 1572872 | tf_op jit(solution)/shard_map/ppermute | solution.py:385
  7.6 18.4 %collective-permute-start.1 = (f32[128,2048]{1,0:T(8,128)S(1)}, f32[128,2048]{1,0:T(8,128)S(1)}, u32[]{:S(2)}, u32[]{:S(2)}) collective-permute-start(f32[128,2048]{1,0:T(8,128)S(1)} %get-tuple-element.41), channel_id=1, source_target_pairs={{0,4},{4,8},{8,12},{12,16},{16,20},{20,24},{24,28},{1,5},{5,9},{9,... | collective-permute-start | bytes 3145736 | tf_op jit(solution)/shard_map/ppermute | solution.py:457
  18.1 13.6 %collective-permute-start.4 = (f32[8,128,128]{2,1,0:T(8,128)S(1)}, f32[8,128,128]{2,1,0:T(8,128)S(1)}, u32[]{:S(2)}, u32[]{:S(2)}) collective-permute-start(f32[8,128,128]{2,1,0:T(8,128)S(1)} %message.1.refs_0_), channel_id=1, source_target_pairs={{0,16},{4,12},{8,24},{12,4},{16,0},{20,28},{24,8},{28,20},{1,17},{... | collective-permute-start | bytes 1572872 | tf_op jit(solution)/shard_map/ppermute | solution.py:389
  23.7 19.2 %collective-permute-start.3 = (f32[128,2048]{1,0:T(8,128)S(1)}, f32[128,2048]{1,0:T(8,128)S(1)}, u32[]{:S(2)}, u32[]{:S(2)}) collective-permute-start(f32[128,2048]{1,0:T(8,128)S(1)} %tail.1), channel_id=1, source_target_pairs={{0,4},{4,8},{8,12},{12,16},{16,20},{20,24},{24,28},{1,5},{5,9},{9,... | collective-permute-start | bytes 3145736 | tf_op jit(solution)/shard_map/ppermute | solution.py:473
  31.8 2.0 %collective-permute-start.5 = (f32[8,128,128]{2,1,0:T(8,128)S(1)}, f32[8,128,128]{2,1,0:T(8,128)S(1)}, u32[]{:S(2)}, u32[]{:S(2)}) collective-permute-start(f32[8,128,128]{2,1,0:T(8,128)S(1)} %get-tuple-element.46), channel_id=1, source_target_pairs={{0,4},{4,0},{8,12},{12,8},{16,20},{20,16},{24,28},{28,24},{1,5},{5... | collective-permute-start | bytes 1572872 | tf_op jit(solution)/shard_map/ppermute | solution.py:377
  36.2 11.5 %collective-permute-start.8 = (f32[8,512]{1,0:T(8,128)S(1)}, f32[8,512]{1,0:T(8,128)S(1)}, u32[]{:S(2)}, u32[]{:S(2)}) collective-permute-start(f32[8,512]{1,0:T(8,128)S(1)} %get-tuple-element.52._.refs_0_.refs_2_), channel_id=1, source_target_pairs={{0,3},{1,2},{2,1},{3,0},{4,7},{5,6},{6,5},{7,4},{8,11},{9,10},{10,... | collective-permute-start | bytes 49160 | tf_op jit(solution)/shard_map/ppermute | solution.py:377
  40.3 8.1 %collective-permute-start.7 = (f32[8,512]{1,0:T(8,128)S(1)}, f32[8,512]{1,0:T(8,128)S(1)}, u32[]{:S(2)}, u32[]{:S(2)}) collective-permute-start(f32[8,512]{1,0:T(8,128)S(1)} %get-tuple-element.52._.refs_0_.refs_2_), channel_id=1, source_target_pairs={{0,2},{1,3},{2,0},{3,1},{4,6},{5,7},{6,4},{7,5},{8,10},{9,11},{10,... | collective-permute-start | bytes 49160 | tf_op jit(solution)/shard_map/ppermute | solution.py:377
  40.3 8.1 %collective-permute-start.6 = (f32[8,512]{1,0:T(8,128)S(1)}, f32[8,512]{1,0:T(8,128)S(1)}, u32[]{:S(2)}, u32[]{:S(2)}) collective-permute-start(f32[8,512]{1,0:T(8,128)S(1)} %get-tuple-element.52._.refs_0_.refs_2_), channel_id=1, source_target_pairs={{0,1},{1,0},{2,3},{3,2},{4,5},{5,4},{6,7},{7,6},{8,9},{9,8},{10,11... | collective-permute-start | bytes 49160 | tf_op jit(solution)/shard_map/ppermute | solution.py:377
  43.7 6.9 %collective-permute-start.11 = (f32[8,128]{1,0:T(8,128)S(1)}, f32[8,128]{1,0:T(8,128)S(1)}, u32[]{:S(2)}, u32[]{:S(2)}) collective-permute-start(f32[8,128]{1,0:T(8,128)S(1)} %get-tuple-element.54._.refs_6_), channel_id=1, source_target_pairs={{0,3},{1,2},{2,1},{3,0},{4,7},{5,6},{6,5},{7,4},{8,11},{9,10},{10,... | collective-permute-start | bytes 12296 | tf_op jit(solution)/shard_map/ppermute | solution.py:377
  47.8 4.5 %collective-permute-start.10 = (f32[8,128]{1,0:T(8,128)S(1)}, f32[8,128]{1,0:T(8,128)S(1)}, u32[]{:S(2)}, u32[]{:S(2)}) collective-permute-start(f32[8,128]{1,0:T(8,128)S(1)} %get-tuple-element.54._.refs_6_), channel_id=1, source_target_pairs={{0,2},{1,3},{2,0},{3,1},{4,6},{5,7},{6,4},{7,5},{8,10},{9,11},{10,... | collective-permute-start | bytes 12296 | tf_op jit(solution)/shard_map/ppermute | solution.py:377
  47.8 4.5 %collective-permute-start.9 = (f32[8,128]{1,0:T(8,128)S(1)}, f32[8,128]{1,0:T(8,128)S(1)}, u32[]{:S(2)}, u32[]{:S(2)}) collective-permute-start(f32[8,128]{1,0:T(8,128)S(1)} %get-tuple-element.54._.refs_6_), channel_id=1, source_target_pairs={{0,1},{1,0},{2,3},{3,2},{4,5},{5,4},{6,7},{7,6},{8,9},{9,8},{10,11... | collective-permute-start | bytes 12296 | tf_op jit(solution)/shard_map/ppermute | solution.py:377

commit v11 on v10

--- a/solution.py
+++ b/solution.py
@@ -337,9 +337,10 @@
 
 def scale_kernel(parts, _, *refs):
     sums, refs = refs[:parts], refs[parts:]
-    a_refs, b_refs, (out_hbm, out_ref, sems) = refs[:2], refs[2:4], refs[4:]
+    a_refs, b_refs, (out_hbm, first_ref, out_ref, sems) = refs[:2], refs[2:4], refs[4:]
     inverse = inverse_norm(added(sums)).T
     width = a_refs[0].shape[1]
+    top = slice(0, WINDOW)
     copies = []
     for n in range(out_ref.shape[0] // WINDOW):
         held = slice(n * WINDOW, (n + 1) * WINDOW)
@@ -349,25 +350,23 @@
             columns = slice(part * width, (part + 1) * width)
             out_ref[held, columns] = a_refs[part][rows, :] * inverse_a + b_refs[part][rows, :] * inverse_b
             copies.append(write(part, rows, held, out_ref, out_hbm, sems.at[n, part]))
+    for part in range(2):
+        first_ref[:, part * width : (part + 1) * width] = b_refs[part][top, :] * inverse[top, 1:2]
     for copy in copies:
         copy.wait()
 
 
-def first_scale_kernel(parts, a_ref, _, *refs):
-    b_refs, refs = refs[:2], refs[2:]
-    sums, first_sums, (out_hbm, out_ref, sems) = refs[:parts], refs[parts : 2 * parts], refs[2 * parts :]
-    inverse_a = inverse_norm(added(first_sums)).T[:, 0:1]
-    inverse_b = inverse_norm(added(sums)[:, :WINDOW]).T[:, 1:2]
-    width = b_refs[0].shape[1]
+def first_scale_kernel(parts, a_ref, b_ref, _, *refs):
+    sums, (out_hbm, out_ref, sems) = refs[:parts], refs[parts:]
+    inverse_a = inverse_norm(added(sums)).T[:, 0:1]
+    width = b_ref.shape[1] // 2
     copies = []
     pieces = sems.shape[0]
     for n in range(pieces):
         rows = slice(n * WINDOW // pieces, (n + 1) * WINDOW // pieces)
         for part in range(2):
             columns = slice(part * width, (part + 1) * width)
-            out_ref[rows, columns] = (
-                a_ref[rows, columns] * inverse_a[rows] + b_refs[part][rows, :] * inverse_b[rows]
-            )
+            out_ref[rows, columns] = a_ref[rows, columns] * inverse_a[rows] + b_ref[rows, columns]
             copies.append(write(part, rows, rows, out_ref, out_hbm, sems.at[n, part]))
     for copy in copies:
         copy.wait()
@@ -386,7 +385,7 @@
 
 
 def second_phase(message):
-    return lax.ppermute(message, "ctx", [(i, i ^ (4 if i % 2 == 0 else 2)) for i in range(8)])
+    return lax.ppermute(message, "ctx", [(i, i ^ (4 if i % 2 == 0 else 2)) for i in range(8) if i != 3])
 
 
 def doubled_prefix(chip):
@@ -508,23 +507,23 @@
         out_shape=[first_tile, array(8, WINDOW)],
     )(first_weights, first_now, before_v, sums[0])
     first_sums = everyone(first_sums, "head")
-    out = call(
+    out, first_b = call(
         functools.partial(scale_kernel, len(sums)),
         "scale",
         in_specs=[anywhere] + [vmem] * (4 + len(sums)),
-        out_specs=anywhere,
-        out_shape=array(rows, width),
+        out_specs=[anywhere, vmem],
+        out_shape=[array(rows, width), first_tile],
         scratch_shapes=[pltpu.VMEM((rows - WINDOW, width), F32), dma((rows // WINDOW - 1, 2))],
     )(first_sums[0], *sums, *window, *linear)
     return call(
         functools.partial(first_scale_kernel, len(sums)),
         "first_scale",
-        in_specs=[vmem, anywhere] + [vmem] * (2 + 2 * len(sums)),
+        in_specs=[vmem, vmem, anywhere] + [vmem] * len(sums),
         out_specs=anywhere,
         out_shape=array(rows, width),
         scratch_shapes=[pltpu.VMEM((WINDOW, width), F32), dma((4, 2))],
-        input_output_aliases={1: 0},
-    )(first_a, out, *linear, *sums, *first_sums)
+        input_output_aliases={2: 0},
+    )(first_a, first_b, out, *first_sums)
 
 
 def solution(mesh):

time: 53.9 us -> 63.3 us (1.17)
  waiting for transfers between devices: 11.2 us -> 18.5 us
  starting transfers between devices: 16 us -> 17.6 us
    ppermute x1, waiting for transfers between devices: 2.76 us -> 12.3 us  [second_phase(): lax.ppermute(message, 'ctx', [(i, i ^ (4 if i % 2 == 0 else 2)) for i in...]
    ppermute x1, waiting for transfers between devices: 1.97 us -> 0.01 us  [shards(): before_v = lax.ppermute(tail_v, 'ctx', route)]
    ppermute x1, starting transfers between devices: 1 us -> 2.84 us  [second_phase(): lax.ppermute(message, 'ctx', [(i, i ^ (4 if i % 2 == 0 else 2)) for i in...]
  transfers between devices with their start and end apart: 12 -> 12, of which waited for: 6 -> 4; matrix products, arithmetic and copies ran while one was open for 0% -> 0% of each run, Pallas kernels for 41% -> 35%
where the time goes in v11:
time: 63.3 us; the launch traced here: 62.6 us
  Pallas kernels  26.2 us (41%)
  waiting for transfers between devices  18.5 us (29%)
  starting transfers between devices  17.6 us (28%)
    ppermute x1, waiting for transfers between devices, second_phase(): lax.ppermute(message, 'ctx', [(i, i ^ (4 if i % 2 == 0 else 2)) for i in...  12.3 us
    pallas_call x2, Pallas kernels, local(): call(functools.partial(local_kernel, part), 'local', in_specs=[smem, vmem...  10.3 us
    ppermute x8, starting transfers between devices, swap(): lax.ppermute(block, axis, [(i, i ^ bit) for i in range(lax.axis_size(axis...  9.2 us
    pallas_call x2, Pallas kernels, totals(): call(functools.partial(totals_kernel, part), 'totals', in_specs=[anywhere...  5.75 us
    ppermute x8, waiting for transfers between devices, swap(): lax.ppermute(block, axis, [(i, i ^ bit) for i in range(lax.axis_size(axis...  3.57 us
    pallas_call x1, Pallas kernels, shards(): call(first_weights_kernel, 'first_weights', in_specs=[smem] + [vmem] * 7,...  2.86 us
    ppermute x1, starting transfers between devices, second_phase(): lax.ppermute(message, 'ctx', [(i, i ^ (4 if i % 2 == 0 else 2)) for i in...  2.84 us
    ppermute x1, waiting for transfers between devices, first_phase(): lax.ppermute(chip, 'ctx', [(i, i ^ (2 if i % 2 == 0 else 4)) for i in ran...  2.65 us
  transfers between devices with their start and end apart: 12, of which 4 were waited for; matrix products, arithmetic and copies ran while one was open for 0% of the time, Pallas kernels for 35%

profile of v11, /device:TPU:4, one launch (start us, length us, event | category | flops | bytes accessed | tf_op | source)
XLA Modules:
  0.0 62.6 jit_solution(2938575998461809490)
XLA Ops:
  0.0 2.9 %totals.2 = (f32[8,128,128]{2,1,0:T(8,128)S(1)}, f32[8,128,128]{2,1,0:T(8,128)S(1)}, f32[512,1024]{1,0:T(8,128)S(1)}, f32[512,1024]{1,0:T(8,128)S(1)}) custom-call(f32[512,2048]{1,0:T(8,128)} %k_hbm.3, f32[512,2048]{1,0:T(8,128)} %v_hbm.3, f32[512,2048]{1,0:T(8,128)} %q_in_ref.1), custom_call_target="tpu_custom_call" | custom-call | tf_op jit(solution)/shard_map/totals/pallas_call | solution.py:433
  3.0 2.9 %totals.3 = (f32[8,128,128]{2,1,0:T(8,128)S(1)}, f32[8,128,128]{2,1,0:T(8,128)S(1)}, f32[512,1024]{1,0:T(8,128)S(1)}, f32[512,1024]{1,0:T(8,128)S(1)}) custom-call(f32[512,2048]{1,0:T(8,128)} %k_hbm.3, f32[512,2048]{1,0:T(8,128)} %v_hbm.3, f32[8,128,128]{2,1,0:T(8,128)S(1)} %get-tuple-element.36._), custom_call_target="tpu_custom_call" | custom-call | tf_op jit(solution)/shard_map/totals/pallas_call | solution.py:433
  5.9 0.1 chip.1
  6.0 1.6 %collective-permute-start.2 = (f32[8,128,128]{2,1,0:T(8,128)S(1)}, f32[8,128,128]{2,1,0:T(8,128)S(1)}, u32[]{:S(2)}, u32[]{:S(2)}) collective-permute-start(f32[8,128,128]{2,1,0:T(8,128)S(1)} %get-tuple-element.39.refs_0_.chip_ref), channel_id=1, source_target_pairs={{0,8},{4,20},{8,0},{12,28},{16,24},{20,4},{24,16},{28,12},{1,9},{5... | collective-permute-start | bytes 1572872 | tf_op jit(solution)/shard_map/ppermute | solution.py:384
  7.6 1.9 %collective-permute-start.1 = (f32[128,2048]{1,0:T(8,128)S(1)}, f32[128,2048]{1,0:T(8,128)S(1)}, u32[]{:S(2)}, u32[]{:S(2)}) collective-permute-start(f32[128,2048]{1,0:T(8,128)S(1)} %get-tuple-element.43), channel_id=1, source_target_pairs={{0,4},{4,8},{8,12},{12,16},{16,20},{20,24},{24,28},{1,5},{5,9},{9,... | collective-permute-start | bytes 3145736 | tf_op jit(solution)/shard_map/ppermute | solution.py:456
  9.5 5.8 %local.2 = (f32[512,1024]{1,0:T(8,128)S(1)}, f32[512,1024]{1,0:T(8,128)S(1)}, f32[8,512]{1,0:T(8,128)S(1)}, f32[512,1024]{1,0:T(8,128)S(1)}, f32[512,1024]{1,0:T(8,128)S(1)}) custom-call(f32[2,16]{1,0:T(2,128)S(1)} %copy-done, f32[512,2048]{1,0:T(8,128)} %q_in_ref.1, f32[512,1024]{1,0:T(8,128)S(1)} %get-tuple-element.34.first_ref.k_ref.refs_2_, ...), custom_call_target="tpu_custom_call" | custom-call | tf_op jit(solution)/shard_map/local/pallas_call | solution.py:442
  15.3 2.7 %collective-permute-done.2.first_ref = f32[8,128,128]{2,1,0:T(8,128)S(1)} collective-permute-done((f32[8,128,128]{2,1,0:T(8,128)S(1)}, f32[8,128,128]{2,1,0:T(8,128)S(1)}, u32[]{:S(2)}, u32[]{:S(2)}) %collective-permute-start.2) | collective-permute-done | bytes 524320 | tf_op jit(solution)/shard_map/ppermute | solution.py:384
  18.0 0.1 message.1.refs_0_
  18.1 2.8 %collective-permute-start.4 = (f32[8,128,128]{2,1,0:T(8,128)S(1)}, f32[8,128,128]{2,1,0:T(8,128)S(1)}, u32[]{:S(2)}, u32[]{:S(2)}) collective-permute-start(f32[8,128,128]{2,1,0:T(8,128)S(1)} %message.1.refs_0_), channel_id=1, source_target_pairs={{0,16},{4,12},{8,24},{16,0},{20,28},{24,8},{28,20},{1,17},{5,13},{... | collective-permute-start | bytes 1572872 | tf_op jit(solution)/shard_map/ppermute | solution.py:388
  20.9 4.5 %local.3 = (f32[512,1024]{1,0:T(8,128)S(1)}, f32[512,1024]{1,0:T(8,128)S(1)}, f32[8,512]{1,0:T(8,128)S(1)}) custom-call(f32[2,16]{1,0:T(2,128)S(1)} %copy-done, f32[512,1024]{1,0:T(8,128)S(1)} %get-tuple-element.41.refs_1_.q_in_ref.refs_5_, f32[512,1024]{1,0:T(8,128)S(1)} %get-tuple-element.38.second_ref.refs_3_.k_ref, ...), custom_call_target="tpu_custom_call" | custom-call | tf_op jit(solution)/shard_map/local/pallas_call | solution.py:442
  25.5 2.1 %collective-permute-start.3 = (f32[128,2048]{1,0:T(8,128)S(1)}, f32[128,2048]{1,0:T(8,128)S(1)}, u32[]{:S(2)}, u32[]{:S(2)}) collective-permute-start(f32[128,2048]{1,0:T(8,128)S(1)} %tail.1), channel_id=1, source_target_pairs={{0,4},{4,8},{8,12},{12,16},{16,20},{20,24},{24,28},{1,5},{5,9},{9,... | collective-permute-start | bytes 3145736 | tf_op jit(solution)/shard_map/ppermute | solution.py:472
  27.7 2.9 %first_weights.1 = (bf16[128,4096]{1,0:T(8,128)(2,1)S(1)}, f32[128,2048]{1,0:T(8,128)S(1)}) custom-call(f32[2,16]{1,0:T(2,128)S(1)} %copy-done, f32[512,1024]{1,0:T(8,128)S(1)} %get-tuple-element.40.refs_0_.refs_4_, f32[512,1024]{1,0:T(8,128)S(1)} %get-tuple-element.41.refs_1_.q_in_ref.refs_5_, f32[512,1024]{1,0:T(8,128)S(1)} %get-tuple-element.34.first_ref.k_ref.refs_2_, ...), custom_call_target="tpu_custom_call" | custom-call | tf_op jit(solution)/shard_map/first_weights/pallas_call | solution.py:473
  30.5 12.3 %collective-permute-done.4.second_ref = f32[8,128,128]{2,1,0:T(8,128)S(1)} collective-permute-done((f32[8,128,128]{2,1,0:T(8,128)S(1)}, f32[8,128,128]{2,1,0:T(8,128)S(1)}, u32[]{:S(2)}, u32[]{:S(2)}) %collective-permute-start.4) | collective-permute-done | bytes 524320 | tf_op jit(solution)/shard_map/ppermute | solution.py:388
  42.8 0.2 prefix.1
  43.1 1.9 %collective-permute-done.5.refs_0_ = f32[8,128,128]{2,1,0:T(8,128)S(1)} collective-permute-done((f32[8,128,128]{2,1,0:T(8,128)S(1)}, f32[8,128,128]{2,1,0:T(8,128)S(1)}, u32[]{:S(2)}, u32[]{:S(2)}) %collective-permute-start.5) | collective-permute-done | bytes 524320 | tf_op jit(solution)/shard_map/ppermute | solution.py:376
  45.0 2.4 %earlier.1 = (f32[512,1024]{1,0:T(8,128)S(1)}, f32[512,1024]{1,0:T(8,128)S(1)}, f32[8,512]{1,0:T(8,128)S(1)}) custom-call(f32[2,16]{1,0:T(2,128)S(1)} %copy-done, f32[8,128,128]{2,1,0:T(8,128)S(1)} %collective-permute-done.5.refs_0_, f32[8,128,128]{2,1,0:T(8,128)S(1)} %get-tuple-element.49.refs_1_, f32[8,128,128]{2,1,0:T(8,128)S(1)} %get-tuple-element.50.refs_2_, ...), custom_call_target="tpu_custom_call" | custom-call | tf_op jit(solution)/shard_map/earlier/pallas_call | solution.py:495
  47.5 4.1 %collective-permute-start.8 = (f32[8,512]{1,0:T(8,128)S(1)}, f32[8,512]{1,0:T(8,128)S(1)}, u32[]{:S(2)}, u32[]{:S(2)}) collective-permute-start(f32[8,512]{1,0:T(8,128)S(1)} %get-tuple-element.54._.refs_0_), channel_id=1, source_target_pairs={{0,3},{1,2},{2,1},{3,0},{4,7},{5,6},{6,5},{7,4},{8,11},{9,10},{10,... | collective-permute-start | bytes 49160 | tf_op jit(solution)/shard_map/ppermute | solution.py:376
  51.5 0.6 collective-permute-start.6
  52.1 0.8 %first_values.1 = (f32[128,2048]{1,0:T(8,128)S(1)}, f32[8,128]{1,0:T(8,128)S(1)}) custom-call(bf16[128,4096]{1,0:T(8,128)(2,1)S(1)} %get-tuple-element.44.weights_ref, f32[128,2048]{1,0:T(8,128)S(1)} %get-tuple-element.45._.now_ref, f32[128,2048]{1,0:T(8,128)S(1)} %collective-permute-done.3.tail_ref, f32[8,512]{1,0:T(8,128)S(1)} %get-tuple-element.54._.refs_0_), custom_call_target="tpu_custom_call" | custom-call | tf_op jit(solution)/shard_map/first_values/pallas_call | solution.py:503
  52.9 3.8 %collective-permute-start.11 = (f32[8,128]{1,0:T(8,128)S(1)}, f32[8,128]{1,0:T(8,128)S(1)}, u32[]{:S(2)}, u32[]{:S(2)}) collective-permute-start(f32[8,128]{1,0:T(8,128)S(1)} %get-tuple-element.56._.refs_0_), channel_id=1, source_target_pairs={{0,3},{1,2},{2,1},{3,0},{4,7},{5,6},{6,5},{7,4},{8,11},{9,10},{10,... | collective-permute-start | bytes 12296 | tf_op jit(solution)/shard_map/ppermute | solution.py:376
  56.7 0.6 collective-permute-start.9
  57.4 2.2 %scale.1 = (f32[512,2048]{1,0:T(8,128)}, f32[128,2048]{1,0:T(8,128)S(1)}) custom-call(f32[8,128]{1,0:T(8,128)S(1)} %get-tuple-element.56._.refs_0_, f32[8,512]{1,0:T(8,128)S(1)} %get-tuple-element.54._.refs_0_, f32[8,512]{1,0:T(8,128)S(1)} %collective-permute-done.6.refs_1_, f32[8,512]{1,0:T(8,128)S(1)} %collective-permute-done.7.refs_2_, ...), custom_call_target="tpu_custom_call" | custom-call | tf_op jit(solution)/shard_map/scale/pallas_call | solution.py:510
  59.6 1.7 %collective-permute-done.10.refs_2_ = f32[8,128]{1,0:T(8,128)S(1)} collective-permute-done((f32[8,128]{1,0:T(8,128)S(1)}, f32[8,128]{1,0:T(8,128)S(1)}, u32[]{:S(2)}, u32[]{:S(2)}) %collective-permute-start.10) | collective-permute-done | bytes 4128 | tf_op jit(solution)/shard_map/ppermute | solution.py:376
  61.3 1.2 %first_scale.1 = f32[512,2048]{1,0:T(8,128)} custom-call(f32[128,2048]{1,0:T(8,128)S(1)} %get-tuple-element.55.a_ref, f32[128,2048]{1,0:T(8,128)S(1)} %get-tuple-element.61.b_ref, f32[512,2048]{1,0:T(8,128)} %get-tuple-element.62._, f32[8,128]{1,0:T(8,128)S(1)} %get-tuple-element.56._.refs_0_, ...), custom_call_target="tpu_custom_call", output_to_operand_aliasing={{}: (2, {})} | custom-call | tf_op jit(solution)/shard_map/first_scale/pallas_call | solution.py:518
  (15 shorter events, 0.3 us)
Async XLA Ops:
  2.9 3.0 %collective-permute-start = (f32[8,128,128]{2,1,0:T(8,128)S(1)}, f32[8,128,128]{2,1,0:T(8,128)S(1)}, u32[]{:S(2)}, u32[]{:S(2)}) collective-permute-start(f32[8,128,128]{2,1,0:T(8,128)S(1)} %get-tuple-element.36._), channel_id=1, source_target_pairs={{0,4},{4,0},{8,12},{12,8},{16,20},{20,16},{24,28},{28,24},{1,5},{5... | collective-permute-start | bytes 1572872 | tf_op jit(solution)/shard_map/ppermute | solution.py:376
  5.9 3.6 %copy-start = (f32[2,16]{1,0:T(2,128)S(1)}, f32[2,16]{1,0:T(2,128)}, u32[]{:S(2)}) copy-start(f32[2,16]{1,0:T(2,128)} %gain_ref.7) | copy-start | bytes 388
  6.0 12.0 %collective-permute-start.2 = (f32[8,128,128]{2,1,0:T(8,128)S(1)}, f32[8,128,128]{2,1,0:T(8,128)S(1)}, u32[]{:S(2)}, u32[]{:S(2)}) collective-permute-start(f32[8,128,128]{2,1,0:T(8,128)S(1)} %get-tuple-element.39.refs_0_.chip_ref), channel_id=1, source_target_pairs={{0,8},{4,20},{8,0},{12,28},{16,24},{20,4},{24,16},{28,12},{1,9},{5... | collective-permute-start | bytes 1572872 | tf_op jit(solution)/shard_map/ppermute | solution.py:384
  7.6 20.1 %collective-permute-start.1 = (f32[128,2048]{1,0:T(8,128)S(1)}, f32[128,2048]{1,0:T(8,128)S(1)}, u32[]{:S(2)}, u32[]{:S(2)}) collective-permute-start(f32[128,2048]{1,0:T(8,128)S(1)} %get-tuple-element.43), channel_id=1, source_target_pairs={{0,4},{4,8},{8,12},{12,16},{16,20},{20,24},{24,28},{1,5},{5,9},{9,... | collective-permute-start | bytes 3145736 | tf_op jit(solution)/shard_map/ppermute | solution.py:456
  18.1 24.8 %collective-permute-start.4 = (f32[8,128,128]{2,1,0:T(8,128)S(1)}, f32[8,128,128]{2,1,0:T(8,128)S(1)}, u32[]{:S(2)}, u32[]{:S(2)}) collective-permute-start(f32[8,128,128]{2,1,0:T(8,128)S(1)} %message.1.refs_0_), channel_id=1, source_target_pairs={{0,16},{4,12},{8,24},{16,0},{20,28},{24,8},{28,20},{1,17},{5,13},{... | collective-permute-start | bytes 1572872 | tf_op jit(solution)/shard_map/ppermute | solution.py:388
  25.5 26.6 %collective-permute-start.3 = (f32[128,2048]{1,0:T(8,128)S(1)}, f32[128,2048]{1,0:T(8,128)S(1)}, u32[]{:S(2)}, u32[]{:S(2)}) collective-permute-start(f32[128,2048]{1,0:T(8,128)S(1)} %tail.1), channel_id=1, source_target_pairs={{0,4},{4,8},{8,12},{12,16},{16,20},{20,24},{24,28},{1,5},{5,9},{9,... | collective-permute-start | bytes 3145736 | tf_op jit(solution)/shard_map/ppermute | solution.py:472
  43.1 2.0 %collective-permute-start.5 = (f32[8,128,128]{2,1,0:T(8,128)S(1)}, f32[8,128,128]{2,1,0:T(8,128)S(1)}, u32[]{:S(2)}, u32[]{:S(2)}) collective-permute-start(f32[8,128,128]{2,1,0:T(8,128)S(1)} %get-tuple-element.48), channel_id=1, source_target_pairs={{0,4},{4,0},{8,12},{12,8},{16,20},{20,16},{24,28},{28,24},{1,5},{5... | collective-permute-start | bytes 1572872 | tf_op jit(solution)/shard_map/ppermute | solution.py:376
  47.5 9.3 %collective-permute-start.8 = (f32[8,512]{1,0:T(8,128)S(1)}, f32[8,512]{1,0:T(8,128)S(1)}, u32[]{:S(2)}, u32[]{:S(2)}) collective-permute-start(f32[8,512]{1,0:T(8,128)S(1)} %get-tuple-element.54._.refs_0_), channel_id=1, source_target_pairs={{0,3},{1,2},{2,1},{3,0},{4,7},{5,6},{6,5},{7,4},{8,11},{9,10},{10,... | collective-permute-start | bytes 49160 | tf_op jit(solution)/shard_map/ppermute | solution.py:376
  51.5 5.8 %collective-permute-start.7 = (f32[8,512]{1,0:T(8,128)S(1)}, f32[8,512]{1,0:T(8,128)S(1)}, u32[]{:S(2)}, u32[]{:S(2)}) collective-permute-start(f32[8,512]{1,0:T(8,128)S(1)} %get-tuple-element.54._.refs_0_), channel_id=1, source_target_pairs={{0,2},{1,3},{2,0},{3,1},{4,6},{5,7},{6,4},{7,5},{8,10},{9,11},{10,... | collective-permute-start | bytes 49160 | tf_op jit(solution)/shard_map/ppermute | solution.py:376
  51.5 5.8 %collective-permute-start.6 = (f32[8,512]{1,0:T(8,128)S(1)}, f32[8,512]{1,0:T(8,128)S(1)}, u32[]{:S(2)}, u32[]{:S(2)}) collective-permute-start(f32[8,512]{1,0:T(8,128)S(1)} %get-tuple-element.54._.refs_0_), channel_id=1, source_target_pairs={{0,1},{1,0},{2,3},{3,2},{4,5},{5,4},{6,7},{7,6},{8,9},{9,8},{10,11... | collective-permute-start | bytes 49160 | tf_op jit(solution)/shard_map/ppermute | solution.py:376
  52.9 6.6 %collective-permute-start.11 = (f32[8,128]{1,0:T(8,128)S(1)}, f32[8,128]{1,0:T(8,128)S(1)}, u32[]{:S(2)}, u32[]{:S(2)}) collective-permute-start(f32[8,128]{1,0:T(8,128)S(1)} %get-tuple-element.56._.refs_0_), channel_id=1, source_target_pairs={{0,3},{1,2},{2,1},{3,0},{4,7},{5,6},{6,5},{7,4},{8,11},{9,10},{10,... | collective-permute-start | bytes 12296 | tf_op jit(solution)/shard_map/ppermute | solution.py:376
  56.7 4.5 %collective-permute-start.10 = (f32[8,128]{1,0:T(8,128)S(1)}, f32[8,128]{1,0:T(8,128)S(1)}, u32[]{:S(2)}, u32[]{:S(2)}) collective-permute-start(f32[8,128]{1,0:T(8,128)S(1)} %get-tuple-element.56._.refs_0_), channel_id=1, source_target_pairs={{0,2},{1,3},{2,0},{3,1},{4,6},{5,7},{6,4},{7,5},{8,10},{9,11},{10,... | collective-permute-start | bytes 12296 | tf_op jit(solution)/shard_map/ppermute | solution.py:376
  56.7 4.5 %collective-permute-start.9 = (f32[8,128]{1,0:T(8,128)S(1)}, f32[8,128]{1,0:T(8,128)S(1)}, u32[]{:S(2)}, u32[]{:S(2)}) collective-permute-start(f32[8,128]{1,0:T(8,128)S(1)} %get-tuple-element.56._.refs_0_), channel_id=1, source_target_pairs={{0,1},{1,0},{2,3},{3,2},{4,5},{5,4},{6,7},{7,6},{8,9},{9,8},{10,11... | collective-permute-start | bytes 12296 | tf_op jit(solution)/shard_map/ppermute | solution.py:376

commit v12 on v11

--- a/solution.py
+++ b/solution.py
@@ -63,12 +63,12 @@
 
 
 def wide_keys(k_high, k_low):
-    return stack(side(k_high, k_high), side(k_low, jnp.zeros_like(k_low)))
+    return stack(side(k_high, k_high), side(k_low, k_low))
 
 
 def wide_state(state):
     high, low = halves(state)
-    return stack(side(high, low), side(high, jnp.zeros_like(high)))
+    return stack(side(high, low), side(high, low))
 
 
 def folded(wide):
@@ -385,7 +385,7 @@
 
 
 def second_phase(message):
-    return lax.ppermute(message, "ctx", [(i, i ^ (4 if i % 2 == 0 else 2)) for i in range(8) if i != 3])
+    return lax.ppermute(message, "ctx", [(i, i ^ (4 if i % 2 == 0 else 2)) for i in range(8)])
 
 
 def doubled_prefix(chip):

time: 63.3 us -> 53.8 us (0.85)
  waiting for transfers between devices: 18.5 us -> 11.3 us
  starting transfers between devices: 17.6 us -> 16 us
    ppermute x1, waiting for transfers between devices: 12.3 us -> 2.78 us  [second_phase(): lax.ppermute(message, 'ctx', [(i, i ^ (4 if i % 2 == 0 else 2)) for i in...]
    ppermute x1, waiting for transfers between devices: 0.01 us -> 1.93 us  [shards(): before_v = lax.ppermute(tail_v, 'ctx', route)]
    ppermute x1, starting transfers between devices: 2.84 us -> 1 us  [second_phase(): lax.ppermute(message, 'ctx', [(i, i ^ (4 if i % 2 == 0 else 2)) for i in...]
  transfers between devices with their start and end apart: 12 -> 12, of which waited for: 4 -> 6; matrix products, arithmetic and copies ran while one was open for 0% -> 0% of each run, Pallas kernels for 35% -> 41%
where the time goes in v12:
time: 53.8 us; the launch traced here: 53.6 us
  Pallas kernels  26 us (48%)
  starting transfers between devices  16 us (30%)
  waiting for transfers between devices  11.3 us (21%)
    pallas_call x2, Pallas kernels, local(): call(functools.partial(local_kernel, part), 'local', in_specs=[smem, vmem...  10.2 us
    ppermute x8, starting transfers between devices, swap(): lax.ppermute(block, axis, [(i, i ^ bit) for i in range(lax.axis_size(axis...  9.48 us
    pallas_call x2, Pallas kernels, totals(): call(functools.partial(totals_kernel, part), 'totals', in_specs=[anywhere...  5.75 us
    ppermute x8, waiting for transfers between devices, swap(): lax.ppermute(block, axis, [(i, i ^ bit) for i in range(lax.axis_size(axis...  3.57 us
    pallas_call x1, Pallas kernels, shards(): call(first_weights_kernel, 'first_weights', in_specs=[smem] + [vmem] * 7,...  2.83 us
    ppermute x1, waiting for transfers between devices, second_phase(): lax.ppermute(message, 'ctx', [(i, i ^ (4 if i % 2 == 0 else 2)) for i in...  2.78 us
    ppermute x1, waiting for transfers between devices, first_phase(): lax.ppermute(chip, 'ctx', [(i, i ^ (2 if i % 2 == 0 else 4)) for i in ran...  2.72 us
    pallas_call x1, Pallas kernels, shards(): call(earlier_kernel, 'earlier', in_specs=[smem] + [vmem] * 10, out_shape=...  2.44 us
  transfers between devices with their start and end apart: 12, of which 6 were waited for; matrix products, arithmetic and copies ran while one was open for 0% of the time, Pallas kernels for 41%

profile of v12, /device:TPU:4, one launch (start us, length us, event | category | flops | bytes accessed | tf_op | source)
XLA Modules:
  0.0 53.6 jit_solution(7182621398655027812)
XLA Ops:
  0.0 2.9 %totals.2 = (f32[8,128,128]{2,1,0:T(8,128)S(1)}, f32[8,128,128]{2,1,0:T(8,128)S(1)}, f32[512,1024]{1,0:T(8,128)S(1)}, f32[512,1024]{1,0:T(8,128)S(1)}) custom-call(f32[512,2048]{1,0:T(8,128)} %k_hbm.3, f32[512,2048]{1,0:T(8,128)} %v_hbm.3, f32[512,2048]{1,0:T(8,128)} %q_in_ref.1), custom_call_target="tpu_custom_call" | custom-call | tf_op jit(solution)/shard_map/totals/pallas_call | solution.py:433
  3.0 2.9 %totals.3 = (f32[8,128,128]{2,1,0:T(8,128)S(1)}, f32[8,128,128]{2,1,0:T(8,128)S(1)}, f32[512,1024]{1,0:T(8,128)S(1)}, f32[512,1024]{1,0:T(8,128)S(1)}) custom-call(f32[512,2048]{1,0:T(8,128)} %k_hbm.3, f32[512,2048]{1,0:T(8,128)} %v_hbm.3, f32[8,128,128]{2,1,0:T(8,128)S(1)} %get-tuple-element.36._), custom_call_target="tpu_custom_call" | custom-call | tf_op jit(solution)/shard_map/totals/pallas_call | solution.py:433
  6.0 1.6 %collective-permute-start.2 = (f32[8,128,128]{2,1,0:T(8,128)S(1)}, f32[8,128,128]{2,1,0:T(8,128)S(1)}, u32[]{:S(2)}, u32[]{:S(2)}) collective-permute-start(f32[8,128,128]{2,1,0:T(8,128)S(1)} %get-tuple-element.39.refs_0_.chip_ref), channel_id=1, source_target_pairs={{0,8},{4,20},{8,0},{12,28},{16,24},{20,4},{24,16},{28,12},{1,9},{5... | collective-permute-start | bytes 1572872 | tf_op jit(solution)/shard_map/ppermute | solution.py:384
  7.6 1.9 %collective-permute-start.1 = (f32[128,2048]{1,0:T(8,128)S(1)}, f32[128,2048]{1,0:T(8,128)S(1)}, u32[]{:S(2)}, u32[]{:S(2)}) collective-permute-start(f32[128,2048]{1,0:T(8,128)S(1)} %get-tuple-element.43), channel_id=1, source_target_pairs={{0,4},{4,8},{8,12},{12,16},{16,20},{20,24},{24,28},{1,5},{5,9},{9,... | collective-permute-start | bytes 3145736 | tf_op jit(solution)/shard_map/ppermute | solution.py:456
  9.5 5.8 %local.2 = (f32[512,1024]{1,0:T(8,128)S(1)}, f32[512,1024]{1,0:T(8,128)S(1)}, f32[8,512]{1,0:T(8,128)S(1)}, f32[512,1024]{1,0:T(8,128)S(1)}, f32[512,1024]{1,0:T(8,128)S(1)}) custom-call(f32[2,16]{1,0:T(2,128)S(1)} %copy-done, f32[512,2048]{1,0:T(8,128)} %q_in_ref.1, f32[512,1024]{1,0:T(8,128)S(1)} %get-tuple-element.34.first_ref.k_ref.refs_2_, ...), custom_call_target="tpu_custom_call" | custom-call | tf_op jit(solution)/shard_map/local/pallas_call | solution.py:442
  15.2 2.7 %collective-permute-done.2.first_ref = f32[8,128,128]{2,1,0:T(8,128)S(1)} collective-permute-done((f32[8,128,128]{2,1,0:T(8,128)S(1)}, f32[8,128,128]{2,1,0:T(8,128)S(1)}, u32[]{:S(2)}, u32[]{:S(2)}) %collective-permute-start.2) | collective-permute-done | bytes 524320 | tf_op jit(solution)/shard_map/ppermute | solution.py:384
  18.1 1.0 %collective-permute-start.4 = (f32[8,128,128]{2,1,0:T(8,128)S(1)}, f32[8,128,128]{2,1,0:T(8,128)S(1)}, u32[]{:S(2)}, u32[]{:S(2)}) collective-permute-start(f32[8,128,128]{2,1,0:T(8,128)S(1)} %message.1.refs_0_), channel_id=1, source_target_pairs={{0,16},{4,12},{8,24},{12,4},{16,0},{20,28},{24,8},{28,20},{1,17},{... | collective-permute-start | bytes 1572872 | tf_op jit(solution)/shard_map/ppermute | solution.py:388
  19.1 4.5 %local.3 = (f32[512,1024]{1,0:T(8,128)S(1)}, f32[512,1024]{1,0:T(8,128)S(1)}, f32[8,512]{1,0:T(8,128)S(1)}) custom-call(f32[2,16]{1,0:T(2,128)S(1)} %copy-done, f32[512,1024]{1,0:T(8,128)S(1)} %get-tuple-element.41.refs_1_.q_in_ref.refs_5_, f32[512,1024]{1,0:T(8,128)S(1)} %get-tuple-element.38.second_ref.refs_3_.k_ref, ...), custom_call_target="tpu_custom_call" | custom-call | tf_op jit(solution)/shard_map/local/pallas_call | solution.py:442
  23.6 2.1 %collective-permute-start.3 = (f32[128,2048]{1,0:T(8,128)S(1)}, f32[128,2048]{1,0:T(8,128)S(1)}, u32[]{:S(2)}, u32[]{:S(2)}) collective-permute-start(f32[128,2048]{1,0:T(8,128)S(1)} %tail.1), channel_id=1, source_target_pairs={{0,4},{4,8},{8,12},{12,16},{16,20},{20,24},{24,28},{1,5},{5,9},{9,... | collective-permute-start | bytes 3145736 | tf_op jit(solution)/shard_map/ppermute | solution.py:472
  25.7 0.3 collective-permute-done.1.refs_6_
  26.0 2.8 %first_weights.1 = (bf16[128,4096]{1,0:T(8,128)(2,1)S(1)}, f32[128,2048]{1,0:T(8,128)S(1)}) custom-call(f32[2,16]{1,0:T(2,128)S(1)} %copy-done, f32[512,1024]{1,0:T(8,128)S(1)} %get-tuple-element.40.refs_0_.refs_4_, f32[512,1024]{1,0:T(8,128)S(1)} %get-tuple-element.41.refs_1_.q_in_ref.refs_5_, f32[512,1024]{1,0:T(8,128)S(1)} %get-tuple-element.34.first_ref.k_ref.refs_2_, ...), custom_call_target="tpu_custom_call" | custom-call | tf_op jit(solution)/shard_map/first_weights/pallas_call | solution.py:473
  28.8 2.8 %collective-permute-done.4.second_ref = f32[8,128,128]{2,1,0:T(8,128)S(1)} collective-permute-done((f32[8,128,128]{2,1,0:T(8,128)S(1)}, f32[8,128,128]{2,1,0:T(8,128)S(1)}, u32[]{:S(2)}, u32[]{:S(2)}) %collective-permute-start.4) | collective-permute-done | bytes 524320 | tf_op jit(solution)/shard_map/ppermute | solution.py:388
  31.6 0.2 prefix.1
  31.9 1.9 %collective-permute-done.5.refs_0_ = f32[8,128,128]{2,1,0:T(8,128)S(1)} collective-permute-done((f32[8,128,128]{2,1,0:T(8,128)S(1)}, f32[8,128,128]{2,1,0:T(8,128)S(1)}, u32[]{:S(2)}, u32[]{:S(2)}) %collective-permute-start.5) | collective-permute-done | bytes 524320 | tf_op jit(solution)/shard_map/ppermute | solution.py:376
  33.8 2.4 %earlier.1 = (f32[512,1024]{1,0:T(8,128)S(1)}, f32[512,1024]{1,0:T(8,128)S(1)}, f32[8,512]{1,0:T(8,128)S(1)}) custom-call(f32[2,16]{1,0:T(2,128)S(1)} %copy-done, f32[8,128,128]{2,1,0:T(8,128)S(1)} %collective-permute-done.5.refs_0_, f32[8,128,128]{2,1,0:T(8,128)S(1)} %get-tuple-element.49.refs_1_, f32[8,128,128]{2,1,0:T(8,128)S(1)} %get-tuple-element.50.refs_2_, ...), custom_call_target="tpu_custom_call" | custom-call | tf_op jit(solution)/shard_map/earlier/pallas_call | solution.py:495
  36.3 4.0 %collective-permute-start.8 = (f32[8,512]{1,0:T(8,128)S(1)}, f32[8,512]{1,0:T(8,128)S(1)}, u32[]{:S(2)}, u32[]{:S(2)}) collective-permute-start(f32[8,512]{1,0:T(8,128)S(1)} %get-tuple-element.54._.refs_0_), channel_id=1, source_target_pairs={{0,3},{1,2},{2,1},{3,0},{4,7},{5,6},{6,5},{7,4},{8,11},{9,10},{10,... | collective-permute-start | bytes 49160 | tf_op jit(solution)/shard_map/ppermute | solution.py:376
  40.3 0.6 %collective-permute-start.6 = (f32[8,512]{1,0:T(8,128)S(1)}, f32[8,512]{1,0:T(8,128)S(1)}, u32[]{:S(2)}, u32[]{:S(2)}) collective-permute-start(f32[8,512]{1,0:T(8,128)S(1)} %get-tuple-element.54._.refs_0_), channel_id=1, source_target_pairs={{0,1},{1,0},{2,3},{3,2},{4,5},{5,4},{6,7},{7,6},{8,9},{9,8},{10,11... | collective-permute-start | bytes 49160 | tf_op jit(solution)/shard_map/ppermute | solution.py:376
  40.9 1.9 %collective-permute-done.3.tail_ref = f32[128,2048]{1,0:T(8,128)S(1)} collective-permute-done((f32[128,2048]{1,0:T(8,128)S(1)}, f32[128,2048]{1,0:T(8,128)S(1)}, u32[]{:S(2)}, u32[]{:S(2)}) %collective-permute-start.3) | collective-permute-done | bytes 1048608 | tf_op jit(solution)/shard_map/ppermute | solution.py:472
  42.8 0.8 %first_values.1 = (f32[128,2048]{1,0:T(8,128)S(1)}, f32[8,128]{1,0:T(8,128)S(1)}) custom-call(bf16[128,4096]{1,0:T(8,128)(2,1)S(1)} %get-tuple-element.44.weights_ref, f32[128,2048]{1,0:T(8,128)S(1)} %get-tuple-element.45._.now_ref, f32[128,2048]{1,0:T(8,128)S(1)} %collective-permute-done.3.tail_ref, f32[8,512]{1,0:T(8,128)S(1)} %get-tuple-element.54._.refs_0_), custom_call_target="tpu_custom_call" | custom-call | tf_op jit(solution)/shard_map/first_values/pallas_call | solution.py:503
  43.7 4.1 %collective-permute-start.11 = (f32[8,128]{1,0:T(8,128)S(1)}, f32[8,128]{1,0:T(8,128)S(1)}, u32[]{:S(2)}, u32[]{:S(2)}) collective-permute-start(f32[8,128]{1,0:T(8,128)S(1)} %get-tuple-element.56._.refs_0_), channel_id=1, source_target_pairs={{0,3},{1,2},{2,1},{3,0},{4,7},{5,6},{6,5},{7,4},{8,11},{9,10},{10,... | collective-permute-start | bytes 12296 | tf_op jit(solution)/shard_map/ppermute | solution.py:376
  47.8 0.6 %collective-permute-start.9 = (f32[8,128]{1,0:T(8,128)S(1)}, f32[8,128]{1,0:T(8,128)S(1)}, u32[]{:S(2)}, u32[]{:S(2)}) collective-permute-start(f32[8,128]{1,0:T(8,128)S(1)} %get-tuple-element.56._.refs_0_), channel_id=1, source_target_pairs={{0,1},{1,0},{2,3},{3,2},{4,5},{5,4},{6,7},{7,6},{8,9},{9,8},{10,11... | collective-permute-start | bytes 12296 | tf_op jit(solution)/shard_map/ppermute | solution.py:376
  48.4 2.2 %scale.1 = (f32[512,2048]{1,0:T(8,128)}, f32[128,2048]{1,0:T(8,128)S(1)}) custom-call(f32[8,128]{1,0:T(8,128)S(1)} %get-tuple-element.56._.refs_0_, f32[8,512]{1,0:T(8,128)S(1)} %get-tuple-element.54._.refs_0_, f32[8,512]{1,0:T(8,128)S(1)} %collective-permute-done.6.refs_1_, f32[8,512]{1,0:T(8,128)S(1)} %collective-permute-done.7.refs_2_, ...), custom_call_target="tpu_custom_call" | custom-call | tf_op jit(solution)/shard_map/scale/pallas_call | solution.py:510
  50.6 1.7 %collective-permute-done.10.refs_2_ = f32[8,128]{1,0:T(8,128)S(1)} collective-permute-done((f32[8,128]{1,0:T(8,128)S(1)}, f32[8,128]{1,0:T(8,128)S(1)}, u32[]{:S(2)}, u32[]{:S(2)}) %collective-permute-start.10) | collective-permute-done | bytes 4128 | tf_op jit(solution)/shard_map/ppermute | solution.py:376
  52.3 1.2 %first_scale.1 = f32[512,2048]{1,0:T(8,128)} custom-call(f32[128,2048]{1,0:T(8,128)S(1)} %get-tuple-element.55.a_ref, f32[128,2048]{1,0:T(8,128)S(1)} %get-tuple-element.61.b_ref, f32[512,2048]{1,0:T(8,128)} %get-tuple-element.62._, f32[8,128]{1,0:T(8,128)S(1)} %get-tuple-element.56._.refs_0_, ...), custom_call_target="tpu_custom_call", output_to_operand_aliasing={{}: (2, {})} | custom-call | tf_op jit(solution)/shard_map/first_scale/pallas_call | solution.py:518
  (15 shorter events, 0.5 us)
Async XLA Ops:
  2.9 3.0 %collective-permute-start = (f32[8,128,128]{2,1,0:T(8,128)S(1)}, f32[8,128,128]{2,1,0:T(8,128)S(1)}, u32[]{:S(2)}, u32[]{:S(2)}) collective-permute-start(f32[8,128,128]{2,1,0:T(8,128)S(1)} %get-tuple-element.36._), channel_id=1, source_target_pairs={{0,4},{4,0},{8,12},{12,8},{16,20},{20,16},{24,28},{28,24},{1,5},{5... | collective-permute-start | bytes 1572872 | tf_op jit(solution)/shard_map/ppermute | solution.py:376
  5.9 3.6 %copy-start = (f32[2,16]{1,0:T(2,128)S(1)}, f32[2,16]{1,0:T(2,128)}, u32[]{:S(2)}) copy-start(f32[2,16]{1,0:T(2,128)} %gain_ref.7) | copy-start | bytes 388
  6.0 12.0 %collective-permute-start.2 = (f32[8,128,128]{2,1,0:T(8,128)S(1)}, f32[8,128,128]{2,1,0:T(8,128)S(1)}, u32[]{:S(2)}, u32[]{:S(2)}) collective-permute-start(f32[8,128,128]{2,1,0:T(8,128)S(1)} %get-tuple-element.39.refs_0_.chip_ref), channel_id=1, source_target_pairs={{0,8},{4,20},{8,0},{12,28},{16,24},{20,4},{24,16},{28,12},{1,9},{5... | collective-permute-start | bytes 1572872 | tf_op jit(solution)/shard_map/ppermute | solution.py:384
  7.6 18.4 %collective-permute-start.1 = (f32[128,2048]{1,0:T(8,128)S(1)}, f32[128,2048]{1,0:T(8,128)S(1)}, u32[]{:S(2)}, u32[]{:S(2)}) collective-permute-start(f32[128,2048]{1,0:T(8,128)S(1)} %get-tuple-element.43), channel_id=1, source_target_pairs={{0,4},{4,8},{8,12},{12,16},{16,20},{20,24},{24,28},{1,5},{5,9},{9,... | collective-permute-start | bytes 3145736 | tf_op jit(solution)/shard_map/ppermute | solution.py:456
  18.1 13.6 %collective-permute-start.4 = (f32[8,128,128]{2,1,0:T(8,128)S(1)}, f32[8,128,128]{2,1,0:T(8,128)S(1)}, u32[]{:S(2)}, u32[]{:S(2)}) collective-permute-start(f32[8,128,128]{2,1,0:T(8,128)S(1)} %message.1.refs_0_), channel_id=1, source_target_pairs={{0,16},{4,12},{8,24},{12,4},{16,0},{20,28},{24,8},{28,20},{1,17},{... | collective-permute-start | bytes 1572872 | tf_op jit(solution)/shard_map/ppermute | solution.py:388
  23.6 19.2 %collective-permute-start.3 = (f32[128,2048]{1,0:T(8,128)S(1)}, f32[128,2048]{1,0:T(8,128)S(1)}, u32[]{:S(2)}, u32[]{:S(2)}) collective-permute-start(f32[128,2048]{1,0:T(8,128)S(1)} %tail.1), channel_id=1, source_target_pairs={{0,4},{4,8},{8,12},{12,16},{16,20},{20,24},{24,28},{1,5},{5,9},{9,... | collective-permute-start | bytes 3145736 | tf_op jit(solution)/shard_map/ppermute | solution.py:472
  31.8 2.0 %collective-permute-start.5 = (f32[8,128,128]{2,1,0:T(8,128)S(1)}, f32[8,128,128]{2,1,0:T(8,128)S(1)}, u32[]{:S(2)}, u32[]{:S(2)}) collective-permute-start(f32[8,128,128]{2,1,0:T(8,128)S(1)} %get-tuple-element.48), channel_id=1, source_target_pairs={{0,4},{4,0},{8,12},{12,8},{16,20},{20,16},{24,28},{28,24},{1,5},{5... | collective-permute-start | bytes 1572872 | tf_op jit(solution)/shard_map/ppermute | solution.py:376
  36.3 11.5 %collective-permute-start.8 = (f32[8,512]{1,0:T(8,128)S(1)}, f32[8,512]{1,0:T(8,128)S(1)}, u32[]{:S(2)}, u32[]{:S(2)}) collective-permute-start(f32[8,512]{1,0:T(8,128)S(1)} %get-tuple-element.54._.refs_0_), channel_id=1, source_target_pairs={{0,3},{1,2},{2,1},{3,0},{4,7},{5,6},{6,5},{7,4},{8,11},{9,10},{10,... | collective-permute-start | bytes 49160 | tf_op jit(solution)/shard_map/ppermute | solution.py:376
  40.3 8.1 %collective-permute-start.7 = (f32[8,512]{1,0:T(8,128)S(1)}, f32[8,512]{1,0:T(8,128)S(1)}, u32[]{:S(2)}, u32[]{:S(2)}) collective-permute-start(f32[8,512]{1,0:T(8,128)S(1)} %get-tuple-element.54._.refs_0_), channel_id=1, source_target_pairs={{0,2},{1,3},{2,0},{3,1},{4,6},{5,7},{6,4},{7,5},{8,10},{9,11},{10,... | collective-permute-start | bytes 49160 | tf_op jit(solution)/shard_map/ppermute | solution.py:376
  40.3 8.1 %collective-permute-start.6 = (f32[8,512]{1,0:T(8,128)S(1)}, f32[8,512]{1,0:T(8,128)S(1)}, u32[]{:S(2)}, u32[]{:S(2)}) collective-permute-start(f32[8,512]{1,0:T(8,128)S(1)} %get-tuple-element.54._.refs_0_), channel_id=1, source_target_pairs={{0,1},{1,0},{2,3},{3,2},{4,5},{5,4},{6,7},{7,6},{8,9},{9,8},{10,11... | collective-permute-start | bytes 49160 | tf_op jit(solution)/shard_map/ppermute | solution.py:376
  43.7 6.9 %collective-permute-start.11 = (f32[8,128]{1,0:T(8,128)S(1)}, f32[8,128]{1,0:T(8,128)S(1)}, u32[]{:S(2)}, u32[]{:S(2)}) collective-permute-start(f32[8,128]{1,0:T(8,128)S(1)} %get-tuple-element.56._.refs_0_), channel_id=1, source_target_pairs={{0,3},{1,2},{2,1},{3,0},{4,7},{5,6},{6,5},{7,4},{8,11},{9,10},{10,... | collective-permute-start | bytes 12296 | tf_op jit(solution)/shard_map/ppermute | solution.py:376
  47.8 4.5 %collective-permute-start.10 = (f32[8,128]{1,0:T(8,128)S(1)}, f32[8,128]{1,0:T(8,128)S(1)}, u32[]{:S(2)}, u32[]{:S(2)}) collective-permute-start(f32[8,128]{1,0:T(8,128)S(1)} %get-tuple-element.56._.refs_0_), channel_id=1, source_target_pairs={{0,2},{1,3},{2,0},{3,1},{4,6},{5,7},{6,4},{7,5},{8,10},{9,11},{10,... | collective-permute-start | bytes 12296 | tf_op jit(solution)/shard_map/ppermute | solution.py:376
  47.8 4.5 %collective-permute-start.9 = (f32[8,128]{1,0:T(8,128)S(1)}, f32[8,128]{1,0:T(8,128)S(1)}, u32[]{:S(2)}, u32[]{:S(2)}) collective-permute-start(f32[8,128]{1,0:T(8,128)S(1)} %get-tuple-element.56._.refs_0_), channel_id=1, source_target_pairs={{0,1},{1,0},{2,3},{3,2},{4,5},{5,4},{6,7},{7,6},{8,9},{9,8},{10,11... | collective-permute-start | bytes 12296 | tf_op jit(solution)/shard_map/ppermute | solution.py:376

commit v13 on v12

--- a/solution.py
+++ b/solution.py
@@ -120,11 +120,29 @@
             total_ref[head] = first + second
 
 
-def chip_kernel(keep_ref, beside_ref, first_ref, second_ref, out_ref, tail_ref):
+def chip_kernel(keep_ref, beside_ref, out_ref):
     out_ref[...] = keep_ref[...] + beside_ref[...]
-    rows, width = first_ref.shape
-    tail_ref[:, :width] = first_ref[rows - WINDOW :, :]
-    tail_ref[:, width:] = second_ref[rows - WINDOW :, :]
+
+
+def key_tail_kernel(k_hbm, tail_ref, sems):
+    rows, width = k_hbm.shape
+    copies = []
+    for part in range(2):
+        there = pl.ds(pl.multiple_of(first_head(part, width // HD) * HD, HD), width // 2)
+        here = pl.ds(part * (width // 2), width // 2)
+        copies.append(
+            pltpu.make_async_copy(
+                k_hbm.at[pl.ds(rows - WINDOW, WINDOW), there], tail_ref.at[:, here], sems.at[part]
+            )
+        )
+    for copy in copies:
+        copy.start()
+    for copy in copies:
+        copy.wait()
+
+
+def relay_kernel(tail_ref, relayed_ref, _, out_ref):
+    out_ref[...] = jnp.where(lax.axis_index("ctx") == 7, relayed_ref[...], tail_ref[...])
 
 
 def tail_kernel(first_ref, second_ref, _, tail_ref):
@@ -265,9 +283,16 @@
     sums_ref[...] = jnp.where(row == 0, sum(ref[...] for ref in sum_refs), sums)
 
 
+def added_columns(refs, columns):
+    total = refs[0][:, columns]
+    for ref in refs[1:]:
+        total = total + ref[:, columns]
+    return total
+
+
 def first_weights_kernel(gain_ref, *refs):
     q_refs, k_refs, v_refs = (refs[2 * i : 2 * i + 2] for i in range(3))
-    tail_ref, weights_ref, out_ref = refs[6:]
+    *tail_refs, weights_ref, out_ref = refs[6:]
     lower = lower_mask()
     reachable = jnp.logical_or(lower, lax.axis_index("ctx") > 0)
     top = slice(0, WINDOW)
@@ -280,7 +305,7 @@
             sent = (1 - part) * width + head * HD
             qq = side(*halves(q_refs[part][top, columns]))
             now = folded(dot_rows(qq, wide_keys(*halves(k_refs[part][top, columns]))))
-            before = folded(dot_rows(qq, wide_keys(*halves(tail_ref[:, sent : sent + HD]))))
+            before = folded(dot_rows(qq, wide_keys(*halves(added_columns(tail_refs, slice(sent, sent + HD))))))
             scores.append(jnp.where(reachable, jnp.where(lower, now, before), -jnp.inf))
         for head in range(width // HD):
             columns = slice(head * HD, (head + 1) * HD)
@@ -448,13 +473,30 @@
         )(head_gain, query_source, held_k[part], held_v[part], after)
 
     route = [(i, i + 1) for i in range(lax.axis_size("ctx") - 1)]
+    short = lax.axis_size("ctx") == 8
+    tail_k = call(
+        key_tail_kernel,
+        "key_tail",
+        in_specs=[anywhere],
+        out_shape=first_tile,
+        scratch_shapes=[dma((2,))],
+    )(keys)
+    before_k = [lax.ppermute(tail_k, "ctx", [(1, 2), (5, 6)])] if short else []
     send, *held_0 = totals(0, queries)
     beside = swap(send, "ctx", 1)
     keep, *held_1 = totals(1, send)
     early, held_k, held_v = zip(held_0, held_1)
-    chip, tail_k = call(chip_kernel, "chip", out_shape=[packed, first_tile])(keep, beside, *held_k)
-    before_k = lax.ppermute(tail_k, "ctx", route)
-    *local_0, query_0, query_1 = local(0, queries, chip)
+    chip = call(chip_kernel, "chip", in_specs=[vmem, vmem], out_shape=packed)(keep, beside)
+    tail_k, tail_v = (
+        call(tail_kernel, "tail", in_specs=[vmem, vmem, anywhere], out_shape=first_tile)(*held, chip)
+        for held in (held_k, held_v)
+    )
+    later = [pair for pair in route if not short or pair not in ((1, 2), (5, 6))]
+    before_k.append(lax.ppermute(tail_k, "ctx", later))
+    if short:
+        relayed = lax.ppermute(tail_v, "ctx", [(3, 7)])
+        route = [pair for pair in route if pair != (3, 4)] + [(7, 4)]
+    *local_0, query_0, query_1 = local(0, queries, before_k[0])
     message = local_0[2]
     if lax.axis_size("ctx") == 8:
         first = first_phase(chip)
@@ -466,16 +508,17 @@
         )(first, chip, message)
     held_q = query_0, query_1
     window, linear, window_sums = zip(local_0, local(1, query_1, message))
-    tail_v = call(
-        tail_kernel, "tail", in_specs=[vmem, vmem, anywhere], out_shape=first_tile
-    )(*held_v, window_sums[1])
+    if short:
+        tail_v = call(
+            relay_kernel, "relay", in_specs=[vmem, vmem, anywhere], out_shape=first_tile
+        )(tail_v, relayed, window_sums[1])
     before_v = lax.ppermute(tail_v, "ctx", route)
     first_weights, first_now = call(
         first_weights_kernel,
         "first_weights",
-        in_specs=[smem] + [vmem] * 7,
+        in_specs=[smem] + [vmem] * (6 + len(before_k)),
         out_shape=[array(WINDOW, 2 * width, dtype=BF16), first_tile],
-    )(head_gain, *held_q, *held_k, *held_v, before_k)
+    )(head_gain, *held_q, *held_k, *held_v, *before_k)
 
     if lax.axis_size("ctx") == 8:
         second = second_phase(message)

time: 53.8 us -> 66.8 us (1.24)
  the two profiles are of different devices: /device:TPU:4 before, /device:TPU:0 now
where the time goes in v13:
time: 66.8 us; the launch traced here: 66.6 us
  starting transfers between devices  31.8 us (48%)
  Pallas kernels  27.4 us (41%)
  waiting for transfers between devices  7.02 us (11%)
    ppermute x8, starting transfers between devices, swap(): lax.ppermute(block, axis, [(i, i ^ bit) for i in range(lax.axis_size(axis...  12.2 us
    pallas_call x2, Pallas kernels, local(): call(functools.partial(local_kernel, part), 'local', in_specs=[smem, vmem...  10.2 us
    ppermute x1, starting transfers between devices, shards(): before_v = lax.ppermute(tail_v, 'ctx', route)  9.4 us
    pallas_call x2, Pallas kernels, totals(): call(functools.partial(totals_kernel, part), 'totals', in_specs=[anywhere...  5.76 us
    ppermute x8, waiting for transfers between devices, swap(): lax.ppermute(block, axis, [(i, i ^ bit) for i in range(lax.axis_size(axis...  4.48 us
    ppermute x1, starting transfers between devices, shards(): before_k.append(lax.ppermute(tail_k, 'ctx', later))  4.01 us
    ppermute x1, starting transfers between devices, first_phase(): lax.ppermute(chip, 'ctx', [(i, i ^ (2 if i % 2 == 0 else 4)) for i in ran...  3.14 us
    pallas_call x1, Pallas kernels, shards(): call(first_weights_kernel, 'first_weights', in_specs=[smem] + [vmem] * (6...  2.85 us
  transfers between devices with their start and end apart: 14, of which 4 were waited for; matrix products, arithmetic and copies ran while one was open for 0% of the time, Pallas kernels for 35%

profile of v13, /device:TPU:0, one launch (start us, length us, event | category | flops | bytes accessed | tf_op | source)
XLA Modules:
  0.0 66.6 jit_solution(1760944257665598956)
XLA Ops:
  0.0 2.9 %totals.2 = (f32[8,128,128]{2,1,0:T(8,128)S(1)}, f32[8,128,128]{2,1,0:T(8,128)S(1)}, f32[512,1024]{1,0:T(8,128)S(1)}, f32[512,1024]{1,0:T(8,128)S(1)}) custom-call(f32[512,2048]{1,0:T(8,128)} %k_hbm.5, f32[512,2048]{1,0:T(8,128)} %v_hbm.3, f32[512,2048]{1,0:T(8,128)} %q_in_ref.1), custom_call_target="tpu_custom_call" | custom-call | tf_op jit(solution)/shard_map/totals/pallas_call | solution.py:458
  3.4 1.2 %key_tail.1 = f32[128,2048]{1,0:T(8,128)S(1)} custom-call(f32[512,2048]{1,0:T(8,128)} %k_hbm.5), custom_call_target="tpu_custom_call" | custom-call | tf_op jit(solution)/shard_map/key_tail/pallas_call | solution.py:477
  4.6 0.7 %collective-permute-start = (f32[128,2048]{1,0:T(8,128)S(1)}, f32[128,2048]{1,0:T(8,128)S(1)}, u32[]{:S(2)}, u32[]{:S(2)}) collective-permute-start(f32[128,2048]{1,0:T(8,128)S(1)} %key_tail.1), channel_id=1, source_target_pairs={{4,8},{20,24},{5,9},{21,25},{6,10},{22,26},{7,11},{23,27}} | collective-permute-start | bytes 3145736 | tf_op jit(solution)/shard_map/ppermute | solution.py:484
  5.4 2.9 %totals.3 = (f32[8,128,128]{2,1,0:T(8,128)S(1)}, f32[8,128,128]{2,1,0:T(8,128)S(1)}, f32[512,1024]{1,0:T(8,128)S(1)}, f32[512,1024]{1,0:T(8,128)S(1)}) custom-call(f32[512,2048]{1,0:T(8,128)} %k_hbm.5, f32[512,2048]{1,0:T(8,128)} %v_hbm.3, f32[8,128,128]{2,1,0:T(8,128)S(1)} %get-tuple-element.36._), custom_call_target="tpu_custom_call" | custom-call | tf_op jit(solution)/shard_map/totals/pallas_call | solution.py:458
  8.4 0.7 %collective-permute-start.3 = (f32[128,2048]{1,0:T(8,128)S(1)}, f32[128,2048]{1,0:T(8,128)S(1)}, u32[]{:S(2)}, u32[]{:S(2)}) collective-permute-start(f32[128,2048]{1,0:T(8,128)S(1)} %tail.3.tail_ref), channel_id=1, source_target_pairs={{12,28},{13,29},{14,30},{15,31}} | collective-permute-start | bytes 3145736 | tf_op jit(solution)/shard_map/ppermute | solution.py:497
  9.1 3.1 %collective-permute-start.4 = (f32[8,128,128]{2,1,0:T(8,128)S(1)}, f32[8,128,128]{2,1,0:T(8,128)S(1)}, u32[]{:S(2)}, u32[]{:S(2)}) collective-permute-start(f32[8,128,128]{2,1,0:T(8,128)S(1)} %chip.1._.chip_ref), channel_id=1, source_target_pairs={{0,8},{4,20},{8,0},{12,28},{16,24},{20,4},{24,16},{28,12},{1,9},{5... | collective-permute-start | bytes 1572872 | tf_op jit(solution)/shard_map/ppermute | solution.py:409
  12.4 4.0 %collective-permute-start.2 = (f32[128,2048]{1,0:T(8,128)S(1)}, f32[128,2048]{1,0:T(8,128)S(1)}, u32[]{:S(2)}, u32[]{:S(2)}) collective-permute-start(f32[128,2048]{1,0:T(8,128)S(1)} %tail.2), channel_id=1, source_target_pairs={{0,4},{8,12},{12,16},{16,20},{24,28},{1,5},{9,13},{13,17},{17,21},... | collective-permute-start | bytes 3145736 | tf_op jit(solution)/shard_map/ppermute | solution.py:495
  16.4 5.7 %local.2 = (f32[512,1024]{1,0:T(8,128)S(1)}, f32[512,1024]{1,0:T(8,128)S(1)}, f32[8,512]{1,0:T(8,128)S(1)}, f32[512,1024]{1,0:T(8,128)S(1)}, f32[512,1024]{1,0:T(8,128)S(1)}) custom-call(f32[2,16]{1,0:T(2,128)S(1)} %copy-done, f32[512,2048]{1,0:T(8,128)} %q_in_ref.1, f32[512,1024]{1,0:T(8,128)S(1)} %get-tuple-element.32.k_ref.first_ref.refs_2_, ...), custom_call_target="tpu_custom_call" | custom-call | tf_op jit(solution)/shard_map/local/pallas_call | solution.py:467
  22.1 2.5 %collective-permute-done.4.first_ref = f32[8,128,128]{2,1,0:T(8,128)S(1)} collective-permute-done((f32[8,128,128]{2,1,0:T(8,128)S(1)}, f32[8,128,128]{2,1,0:T(8,128)S(1)}, u32[]{:S(2)}, u32[]{:S(2)}) %collective-permute-start.4) | collective-permute-done | bytes 524320 | tf_op jit(solution)/shard_map/ppermute | solution.py:409
  24.8 1.6 %collective-permute-start.6 = (f32[8,128,128]{2,1,0:T(8,128)S(1)}, f32[8,128,128]{2,1,0:T(8,128)S(1)}, u32[]{:S(2)}, u32[]{:S(2)}) collective-permute-start(f32[8,128,128]{2,1,0:T(8,128)S(1)} %message.1.refs_0_), channel_id=1, source_target_pairs={{0,16},{4,12},{8,24},{12,4},{16,0},{20,28},{24,8},{28,20},{1,17},{... | collective-permute-start | bytes 1572872 | tf_op jit(solution)/shard_map/ppermute | solution.py:413
  26.3 4.5 %local.3 = (f32[512,1024]{1,0:T(8,128)S(1)}, f32[512,1024]{1,0:T(8,128)S(1)}, f32[8,512]{1,0:T(8,128)S(1)}) custom-call(f32[2,16]{1,0:T(2,128)S(1)} %copy-done, f32[512,1024]{1,0:T(8,128)S(1)} %get-tuple-element.35.refs_1_.q_in_ref.refs_5_, f32[512,1024]{1,0:T(8,128)S(1)} %get-tuple-element.37.second_ref.refs_3_.k_ref, ...), custom_call_target="tpu_custom_call" | custom-call | tf_op jit(solution)/shard_map/local/pallas_call | solution.py:467
  31.0 9.4 %collective-permute-start.5 = (f32[128,2048]{1,0:T(8,128)S(1)}, f32[128,2048]{1,0:T(8,128)S(1)}, u32[]{:S(2)}, u32[]{:S(2)}) collective-permute-start(f32[128,2048]{1,0:T(8,128)S(1)} %relay.1), channel_id=1, source_target_pairs={{0,4},{4,8},{8,12},{16,20},{20,24},{24,28},{28,16},{1,5},{5,9},{9,... | collective-permute-start | bytes 3145736 | tf_op jit(solution)/shard_map/ppermute | solution.py:515
  40.4 2.9 %first_weights.1 = (bf16[128,4096]{1,0:T(8,128)(2,1)S(1)}, f32[128,2048]{1,0:T(8,128)S(1)}) custom-call(f32[2,16]{1,0:T(2,128)S(1)} %copy-done, f32[512,1024]{1,0:T(8,128)S(1)} %get-tuple-element.34.refs_0_.refs_4_, f32[512,1024]{1,0:T(8,128)S(1)} %get-tuple-element.35.refs_1_.q_in_ref.refs_5_, f32[512,1024]{1,0:T(8,128)S(1)} %get-tuple-element.32.k_ref.first_ref.refs_2_, ...), custom_call_target="tpu_custom_call" | custom-call | tf_op jit(solution)/shard_map/first_weights/pallas_call | solution.py:516
  43.5 2.9 %collective-permute-start.7 = (f32[8,128,128]{2,1,0:T(8,128)S(1)}, f32[8,128,128]{2,1,0:T(8,128)S(1)}, u32[]{:S(2)}, u32[]{:S(2)}) collective-permute-start(f32[8,128,128]{2,1,0:T(8,128)S(1)} %get-tuple-element.44), channel_id=1, source_target_pairs={{0,4},{4,0},{8,12},{12,8},{16,20},{20,16},{24,28},{28,24},{1,5},{5... | collective-permute-start | bytes 1572872 | tf_op jit(solution)/shard_map/ppermute | solution.py:401
  46.4 1.5 %collective-permute-done.7.refs_0_ = f32[8,128,128]{2,1,0:T(8,128)S(1)} collective-permute-done((f32[8,128,128]{2,1,0:T(8,128)S(1)}, f32[8,128,128]{2,1,0:T(8,128)S(1)}, u32[]{:S(2)}, u32[]{:S(2)}) %collective-permute-start.7) | collective-permute-done | bytes 524320 | tf_op jit(solution)/shard_map/ppermute | solution.py:401
  47.9 2.4 %earlier.1 = (f32[512,1024]{1,0:T(8,128)S(1)}, f32[512,1024]{1,0:T(8,128)S(1)}, f32[8,512]{1,0:T(8,128)S(1)}) custom-call(f32[2,16]{1,0:T(2,128)S(1)} %copy-done, f32[8,128,128]{2,1,0:T(8,128)S(1)} %collective-permute-done.7.refs_0_, f32[8,128,128]{2,1,0:T(8,128)S(1)} %get-tuple-element.45.refs_1_, f32[8,128,128]{2,1,0:T(8,128)S(1)} %get-tuple-element.46.refs_2_, ...), custom_call_target="tpu_custom_call" | custom-call | tf_op jit(solution)/shard_map/earlier/pallas_call | solution.py:538
  50.4 1.6 %collective-permute-start.8 = (f32[8,512]{1,0:T(8,128)S(1)}, f32[8,512]{1,0:T(8,128)S(1)}, u32[]{:S(2)}, u32[]{:S(2)}) collective-permute-start(f32[8,512]{1,0:T(8,128)S(1)} %get-tuple-element.50._.refs_0_), channel_id=1, source_target_pairs={{0,1},{1,0},{2,3},{3,2},{4,5},{5,4},{6,7},{7,6},{8,9},{9,8},{10,11... | collective-permute-start | bytes 49160 | tf_op jit(solution)/shard_map/ppermute | solution.py:401
  52.0 2.6 %collective-permute-start.9 = (f32[8,512]{1,0:T(8,128)S(1)}, f32[8,512]{1,0:T(8,128)S(1)}, u32[]{:S(2)}, u32[]{:S(2)}) collective-permute-start(f32[8,512]{1,0:T(8,128)S(1)} %get-tuple-element.50._.refs_0_), channel_id=1, source_target_pairs={{0,2},{1,3},{2,0},{3,1},{4,6},{5,7},{6,4},{7,5},{8,10},{9,11},{10,... | collective-permute-start | bytes 49160 | tf_op jit(solution)/shard_map/ppermute | solution.py:401
  54.8 0.8 %first_values.1 = (f32[128,2048]{1,0:T(8,128)S(1)}, f32[8,128]{1,0:T(8,128)S(1)}) custom-call(bf16[128,4096]{1,0:T(8,128)(2,1)S(1)} %get-tuple-element.40.weights_ref, f32[128,2048]{1,0:T(8,128)S(1)} %get-tuple-element.41._.now_ref, f32[128,2048]{1,0:T(8,128)S(1)} %collective-permute-done.5.tail_ref, f32[8,512]{1,0:T(8,128)S(1)} %get-tuple-element.50._.refs_0_), custom_call_target="tpu_custom_call" | custom-call | tf_op jit(solution)/shard_map/first_values/pallas_call | solution.py:546
  55.6 0.7 %collective-permute-start.11 = (f32[8,128]{1,0:T(8,128)S(1)}, f32[8,128]{1,0:T(8,128)S(1)}, u32[]{:S(2)}, u32[]{:S(2)}) collective-permute-start(f32[8,128]{1,0:T(8,128)S(1)} %get-tuple-element.52._.refs_0_), channel_id=1, source_target_pairs={{0,1},{1,0},{2,3},{3,2},{4,5},{5,4},{6,7},{7,6},{8,9},{9,8},{10,11... | collective-permute-start | bytes 12296 | tf_op jit(solution)/shard_map/ppermute | solution.py:401
  56.3 3.5 %collective-permute-start.12 = (f32[8,128]{1,0:T(8,128)S(1)}, f32[8,128]{1,0:T(8,128)S(1)}, u32[]{:S(2)}, u32[]{:S(2)}) collective-permute-start(f32[8,128]{1,0:T(8,128)S(1)} %get-tuple-element.52._.refs_0_), channel_id=1, source_target_pairs={{0,2},{1,3},{2,0},{3,1},{4,6},{5,7},{6,4},{7,5},{8,10},{9,11},{10,... | collective-permute-start | bytes 12296 | tf_op jit(solution)/shard_map/ppermute | solution.py:401
  60.1 2.2 %scale.1 = (f32[512,2048]{1,0:T(8,128)}, f32[128,2048]{1,0:T(8,128)S(1)}) custom-call(f32[8,128]{1,0:T(8,128)S(1)} %get-tuple-element.52._.refs_0_, f32[8,512]{1,0:T(8,128)S(1)} %get-tuple-element.50._.refs_0_, f32[8,512]{1,0:T(8,128)S(1)} %collective-permute-done.8.refs_1_, f32[8,512]{1,0:T(8,128)S(1)} %collective-permute-done.9.refs_2_, ...), custom_call_target="tpu_custom_call" | custom-call | tf_op jit(solution)/shard_map/scale/pallas_call | solution.py:553
  62.3 2.9 %collective-permute-done.13.refs_3_ = f32[8,128]{1,0:T(8,128)S(1)} collective-permute-done((f32[8,128]{1,0:T(8,128)S(1)}, f32[8,128]{1,0:T(8,128)S(1)}, u32[]{:S(2)}, u32[]{:S(2)}) %collective-permute-start.13) | collective-permute-done | bytes 4128 | tf_op jit(solution)/shard_map/ppermute | solution.py:401
  65.2 1.2 %first_scale.1 = f32[512,2048]{1,0:T(8,128)} custom-call(f32[128,2048]{1,0:T(8,128)S(1)} %get-tuple-element.51.a_ref, f32[128,2048]{1,0:T(8,128)S(1)} %get-tuple-element.57.b_ref, f32[512,2048]{1,0:T(8,128)} %get-tuple-element.58._, f32[8,128]{1,0:T(8,128)S(1)} %get-tuple-element.52._.refs_0_, ...), custom_call_target="tpu_custom_call", output_to_operand_aliasing={{}: (2, {})} | custom-call | tf_op jit(solution)/shard_map/first_scale/pallas_call | solution.py:561
  (22 shorter events, 1.7 us)
Async XLA Ops:
  2.9 5.4 %collective-permute-start.1 = (f32[8,128,128]{2,1,0:T(8,128)S(1)}, f32[8,128,128]{2,1,0:T(8,128)S(1)}, u32[]{:S(2)}, u32[]{:S(2)}) collective-permute-start(f32[8,128,128]{2,1,0:T(8,128)S(1)} %get-tuple-element.36._), channel_id=1, source_target_pairs={{0,4},{4,0},{8,12},{12,8},{16,20},{20,16},{24,28},{28,24},{1,5},{5... | collective-permute-start | bytes 1572872 | tf_op jit(solution)/shard_map/ppermute | solution.py:401
  4.6 11.8 %collective-permute-start = (f32[128,2048]{1,0:T(8,128)S(1)}, f32[128,2048]{1,0:T(8,128)S(1)}, u32[]{:S(2)}, u32[]{:S(2)}) collective-permute-start(f32[128,2048]{1,0:T(8,128)S(1)} %key_tail.1), channel_id=1, source_target_pairs={{4,8},{20,24},{5,9},{21,25},{6,10},{22,26},{7,11},{23,27}} | collective-permute-start | bytes 3145736 | tf_op jit(solution)/shard_map/ppermute | solution.py:484
  8.4 22.4 %collective-permute-start.3 = (f32[128,2048]{1,0:T(8,128)S(1)}, f32[128,2048]{1,0:T(8,128)S(1)}, u32[]{:S(2)}, u32[]{:S(2)}) collective-permute-start(f32[128,2048]{1,0:T(8,128)S(1)} %tail.3.tail_ref), channel_id=1, source_target_pairs={{12,28},{13,29},{14,30},{15,31}} | collective-permute-start | bytes 3145736 | tf_op jit(solution)/shard_map/ppermute | solution.py:497
  9.1 15.5 %collective-permute-start.4 = (f32[8,128,128]{2,1,0:T(8,128)S(1)}, f32[8,128,128]{2,1,0:T(8,128)S(1)}, u32[]{:S(2)}, u32[]{:S(2)}) collective-permute-start(f32[8,128,128]{2,1,0:T(8,128)S(1)} %chip.1._.chip_ref), channel_id=1, source_target_pairs={{0,8},{4,20},{8,0},{12,28},{16,24},{20,4},{24,16},{28,12},{1,9},{5... | collective-permute-start | bytes 1572872 | tf_op jit(solution)/shard_map/ppermute | solution.py:409
  12.3 4.1 %copy-start = (f32[2,16]{1,0:T(2,128)S(1)}, f32[2,16]{1,0:T(2,128)}, u32[]{:S(2)}) copy-start(f32[2,16]{1,0:T(2,128)} %gain_ref.7) | copy-start | bytes 388
  12.4 28.0 %collective-permute-start.2 = (f32[128,2048]{1,0:T(8,128)S(1)}, f32[128,2048]{1,0:T(8,128)S(1)}, u32[]{:S(2)}, u32[]{:S(2)}) collective-permute-start(f32[128,2048]{1,0:T(8,128)S(1)} %tail.2), channel_id=1, source_target_pairs={{0,4},{8,12},{12,16},{16,20},{24,28},{1,5},{9,13},{13,17},{17,21},... | collective-permute-start | bytes 3145736 | tf_op jit(solution)/shard_map/ppermute | solution.py:495
  24.8 18.5 %collective-permute-start.6 = (f32[8,128,128]{2,1,0:T(8,128)S(1)}, f32[8,128,128]{2,1,0:T(8,128)S(1)}, u32[]{:S(2)}, u32[]{:S(2)}) collective-permute-start(f32[8,128,128]{2,1,0:T(8,128)S(1)} %message.1.refs_0_), channel_id=1, source_target_pairs={{0,16},{4,12},{8,24},{12,4},{16,0},{20,28},{24,8},{28,20},{1,17},{... | collective-permute-start | bytes 1572872 | tf_op jit(solution)/shard_map/ppermute | solution.py:413
  31.0 23.8 %collective-permute-start.5 = (f32[128,2048]{1,0:T(8,128)S(1)}, f32[128,2048]{1,0:T(8,128)S(1)}, u32[]{:S(2)}, u32[]{:S(2)}) collective-permute-start(f32[128,2048]{1,0:T(8,128)S(1)} %relay.1), channel_id=1, source_target_pairs={{0,4},{4,8},{8,12},{16,20},{20,24},{24,28},{28,16},{1,5},{5,9},{9,... | collective-permute-start | bytes 3145736 | tf_op jit(solution)/shard_map/ppermute | solution.py:515
  43.5 4.4 %collective-permute-start.7 = (f32[8,128,128]{2,1,0:T(8,128)S(1)}, f32[8,128,128]{2,1,0:T(8,128)S(1)}, u32[]{:S(2)}, u32[]{:S(2)}) collective-permute-start(f32[8,128,128]{2,1,0:T(8,128)S(1)} %get-tuple-element.44), channel_id=1, source_target_pairs={{0,4},{4,0},{8,12},{12,8},{16,20},{20,16},{24,28},{28,24},{1,5},{5... | collective-permute-start | bytes 1572872 | tf_op jit(solution)/shard_map/ppermute | solution.py:401
  50.4 9.4 %collective-permute-start.8 = (f32[8,512]{1,0:T(8,128)S(1)}, f32[8,512]{1,0:T(8,128)S(1)}, u32[]{:S(2)}, u32[]{:S(2)}) collective-permute-start(f32[8,512]{1,0:T(8,128)S(1)} %get-tuple-element.50._.refs_0_), channel_id=1, source_target_pairs={{0,1},{1,0},{2,3},{3,2},{4,5},{5,4},{6,7},{7,6},{8,9},{9,8},{10,11... | collective-permute-start | bytes 49160 | tf_op jit(solution)/shard_map/ppermute | solution.py:401
  52.0 8.1 %collective-permute-start.9 = (f32[8,512]{1,0:T(8,128)S(1)}, f32[8,512]{1,0:T(8,128)S(1)}, u32[]{:S(2)}, u32[]{:S(2)}) collective-permute-start(f32[8,512]{1,0:T(8,128)S(1)} %get-tuple-element.50._.refs_0_), channel_id=1, source_target_pairs={{0,2},{1,3},{2,0},{3,1},{4,6},{5,7},{6,4},{7,5},{8,10},{9,11},{10,... | collective-permute-start | bytes 49160 | tf_op jit(solution)/shard_map/ppermute | solution.py:401
  54.6 5.5 %collective-permute-start.10 = (f32[8,512]{1,0:T(8,128)S(1)}, f32[8,512]{1,0:T(8,128)S(1)}, u32[]{:S(2)}, u32[]{:S(2)}) collective-permute-start(f32[8,512]{1,0:T(8,128)S(1)} %get-tuple-element.50._.refs_0_), channel_id=1, source_target_pairs={{0,3},{1,2},{2,1},{3,0},{4,7},{5,6},{6,5},{7,4},{8,11},{9,10},{10,... | collective-permute-start | bytes 49160 | tf_op jit(solution)/shard_map/ppermute | solution.py:401
  55.6 6.7 %collective-permute-start.11 = (f32[8,128]{1,0:T(8,128)S(1)}, f32[8,128]{1,0:T(8,128)S(1)}, u32[]{:S(2)}, u32[]{:S(2)}) collective-permute-start(f32[8,128]{1,0:T(8,128)S(1)} %get-tuple-element.52._.refs_0_), channel_id=1, source_target_pairs={{0,1},{1,0},{2,3},{3,2},{4,5},{5,4},{6,7},{7,6},{8,9},{9,8},{10,11... | collective-permute-start | bytes 12296 | tf_op jit(solution)/shard_map/ppermute | solution.py:401
  56.3 6.0 %collective-permute-start.12 = (f32[8,128]{1,0:T(8,128)S(1)}, f32[8,128]{1,0:T(8,128)S(1)}, u32[]{:S(2)}, u32[]{:S(2)}) collective-permute-start(f32[8,128]{1,0:T(8,128)S(1)} %get-tuple-element.52._.refs_0_), channel_id=1, source_target_pairs={{0,2},{1,3},{2,0},{3,1},{4,6},{5,7},{6,4},{7,5},{8,10},{9,11},{10,... | collective-permute-start | bytes 12296 | tf_op jit(solution)/shard_map/ppermute | solution.py:401
  59.8 5.4 %collective-permute-start.13 = (f32[8,128]{1,0:T(8,128)S(1)}, f32[8,128]{1,0:T(8,128)S(1)}, u32[]{:S(2)}, u32[]{:S(2)}) collective-permute-start(f32[8,128]{1,0:T(8,128)S(1)} %get-tuple-element.52._.refs_0_), channel_id=1, source_target_pairs={{0,3},{1,2},{2,1},{3,0},{4,7},{5,6},{6,5},{7,4},{8,11},{9,10},{10,... | collective-permute-start | bytes 12296 | tf_op jit(solution)/shard_map/ppermute | solution.py:401

commit v14 on v6

--- a/solution.py
+++ b/solution.py
@@ -426,9 +426,6 @@
         out_shape=array(rows, width),
         scratch_shapes=[dma((4,))],
     )(queries, chip)
-    route = [(i, i + 1) for i in range(lax.axis_size("ctx") - 1)]
-    before_k = lax.ppermute(tail_k, "ctx", route)
-
     def local(begin, count, after):
         taken = count * HD
         after = [] if after is None else [after]
@@ -451,7 +448,11 @@
         )(array_now, after)
 
     begin = heads * 3 // 4 // GROUP * GROUP
-    parts = [local(0, begin, None)]
+    parts = [local(0, GROUP, None)]
+    route = [(i, i + 1) for i in range(lax.axis_size("ctx") - 1)]
+    before_k = lax.ppermute(pass_on(tail_k, parts[0][2]), "ctx", route)
+    if begin > GROUP:
+        parts.append(local(GROUP, begin - GROUP, parts[0][2]))
     message = None
     if lax.axis_size("ctx") == 8:
         first = first_phase(chip)
@@ -460,10 +461,10 @@
             "message",
             in_specs=[vmem, vmem, anywhere],
             out_shape=packed,
-        )(first, chip, parts[0][2])
-    parts.append(local(begin, heads - begin, message))
+        )(first, chip, parts[-1][2])
+    parts.append(local(begin, heads - begin, parts[-1][2] if message is None else message))
     window, linear, window_sums = zip(*parts)
-    before_v = lax.ppermute(pass_on(tail_v, window_sums[1]), "ctx", route)
+    before_v = lax.ppermute(pass_on(tail_v, window_sums[-1]), "ctx", route)
     first_weights, first_now = call(
         first_weights_kernel,
         "first_weights",

time: 53.8 us -> 56.9 us (1.058)
  waiting for transfers between devices: 12.4 us -> 15.5 us
  starting transfers between devices: 15.9 us -> 15 us
  Pallas kernels: 25.3 us -> 25.9 us
    ppermute x2, waiting for transfers between devices: 4.27 us -> 7.39 us  [the longest x1 5.18 us: shards(): before_k = lax.ppermute(pass_on(tail_k, parts[0][2]), 'ctx', route)]
    ppermute x8, starting transfers between devices: 9.57 us -> 8.72 us  [swap(): lax.ppermute(block, axis, [(i, i ^ bit) for i in range(lax.axis_size(axis...]
    pallas_call x2 -> x3, Pallas kernels: 8.94 us -> 9.59 us  [local(): call(functools.partial(local_kernel, begin, len(after)), 'local', in_spec...]
  transfers between devices with their start and end apart: 12 -> 12, of which waited for: 6 -> 6; matrix products, arithmetic and copies ran while one was open for 0% -> 0% of each run, Pallas kernels for 37% -> 36%
where the time goes in v14:
time: 56.9 us; the launch traced here: 56.7 us
  Pallas kernels  25.9 us (46%)
  waiting for transfers between devices  15.5 us (27%)
  starting transfers between devices  15 us (26%)
    pallas_call x3, Pallas kernels, local(): call(functools.partial(local_kernel, begin, len(after)), 'local', in_spec...  9.59 us
    ppermute x8, starting transfers between devices, swap(): lax.ppermute(block, axis, [(i, i ^ bit) for i in range(lax.axis_size(axis...  8.72 us
    ppermute x8, waiting for transfers between devices, swap(): lax.ppermute(block, axis, [(i, i ^ bit) for i in range(lax.axis_size(axis...  5.43 us
    ppermute x1, waiting for transfers between devices, shards(): before_k = lax.ppermute(pass_on(tail_k, parts[0][2]), 'ctx', route)  5.18 us
    pallas_call x1, Pallas kernels, shards(): call(totals_kernel, 'totals', in_specs=[anywhere, anywhere], out_shape=[p...  4.16 us
    pallas_call x1, Pallas kernels, shards(): call(first_weights_kernel, 'first_weights', in_specs=[smem] + [vmem] * 4,...  2.84 us
    ppermute x1, waiting for transfers between devices, second_phase(): lax.ppermute(message, 'ctx', [(i, i ^ (4 if i % 2 == 0 else 2)) for i in...  2.66 us
    pallas_call x1, Pallas kernels, shards(): call(functools.partial(earlier_kernel, len(parts)), 'earlier', in_specs=[...  2.47 us
  transfers between devices with their start and end apart: 12, of which 6 were waited for; matrix products, arithmetic and copies ran while one was open for 0% of the time, Pallas kernels for 36%

profile of v14, /device:TPU:4, one launch (start us, length us, event | category | flops | bytes accessed | tf_op | source)
XLA Modules:
  0.0 56.7 jit_solution(3869131288940993804)
XLA Ops:
  0.0 4.2 %totals.1 = (f32[8,128,128]{2,1,0:T(8,128)S(1)}, f32[8,128,128]{2,1,0:T(8,128)S(1)}, f32[16,128,128]{2,1,0:T(8,128)S(1)}, f32[512,2048]{1,0:T(8,128)S(1)}, f32[5...) custom-call(f32[512,2048]{1,0:T(8,128)} %k_hbm.1, f32[512,2048]{1,0:T(8,128)} %v_hbm.1), custom_call_target="tpu_custom_call" | custom-call | tf_op jit(solution)/shard_map/totals/pallas_call | solution.py:398
  4.2 1.9 %collective-permute-done.beside_ref = f32[8,128,128]{2,1,0:T(8,128)S(1)} collective-permute-done((f32[8,128,128]{2,1,0:T(8,128)S(1)}, f32[8,128,128]{2,1,0:T(8,128)S(1)}, u32[]{:S(2)}, u32[]{:S(2)}) %collective-permute-start) | collective-permute-done | bytes 524320 | tf_op jit(solution)/shard_map/ppermute | solution.py:345
  6.2 1.6 %collective-permute-start.2 = (f32[8,128,128]{2,1,0:T(8,128)S(1)}, f32[8,128,128]{2,1,0:T(8,128)S(1)}, u32[]{:S(2)}, u32[]{:S(2)}) collective-permute-start(f32[8,128,128]{2,1,0:T(8,128)S(1)} %get-tuple-element.36._.chip_ref), channel_id=1, source_target_pairs={{0,8},{4,20},{8,0},{12,28},{16,24},{20,4},{24,16},{28,12},{1,9},{5... | collective-permute-start | bytes 1572872 | tf_op jit(solution)/shard_map/ppermute | solution.py:353
  7.8 2.2 %load.1.q_ref = f32[512,2048]{1,0:T(8,128)S(1)} custom-call(f32[512,2048]{1,0:T(8,128)} %q_hbm.1, f32[8,128,128]{2,1,0:T(8,128)S(1)} %get-tuple-element.36._.chip_ref), custom_call_target="tpu_custom_call" | custom-call | tf_op jit(solution)/shard_map/load/pallas_call | solution.py:422
  10.0 2.5 %local.3 = (f32[512,512]{1,0:T(8,128)S(1)}, f32[512,512]{1,0:T(8,128)S(1)}, f32[8,512]{1,0:T(8,128)S(1)}) custom-call(f32[2,16]{1,0:T(2,128)S(1)} %copy-done, f32[512,2048]{1,0:T(8,128)S(1)} %load.1.q_ref, f32[512,2048]{1,0:T(8,128)S(1)} %get-tuple-element.37.k_ref, f32[512,2048]{1,0:T(8,128)S(1)} %get-tuple-element.38.v_ref), custom_call_target="tpu_custom_call" | custom-call | tf_op jit(solution)/shard_map/local/pallas_call | solution.py:432
  12.5 1.9 %collective-permute-start.1 = (f32[128,2048]{1,0:T(8,128)S(1)}, f32[128,2048]{1,0:T(8,128)S(1)}, u32[]{:S(2)}, u32[]{:S(2)}) collective-permute-start(f32[128,2048]{1,0:T(8,128)S(1)} %pass.2), channel_id=1, source_target_pairs={{0,4},{4,8},{8,12},{12,16},{16,20},{20,24},{24,28},{1,5},{5,9},{9,... | collective-permute-start | bytes 3145736 | tf_op jit(solution)/shard_map/ppermute | solution.py:453
  14.5 4.5 %local.4 = (f32[512,1024]{1,0:T(8,128)S(1)}, f32[512,1024]{1,0:T(8,128)S(1)}, f32[8,512]{1,0:T(8,128)S(1)}) custom-call(f32[2,16]{1,0:T(2,128)S(1)} %copy-done, f32[512,2048]{1,0:T(8,128)S(1)} %load.1.q_ref, f32[512,2048]{1,0:T(8,128)S(1)} %get-tuple-element.37.k_ref, f32[512,2048]{1,0:T(8,128)S(1)} %get-tuple-element.38.v_ref, ...), custom_call_target="tpu_custom_call" | custom-call | tf_op jit(solution)/shard_map/local/pallas_call | solution.py:432
  19.1 0.5 collective-permute-start.4
  19.6 2.5 %local.5 = (f32[512,512]{1,0:T(8,128)S(1)}, f32[512,512]{1,0:T(8,128)S(1)}, f32[8,512]{1,0:T(8,128)S(1)}) custom-call(f32[2,16]{1,0:T(2,128)S(1)} %copy-done, f32[512,2048]{1,0:T(8,128)S(1)} %load.1.q_ref, f32[512,2048]{1,0:T(8,128)S(1)} %get-tuple-element.37.k_ref, f32[512,2048]{1,0:T(8,128)S(1)} %get-tuple-element.38.v_ref, f32[8,128,128]{2,1,0:T(8,128)S(1)} %message.1.refs_0_), custom_call_target="tpu_custom_call" | custom-call | tf_op jit(solution)/shard_map/local/pallas_call | solution.py:432
  22.2 2.3 %collective-permute-start.3 = (f32[128,2048]{1,0:T(8,128)S(1)}, f32[128,2048]{1,0:T(8,128)S(1)}, u32[]{:S(2)}, u32[]{:S(2)}) collective-permute-start(f32[128,2048]{1,0:T(8,128)S(1)} %pass.3), channel_id=1, source_target_pairs={{0,4},{4,8},{8,12},{12,16},{16,20},{20,24},{24,28},{1,5},{5,9},{9,... | collective-permute-start | bytes 3145736 | tf_op jit(solution)/shard_map/ppermute | solution.py:467
  24.5 5.2 %collective-permute-done.1.tail_ref = f32[128,2048]{1,0:T(8,128)S(1)} collective-permute-done((f32[128,2048]{1,0:T(8,128)S(1)}, f32[128,2048]{1,0:T(8,128)S(1)}, u32[]{:S(2)}, u32[]{:S(2)}) %collective-permute-start.1) | collective-permute-done | bytes 1048608 | tf_op jit(solution)/shard_map/ppermute | solution.py:453
  29.7 2.8 %first_weights.1 = (bf16[128,4096]{1,0:T(8,128)(2,1)S(1)}, f32[128,2048]{1,0:T(8,128)S(1)}) custom-call(f32[2,16]{1,0:T(2,128)S(1)} %copy-done, f32[512,2048]{1,0:T(8,128)S(1)} %load.1.q_ref, f32[512,2048]{1,0:T(8,128)S(1)} %get-tuple-element.37.k_ref, f32[512,2048]{1,0:T(8,128)S(1)} %get-tuple-element.38.v_ref, f32[128,2048]{1,0:T(8,128)S(1)} %collective-permute-done.1.tail_ref), custom_call_target="tpu_custom_call" | custom-call | tf_op jit(solution)/shard_map/first_weights/pallas_call | solution.py:468
  32.5 2.7 %collective-permute-done.4.second_ref = f32[8,128,128]{2,1,0:T(8,128)S(1)} collective-permute-done((f32[8,128,128]{2,1,0:T(8,128)S(1)}, f32[8,128,128]{2,1,0:T(8,128)S(1)}, u32[]{:S(2)}, u32[]{:S(2)}) %collective-permute-start.4) | collective-permute-done | bytes 524320 | tf_op jit(solution)/shard_map/ppermute | solution.py:357
  35.5 1.9 %collective-permute-done.5.other_ref = f32[8,128,128]{2,1,0:T(8,128)S(1)} collective-permute-done((f32[8,128,128]{2,1,0:T(8,128)S(1)}, f32[8,128,128]{2,1,0:T(8,128)S(1)}, u32[]{:S(2)}, u32[]{:S(2)}) %collective-permute-start.5) | collective-permute-done | bytes 524320 | tf_op jit(solution)/shard_map/ppermute | solution.py:345
  37.4 2.5 %earlier.1 = (f32[512,512]{1,0:T(8,128)S(1)}, f32[512,1024]{1,0:T(8,128)S(1)}, f32[512,512]{1,0:T(8,128)S(1)}, f32[8,512]{1,0:T(8,128)S(1)}) custom-call(f32[2,16]{1,0:T(2,128)S(1)} %copy-done, f32[16,128,128]{2,1,0:T(8,128)S(1)} %get-tuple-element.46.half_ref, f32[8,128,128]{2,1,0:T(8,128)S(1)} %get-tuple-element.47.mine_ref, ...), custom_call_target="tpu_custom_call" | custom-call | tf_op jit(solution)/shard_map/earlier/pallas_call | solution.py:490
  39.9 1.6 %collective-permute-start.6 = (f32[8,512]{1,0:T(8,128)S(1)}, f32[8,512]{1,0:T(8,128)S(1)}, u32[]{:S(2)}, u32[]{:S(2)}) collective-permute-start(f32[8,512]{1,0:T(8,128)S(1)} %get-tuple-element.52._.refs_0_.refs_3_), channel_id=1, source_target_pairs={{0,1},{1,0},{2,3},{3,2},{4,5},{5,4},{6,7},{7,6},{8,9},{9,8},{10,11... | collective-permute-start | bytes 49160 | tf_op jit(solution)/shard_map/ppermute | solution.py:345
  41.4 2.6 %collective-permute-start.7 = (f32[8,512]{1,0:T(8,128)S(1)}, f32[8,512]{1,0:T(8,128)S(1)}, u32[]{:S(2)}, u32[]{:S(2)}) collective-permute-start(f32[8,512]{1,0:T(8,128)S(1)} %get-tuple-element.52._.refs_0_.refs_3_), channel_id=1, source_target_pairs={{0,2},{1,3},{2,0},{3,1},{4,6},{5,7},{6,4},{7,5},{8,10},{9,11},{10,... | collective-permute-start | bytes 49160 | tf_op jit(solution)/shard_map/ppermute | solution.py:345
  44.3 2.2 %collective-permute-done.3.tail_v_ref = f32[128,2048]{1,0:T(8,128)S(1)} collective-permute-done((f32[128,2048]{1,0:T(8,128)S(1)}, f32[128,2048]{1,0:T(8,128)S(1)}, u32[]{:S(2)}, u32[]{:S(2)}) %collective-permute-start.3) | collective-permute-done | bytes 1048608 | tf_op jit(solution)/shard_map/ppermute | solution.py:467
  46.5 0.8 %first_values.1 = (f32[128,2048]{1,0:T(8,128)S(1)}, f32[8,128]{1,0:T(8,128)S(1)}) custom-call(bf16[128,4096]{1,0:T(8,128)(2,1)S(1)} %get-tuple-element.41.weights_ref, f32[128,2048]{1,0:T(8,128)S(1)} %get-tuple-element.42.refs_0_.now_ref, f32[128,2048]{1,0:T(8,128)S(1)} %collective-permute-done.3.tail_v_ref, f32[8,512]{1,0:T(8,128)S(1)} %get-tuple-element.52._.refs_0_.refs_3_), custom_call_target="tpu_custom_call" | custom-call | tf_op jit(solution)/shard_map/first_values/pallas_call | solution.py:498
  47.3 2.6 %collective-permute-start.10 = (f32[8,128]{1,0:T(8,128)S(1)}, f32[8,128]{1,0:T(8,128)S(1)}, u32[]{:S(2)}, u32[]{:S(2)}) collective-permute-start(f32[8,128]{1,0:T(8,128)S(1)} %get-tuple-element.54._.refs_7_), channel_id=1, source_target_pairs={{0,2},{1,3},{2,0},{3,1},{4,6},{5,7},{6,4},{7,5},{8,10},{9,11},{10,... | collective-permute-start | bytes 12296 | tf_op jit(solution)/shard_map/ppermute | solution.py:345
  49.9 1.3 %collective-permute-start.11 = (f32[8,128]{1,0:T(8,128)S(1)}, f32[8,128]{1,0:T(8,128)S(1)}, u32[]{:S(2)}, u32[]{:S(2)}) collective-permute-start(f32[8,128]{1,0:T(8,128)S(1)} %get-tuple-element.54._.refs_7_), channel_id=1, source_target_pairs={{0,3},{1,2},{2,1},{3,0},{4,7},{5,6},{6,5},{7,4},{8,11},{9,10},{10,... | collective-permute-start | bytes 12296 | tf_op jit(solution)/shard_map/ppermute | solution.py:345
  51.5 2.2 %scale.1._ = f32[512,2048]{1,0:T(8,128)} custom-call(f32[8,128]{1,0:T(8,128)S(1)} %get-tuple-element.54._.refs_7_, f32[8,512]{1,0:T(8,128)S(1)} %get-tuple-element.52._.refs_0_.refs_3_, f32[8,512]{1,0:T(8,128)S(1)} %collective-permute-done.6.refs_1_.refs_4_, f32[8,512]{1,0:T(8,128)S(1)} %collective-permute-done.7.refs_2_.refs_5_, ...), custom_call_target="tpu_custom_call" | custom-call | tf_op jit(solution)/shard_map/scale/pallas_call | solution.py:505
  53.7 1.6 %collective-permute-done.11.refs_10_ = f32[8,128]{1,0:T(8,128)S(1)} collective-permute-done((f32[8,128]{1,0:T(8,128)S(1)}, f32[8,128]{1,0:T(8,128)S(1)}, u32[]{:S(2)}, u32[]{:S(2)}) %collective-permute-start.11) | collective-permute-done | bytes 4128 | tf_op jit(solution)/shard_map/ppermute | solution.py:345
  55.3 1.2 %first_scale.1 = f32[512,2048]{1,0:T(8,128)} custom-call(f32[128,2048]{1,0:T(8,128)S(1)} %get-tuple-element.53.a_ref, f32[512,2048]{1,0:T(8,128)} %scale.1._, f32[512,512]{1,0:T(8,128)S(1)} %get-tuple-element.58.refs_7_.refs_0_, f32[512,1024]{1,0:T(8,128)S(1)} %get-tuple-element.59.refs_8_.refs_1_, ...), custom_call_target="tpu_custom_call", output_to_operand_aliasing={{}: (1, {})} | custom-call | tf_op jit(solution)/shard_map/first_scale/pallas_call | solution.py:513
  (17 shorter events, 1.0 us)
Async XLA Ops:
  4.2 2.0 %collective-permute-start = (f32[8,128,128]{2,1,0:T(8,128)S(1)}, f32[8,128,128]{2,1,0:T(8,128)S(1)}, u32[]{:S(2)}, u32[]{:S(2)}) collective-permute-start(f32[8,128,128]{2,1,0:T(8,128)S(1)} %get-tuple-element.34), channel_id=1, source_target_pairs={{0,4},{4,0},{8,12},{12,8},{16,20},{20,16},{24,28},{28,24},{1,5},{5... | collective-permute-start | bytes 1572872 | tf_op jit(solution)/shard_map/ppermute | solution.py:345
  6.2 3.8 %copy-start = (f32[2,16]{1,0:T(2,128)S(1)}, f32[2,16]{1,0:T(2,128)}, u32[]{:S(2)}) copy-start(f32[2,16]{1,0:T(2,128)} %gain_ref.9) | copy-start | bytes 388
  6.2 12.8 %collective-permute-start.2 = (f32[8,128,128]{2,1,0:T(8,128)S(1)}, f32[8,128,128]{2,1,0:T(8,128)S(1)}, u32[]{:S(2)}, u32[]{:S(2)}) collective-permute-start(f32[8,128,128]{2,1,0:T(8,128)S(1)} %get-tuple-element.36._.chip_ref), channel_id=1, source_target_pairs={{0,8},{4,20},{8,0},{12,28},{16,24},{20,4},{24,16},{28,12},{1,9},{5... | collective-permute-start | bytes 1572872 | tf_op jit(solution)/shard_map/ppermute | solution.py:353
  12.5 17.1 %collective-permute-start.1 = (f32[128,2048]{1,0:T(8,128)S(1)}, f32[128,2048]{1,0:T(8,128)S(1)}, u32[]{:S(2)}, u32[]{:S(2)}) collective-permute-start(f32[128,2048]{1,0:T(8,128)S(1)} %pass.2), channel_id=1, source_target_pairs={{0,4},{4,8},{8,12},{12,16},{16,20},{20,24},{24,28},{1,5},{5,9},{9,... | collective-permute-start | bytes 3145736 | tf_op jit(solution)/shard_map/ppermute | solution.py:453
  19.1 16.0 %collective-permute-start.4 = (f32[8,128,128]{2,1,0:T(8,128)S(1)}, f32[8,128,128]{2,1,0:T(8,128)S(1)}, u32[]{:S(2)}, u32[]{:S(2)}) collective-permute-start(f32[8,128,128]{2,1,0:T(8,128)S(1)} %message.1.refs_0_), channel_id=1, source_target_pairs={{0,16},{4,12},{8,24},{12,4},{16,0},{20,28},{24,8},{28,20},{1,17},{... | collective-permute-start | bytes 1572872 | tf_op jit(solution)/shard_map/ppermute | solution.py:357
  22.2 24.3 %collective-permute-start.3 = (f32[128,2048]{1,0:T(8,128)S(1)}, f32[128,2048]{1,0:T(8,128)S(1)}, u32[]{:S(2)}, u32[]{:S(2)}) collective-permute-start(f32[128,2048]{1,0:T(8,128)S(1)} %pass.3), channel_id=1, source_target_pairs={{0,4},{4,8},{8,12},{12,16},{16,20},{20,24},{24,28},{1,5},{5,9},{9,... | collective-permute-start | bytes 3145736 | tf_op jit(solution)/shard_map/ppermute | solution.py:467
  35.4 2.0 %collective-permute-start.5 = (f32[8,128,128]{2,1,0:T(8,128)S(1)}, f32[8,128,128]{2,1,0:T(8,128)S(1)}, u32[]{:S(2)}, u32[]{:S(2)}) collective-permute-start(f32[8,128,128]{2,1,0:T(8,128)S(1)} %get-tuple-element.48), channel_id=1, source_target_pairs={{0,4},{4,0},{8,12},{12,8},{16,20},{20,16},{24,28},{28,24},{1,5},{5... | collective-permute-start | bytes 1572872 | tf_op jit(solution)/shard_map/ppermute | solution.py:345
  39.9 11.4 %collective-permute-start.6 = (f32[8,512]{1,0:T(8,128)S(1)}, f32[8,512]{1,0:T(8,128)S(1)}, u32[]{:S(2)}, u32[]{:S(2)}) collective-permute-start(f32[8,512]{1,0:T(8,128)S(1)} %get-tuple-element.52._.refs_0_.refs_3_), channel_id=1, source_target_pairs={{0,1},{1,0},{2,3},{3,2},{4,5},{5,4},{6,7},{7,6},{8,9},{9,8},{10,11... | collective-permute-start | bytes 49160 | tf_op jit(solution)/shard_map/ppermute | solution.py:345
  41.4 10.0 %collective-permute-start.7 = (f32[8,512]{1,0:T(8,128)S(1)}, f32[8,512]{1,0:T(8,128)S(1)}, u32[]{:S(2)}, u32[]{:S(2)}) collective-permute-start(f32[8,512]{1,0:T(8,128)S(1)} %get-tuple-element.52._.refs_0_.refs_3_), channel_id=1, source_target_pairs={{0,2},{1,3},{2,0},{3,1},{4,6},{5,7},{6,4},{7,5},{8,10},{9,11},{10,... | collective-permute-start | bytes 49160 | tf_op jit(solution)/shard_map/ppermute | solution.py:345
  44.0 7.5 %collective-permute-start.8 = (f32[8,512]{1,0:T(8,128)S(1)}, f32[8,512]{1,0:T(8,128)S(1)}, u32[]{:S(2)}, u32[]{:S(2)}) collective-permute-start(f32[8,512]{1,0:T(8,128)S(1)} %get-tuple-element.52._.refs_0_.refs_3_), channel_id=1, source_target_pairs={{0,3},{1,2},{2,1},{3,0},{4,7},{5,6},{6,5},{7,4},{8,11},{9,10},{10,... | collective-permute-start | bytes 49160 | tf_op jit(solution)/shard_map/ppermute | solution.py:345
  47.3 6.4 %collective-permute-start.10 = (f32[8,128]{1,0:T(8,128)S(1)}, f32[8,128]{1,0:T(8,128)S(1)}, u32[]{:S(2)}, u32[]{:S(2)}) collective-permute-start(f32[8,128]{1,0:T(8,128)S(1)} %get-tuple-element.54._.refs_7_), channel_id=1, source_target_pairs={{0,2},{1,3},{2,0},{3,1},{4,6},{5,7},{6,4},{7,5},{8,10},{9,11},{10,... | collective-permute-start | bytes 12296 | tf_op jit(solution)/shard_map/ppermute | solution.py:345
  49.9 5.4 %collective-permute-start.11 = (f32[8,128]{1,0:T(8,128)S(1)}, f32[8,128]{1,0:T(8,128)S(1)}, u32[]{:S(2)}, u32[]{:S(2)}) collective-permute-start(f32[8,128]{1,0:T(8,128)S(1)} %get-tuple-element.54._.refs_7_), channel_id=1, source_target_pairs={{0,3},{1,2},{2,1},{3,0},{4,7},{5,6},{6,5},{7,4},{8,11},{9,10},{10,... | collective-permute-start | bytes 12296 | tf_op jit(solution)/shard_map/ppermute | solution.py:345
  51.2 4.1 %collective-permute-start.9 = (f32[8,128]{1,0:T(8,128)S(1)}, f32[8,128]{1,0:T(8,128)S(1)}, u32[]{:S(2)}, u32[]{:S(2)}) collective-permute-start(f32[8,128]{1,0:T(8,128)S(1)} %get-tuple-element.54._.refs_7_), channel_id=1, source_target_pairs={{0,1},{1,0},{2,3},{3,2},{4,5},{5,4},{6,7},{7,6},{8,9},{9,8},{10,11... | collective-permute-start | bytes 12296 | tf_op jit(solution)/shard_map/ppermute | solution.py:345

commit v15 on v6

--- a/solution.py
+++ b/solution.py
@@ -63,12 +63,12 @@
 
 
 def wide_keys(k_high, k_low):
-    return stack(side(k_high, k_high), side(k_low, jnp.zeros_like(k_low)))
+    return stack(side(k_high, k_high), side(k_low, k_low))
 
 
 def wide_state(state):
     high, low = halves(state)
-    return stack(side(high, low), side(high, jnp.zeros_like(high)))
+    return stack(side(high, low), side(high, low))
 
 
 def folded(wide):
@@ -96,7 +96,7 @@
     pass
 
 
-def chip_kernel(keep_ref, beside_ref, _, out_ref, __):
+def chip_kernel(keep_ref, beside_ref, _, __, out_ref, ___):
     out_ref[...] = keep_ref[...] + beside_ref[...]
 
 
@@ -411,21 +411,21 @@
         scratch_shapes=[dma((2, heads // GROUP))],
     )(keys, values)
     beside = swap(send, "ctx", 1)
-    chip, tail_k = call(
-        chip_kernel,
-        "chip",
-        in_specs=[vmem, vmem, anywhere],
-        out_specs=[vmem, anywhere],
-        out_shape=[packed, first_tile],
-        input_output_aliases={2: 1},
-    )(keep, beside, tail_k)
     held_q = call(
         load_kernel,
         "load",
         in_specs=[anywhere, anywhere],
         out_shape=array(rows, width),
         scratch_shapes=[dma((4,))],
-    )(queries, chip)
+    )(queries, send)
+    chip, tail_k = call(
+        chip_kernel,
+        "chip",
+        in_specs=[vmem, vmem, anywhere, anywhere],
+        out_specs=[vmem, anywhere],
+        out_shape=[packed, first_tile],
+        input_output_aliases={3: 1},
+    )(keep, beside, held_q, tail_k)
     route = [(i, i + 1) for i in range(lax.axis_size("ctx") - 1)]
     before_k = lax.ppermute(tail_k, "ctx", route)
 

time: 53.8 us -> 54.2 us (level)
  starting transfers between devices: 15.9 us -> 23.3 us
  waiting for transfers between devices: 12.4 us -> 5.31 us
    ppermute x1, starting transfers between devices: 1.93 us -> 9.12 us  [shards(): before_v = lax.ppermute(pass_on(tail_v, window_sums[1]), 'ctx', route)]
    ppermute x1, waiting for transfers between devices: 2.65 us -> 0.01 us  [second_phase(): lax.ppermute(message, 'ctx', [(i, i ^ (4 if i % 2 == 0 else 2)) for i in...]
    ppermute x1, waiting for transfers between devices: 2.38 us -> 0.01 us  [shards(): before_k = lax.ppermute(tail_k, 'ctx', route)]
    ppermute x8, waiting for transfers between devices: 5.43 us -> 3.17 us  [swap(): lax.ppermute(block, axis, [(i, i ^ bit) for i in range(lax.axis_size(axis...]
    ppermute x1, waiting for transfers between devices: 0.01 us -> 2.13 us  [first_phase(): lax.ppermute(chip, 'ctx', [(i, i ^ (2 if i % 2 == 0 else 4)) for i in ran...]
    ppermute x1, waiting for transfers between devices: 1.89 us -> 0.01 us  [shards(): before_v = lax.ppermute(pass_on(tail_v, window_sums[1]), 'ctx', route)]
  transfers between devices with their start and end apart: 12 -> 12, of which waited for: 6 -> 3; matrix products, arithmetic and copies ran while one was open for 0% -> 0% of each run, Pallas kernels for 37% -> 37%
where the time goes in v15:
time: 54.2 us; the launch traced here: 54 us
  Pallas kernels  25.2 us (46%)
  starting transfers between devices  23.3 us (43%)
  waiting for transfers between devices  5.31 us (10%)
    ppermute x8, starting transfers between devices, swap(): lax.ppermute(block, axis, [(i, i ^ bit) for i in range(lax.axis_size(axis...  9.79 us
    ppermute x1, starting transfers between devices, shards(): before_v = lax.ppermute(pass_on(tail_v, window_sums[1]), 'ctx', route)  9.12 us
    pallas_call x2, Pallas kernels, local(): call(functools.partial(local_kernel, begin, len(after)), 'local', in_spec...  8.84 us
    pallas_call x1, Pallas kernels, shards(): call(totals_kernel, 'totals', in_specs=[anywhere, anywhere], out_shape=[p...  4.16 us
    ppermute x8, waiting for transfers between devices, swap(): lax.ppermute(block, axis, [(i, i ^ bit) for i in range(lax.axis_size(axis...  3.17 us
    pallas_call x1, Pallas kernels, shards(): call(first_weights_kernel, 'first_weights', in_specs=[smem] + [vmem] * 4,...  2.83 us
    pallas_call x1, Pallas kernels, shards(): call(functools.partial(earlier_kernel, len(parts)), 'earlier', in_specs=[...  2.48 us
    pallas_call x1, Pallas kernels, shards(): call(load_kernel, 'load', in_specs=[anywhere, anywhere], out_shape=array(...  2.22 us
  transfers between devices with their start and end apart: 12, of which 3 were waited for; matrix products, arithmetic and copies ran while one was open for 0% of the time, Pallas kernels for 37%

profile of v15, /device:TPU:4, one launch (start us, length us, event | category | flops | bytes accessed | tf_op | source)
XLA Modules:
  0.0 54.0 jit_solution(13328268810260292561)
XLA Ops:
  0.0 4.2 %totals.1 = (f32[8,128,128]{2,1,0:T(8,128)S(1)}, f32[8,128,128]{2,1,0:T(8,128)S(1)}, f32[16,128,128]{2,1,0:T(8,128)S(1)}, f32[512,2048]{1,0:T(8,128)S(1)}, f32[5...) custom-call(f32[512,2048]{1,0:T(8,128)} %k_hbm.1, f32[512,2048]{1,0:T(8,128)} %v_hbm.1), custom_call_target="tpu_custom_call" | custom-call | tf_op jit(solution)/shard_map/totals/pallas_call | solution.py:398
  4.2 2.2 %load.1._.q_ref = f32[512,2048]{1,0:T(8,128)S(1)} custom-call(f32[512,2048]{1,0:T(8,128)} %q_hbm.1, f32[8,128,128]{2,1,0:T(8,128)S(1)} %get-tuple-element.29._), custom_call_target="tpu_custom_call" | custom-call | tf_op jit(solution)/shard_map/load/pallas_call | solution.py:414
  6.6 1.6 %collective-permute-start.2 = (f32[8,128,128]{2,1,0:T(8,128)S(1)}, f32[8,128,128]{2,1,0:T(8,128)S(1)}, u32[]{:S(2)}, u32[]{:S(2)}) collective-permute-start(f32[8,128,128]{2,1,0:T(8,128)S(1)} %get-tuple-element.38.chip_ref), channel_id=1, source_target_pairs={{0,8},{4,20},{8,0},{12,28},{16,24},{20,4},{24,16},{28,12},{1,9},{5... | collective-permute-start | bytes 1572872 | tf_op jit(solution)/shard_map/ppermute | solution.py:353
  8.1 1.9 %collective-permute-start.1 = (f32[128,2048]{1,0:T(8,128)S(1)}, f32[128,2048]{1,0:T(8,128)S(1)}, u32[]{:S(2)}, u32[]{:S(2)}) collective-permute-start(f32[128,2048]{1,0:T(8,128)S(1)} %get-tuple-element.34), channel_id=1, source_target_pairs={{0,4},{4,8},{8,12},{12,16},{16,20},{20,24},{24,28},{1,5},{5,9},{9,... | collective-permute-start | bytes 3145736 | tf_op jit(solution)/shard_map/ppermute | solution.py:430
  10.0 6.3 %local.2 = (f32[512,1536]{1,0:T(8,128)S(1)}, f32[512,1536]{1,0:T(8,128)S(1)}, f32[8,512]{1,0:T(8,128)S(1)}) custom-call(f32[2,16]{1,0:T(2,128)S(1)} %copy-done, f32[512,2048]{1,0:T(8,128)S(1)} %load.1._.q_ref, f32[512,2048]{1,0:T(8,128)S(1)} %get-tuple-element.30.k_ref, f32[512,2048]{1,0:T(8,128)S(1)} %get-tuple-element.31.v_ref), custom_call_target="tpu_custom_call" | custom-call | tf_op jit(solution)/shard_map/local/pallas_call | solution.py:435
  16.4 2.1 %collective-permute-done.2.first_ref = f32[8,128,128]{2,1,0:T(8,128)S(1)} collective-permute-done((f32[8,128,128]{2,1,0:T(8,128)S(1)}, f32[8,128,128]{2,1,0:T(8,128)S(1)}, u32[]{:S(2)}, u32[]{:S(2)}) %collective-permute-start.2) | collective-permute-done | bytes 524320 | tf_op jit(solution)/shard_map/ppermute | solution.py:353
  18.5 0.1 message.1.refs_0_
  18.6 1.0 %collective-permute-start.4 = (f32[8,128,128]{2,1,0:T(8,128)S(1)}, f32[8,128,128]{2,1,0:T(8,128)S(1)}, u32[]{:S(2)}, u32[]{:S(2)}) collective-permute-start(f32[8,128,128]{2,1,0:T(8,128)S(1)} %message.1.refs_0_), channel_id=1, source_target_pairs={{0,16},{4,12},{8,24},{12,4},{16,0},{20,28},{24,8},{28,20},{1,17},{... | collective-permute-start | bytes 1572872 | tf_op jit(solution)/shard_map/ppermute | solution.py:357
  19.6 2.5 %local.3 = (f32[512,512]{1,0:T(8,128)S(1)}, f32[512,512]{1,0:T(8,128)S(1)}, f32[8,512]{1,0:T(8,128)S(1)}) custom-call(f32[2,16]{1,0:T(2,128)S(1)} %copy-done, f32[512,2048]{1,0:T(8,128)S(1)} %load.1._.q_ref, f32[512,2048]{1,0:T(8,128)S(1)} %get-tuple-element.30.k_ref, f32[512,2048]{1,0:T(8,128)S(1)} %get-tuple-element.31.v_ref, ...), custom_call_target="tpu_custom_call" | custom-call | tf_op jit(solution)/shard_map/local/pallas_call | solution.py:435
  22.1 9.1 %collective-permute-start.3 = (f32[128,2048]{1,0:T(8,128)S(1)}, f32[128,2048]{1,0:T(8,128)S(1)}, u32[]{:S(2)}, u32[]{:S(2)}) collective-permute-start(f32[128,2048]{1,0:T(8,128)S(1)} %pass.1), channel_id=1, source_target_pairs={{0,4},{4,8},{8,12},{12,16},{16,20},{20,24},{24,28},{1,5},{5,9},{9,... | collective-permute-start | bytes 3145736 | tf_op jit(solution)/shard_map/ppermute | solution.py:466
  31.2 2.8 %first_weights.1 = (bf16[128,4096]{1,0:T(8,128)(2,1)S(1)}, f32[128,2048]{1,0:T(8,128)S(1)}) custom-call(f32[2,16]{1,0:T(2,128)S(1)} %copy-done, f32[512,2048]{1,0:T(8,128)S(1)} %load.1._.q_ref, f32[512,2048]{1,0:T(8,128)S(1)} %get-tuple-element.30.k_ref, f32[512,2048]{1,0:T(8,128)S(1)} %get-tuple-element.31.v_ref, ...), custom_call_target="tpu_custom_call" | custom-call | tf_op jit(solution)/shard_map/first_weights/pallas_call | solution.py:467
  34.1 0.2 prefix.1
  34.3 1.1 %collective-permute-start.5 = (f32[8,128,128]{2,1,0:T(8,128)S(1)}, f32[8,128,128]{2,1,0:T(8,128)S(1)}, u32[]{:S(2)}, u32[]{:S(2)}) collective-permute-start(f32[8,128,128]{2,1,0:T(8,128)S(1)} %get-tuple-element.43), channel_id=1, source_target_pairs={{0,4},{4,0},{8,12},{12,8},{16,20},{20,16},{24,28},{28,24},{1,5},{5... | collective-permute-start | bytes 1572872 | tf_op jit(solution)/shard_map/ppermute | solution.py:345
  35.4 1.5 %collective-permute-done.5.other_ref = f32[8,128,128]{2,1,0:T(8,128)S(1)} collective-permute-done((f32[8,128,128]{2,1,0:T(8,128)S(1)}, f32[8,128,128]{2,1,0:T(8,128)S(1)}, u32[]{:S(2)}, u32[]{:S(2)}) %collective-permute-start.5) | collective-permute-done | bytes 524320 | tf_op jit(solution)/shard_map/ppermute | solution.py:345
  36.9 2.5 %earlier.1 = (f32[512,1536]{1,0:T(8,128)S(1)}, f32[512,512]{1,0:T(8,128)S(1)}, f32[8,512]{1,0:T(8,128)S(1)}) custom-call(f32[2,16]{1,0:T(2,128)S(1)} %copy-done, f32[16,128,128]{2,1,0:T(8,128)S(1)} %get-tuple-element.41.half_ref, f32[8,128,128]{2,1,0:T(8,128)S(1)} %get-tuple-element.42.mine_ref, f32[8,128,128]{2,1,0:T(8,128)S(1)} %collective-permute-done.5.other_ref, ...), custom_call_target="tpu_custom_call" | custom-call | tf_op jit(solution)/shard_map/earlier/pallas_call | solution.py:489
  39.4 2.0 %collective-permute-start.7 = (f32[8,512]{1,0:T(8,128)S(1)}, f32[8,512]{1,0:T(8,128)S(1)}, u32[]{:S(2)}, u32[]{:S(2)}) collective-permute-start(f32[8,512]{1,0:T(8,128)S(1)} %get-tuple-element.46._.refs_0_.refs_2_), channel_id=1, source_target_pairs={{0,2},{1,3},{2,0},{3,1},{4,6},{5,7},{6,4},{7,5},{8,10},{9,11},{10,... | collective-permute-start | bytes 49160 | tf_op jit(solution)/shard_map/ppermute | solution.py:345
  41.5 2.4 %collective-permute-start.8 = (f32[8,512]{1,0:T(8,128)S(1)}, f32[8,512]{1,0:T(8,128)S(1)}, u32[]{:S(2)}, u32[]{:S(2)}) collective-permute-start(f32[8,512]{1,0:T(8,128)S(1)} %get-tuple-element.46._.refs_0_.refs_2_), channel_id=1, source_target_pairs={{0,3},{1,2},{2,1},{3,0},{4,7},{5,6},{6,5},{7,4},{8,11},{9,10},{10,... | collective-permute-start | bytes 49160 | tf_op jit(solution)/shard_map/ppermute | solution.py:345
  43.8 0.8 %first_values.1 = (f32[128,2048]{1,0:T(8,128)S(1)}, f32[8,128]{1,0:T(8,128)S(1)}) custom-call(bf16[128,4096]{1,0:T(8,128)(2,1)S(1)} %get-tuple-element.35.weights_ref, f32[128,2048]{1,0:T(8,128)S(1)} %get-tuple-element.36.refs_0_.now_ref, f32[128,2048]{1,0:T(8,128)S(1)} %collective-permute-done.3.tail_v_ref, f32[8,512]{1,0:T(8,128)S(1)} %get-tuple-element.46._.refs_0_.refs_2_), custom_call_target="tpu_custom_call" | custom-call | tf_op jit(solution)/shard_map/first_values/pallas_call | solution.py:497
  44.7 2.6 %collective-permute-start.10 = (f32[8,128]{1,0:T(8,128)S(1)}, f32[8,128]{1,0:T(8,128)S(1)}, u32[]{:S(2)}, u32[]{:S(2)}) collective-permute-start(f32[8,128]{1,0:T(8,128)S(1)} %get-tuple-element.48._.refs_6_), channel_id=1, source_target_pairs={{0,2},{1,3},{2,0},{3,1},{4,6},{5,7},{6,4},{7,5},{8,10},{9,11},{10,... | collective-permute-start | bytes 12296 | tf_op jit(solution)/shard_map/ppermute | solution.py:345
  47.3 1.3 %collective-permute-start.11 = (f32[8,128]{1,0:T(8,128)S(1)}, f32[8,128]{1,0:T(8,128)S(1)}, u32[]{:S(2)}, u32[]{:S(2)}) collective-permute-start(f32[8,128]{1,0:T(8,128)S(1)} %get-tuple-element.48._.refs_6_), channel_id=1, source_target_pairs={{0,3},{1,2},{2,1},{3,0},{4,7},{5,6},{6,5},{7,4},{8,11},{9,10},{10,... | collective-permute-start | bytes 12296 | tf_op jit(solution)/shard_map/ppermute | solution.py:345
  48.7 0.2 collective-permute-start.9
  48.9 2.2 %scale.1._ = f32[512,2048]{1,0:T(8,128)} custom-call(f32[8,128]{1,0:T(8,128)S(1)} %get-tuple-element.48._.refs_6_, f32[8,512]{1,0:T(8,128)S(1)} %get-tuple-element.46._.refs_0_.refs_2_, f32[8,512]{1,0:T(8,128)S(1)} %collective-permute-done.6.refs_1_.refs_3_, f32[8,512]{1,0:T(8,128)S(1)} %collective-permute-done.7.refs_2_.refs_4_, ...), custom_call_target="tpu_custom_call" | custom-call | tf_op jit(solution)/shard_map/scale/pallas_call | solution.py:504
  51.1 1.6 %collective-permute-done.11.refs_9_ = f32[8,128]{1,0:T(8,128)S(1)} collective-permute-done((f32[8,128]{1,0:T(8,128)S(1)}, f32[8,128]{1,0:T(8,128)S(1)}, u32[]{:S(2)}, u32[]{:S(2)}) %collective-permute-start.11) | collective-permute-done | bytes 4128 | tf_op jit(solution)/shard_map/ppermute | solution.py:345
  52.7 1.2 %first_scale.1 = f32[512,2048]{1,0:T(8,128)} custom-call(f32[128,2048]{1,0:T(8,128)S(1)} %get-tuple-element.47.a_ref, f32[512,2048]{1,0:T(8,128)} %scale.1._, f32[512,1536]{1,0:T(8,128)S(1)} %get-tuple-element.51.refs_6_.refs_0_, f32[512,512]{1,0:T(8,128)S(1)} %get-tuple-element.52.refs_7_.refs_1_, ...), custom_call_target="tpu_custom_call", output_to_operand_aliasing={{}: (1, {})} | custom-call | tf_op jit(solution)/shard_map/first_scale/pallas_call | solution.py:512
  (15 shorter events, 0.2 us)
Async XLA Ops:
  4.2 2.3 %collective-permute-start = (f32[8,128,128]{2,1,0:T(8,128)S(1)}, f32[8,128,128]{2,1,0:T(8,128)S(1)}, u32[]{:S(2)}, u32[]{:S(2)}) collective-permute-start(f32[8,128,128]{2,1,0:T(8,128)S(1)} %get-tuple-element.29._), channel_id=1, source_target_pairs={{0,4},{4,0},{8,12},{12,8},{16,20},{20,16},{24,28},{28,24},{1,5},{5... | collective-permute-start | bytes 1572872 | tf_op jit(solution)/shard_map/ppermute | solution.py:345
  6.5 3.6 %copy-start = (f32[2,16]{1,0:T(2,128)S(1)}, f32[2,16]{1,0:T(2,128)}, u32[]{:S(2)}) copy-start(f32[2,16]{1,0:T(2,128)} %gain_ref.7) | copy-start | bytes 388
  6.6 12.0 %collective-permute-start.2 = (f32[8,128,128]{2,1,0:T(8,128)S(1)}, f32[8,128,128]{2,1,0:T(8,128)S(1)}, u32[]{:S(2)}, u32[]{:S(2)}) collective-permute-start(f32[8,128,128]{2,1,0:T(8,128)S(1)} %get-tuple-element.38.chip_ref), channel_id=1, source_target_pairs={{0,8},{4,20},{8,0},{12,28},{16,24},{20,4},{24,16},{28,12},{1,9},{5... | collective-permute-start | bytes 1572872 | tf_op jit(solution)/shard_map/ppermute | solution.py:353
  8.1 23.1 %collective-permute-start.1 = (f32[128,2048]{1,0:T(8,128)S(1)}, f32[128,2048]{1,0:T(8,128)S(1)}, u32[]{:S(2)}, u32[]{:S(2)}) collective-permute-start(f32[128,2048]{1,0:T(8,128)S(1)} %get-tuple-element.34), channel_id=1, source_target_pairs={{0,4},{4,8},{8,12},{12,16},{16,20},{20,24},{24,28},{1,5},{5,9},{9,... | collective-permute-start | bytes 3145736 | tf_op jit(solution)/shard_map/ppermute | solution.py:430
  18.6 15.4 %collective-permute-start.4 = (f32[8,128,128]{2,1,0:T(8,128)S(1)}, f32[8,128,128]{2,1,0:T(8,128)S(1)}, u32[]{:S(2)}, u32[]{:S(2)}) collective-permute-start(f32[8,128,128]{2,1,0:T(8,128)S(1)} %message.1.refs_0_), channel_id=1, source_target_pairs={{0,16},{4,12},{8,24},{12,4},{16,0},{20,28},{24,8},{28,20},{1,17},{... | collective-permute-start | bytes 1572872 | tf_op jit(solution)/shard_map/ppermute | solution.py:357
  22.1 21.7 %collective-permute-start.3 = (f32[128,2048]{1,0:T(8,128)S(1)}, f32[128,2048]{1,0:T(8,128)S(1)}, u32[]{:S(2)}, u32[]{:S(2)}) collective-permute-start(f32[128,2048]{1,0:T(8,128)S(1)} %pass.1), channel_id=1, source_target_pairs={{0,4},{4,8},{8,12},{12,16},{16,20},{20,24},{24,28},{1,5},{5,9},{9,... | collective-permute-start | bytes 3145736 | tf_op jit(solution)/shard_map/ppermute | solution.py:466
  34.3 2.6 %collective-permute-start.5 = (f32[8,128,128]{2,1,0:T(8,128)S(1)}, f32[8,128,128]{2,1,0:T(8,128)S(1)}, u32[]{:S(2)}, u32[]{:S(2)}) collective-permute-start(f32[8,128,128]{2,1,0:T(8,128)S(1)} %get-tuple-element.43), channel_id=1, source_target_pairs={{0,4},{4,0},{8,12},{12,8},{16,20},{20,16},{24,28},{28,24},{1,5},{5... | collective-permute-start | bytes 1572872 | tf_op jit(solution)/shard_map/ppermute | solution.py:345
  39.4 9.3 %collective-permute-start.6 = (f32[8,512]{1,0:T(8,128)S(1)}, f32[8,512]{1,0:T(8,128)S(1)}, u32[]{:S(2)}, u32[]{:S(2)}) collective-permute-start(f32[8,512]{1,0:T(8,128)S(1)} %get-tuple-element.46._.refs_0_.refs_2_), channel_id=1, source_target_pairs={{0,1},{1,0},{2,3},{3,2},{4,5},{5,4},{6,7},{7,6},{8,9},{9,8},{10,11... | collective-permute-start | bytes 49160 | tf_op jit(solution)/shard_map/ppermute | solution.py:345
  39.4 9.5 %collective-permute-start.7 = (f32[8,512]{1,0:T(8,128)S(1)}, f32[8,512]{1,0:T(8,128)S(1)}, u32[]{:S(2)}, u32[]{:S(2)}) collective-permute-start(f32[8,512]{1,0:T(8,128)S(1)} %get-tuple-element.46._.refs_0_.refs_2_), channel_id=1, source_target_pairs={{0,2},{1,3},{2,0},{3,1},{4,6},{5,7},{6,4},{7,5},{8,10},{9,11},{10,... | collective-permute-start | bytes 49160 | tf_op jit(solution)/shard_map/ppermute | solution.py:345
  41.5 7.5 %collective-permute-start.8 = (f32[8,512]{1,0:T(8,128)S(1)}, f32[8,512]{1,0:T(8,128)S(1)}, u32[]{:S(2)}, u32[]{:S(2)}) collective-permute-start(f32[8,512]{1,0:T(8,128)S(1)} %get-tuple-element.46._.refs_0_.refs_2_), channel_id=1, source_target_pairs={{0,3},{1,2},{2,1},{3,0},{4,7},{5,6},{6,5},{7,4},{8,11},{9,10},{10,... | collective-permute-start | bytes 49160 | tf_op jit(solution)/shard_map/ppermute | solution.py:345
  44.7 6.4 %collective-permute-start.10 = (f32[8,128]{1,0:T(8,128)S(1)}, f32[8,128]{1,0:T(8,128)S(1)}, u32[]{:S(2)}, u32[]{:S(2)}) collective-permute-start(f32[8,128]{1,0:T(8,128)S(1)} %get-tuple-element.48._.refs_6_), channel_id=1, source_target_pairs={{0,2},{1,3},{2,0},{3,1},{4,6},{5,7},{6,4},{7,5},{8,10},{9,11},{10,... | collective-permute-start | bytes 12296 | tf_op jit(solution)/shard_map/ppermute | solution.py:345
  47.3 5.4 %collective-permute-start.11 = (f32[8,128]{1,0:T(8,128)S(1)}, f32[8,128]{1,0:T(8,128)S(1)}, u32[]{:S(2)}, u32[]{:S(2)}) collective-permute-start(f32[8,128]{1,0:T(8,128)S(1)} %get-tuple-element.48._.refs_6_), channel_id=1, source_target_pairs={{0,3},{1,2},{2,1},{3,0},{4,7},{5,6},{6,5},{7,4},{8,11},{9,10},{10,... | collective-permute-start | bytes 12296 | tf_op jit(solution)/shard_map/ppermute | solution.py:345
  48.7 4.1 %collective-permute-start.9 = (f32[8,128]{1,0:T(8,128)S(1)}, f32[8,128]{1,0:T(8,128)S(1)}, u32[]{:S(2)}, u32[]{:S(2)}) collective-permute-start(f32[8,128]{1,0:T(8,128)S(1)} %get-tuple-element.48._.refs_6_), channel_id=1, source_target_pairs={{0,1},{1,0},{2,3},{3,2},{4,5},{5,4},{6,7},{7,6},{8,9},{9,8},{10,11... | collective-permute-start | bytes 12296 | tf_op jit(solution)/shard_map/ppermute | solution.py:345
